TPU v7x, 32 devices: a whole 2x2x4 slice. The times are simulated.
32 devices in a mesh: sample: 4 (over z), marker: 8 (over y, x, core).
Axes of the slice: x: 2, y: 2, z: 4, core: 2. Of those that a mesh axis runs over, the one named last changes fastest.
Arguments:
- genotypes: bfloat16 [8192, 131072], P('sample', 'marker'), may hold values from -6 to 6
- phenotypes: float32 [16, 8192], P(None, 'sample'), may hold values from -6 to 6
- message: float32 [16, 131072], P(None, 'marker'), may hold values from -6 to 6
- probes: float32 [112, 131072], P(None, 'marker'), may hold values from -16 to 16
- inclusion: float32 [16], replicated, may hold values from 0.3 to 0.6
- slab_ratio: float32 [16], replicated, may hold values from 0.25 to 0.67
- input_precision: float32 [16], replicated, may hold values from 0.5 to 2
- noise_precision: float32 [16], replicated, may hold values from 4 to 16
Outputs:
- estimate: float32 [16, 131072], P(None, 'marker')
- lmmse_estimate: float32 [16, 131072], P(None, 'marker')
All inputs are finite; a program needn't handle non-finite values.
Results may differ from a plain program's by a relative error of at most 0.0013.
Values may be sent and summed in bfloat16 or wider, within the bound.
No kernel may reach another device: no remote copies, remote signals or barrier semaphores. Data moves between devices by JAX's collectives and lax.ppermute only.
A program may use at most 192 MiB of HBM per device.

v0:
```python
import jax
import jax.numpy as jnp
from jax import lax
from jax.sharding import PartitionSpec as P

MARKERS = 131072
ITERS = 2


def denoise(signal, precision, shrink, logit_base):
    energy = shrink * precision * signal * signal
    weight = jax.nn.sigmoid(logit_base + 0.5 * energy)
    return (shrink * weight * signal, shrink * weight * (1.0 + (1.0 - weight) * energy))


def contract_rows(vectors, genotypes):
    return lax.dot_general(
        vectors, genotypes, (((1,), (1,)), ((), ())), preferred_element_type=jnp.float32
    )


def project(vectors_b, genotypes, offset):
    partial_value = contract_rows(vectors_b, genotypes)
    predicted = lax.psum(partial_value, "marker")
    if offset is not None:
        predicted = offset - predicted
    predicted_b = predicted.astype(jnp.bfloat16)
    widened = predicted_b.astype(jnp.float32)
    back_sum = jnp.dot(predicted_b, genotypes, preferred_element_type=jnp.float32)
    return (back_sum, jnp.sum(widened * widened, axis=1))


def per_device(
    genotypes, phenotypes, message, probes, inclusion, slab_ratio, input_precision, noise_precision
):
    people = genotypes.shape[0] * lax.axis_size("sample")
    traits = message.shape[0]
    copies = probes.shape[0] // traits + 1
    shrink = (slab_ratio / (1.0 + slab_ratio))[:, None]
    odds = jnp.log(inclusion / (1.0 - inclusion))[:, None]
    logit_base = odds + 0.5 * jnp.log(1.0 - shrink)
    first, slopes = denoise(message, input_precision[:, None], shrink, logit_base)
    first_slope = lax.psum(jnp.sum(slopes, axis=1), "marker") / MARKERS
    second_precision = input_precision * (1.0 - first_slope) / first_slope
    centre = (first - first_slope[:, None] * message) / (1.0 - first_slope)[:, None]
    start_back, unused_square = project(centre.astype(jnp.bfloat16), genotypes, phenotypes)
    start_back = lax.psum(start_back, "sample")
    start_res = noise_precision[:, None] / people * start_back
    scale_col = jnp.tile(noise_precision / people, copies)[:, None]
    prec_col = jnp.tile(second_precision, copies)[:, None]
    iterate = jnp.concatenate([centre, jnp.zeros(probes.shape, jnp.float32)], axis=0)
    residual = jnp.concatenate([start_res, probes], axis=0)
    direction = residual
    norm_start = lax.psum(jnp.sum(residual * residual, axis=1), "marker")
    norm_now = norm_start
    dir_norm = norm_start
    for iteration in range(ITERS):
        back_sum, square = project(direction.astype(jnp.bfloat16), genotypes, None)
        back_sum, square = lax.psum((back_sum, square), "sample")
        applied = scale_col * back_sum + prec_col * direction
        curvature = scale_col[:, 0] * square + prec_col[:, 0] * dir_norm
        step_size = norm_now / curvature
        iterate = iterate + step_size[:, None] * direction
        if iteration + 1 < ITERS:
            residual = residual - step_size[:, None] * applied
            norm_next, cross_term = lax.psum(
                (jnp.sum(residual * residual, axis=1), jnp.sum(residual * direction, axis=1)),
                "marker",
            )
            beta_ratio = norm_next / norm_now
            dir_norm = (
                norm_next + 2.0 * beta_ratio * cross_term + beta_ratio * beta_ratio * dir_norm
            )
            direction = residual + beta_ratio[:, None] * direction
            norm_now = norm_next
    lmmse_estimate = iterate[:traits]
    probe_local = jnp.sum(
        jnp.sum(probes * iterate[traits:], axis=1).reshape(copies - 1, traits), axis=0
    )
    probe_dot = lax.psum(probe_local, "marker")
    probe_norm = jnp.sum(norm_start[traits:].reshape(copies - 1, traits), axis=0)
    second_slope = second_precision * probe_dot / (probe_norm + 1e-06)
    next_precision = second_precision * (1.0 - second_slope) / second_slope
    next_message = (lmmse_estimate - second_slope[:, None] * centre) / (1.0 - second_slope)[:, None]
    slab_var = slab_ratio / input_precision
    next_shrink = (slab_var * next_precision / (1.0 + slab_var * next_precision))[:, None]
    next_base = odds + 0.5 * jnp.log(1.0 - next_shrink)
    estimate, unused_slopes = denoise(next_message, next_precision[:, None], next_shrink, next_base)
    return (estimate, lmmse_estimate)


def solution(mesh):
    return jax.shard_map(
        per_device,
        mesh=mesh,
        in_specs=(
            P("sample", "marker"),
            P(None, "sample"),
            P(None, "marker"),
            P(None, "marker"),
            P(),
            P(),
            P(),
            P(),
        ),
        out_specs=(P(None, "marker"), P(None, "marker")),
        check_vma=False,
    )
```

profile of v0, /device:TPU:0, one launch (start us, length us, event | category | flops | bytes accessed | tf_op | source)
XLA Modules:
  0.0 736.6 jit_solution(16172849491147346062)
XLA Ops:
  7.2 0.0 all-reduce.9.cloned.1.call-start
  7.2 0.7 multiply_add_fusion.4
  7.9 0.7 mul.206
  8.6 1.9 multiply_reduce_fusion.5
  10.4 15.1 %psum.84 = f32[16]{0:T(128)S(1)} all-reduce(f32[16]{0:T(128)S(1)} %multiply_reduce_fusion.5), channel_id=1, replica_groups=mesh['sample'=4,'marker'=8] {'marker'}, use_global_device_ids=true, to_apply=%region_1.0 | all-reduce | flops 16 | bytes 128 | tf_op jit(solution)/shard_map/psum | solution.py:43
  25.6 0.7 multiply_divide_fusion.1
  26.2 1.7 subtract_divide_fusion
  28.0 0.0 copy-start.3
  28.0 26.1 %fusion.13 = f32[16,2048]{1,0:T(8,128)} fusion(bf16[2048,16384]{1,0:T(8,128)(2,1)} %param.8, f32[16,16384]{1,0:T(8,128)S(1)} %subtract_divide_fusion), kind=kOutput, calls=%fused_computation.28 | convolution fusion | flops 1074003968 | bytes 68288512 | tf_op jit(solution)/shard_map/dot_general | solution.py:17
  54.1 0.0 all-reduce.9.cloned.1.call-update
  54.1 0.0 copy-start.6
  54.1 0.0 all-reduce.11.cloned.1.call-start
  54.1 52.4 %all-reduce.9.cloned.1.call-done = f32[16,2048]{1,0:T(8,128)} async-done(((f32[16,2048]{1,0:T(8,128)}), f32[16,2048]{1,0:T(8,128)}) %all-reduce.9.cloned.1.call-update) | async-done | bytes 131088 | tf_op jit(solution)/shard_map/psum | solution.py:24
  106.5 0.0 copy-done.3
  106.5 24.4 %fusion.17 = f32[16,16384]{1,0:T(8,128)} fusion(bf16[2048,16384]{1,0:T(8,128)(2,1)} %param.8, f32[16,2048]{1,0:T(8,128)S(1)} %copy-done.3, f32[16,2048]{1,0:T(8,128)} %all-reduce.9.cloned.1.call-done), kind=kOutput, calls=%fused_computation.34 | convolution fusion | flops 1073807360 | bytes 68419584 | tf_op jit(solution)/shard_map/dot_general | solution.py:29
  130.9 0.0 all-reduce.11.cloned.1.call-update
  131.0 0.0 all-reduce.13.cloned.1.call-start
  131.0 0.0 copy-done.6
  131.0 51.3 %all-reduce.11.cloned.1.call-done = f32[16,16384]{1,0:T(8,128)} async-done(((f32[16,16384]{1,0:T(8,128)}), f32[16,16384]{1,0:T(8,128)}) %all-reduce.11.cloned.1.call-update) | async-done | bytes 1048592 | tf_op jit(solution)/shard_map/psum | solution.py:47
  182.3 1.4 broadcast_multiply_fusion
  183.7 3.5 multiply_reduce_fusion.2
  187.2 30.6 %fusion.3 = f32[128,2048]{1,0:T(8,128)S(1)} fusion(bf16[2048,16384]{1,0:T(8,128)(2,1)} %param.8, f32[112,16384]{1,0:T(8,128)} %param.11, f32[16,16384]{1,0:T(8,128)S(1)} %broadcast_multiply_fusion), kind=kOutput, calls=%fused_computation.11 | convolution fusion | flops 8598323200 | bytes 76546048 | tf_op jit(solution)/shard_map/dot_general | solution.py:17
  217.8 52.5 %all-reduce.14 = (bf16[128,2048]{1,0:T(8,128)(2,1)}, f32[128]{0:T(128)S(1)}) all-reduce(f32[128,2048]{1,0:T(8,128)S(1)} %fusion.3, f32[128]{0:T(128)S(1)} %multiply_reduce_fusion.2), channel_id=1, replica_groups=mesh['sample'=4,'marker'=8] {'marker'}, use_global_device_ids=true, to_apply=%region_6.0 | all-reduce | flops 262272 | bytes 1573888 | tf_op jit(solution)/shard_map/psum | solution.py:24
  270.3 27.3 %fusion.22 = f32[128,16384]{1,0:T(8,128)} fusion(bf16[128,2048]{1,0:T(8,128)(2,1)} %get-tuple-element.6, bf16[2048,16384]{1,0:T(8,128)(2,1)} %param.8), kind=kOutput, calls=%fused_computation.52 | convolution fusion | flops 8589934592 | bytes 76021760 | tf_op jit(solution)/shard_map/dot_general | solution.py:29
  297.5 0.0 all-reduce.13.cloned.1.call-update
  297.6 0.1 squeeze_broadcast_in_dim_tile.9
  297.7 0.1 squeeze_broadcast_in_dim_tile.8
  297.7 0.1 slice.18
  297.8 0.1 reshape.48
  297.9 0.7 copy-done.2
  298.6 0.2 multiply_reduce_fusion.4
  298.8 10.5 %psum.89 = f32[128]{0:T(128)S(1)} all-reduce(f32[128]{0:T(128)S(1)} %multiply_reduce_fusion.4), channel_id=1, replica_groups=mesh['sample'=4,'marker'=8] {'sample'}, use_global_device_ids=true, to_apply=%region_8.0 | all-reduce | flops 128 | bytes 1024 | tf_op jit(solution)/shard_map/psum | solution.py:59
  309.2 277.1 %all-reduce.13.cloned.1.call-done = f32[128,16384]{1,0:T(8,128)} async-done(((f32[128,16384]{1,0:T(8,128)}), f32[128,16384]{1,0:T(8,128)}) %all-reduce.13.cloned.1.call-update) | async-done | bytes 8388624 | tf_op jit(solution)/shard_map/psum | solution.py:59
  586.4 7.0 multiply_reduce_fusion
  593.4 13.6 %psum.91 = f32[128]{0:T(128)S(1)} all-reduce(f32[128]{0:T(128)S(1)} %get-tuple-element.3), channel_id=1, replica_groups=mesh['sample'=4,'marker'=8] {'marker'}, use_global_device_ids=true, to_apply=%region_11.0 | all-reduce | flops 128 | bytes 1024 | tf_op jit(solution)/shard_map/psum | solution.py:66
  607.0 30.8 %fusion.1 = f32[128,2048]{1,0:T(8,128)S(1)} fusion(bf16[2048,16384]{1,0:T(8,128)(2,1)} %param.8, f32[128]{0:T(128)S(1)} %div.69, f32[112,16384]{1,0:T(8,128)} %param.11, f32[16,16384]{1,0:T(8,128)S(1)} %broadcast_multiply_fusion, f32[128,16384]{1,0:T(8,128)} %all-reduce.13.cloned.1.call-done, f32[128]{0:T(128)S(1)} %squeeze_broadcast_in_dim_tile.9, ...), kind=kOutput, calls=%fused_computation.9 | convolution fusion | flops 8608808960 | bytes 84936704 | tf_op jit(solution)/shard_map/dot_general | solution.py:17
  637.9 50.5 %all-reduce.15 = (f32[128]{0:T(128)S(1)}, bf16[128,2048]{1,0:T(8,128)(2,1)}) all-reduce(f32[128]{0:T(128)S(1)} %get-tuple-element.2, f32[128,2048]{1,0:T(8,128)S(1)} %fusion.1), channel_id=1, replica_groups=mesh['sample'=4,'marker'=8] {'marker'}, use_global_device_ids=true, to_apply=%region_16.0 | all-reduce | flops 262272 | bytes 1573888 | tf_op jit(solution)/shard_map/psum | solution.py:66
  688.4 1.2 multiply_reduce_fusion.3
  689.6 9.9 %psum.93 = f32[128]{0:T(128)S(1)} all-reduce(f32[128]{0:T(128)S(1)} %multiply_reduce_fusion.3), channel_id=1, replica_groups=mesh['sample'=4,'marker'=8] {'sample'}, use_global_device_ids=true, to_apply=%region_14.0 | all-reduce | flops 128 | bytes 1024 | tf_op jit(solution)/shard_map/psum | solution.py:59
  699.5 7.4 multiply_add_fusion
  706.9 0.0 copy-start
  706.9 3.2 copy-done
  710.1 4.5 fusion
  714.7 0.1 reshape.47
  714.8 11.8 %psum.95 = f32[16]{0:T(128)S(1)} all-reduce(f32[16]{0:T(128)S(1)} %reduce_sum.88), channel_id=1, replica_groups=mesh['sample'=4,'marker'=8] {'marker'}, use_global_device_ids=true, to_apply=%region_19.0 | all-reduce | flops 16 | bytes 128 | tf_op jit(solution)/shard_map/psum | solution.py:80
  726.6 0.0 copy-done.5
  726.6 0.0 copy-done.1
  726.6 3.4 fusion.12
  (16 shorter events, 0.1 us)
Async XLA Ops:
  7.2 99.4 %all-reduce.9.cloned.1.call-start = ((), (), s32[]{:S(2)}) async-start(), calls=%async_computation | async-start | bytes 262144 | tf_op jit(solution)/shard_map/psum | solution.py:24
  28.0 78.5 %copy-start.3 = (f32[16,2048]{1,0:T(8,128)S(1)}, f32[16,2048]{1,0:T(8,128)}, u32[]{:S(2)}) copy-start(f32[16,2048]{1,0:T(8,128)} %param.9) | copy-start | bytes 393220
  54.1 76.9 %copy-start.6 = (f32[16]{0:T(128)S(1)}, f32[16]{0:T(128)}, u32[]{:S(2)}) copy-start(f32[16]{0:T(128)} %param.15) | copy-start | bytes 196
  54.1 128.2 %all-reduce.11.cloned.1.call-start = ((), (), s32[]{:S(2)}) async-start(), calls=%async_computation.1 | async-start | bytes 2097152 | tf_op jit(solution)/shard_map/psum | solution.py:47
  131.0 455.4 %all-reduce.13.cloned.1.call-start = ((), (), s32[]{:S(2)}) async-start(), calls=%async_computation.2 | async-start | bytes 16777216 | tf_op jit(solution)/shard_map/psum | solution.py:59
  297.5 1.0 copy-start.2
  706.9 3.2 copy-start
  710.1 16.5 %copy-start.4 = (f32[16]{0:T(128)S(1)}, f32[16]{0:T(128)}, u32[]{:S(2)}) copy-start(f32[16]{0:T(128)} %param.13) | copy-start | bytes 196
  710.1 16.5 %copy-start.5 = (f32[16]{0:T(128)S(1)}, f32[16]{0:T(128)}, u32[]{:S(2)}) copy-start(f32[16]{0:T(128)} %param.14) | copy-start | bytes 196
  710.1 16.5 %copy-start.1 = (f32[16,16384]{1,0:T(8,128)S(1)}, f32[16,16384]{1,0:T(8,128)}, u32[]{:S(2)}) copy-start(f32[16,16384]{1,0:T(8,128)} %param.10) | copy-start | bytes 3145732
Sparse Core Ops, SparseCore 0:
  54.2 52.2 all-reduce.8
  131.1 51.1 all-reduce.10
  297.7 288.6 all-reduce.12
where the time goes:
time: 737 us
  waiting for transfers between devices  381 us (52%)
  blocking collectives  164 us (22%)
  matrix products  139 us (19%)
  other arithmetic  34.4 us (5%)
  between operations  13.9 us (2%)
    psum x1, waiting for transfers between devices, per_device(): back_sum, square = lax.psum((back_sum, square), 'sample')  277 us
    dot_general x3, matrix products, contract_rows(): lax.dot_general(vectors, genotypes, (((1,), (1,)), ((), ())), preferred_e...  87.5 us
    psum x2, blocking collectives, per_device(): lax.psum((jnp.sum(residual * residual, axis=1), jnp.sum(residual * direct...  64.2 us
    psum x1, blocking collectives, project(): predicted = lax.psum(partial_value, 'marker')  52.5 us
    psum x1, waiting for transfers between devices, project(): predicted = lax.psum(partial_value, 'marker')  52.4 us
    dot_general x2, matrix products, project(): jnp.dot(predicted_b, genotypes, preferred_element_type=jnp.float32)  51.7 us
    psum x1, waiting for transfers between devices, per_device(): start_back = lax.psum(start_back, 'sample')  51.3 us
    psum x2, blocking collectives, per_device(): back_sum, square = lax.psum((back_sum, square), 'sample')  20.4 us
  transfers between devices with their start and end apart: 3, of which 3 were waited for; matrix products, arithmetic and copies ran while one was open for 0% of the time, Pallas kernels for 0%

commit v1 on v0

v1 whole, which is shorter than its diff:
```python
import functools

import jax
import jax.numpy as jnp
from jax import lax
from jax.experimental import pallas as pl
from jax.experimental.pallas import tpu as pltpu
from jax.sharding import PartitionSpec as P

F32 = jnp.float32
BF16 = jnp.bfloat16
LIMIT = 44 << 20
SLOTS = 4
VMEM = pl.BlockSpec(memory_space=pltpu.VMEM)
ANY = pl.BlockSpec(memory_space=pl.ANY)


def block_of(size, most):
    while size % most:
        most //= 2
    return most


def swap(x, axis, bits):
    n = lax.axis_size(axis)
    return lax.ppermute(x, axis, [(i, i ^ bits) for i in range(n)])


def tree(parts):
    while len(parts) > 1:
        parts = [parts[i] + parts[i + 1] for i in range(0, len(parts), 2)]
    return parts[0]


def sum_direct(x, axis, unit=1):
    n = lax.axis_size(axis)
    return tree([x if k == 0 else swap(x, axis, k) for k in range(0, n, unit)])


def sum_marker(x):
    return sum_direct(x + swap(x, "marker", 1), "marker", 2)


def denoise(signal, precision, shrink, logit_base):
    energy = shrink * precision * signal * signal
    weight = jax.nn.sigmoid(logit_base + 0.5 * energy)
    return (shrink * weight * signal, shrink * weight * (1.0 + (1.0 - weight) * energy))


def stream(place, held, sems, total, prepare, use):
    slots = held.shape[0]

    def copy(c):
        slot = lax.rem(c, slots)
        return pltpu.make_async_copy(place(c), held.at[slot], sems.at[slot])

    for c in range(min(slots, total)):
        copy(c).start()
    prepare()

    def step(c, carry):
        copy(c).wait()
        use(c, held.at[lax.rem(c, slots)])

        @pl.when(c + slots < total)
        def _():
            copy(c + slots).start()

        return carry

    lax.fori_loop(0, total, step, 0)


def ring(rows, columns):
    return [pltpu.VMEM((SLOTS, rows, columns), BF16), pltpu.SemaphoreType.DMA((SLOTS,))]


def forward_loop(g, rows, total, held, sems, off, span, pieces, wide, fresh, prepare):
    people = g.shape[0]
    slots, pb, kb = held.shape
    steps, blocks = span // kb, people // pb

    def place(c):
        k, i = c // blocks, lax.rem(c, blocks)
        col = off[k // steps] * span + lax.rem(k, steps) * kb
        return g.at[pl.ds(pl.multiple_of(i * pb, pb), pb), pl.ds(pl.multiple_of(col, kb), kb)]

    def use(c, slot):
        k, i = c // blocks, lax.rem(c, blocks)
        d = rows[:, pl.ds(pl.multiple_of(k * kb, kb), kb)]
        here = pl.ds(pl.multiple_of(i * pb, pb), pb)
        across = (((1,), (1,)), ((), ()))
        if wide:
            at = (here, slice(None))
            value = lax.dot_general(slot[...], d, across, preferred_element_type=F32)
        else:
            at = (slice(None), here)
            value = lax.dot_general(d, slot[...], across, preferred_element_type=F32)
        if fresh:

            @pl.when(k == 0)
            def _():
                total[at] = value

            @pl.when(k > 0)
            def _():
                total[at] += value

        else:
            total[at] += value

    stream(place, held, sems, pieces * steps * blocks, prepare, use)


def split_people(out, total):
    n, _, share = out.shape
    for b in range(n):
        out[b] = total[b * share : (b + 1) * share, :].T


def first_body(off, message, cols, probes, g, out, centre, rows, held, sems, total):
    t = message.shape[0]

    def prepare():
        precision, shrink, base, slope = [cols[:, j : j + 1] for j in range(4)]
        first, _ = denoise(message[...], precision, shrink, base)
        made = (first - slope * message[...]) / (1.0 - slope)
        centre[...] = made
        rows[:t, :] = made.astype(BF16)
        rows[t:, :] = probes[...].astype(BF16)

    forward_loop(g, rows, total, held, sems, off, g.shape[1], 1, True, True, prepare)
    split_people(out, total)


def cost(rows, people, markers):
    return pl.CostEstimate(
        flops=2 * rows * people * markers, transcendentals=0, bytes_accessed=2 * people * markers
    )


def first_forward(message, cols, probes, genotypes, columns):
    people, markers = genotypes.shape
    r = message.shape[0] + probes.shape[0]
    pb, kb = block_of(people, 1024), block_of(markers, 2048)
    return pl.pallas_call(
        first_body,
        grid_spec=pltpu.PrefetchScalarGridSpec(
            num_scalar_prefetch=1,
            grid=(),
            in_specs=[VMEM, VMEM, VMEM, ANY],
            out_specs=[VMEM, VMEM],
            scratch_shapes=[
                pltpu.VMEM((r, markers), BF16),
                *ring(pb, kb),
                pltpu.VMEM((people, r), F32),
            ],
        ),
        out_shape=[
            jax.ShapeDtypeStruct((columns, r, people // columns), F32),
            jax.ShapeDtypeStruct(message.shape, F32),
        ],
        compiler_params=pltpu.CompilerParams(vmem_limit_bytes=LIMIT),
        cost_estimate=cost(r, people, markers),
        name="first_forward",
    )(jnp.zeros((1,), jnp.int32), message, cols, probes, genotypes)


def narrow_body(n, with_acc, off, *refs):
    refs = list(refs)
    pieces = [refs.pop(0) for _ in range(n)]
    acc = refs.pop(0) if with_acc else None
    g, out, rows, held, sems = refs
    span = pieces[0].shape[1]

    def prepare():
        for j in range(n):
            rows[:, j * span : (j + 1) * span] = pieces[j][...]
        if with_acc:
            out[...] = acc[...]

    forward_loop(g, rows, out, held, sems, off, span, n, False, not with_acc, prepare)


def narrow_forward(pieces, places, acc, genotypes, name):
    people = genotypes.shape[0]
    n, (t, span) = len(pieces), pieces[0].shape
    pb, kb = block_of(people, 1024), block_of(span, 2048)
    operands = [*pieces, *([] if acc is None else [acc]), genotypes]
    return pl.pallas_call(
        functools.partial(narrow_body, n, acc is not None),
        grid_spec=pltpu.PrefetchScalarGridSpec(
            num_scalar_prefetch=1,
            grid=(),
            in_specs=[VMEM] * (len(operands) - 1) + [ANY],
            out_specs=VMEM,
            scratch_shapes=[pltpu.VMEM((t, n * span), BF16), *ring(pb, kb)],
        ),
        out_shape=jax.ShapeDtypeStruct((t, people), F32),
        compiler_params=pltpu.CompilerParams(vmem_limit_bytes=LIMIT),
        cost_estimate=cost(t, people, n * span),
        name=name,
    )(places, *operands)


def wide_body(n, with_acc, off, *refs):
    refs = list(refs)
    pieces = [refs.pop(0) for _ in range(n)]
    probes = refs.pop(0)
    acc = refs.pop(0) if with_acc else None
    if with_acc:
        g, out, rows, held, sems, total = refs
    else:
        g, total, rows, held, sems = refs
    t, span = pieces[0].shape

    def prepare():
        for j in range(n):
            here = slice(j * span, (j + 1) * span)
            rows[:t, here] = pieces[j][...]
            rows[t:, here] = probes[:, pl.ds(pl.multiple_of(off[j] * span, span), span)]
        if with_acc:
            total[...] = acc[...]

    forward_loop(g, rows, total, held, sems, off, span, n, True, not with_acc, prepare)
    if with_acc:
        split_people(out, total)


def wide_forward(pieces, probes, places, acc, genotypes, columns, name):
    people = genotypes.shape[0]
    n, (t, span) = len(pieces), pieces[0].shape
    r = t + probes.shape[0]
    pb, kb = block_of(people, 1024), block_of(span, 2048)
    operands = [*pieces, probes, *([] if acc is None else [acc]), genotypes]
    scratch = [pltpu.VMEM((r, n * span), BF16), *ring(pb, kb)]
    if acc is None:
        shape = (people, r)
    else:
        shape = (columns, r, people // columns)
        scratch.append(pltpu.VMEM((people, r), F32))
    return pl.pallas_call(
        functools.partial(wide_body, n, acc is not None),
        grid_spec=pltpu.PrefetchScalarGridSpec(
            num_scalar_prefetch=1,
            grid=(),
            in_specs=[VMEM] * (len(operands) - 1) + [ANY],
            out_specs=VMEM,
            scratch_shapes=scratch,
        ),
        out_shape=jax.ShapeDtypeStruct(shape, F32),
        compiler_params=pltpu.CompilerParams(vmem_limit_bytes=LIMIT),
        cost_estimate=cost(r, people, n * span),
        name=name,
    )(places, *operands)


def backward_loop(g, rows, total, held, sems, off, span, pieces):
    people = g.shape[0]
    slots, pk, mb = held.shape
    steps, blocks = span // mb, people // pk

    def place(c):
        k, i = c // blocks, lax.rem(c, blocks)
        col = off[k // steps] * span + lax.rem(k, steps) * mb
        return g.at[pl.ds(pl.multiple_of(i * pk, pk), pk), pl.ds(pl.multiple_of(col, mb), mb)]

    def use(c, slot):
        k, i = c // blocks, lax.rem(c, blocks)
        here = pl.ds(pl.multiple_of(k * mb, mb), mb)
        d = rows[:, pl.ds(pl.multiple_of(i * pk, pk), pk)]
        value = jnp.dot(d, slot[...], preferred_element_type=F32)

        @pl.when(i == 0)
        def _():
            total[:, here] = value

        @pl.when(i > 0)
        def _():
            total[:, here] += value

    stream(place, held, sems, pieces * steps * blocks, lambda: None, use)


def narrow_back_body(n, span, off, rows, g, out, held, sems):
    backward_loop(g, rows, out, held, sems, off, span, n)


def wide_back_body(n, span, t, off, rows, g, *refs):
    out, whole, total, made, sent, held, sems = refs[-7:]
    backward_loop(g, rows, total, held, sems, off, span, n)
    made[...] = total[t:, :].astype(BF16)
    copies = []
    for j in range(n):
        cols = pl.ds(pl.multiple_of(off[j] * span, span), span)
        copies.append(
            pltpu.make_async_copy(made.at[:, pl.ds(j * span, span)], whole.at[:, cols], sent.at[j])
        )
        copies[-1].start()
    out[...] = total[:t, :]
    for copy in copies:
        copy.wait()


def backward(rows, places, genotypes, span, t, whole, name):
    people, markers = genotypes.shape
    r, n = rows.shape[0], places.shape[0]
    pk, mb = block_of(people, 1024), block_of(span, 2048)
    operands, specs, aliases = [rows, genotypes], [VMEM, ANY], {}
    if t is None:
        body = functools.partial(narrow_back_body, n, span)
        out_specs, out_shape = VMEM, jax.ShapeDtypeStruct((r, n * span), F32)
        scratch = ring(pk, mb)
    else:
        body = functools.partial(wide_back_body, n, span, t)
        out_specs = [VMEM, ANY]
        out_shape = [
            jax.ShapeDtypeStruct((t, n * span), F32),
            jax.ShapeDtypeStruct((r - t, markers), BF16),
        ]
        scratch = [
            pltpu.VMEM((r, n * span), F32),
            pltpu.VMEM((r - t, n * span), BF16),
            pltpu.SemaphoreType.DMA((n,)),
            *ring(pk, mb),
        ]
        if whole is not None:
            operands.append(whole)
            specs.append(ANY)
            aliases = {3: 1}
    return pl.pallas_call(
        body,
        grid_spec=pltpu.PrefetchScalarGridSpec(
            num_scalar_prefetch=1,
            grid=(),
            in_specs=specs,
            out_specs=out_specs,
            scratch_shapes=scratch,
        ),
        out_shape=out_shape,
        input_output_aliases=aliases,
        compiler_params=pltpu.CompilerParams(vmem_limit_bytes=LIMIT),
        cost_estimate=cost(r, people, n * span),
        name=name,
    )(places, *operands)


def finish_body(n, copies, off, sums, wide_cols, cols, centre, *refs):
    start_hi, back_hi, low = refs[:n], refs[n : 2 * n], refs[2 * n : 3 * n]
    estimate, lmmse = refs[3 * n :]
    t, span = start_hi[0].shape
    norm_start, du, uu, xx, xw, ww = [sums[:, j : j + 1] for j in range(6)]
    tau, gamma = wide_cols[:, 0:1], wide_cols[:, 1:2]
    second_precision, slab_var, odds = [cols[:, j : j + 1] for j in range(3)]

    step_0 = norm_start / (tau * du + gamma * norm_start)
    left, b = 1.0 - step_0 * gamma, step_0 * tau
    norm_next = left * left * norm_start - 2.0 * left * b * du + b * b * uu
    a = left + norm_next / norm_start
    dir_norm = a * a * norm_start - 2.0 * a * b * du + b * b * uu
    dir_square = a * a * xx - 2.0 * a * b * xw + b * b * ww
    step_1 = norm_next / (tau * dir_square + gamma * dir_norm)

    start_coef = (step_0 + step_1 * a)[:t]
    back_coef = (step_1 * b)[:t]
    dots = step_0 * norm_start + step_1 * (a * norm_start - b * du)
    probe_dot = sum(dots[i * t : (i + 1) * t] for i in range(1, copies))
    probe_norm = sum(norm_start[i * t : (i + 1) * t] for i in range(1, copies))
    second_slope = second_precision * probe_dot / (probe_norm + 1e-06)
    next_precision = second_precision * (1.0 - second_slope) / second_slope
    next_shrink = slab_var * next_precision / (1.0 + slab_var * next_precision)
    next_base = odds + 0.5 * jnp.log(1.0 - next_shrink)
    for j in range(n):
        here = pl.ds(pl.multiple_of(off[j] * span, span), span)
        start = start_hi[j][...].astype(F32) + low[j][:t, :].astype(F32)
        back = back_hi[j][...].astype(F32) + low[j][t:, :].astype(F32)
        middle = centre[:, here]
        made = middle + start_coef * start - back_coef * back
        lmmse[:, here] = made
        next_message = (made - second_slope * middle) / (1.0 - second_slope)
        value, _ = denoise(next_message, next_precision, next_shrink, next_base)
        estimate[:, here] = value


def finish(places, sums, wide_cols, cols, centre, start_hi, back_hi, low):
    n = len(low)
    shape = jax.ShapeDtypeStruct(centre.shape, F32)
    copies = sums.shape[0] // centre.shape[0]
    operands = [sums, wide_cols, cols, centre, *start_hi, *back_hi, *low]
    return pl.pallas_call(
        functools.partial(finish_body, n, copies),
        grid_spec=pltpu.PrefetchScalarGridSpec(
            num_scalar_prefetch=1, grid=(), in_specs=[VMEM] * len(operands), out_specs=[VMEM, VMEM]
        ),
        out_shape=[shape, shape],
        compiler_params=pltpu.CompilerParams(vmem_limit_bytes=LIMIT),
        name="finish",
    )(places, *operands)


def per_device(
    genotypes, phenotypes, message, probes, inclusion, slab_ratio, input_precision, noise_precision
):
    samples, columns = lax.axis_size("sample"), lax.axis_size("marker")
    people_here, markers_here = genotypes.shape
    people, markers = people_here * samples, markers_here * columns
    traits = message.shape[0]
    copies = probes.shape[0] // traits + 1
    me, column = lax.axis_index("sample"), lax.axis_index("marker")
    quarter, share = markers_here // samples, people_here // columns
    order = jnp.arange(samples, dtype=jnp.int32) ^ me
    near, far = order[: samples // 2], order[samples // 2 :]
    halves = samples // 2

    shrink = slab_ratio / (1.0 + slab_ratio)
    odds = jnp.log(inclusion / (1.0 - inclusion))
    logit_base = odds + 0.5 * jnp.log(1.0 - shrink)
    _, slopes = denoise(message, input_precision[:, None], shrink[:, None], logit_base[:, None])
    first_slope = sum_marker(jnp.sum(slopes, axis=1, keepdims=True))[:, 0] / markers
    second_precision = input_precision * (1.0 - first_slope) / first_slope
    scale = (noise_precision / people)[:, None]

    cols = jnp.stack([input_precision, shrink, logit_base, first_slope], axis=1)
    value, centre = first_forward(message, cols, probes, genotypes, columns)
    kept_x = jnp.sum(lax.all_to_all(value, "marker", 0, 0), axis=0)
    own = lax.dynamic_slice_in_dim(phenotypes, column * share, share, 1) - kept_x[:traits]
    rows = jnp.concatenate([own, kept_x[traits:]], axis=0).astype(BF16)
    rows = lax.all_gather(rows, "marker", axis=1, tiled=True)
    part, whole = backward(rows, far, genotypes, quarter, traits, None, "first_back_far")
    sent = {k: swap(part[:, (k - halves) * quarter :][:, :quarter], "sample", k) for k in range(halves, samples)}
    part, whole = backward(rows, near, genotypes, quarter, traits, whole, "first_back_near")
    for k in range(halves):
        mine = part[:, k * quarter : (k + 1) * quarter]
        sent[k] = swap(mine, "sample", k) if k else mine
    start = scale * tree([sent[k] for k in range(samples)])
    start_hi = start.astype(BF16)

    probe_back = lax.psum(whole, "sample")

    start_pieces = [swap(start_hi, "sample", k) if k else start_hi for k in range(samples)]
    value = narrow_forward(start_pieces[:halves], near, None, genotypes, "second_forward_near")
    value = narrow_forward(start_pieces[halves:], far, value, genotypes, "second_forward_far")
    value = sum_marker(value)
    kept_s = lax.dynamic_slice_in_dim(value, column * share, share, 1)
    rows = value.astype(BF16)
    part = backward(rows, far, genotypes, quarter, None, None, "second_back_far")
    sent = {k: swap(part[:, (k - halves) * quarter :][:, :quarter], "sample", k) for k in range(halves, samples)}
    part = backward(rows, near, genotypes, quarter, None, None, "second_back_near")
    for k in range(halves):
        mine = part[:, k * quarter : (k + 1) * quarter]
        sent[k] = swap(mine, "sample", k) if k else mine
    back = tree([sent[k] for k in range(samples)])
    back_hi = back.astype(BF16)
    back_pieces = [swap(back_hi, "sample", k) if k else back_hi for k in range(samples)]

    total = wide_forward(
        back_pieces[:halves], probe_back, near, None, genotypes, columns, "third_forward_near"
    )
    low = jnp.concatenate([start - start_hi.astype(F32), back - back_hi.astype(F32)], axis=0)
    low, total = lax.optimization_barrier((low.astype(BF16), total))
    low_pieces = [swap(low, "sample", k) if k else low for k in range(samples)]
    value = wide_forward(
        back_pieces[halves:], probe_back, far, total, genotypes, columns, "third_forward_far"
    )
    last = jnp.sum(lax.all_to_all(value, "marker", 0, 0), axis=0)
    before = jnp.concatenate([kept_s, kept_x[traits:]], axis=0)

    def quarter_of(x):
        return lax.dynamic_slice_in_dim(x, me * quarter, quarter, 1)

    def three(d, u):
        return jnp.stack([jnp.sum(d * d, 1), jnp.sum(d * u, 1), jnp.sum(u * u, 1)], axis=1)

    norms = jnp.concatenate(
        [three(start, back), three(quarter_of(probes), quarter_of(probe_back).astype(F32))], axis=0
    )
    sums = jnp.concatenate([norms, three(before, last)], axis=1)
    sums = sum_direct(sum_marker(sums), "sample")

    wide_cols = jnp.stack(
        [jnp.tile(noise_precision / people, copies), jnp.tile(second_precision, copies)], axis=1
    )
    cols = jnp.stack([second_precision, slab_ratio / input_precision, odds], axis=1)
    return tuple(
        finish(order, sums, wide_cols, cols, centre, start_pieces, back_pieces, low_pieces)
    )


def solution(mesh):
    return jax.shard_map(
        per_device,
        mesh=mesh,
        in_specs=(
            P("sample", "marker"),
            P(None, "sample"),
            P(None, "marker"),
            P(None, "marker"),
            P(),
            P(),
            P(),
            P(),
        ),
        out_specs=(P(None, "marker"), P(None, "marker")),
        check_vma=False,
    )
```

time: 737 us -> 392 us (0.53)
  waiting for transfers between devices: 381 us -> 157 us
  blocking collectives: 164 us -> 10.1 us
  matrix products: 139 us -> 0 us
  Pallas kernels: 0 us -> 135 us
  starting transfers between devices: 0.12 us -> 51.1 us
  other arithmetic: 34.4 us -> 14.8 us
    psum x3 -> x1, waiting for transfers between devices: 381 us -> 54.9 us  [per_device(): probe_back = lax.psum(whole, 'sample')]
    psum x7 -> x0, blocking collectives: 164 us -> none  [the longest x2 64.2 us: per_device(): lax.psum((jnp.sum(residual * residual, axis=1), jnp.sum(residual * direct...]
    dot_general x5 -> x0, matrix products: 139 us -> none  [the longest x3 87.5 us: contract_rows(): lax.dot_general(vectors, genotypes, (((1,), (1,)), ((), ())), preferred_e...]
    pallas_call x0 -> x10, Pallas kernels: none -> 135 us  [the longest x4 49.9 us: backward(): pl.pallas_call(body, grid_spec=pltpu.PrefetchScalarGridSpec(num_scalar_pr...]
    ppermute x0 -> x30, waiting for transfers between devices: none -> 75.9 us  [swap(): return lax.ppermute(x, axis, [(i, i ^ bits) for i in range(n)])]
    ppermute x0 -> x30, starting transfers between devices: none -> 43.5 us  [swap(): return lax.ppermute(x, axis, [(i, i ^ bits) for i in range(n)])]
    all_to_all x0 -> x2, waiting for transfers between devices: none -> 26.7 us  [the longest x1 15.2 us: per_device(): kept_x = jnp.sum(lax.all_to_all(value, 'marker', 0, 0), axis=0)]
    reduce_sum x8 -> x6, other arithmetic: 18.4 us -> 7.39 us  [the longest x3 4.72 us: three(): jnp.sum(d * d, 1)]
  transfers between devices with their start and end apart: 3 -> 33, of which waited for: 3 -> 23; matrix products, arithmetic and copies ran while one was open for 0% -> 2% of each run, Pallas kernels for 0% -> 20%
where the time goes in v1:
time: 392 us; the launch traced here: 390 us
  waiting for transfers between devices  157 us (40%)
  Pallas kernels  135 us (34%)
  starting transfers between devices  51.1 us (13%)
  other arithmetic  14.8 us (4%)
  between operations  14.4 us (4%)
  blocking collectives  10.1 us (3%)
  local copies, waits for them, and re-layouts  7.22 us (2%)
    ppermute x30, waiting for transfers between devices, swap(): return lax.ppermute(x, axis, [(i, i ^ bits) for i in range(n)])  75.9 us
    psum x1, waiting for transfers between devices, per_device(): probe_back = lax.psum(whole, 'sample')  54.9 us
    pallas_call x4, Pallas kernels, backward(): pl.pallas_call(body, grid_spec=pltpu.PrefetchScalarGridSpec(num_scalar_pr...  49.9 us
    ppermute x30, starting transfers between devices, swap(): return lax.ppermute(x, axis, [(i, i ^ bits) for i in range(n)])  43.5 us
    pallas_call x1, Pallas kernels, first_forward(): pl.pallas_call(first_body, grid_spec=pltpu.PrefetchScalarGridSpec(num_sca...  27.8 us
    pallas_call x2, Pallas kernels, wide_forward(): pl.pallas_call(functools.partial(wide_body, n, acc is not None), grid_spe...  27.5 us
    pallas_call x2, Pallas kernels, narrow_forward(): pl.pallas_call(functools.partial(narrow_body, n, acc is not None), grid_s...  26.3 us
    all_to_all x1, waiting for transfers between devices, per_device(): kept_x = jnp.sum(lax.all_to_all(value, 'marker', 0, 0), axis=0)  15.2 us
  transfers between devices with their start and end apart: 33, of which 23 were waited for; matrix products, arithmetic and copies ran while one was open for 2% of the time, Pallas kernels for 20%

profile of v1, /device:TPU:0, one launch (start us, length us, event | category | flops | bytes accessed | tf_op | source)
XLA Modules:
  0.0 389.7 jit_solution(10943694373216481070)
XLA Ops:
  9.5 1.9 multiply_reduce_fusion.1
  12.8 2.8 collective-permute-start.2
  15.6 1.4 collective-permute-start.3
  17.1 2.9 collective-permute-done.3
  20.6 1.2 bitcast_divide_fusion
  23.8 27.8 %first_forward.1 = (f32[8,128,256]{2,1,0:T(8,128)}, f32[16,16384]{1,0:T(8,128)S(1)}) custom-call(s32[1]{0:T(128)} %constant.8.clone.1.off, f32[16,16384]{1,0:T(8,128)S(1)} %copy-done.2, f32[16,4]{1,0:T(8,128)S(1)} %copy.49.cols, f32[112,16384]{1,0:T(8,128)} %probes.1, bf16[2048,16384]{1,0:T(8,128)(2,1)} %refs_4_.1), custom_call_target="tpu_custom_call" | custom-call | flops 8589934592 | bytes 67108864 | tf_op jit(solution)/shard_map/first_forward/pallas_call | solution.py:146
  51.5 3.6 all-to-all-start
  55.3 15.2 %all-to-all-done = f32[8,128,256]{2,1,0:T(8,128)S(1)} async-done(((f32[8,128,256]{2,1,0:T(8,128)}), f32[8,128,256]{2,1,0:T(8,128)S(1)}, u32[]{:S(2)}, u32[]{:S(2)}) %all-to-all-start) | async-done | bytes 1048608 | tf_op jit(solution)/shard_map/all_to_all | solution.py:425
  71.3 10.1 %all_gather.3.rows = bf16[128,2048]{1,0:T(8,128)(2,1)S(1)} all-gather(bf16[128,256]{1,0:T(8,128)(2,1)S(1)} %pad_maximum_fusion.2), channel_id=1, replica_groups=mesh['sample'=4,'marker'=8] {'marker'}, dimensions={1}, use_global_device_ids=true | all-gather | bytes 589824 | tf_op jit(solution)/shard_map/all_gather | solution.py:428
  81.5 12.7 %first_back_far.1 = (f32[16,8192]{1,0:T(8,128)S(1)}, bf16[112,16384]{1,0:T(8,128)(2,1)S(1)}) custom-call(s32[2]{0:T(128)S(1)} %get-tuple-element.47.off, bf16[128,2048]{1,0:T(8,128)(2,1)S(1)} %all_gather.3.rows, bf16[2048,16384]{1,0:T(8,128)(2,1)} %refs_4_.1), custom_call_target="tpu_custom_call" | custom-call | flops 4294967296 | bytes 33554432 | tf_op jit(solution)/shard_map/first_back_far/pallas_call | solution.py:331
  94.2 2.7 collective-permute-start.5
  96.9 1.3 collective-permute-start.6
  98.2 12.7 %first_back_near.1 = (f32[16,8192]{1,0:T(8,128)S(1)}, bf16[112,16384]{1,0:T(8,128)(2,1)S(1)}) custom-call(s32[2]{0:T(128)S(1)} %get-tuple-element.46.off, bf16[128,2048]{1,0:T(8,128)(2,1)S(1)} %all_gather.3.rows, bf16[2048,16384]{1,0:T(8,128)(2,1)} %refs_4_.1, bf16[112,16384]{1,0:T(8,128)(2,1)S(1)} %get-tuple-element.11.refs_0_), custom_call_target="tpu_custom_call", output_to_operand_aliasing={{1}: (3, {})} | custom-call | flops 4294967296 | bytes 33554432 | tf_op jit(solution)/shard_map/first_back_near/pallas_call | solution.py:331
  110.9 1.8 copy-done.1
  113.1 2.5 collective-permute-done.5
  115.5 5.5 %collective-permute-done.4 = f32[16,4096]{1,0:T(8,128)S(1)} collective-permute-done((f32[16,4096]{1,0:T(8,128)S(1)}, f32[16,4096]{1,0:T(8,128)S(1)}, u32[]{:S(2)}, u32[]{:S(2)}) %collective-permute-start.4) | collective-permute-done | bytes 262176 | tf_op jit(solution)/shard_map/ppermute | solution.py:26
  121.5 3.3 collective-permute-start.7
  125.6 2.8 collective-permute-done.9.refs_1_
  128.4 13.4 %second_forward_near.1.refs_2_ = f32[16,2048]{1,0:T(8,128)S(1)} custom-call(s32[2]{0:T(128)S(1)} %get-tuple-element.46.off, bf16[16,4096]{1,0:T(8,128)(2,1)S(1)} %get-tuple-element.31.refs_0_, bf16[16,4096]{1,0:T(8,128)(2,1)S(1)} %collective-permute-done.9.refs_1_, bf16[2048,16384]{1,0:T(8,128)(2,1)} %refs_4_.1), custom_call_target="tpu_custom_call" | custom-call | flops 536870912 | bytes 33554432 | tf_op jit(solution)/shard_map/second_forward_near/pallas_call | solution.py:190
  141.8 12.9 %second_forward_far.1 = f32[16,2048]{1,0:T(8,128)S(1)} custom-call(s32[2]{0:T(128)S(1)} %get-tuple-element.47.off, bf16[16,4096]{1,0:T(8,128)(2,1)S(1)} %collective-permute-done.7.refs_0_.refs_2_, bf16[16,4096]{1,0:T(8,128)(2,1)S(1)} %collective-permute-done.8.refs_1_.refs_3_, f32[16,2048]{1,0:T(8,128)S(1)} %second_forward_near.1.refs_2_, ...), custom_call_target="tpu_custom_call" | custom-call | flops 536870912 | bytes 33554432 | tf_op jit(solution)/shard_map/second_forward_far/pallas_call | solution.py:190
  154.8 1.3 collective-permute-done.10
  156.1 1.6 collective-permute-start.12
  157.7 1.4 collective-permute-start.13
  159.7 4.4 %collective-permute-done.12 = f32[16,2048]{1,0:T(8,128)S(1)} collective-permute-done((f32[16,2048]{1,0:T(8,128)S(1)}, f32[16,2048]{1,0:T(8,128)S(1)}, u32[]{:S(2)}, u32[]{:S(2)}) %collective-permute-start.12) | collective-permute-done | bytes 131104 | tf_op jit(solution)/shard_map/ppermute | solution.py:26
  166.4 12.3 %second_back_far.1 = f32[16,8192]{1,0:T(8,128)S(1)} custom-call(s32[2]{0:T(128)S(1)} %get-tuple-element.47.off, bf16[16,2048]{1,0:T(8,128)(2,1)S(1)} %get-tuple-element.35.rows, bf16[2048,16384]{1,0:T(8,128)(2,1)} %refs_4_.1), custom_call_target="tpu_custom_call" | custom-call | flops 536870912 | bytes 33554432 | tf_op jit(solution)/shard_map/second_back_far/pallas_call | solution.py:331
  178.8 11.3 %collective-permute-start.15 = (f32[16,4096]{1,0:T(8,128)S(1)}, f32[16,4096]{1,0:T(8,128)S(1)}, u32[]{:S(2)}, u32[]{:S(2)}) collective-permute-start(f32[16,4096]{1,0:T(8,128)S(1)} %get-tuple-element.41), channel_id=1, source_target_pairs={{0,16},{8,24},{16,0},{24,8},{1,17},{9,25},{17,1},{25,9},{2,18},{10... | collective-permute-start | bytes 786440 | tf_op jit(solution)/shard_map/ppermute | solution.py:26
  190.2 12.2 %second_back_near.1 = f32[16,8192]{1,0:T(8,128)S(1)} custom-call(s32[2]{0:T(128)S(1)} %get-tuple-element.46.off, bf16[16,2048]{1,0:T(8,128)(2,1)S(1)} %get-tuple-element.35.rows, bf16[2048,16384]{1,0:T(8,128)(2,1)} %refs_4_.1), custom_call_target="tpu_custom_call" | custom-call | flops 536870912 | bytes 33554432 | tf_op jit(solution)/shard_map/second_back_near/pallas_call | solution.py:331
  203.2 8.6 %collective-permute-done.15 = f32[16,4096]{1,0:T(8,128)S(1)} collective-permute-done((f32[16,4096]{1,0:T(8,128)S(1)}, f32[16,4096]{1,0:T(8,128)S(1)}, u32[]{:S(2)}, u32[]{:S(2)}) %collective-permute-start.15) | collective-permute-done | bytes 262176 | tf_op jit(solution)/shard_map/ppermute | solution.py:26
  211.8 1.7 collective-permute-done.16
  213.5 4.7 %collective-permute-done.14 = f32[16,4096]{1,0:T(8,128)S(1)} collective-permute-done((f32[16,4096]{1,0:T(8,128)S(1)}, f32[16,4096]{1,0:T(8,128)S(1)}, u32[]{:S(2)}, u32[]{:S(2)}) %collective-permute-start.14) | collective-permute-done | bytes 262176 | tf_op jit(solution)/shard_map/ppermute | solution.py:26
  219.0 2.1 collective-permute-start.17
  222.6 16.0 %collective-permute-done.19.refs_1_.refs_5_ = bf16[16,4096]{1,0:T(8,128)(2,1)S(1)} collective-permute-done((bf16[16,4096]{1,0:T(8,128)(2,1)S(1)}, bf16[16,4096]{1,0:T(8,128)(2,1)S(1)}, u32[]{:S(2)}, u32[]{:S(2)}) %collective-permute-start.19) | collective-permute-done | bytes 131104 | tf_op jit(solution)/shard_map/ppermute | solution.py:26
  238.6 54.9 %all-reduce.2.cloned.1.call-done.refs_2_ = bf16[112,16384]{1,0:T(8,128)(2,1)} async-done(((bf16[112,16384]{1,0:T(8,128)(2,1)}), bf16[112,16384]{1,0:T(8,128)(2,1)}) %all-reduce.2.cloned.1.call-update) | async-done | bytes 3670032 | tf_op jit(solution)/shard_map/psum | solution.py:438
  293.4 2.0 copy-done
  295.5 13.3 %third_forward_near.1.refs_3_ = f32[2048,128]{1,0:T(8,128)S(1)} custom-call(s32[2]{0:T(128)S(1)} %get-tuple-element.46.off, bf16[16,4096]{1,0:T(8,128)(2,1)S(1)} %get-tuple-element.34.refs_0_.refs_4_, bf16[16,4096]{1,0:T(8,128)(2,1)S(1)} %collective-permute-done.19.refs_1_.refs_5_, bf16[112,16384]{1,0:T(8,128)(2,1)S(1)} %copy-done, bf16[2048,16384]{1,0:T(8,128)(2,1)} %refs_4_.1), custom_call_target="tpu_custom_call" | custom-call | flops 4294967296 | bytes 33554432 | tf_op jit(solution)/shard_map/third_forward_near/pallas_call | solution.py:242
  308.8 14.2 %third_forward_far.1 = f32[8,128,256]{2,1,0:T(8,128)} custom-call(s32[2]{0:T(128)S(1)} %get-tuple-element.47.off, bf16[16,4096]{1,0:T(8,128)(2,1)S(1)} %collective-permute-done.17.refs_0_.refs_6_, bf16[16,4096]{1,0:T(8,128)(2,1)S(1)} %collective-permute-done.18.refs_1_.refs_7_, bf16[112,16384]{1,0:T(8,128)(2,1)S(1)} %copy-done, ...), custom_call_target="tpu_custom_call" | custom-call | flops 4294967296 | bytes 33554432 | tf_op jit(solution)/shard_map/third_forward_far/pallas_call | solution.py:242
  323.1 3.9 %all-to-all-start.1 = ((f32[8,128,256]{2,1,0:T(8,128)}), f32[8,128,256]{2,1,0:T(8,128)S(1)}, u32[]{:S(2)}, u32[]{:S(2)}) async-start(f32[8,128,256]{2,1,0:T(8,128)} %third_forward_far.1), calls=%async_computation.1 | async-start | bytes 2097152 | tf_op jit(solution)/shard_map/all_to_all | solution.py:465
  327.8 2.9 multiply_reduce_fusion
  330.6 11.5 %all-to-all-done.1 = f32[8,128,256]{2,1,0:T(8,128)S(1)} async-done(((f32[8,128,256]{2,1,0:T(8,128)}), f32[8,128,256]{2,1,0:T(8,128)S(1)}, u32[]{:S(2)}, u32[]{:S(2)}) %all-to-all-start.1) | async-done | bytes 1048608 | tf_op jit(solution)/shard_map/all_to_all | solution.py:465
  344.9 1.2 collective-permute-done.20
  346.8 1.4 collective-permute-start.23
  348.2 1.5 collective-permute-start.21
  353.8 3.0 collective-permute-start.27
  356.8 2.4 collective-permute-start.29
  359.2 1.4 collective-permute-start.26
  361.0 15.8 %collective-permute-done.26 = f32[128,6]{1,0:T(8,128)S(1)} collective-permute-done((f32[128,6]{1,0:T(8,128)S(1)}, f32[128,6]{1,0:T(8,128)S(1)}, u32[]{:S(2)}, u32[]{:S(2)}) %collective-permute-start.26) | collective-permute-done | bytes 3104 | tf_op jit(solution)/shard_map/ppermute | solution.py:26
  376.8 2.8 collective-permute-done.28.refs_10_
  379.6 3.3 finish.1
  (91 shorter events, 23.5 us)
Async XLA Ops:
  11.4 1.3 collective-permute-start
  12.8 4.3 %collective-permute-start.2 = (f32[16,1]{0,1:T(1,128)S(1)}, f32[16,1]{0,1:T(1,128)S(1)}, u32[]{:S(2)}, u32[]{:S(2)}) collective-permute-start(f32[16,1]{0,1:T(1,128)S(1)} %bitcast_add_fusion), channel_id=1, source_target_pairs={{0,4},{1,5},{2,6},{3,7},{4,0},{5,1},{6,2},{7,3},{8,12},{9,13},{10,... | collective-permute-start | bytes 200 | tf_op jit(solution)/shard_map/ppermute | solution.py:26
  15.6 4.4 %collective-permute-start.3 = (f32[16,1]{0,1:T(1,128)S(1)}, f32[16,1]{0,1:T(1,128)S(1)}, u32[]{:S(2)}, u32[]{:S(2)}) collective-permute-start(f32[16,1]{0,1:T(1,128)S(1)} %bitcast_add_fusion), channel_id=1, source_target_pairs={{0,6},{1,7},{2,4},{3,5},{4,2},{5,3},{6,0},{7,1},{8,14},{9,15},{10,... | collective-permute-start | bytes 200 | tf_op jit(solution)/shard_map/ppermute | solution.py:26
  17.0 3.5 collective-permute-start.1
  22.6 1.2 copy-start.2
  51.5 18.9 %all-to-all-start = ((f32[8,128,256]{2,1,0:T(8,128)}), f32[8,128,256]{2,1,0:T(8,128)S(1)}, u32[]{:S(2)}, u32[]{:S(2)}) async-start(f32[8,128,256]{2,1,0:T(8,128)} %get-tuple-element.10), calls=%async_computation | async-start | bytes 2097152 | tf_op jit(solution)/shard_map/all_to_all | solution.py:425
  55.1 238.3 %all-reduce.2.cloned.1.call-start = ((), (), s32[]{:S(2)}) async-start(), calls=%async_computation.2 | async-start | bytes 7340032 | tf_op jit(solution)/shard_map/psum | solution.py:438
  55.2 39.0 %copy-start.3 = (s32[4]{0:T(128)}, s32[4]{0:T(128)S(1)}, u32[]{:S(2)}) copy-start(s32[4]{0:T(128)S(1)} %iota_xor_fusion.off) | copy-start | bytes 52
  70.5 23.6 %copy-start.5 = (f32[128,256]{1,0:T(8,128)}, f32[128,256]{1,0:T(8,128)S(1)}, u32[]{:S(2)}) copy-start(f32[128,256]{1,0:T(8,128)S(1)} %reduce_sum.109) | copy-start | bytes 393220
  94.2 21.3 %collective-permute-start.5 = (f32[16,4096]{1,0:T(8,128)S(1)}, f32[16,4096]{1,0:T(8,128)S(1)}, u32[]{:S(2)}, u32[]{:S(2)}) collective-permute-start(f32[16,4096]{1,0:T(8,128)S(1)} %get-tuple-element.43), channel_id=1, source_target_pairs={{0,16},{8,24},{16,0},{24,8},{1,17},{9,25},{17,1},{25,9},{2,18},{10... | collective-permute-start | bytes 786440 | tf_op jit(solution)/shard_map/ppermute | solution.py:26
  96.9 18.7 %collective-permute-start.6 = (f32[16,4096]{1,0:T(8,128)S(1)}, f32[16,4096]{1,0:T(8,128)S(1)}, u32[]{:S(2)}, u32[]{:S(2)}) collective-permute-start(f32[16,4096]{1,0:T(8,128)S(1)} %get-tuple-element.42), channel_id=1, source_target_pairs={{0,24},{8,16},{16,8},{24,0},{1,25},{9,17},{17,9},{25,1},{2,26},{10... | collective-permute-start | bytes 786440 | tf_op jit(solution)/shard_map/ppermute | solution.py:26
  98.2 14.9 %copy-start.8 = (f32[16]{0:T(128)S(1)}, f32[16]{0:T(128)}, u32[]{:S(2)}) copy-start(f32[16]{0:T(128)} %param.15) | copy-start | bytes 196
  110.9 1.8 copy-start.1
  112.8 8.2 %collective-permute-start.4 = (f32[16,4096]{1,0:T(8,128)S(1)}, f32[16,4096]{1,0:T(8,128)S(1)}, u32[]{:S(2)}, u32[]{:S(2)}) collective-permute-start(f32[16,4096]{1,0:T(8,128)S(1)} %slice.42), channel_id=1, source_target_pairs={{0,8},{8,0},{16,24},{24,16},{1,9},{9,1},{17,25},{25,17},{2,10},{10... | collective-permute-start | bytes 786440 | tf_op jit(solution)/shard_map/ppermute | solution.py:26
  113.1 8.4 %copy-start.7 = (f32[16]{0:T(128)}, f32[16]{0:T(128)S(1)}, u32[]{:S(2)}) copy-start(f32[16]{0:T(128)S(1)} %broadcast_multiply_fusion) | copy-start | bytes 196
  121.1 7.3 %collective-permute-start.9 = (bf16[16,4096]{1,0:T(8,128)(2,1)S(1)}, bf16[16,4096]{1,0:T(8,128)(2,1)S(1)}, u32[]{:S(2)}, u32[]{:S(2)}) collective-permute-start(bf16[16,4096]{1,0:T(8,128)(2,1)S(1)} %get-tuple-element.31.refs_0_), channel_id=1, source_target_pairs={{0,8},{8,0},{16,24},{24,16},{1,9},{9,1},{17,25},{25,17},{2,10},{10... | collective-permute-start | bytes 393224 | tf_op jit(solution)/shard_map/ppermute | solution.py:26
  121.5 20.3 %collective-permute-start.7 = (bf16[16,4096]{1,0:T(8,128)(2,1)S(1)}, bf16[16,4096]{1,0:T(8,128)(2,1)S(1)}, u32[]{:S(2)}, u32[]{:S(2)}) collective-permute-start(bf16[16,4096]{1,0:T(8,128)(2,1)S(1)} %get-tuple-element.31.refs_0_), channel_id=1, source_target_pairs={{0,16},{8,24},{16,0},{24,8},{1,17},{9,25},{17,1},{25,9},{2,18},{10... | collective-permute-start | bytes 393224 | tf_op jit(solution)/shard_map/ppermute | solution.py:26
  124.8 17.0 %collective-permute-start.8 = (bf16[16,4096]{1,0:T(8,128)(2,1)S(1)}, bf16[16,4096]{1,0:T(8,128)(2,1)S(1)}, u32[]{:S(2)}, u32[]{:S(2)}) collective-permute-start(bf16[16,4096]{1,0:T(8,128)(2,1)S(1)} %get-tuple-element.31.refs_0_), channel_id=1, source_target_pairs={{0,24},{8,16},{16,8},{24,0},{1,25},{9,17},{17,9},{25,1},{2,26},{10... | collective-permute-start | bytes 393224 | tf_op jit(solution)/shard_map/ppermute | solution.py:26
  154.7 1.4 collective-permute-start.10
  156.1 8.0 %collective-permute-start.12 = (f32[16,2048]{1,0:T(8,128)S(1)}, f32[16,2048]{1,0:T(8,128)S(1)}, u32[]{:S(2)}, u32[]{:S(2)}) collective-permute-start(f32[16,2048]{1,0:T(8,128)S(1)} %add.107), channel_id=1, source_target_pairs={{0,4},{1,5},{2,6},{3,7},{4,0},{5,1},{6,2},{7,3},{8,12},{9,13},{10,... | collective-permute-start | bytes 393224 | tf_op jit(solution)/shard_map/ppermute | solution.py:26
  157.7 7.3 %collective-permute-start.13 = (f32[16,2048]{1,0:T(8,128)S(1)}, f32[16,2048]{1,0:T(8,128)S(1)}, u32[]{:S(2)}, u32[]{:S(2)}) collective-permute-start(f32[16,2048]{1,0:T(8,128)S(1)} %add.107), channel_id=1, source_target_pairs={{0,6},{1,7},{2,4},{3,5},{4,2},{5,3},{6,0},{7,1},{8,14},{9,15},{10,... | collective-permute-start | bytes 393224 | tf_op jit(solution)/shard_map/ppermute | solution.py:26
  159.1 6.6 %collective-permute-start.11 = (f32[16,2048]{1,0:T(8,128)S(1)}, f32[16,2048]{1,0:T(8,128)S(1)}, u32[]{:S(2)}, u32[]{:S(2)}) collective-permute-start(f32[16,2048]{1,0:T(8,128)S(1)} %add.107), channel_id=1, source_target_pairs={{0,2},{1,3},{2,0},{3,1},{4,6},{5,7},{6,4},{7,5},{8,10},{9,11},{10,... | collective-permute-start | bytes 393224 | tf_op jit(solution)/shard_map/ppermute | solution.py:26
  178.8 32.9 %collective-permute-start.15 = (f32[16,4096]{1,0:T(8,128)S(1)}, f32[16,4096]{1,0:T(8,128)S(1)}, u32[]{:S(2)}, u32[]{:S(2)}) collective-permute-start(f32[16,4096]{1,0:T(8,128)S(1)} %get-tuple-element.41), channel_id=1, source_target_pairs={{0,16},{8,24},{16,0},{24,8},{1,17},{9,25},{17,1},{25,9},{2,18},{10... | collective-permute-start | bytes 786440 | tf_op jit(solution)/shard_map/ppermute | solution.py:26
  202.4 11.1 %collective-permute-start.16 = (f32[16,4096]{1,0:T(8,128)S(1)}, f32[16,4096]{1,0:T(8,128)S(1)}, u32[]{:S(2)}, u32[]{:S(2)}) collective-permute-start(f32[16,4096]{1,0:T(8,128)S(1)} %get-tuple-element.40), channel_id=1, source_target_pairs={{0,24},{8,16},{16,8},{24,0},{1,25},{9,17},{17,9},{25,1},{2,26},{10... | collective-permute-start | bytes 786440 | tf_op jit(solution)/shard_map/ppermute | solution.py:26
  202.9 15.3 %collective-permute-start.14 = (f32[16,4096]{1,0:T(8,128)S(1)}, f32[16,4096]{1,0:T(8,128)S(1)}, u32[]{:S(2)}, u32[]{:S(2)}) collective-permute-start(f32[16,4096]{1,0:T(8,128)S(1)} %slice.52), channel_id=1, source_target_pairs={{0,8},{8,0},{16,24},{24,16},{1,9},{9,1},{17,25},{25,17},{2,10},{10... | collective-permute-start | bytes 786440 | tf_op jit(solution)/shard_map/ppermute | solution.py:26
  219.0 89.8 %collective-permute-start.17 = (bf16[16,4096]{1,0:T(8,128)(2,1)S(1)}, bf16[16,4096]{1,0:T(8,128)(2,1)S(1)}, u32[]{:S(2)}, u32[]{:S(2)}) collective-permute-start(bf16[16,4096]{1,0:T(8,128)(2,1)S(1)} %get-tuple-element.34.refs_0_.refs_4_), channel_id=1, source_target_pairs={{0,16},{8,24},{16,0},{24,8},{1,17},{9,25},{17,1},{25,9},{2,18},{10... | collective-permute-start | bytes 393224 | tf_op jit(solution)/shard_map/ppermute | solution.py:26
  221.1 87.7 %collective-permute-start.18 = (bf16[16,4096]{1,0:T(8,128)(2,1)S(1)}, bf16[16,4096]{1,0:T(8,128)(2,1)S(1)}, u32[]{:S(2)}, u32[]{:S(2)}) collective-permute-start(bf16[16,4096]{1,0:T(8,128)(2,1)S(1)} %get-tuple-element.34.refs_0_.refs_4_), channel_id=1, source_target_pairs={{0,24},{8,16},{16,8},{24,0},{1,25},{9,17},{17,9},{25,1},{2,26},{10... | collective-permute-start | bytes 393224 | tf_op jit(solution)/shard_map/ppermute | solution.py:26
  222.1 16.5 %collective-permute-start.19 = (bf16[16,4096]{1,0:T(8,128)(2,1)S(1)}, bf16[16,4096]{1,0:T(8,128)(2,1)S(1)}, u32[]{:S(2)}, u32[]{:S(2)}) collective-permute-start(bf16[16,4096]{1,0:T(8,128)(2,1)S(1)} %get-tuple-element.34.refs_0_.refs_4_), channel_id=1, source_target_pairs={{0,8},{8,0},{16,24},{24,16},{1,9},{9,1},{17,25},{25,17},{2,10},{10... | collective-permute-start | bytes 393224 | tf_op jit(solution)/shard_map/ppermute | solution.py:26
  293.4 2.0 copy-start
  323.1 19.8 %slice-start = ((f32[128,256]{1,0:T(8,128)}), f32[112,256]{1,0:T(8,128)S(1)}, s32[]{:S(2)}) async-start(f32[128,256]{1,0:T(8,128)} %copy-done.5), calls=%async_computation.3 | async-start | bytes 229376 | tf_op jit(solution)/shard_map/slice | solution.py:427
  323.1 30.0 %copy-start.6 = (f32[16]{0:T(128)S(1)}, f32[16]{0:T(128)}, u32[]{:S(2)}) copy-start(f32[16]{0:T(128)} %get-tuple-element.27) | copy-start | bytes 196
  323.1 56.5 %copy-start.4 = (s32[4]{0:T(128)S(1)}, s32[4]{0:T(128)}, u32[]{:S(2)}) copy-start(s32[4]{0:T(128)} %copy-done.3) | copy-start | bytes 52
  323.1 19.1 %all-to-all-start.1 = ((f32[8,128,256]{2,1,0:T(8,128)}), f32[8,128,256]{2,1,0:T(8,128)S(1)}, u32[]{:S(2)}, u32[]{:S(2)}) async-start(f32[8,128,256]{2,1,0:T(8,128)} %third_forward_far.1), calls=%async_computation.1 | async-start | bytes 2097152 | tf_op jit(solution)/shard_map/all_to_all | solution.py:465
  344.8 1.3 collective-permute-start.20
  346.1 5.0 %collective-permute-start.22 = (f32[128,6]{1,0:T(8,128)S(1)}, f32[128,6]{1,0:T(8,128)S(1)}, u32[]{:S(2)}, u32[]{:S(2)}) collective-permute-start(f32[128,6]{1,0:T(8,128)S(1)} %add.115), channel_id=1, source_target_pairs={{0,4},{1,5},{2,6},{3,7},{4,0},{5,1},{6,2},{7,3},{8,12},{9,13},{10,... | collective-permute-start | bytes 9224 | tf_op jit(solution)/shard_map/ppermute | solution.py:26
  346.8 5.5 %collective-permute-start.23 = (f32[128,6]{1,0:T(8,128)S(1)}, f32[128,6]{1,0:T(8,128)S(1)}, u32[]{:S(2)}, u32[]{:S(2)}) collective-permute-start(f32[128,6]{1,0:T(8,128)S(1)} %add.115), channel_id=1, source_target_pairs={{0,6},{1,7},{2,4},{3,5},{4,2},{5,3},{6,0},{7,1},{8,14},{9,15},{10,... | collective-permute-start | bytes 9224 | tf_op jit(solution)/shard_map/ppermute | solution.py:26
  348.2 4.8 %collective-permute-start.21 = (f32[128,6]{1,0:T(8,128)S(1)}, f32[128,6]{1,0:T(8,128)S(1)}, u32[]{:S(2)}, u32[]{:S(2)}) collective-permute-start(f32[128,6]{1,0:T(8,128)S(1)} %add.115), channel_id=1, source_target_pairs={{0,2},{1,3},{2,0},{3,1},{4,6},{5,7},{6,4},{7,5},{8,10},{9,11},{10,... | collective-permute-start | bytes 9224 | tf_op jit(solution)/shard_map/ppermute | solution.py:26
  353.0 7.7 %collective-permute-start.25 = (f32[128,6]{1,0:T(8,128)S(1)}, f32[128,6]{1,0:T(8,128)S(1)}, u32[]{:S(2)}, u32[]{:S(2)}) collective-permute-start(f32[128,6]{1,0:T(8,128)S(1)} %add_add_fusion.2), channel_id=1, source_target_pairs={{0,16},{8,24},{16,0},{24,8},{1,17},{9,25},{17,1},{25,9},{2,18},{10... | collective-permute-start | bytes 9224 | tf_op jit(solution)/shard_map/ppermute | solution.py:26
  353.8 23.0 %collective-permute-start.27 = (bf16[32,4096]{1,0:T(8,128)(2,1)S(1)}, bf16[32,4096]{1,0:T(8,128)(2,1)S(1)}, u32[]{:S(2)}, u32[]{:S(2)}) collective-permute-start(bf16[32,4096]{1,0:T(8,128)(2,1)S(1)} %pad_maximum_fusion.refs_8_), channel_id=1, source_target_pairs={{0,8},{8,0},{16,24},{24,16},{1,9},{9,1},{17,25},{25,17},{2,10},{10... | collective-permute-start | bytes 786440 | tf_op jit(solution)/shard_map/ppermute | solution.py:26
  356.8 22.8 %collective-permute-start.28 = (bf16[32,4096]{1,0:T(8,128)(2,1)S(1)}, bf16[32,4096]{1,0:T(8,128)(2,1)S(1)}, u32[]{:S(2)}, u32[]{:S(2)}) collective-permute-start(bf16[32,4096]{1,0:T(8,128)(2,1)S(1)} %pad_maximum_fusion.refs_8_), channel_id=1, source_target_pairs={{0,16},{8,24},{16,0},{24,8},{1,17},{9,25},{17,1},{25,9},{2,18},{10... | collective-permute-start | bytes 786440 | tf_op jit(solution)/shard_map/ppermute | solution.py:26
  356.8 22.8 %collective-permute-start.29 = (bf16[32,4096]{1,0:T(8,128)(2,1)S(1)}, bf16[32,4096]{1,0:T(8,128)(2,1)S(1)}, u32[]{:S(2)}, u32[]{:S(2)}) collective-permute-start(bf16[32,4096]{1,0:T(8,128)(2,1)S(1)} %pad_maximum_fusion.refs_8_), channel_id=1, source_target_pairs={{0,24},{8,16},{16,8},{24,0},{1,25},{9,17},{17,9},{25,1},{2,26},{10... | collective-permute-start | bytes 786440 | tf_op jit(solution)/shard_map/ppermute | solution.py:26
  359.2 17.5 %collective-permute-start.26 = (f32[128,6]{1,0:T(8,128)S(1)}, f32[128,6]{1,0:T(8,128)S(1)}, u32[]{:S(2)}, u32[]{:S(2)}) collective-permute-start(f32[128,6]{1,0:T(8,128)S(1)} %add_add_fusion.2), channel_id=1, source_target_pairs={{0,24},{8,16},{16,8},{24,0},{1,25},{9,17},{17,9},{25,1},{2,26},{10... | collective-permute-start | bytes 9224 | tf_op jit(solution)/shard_map/ppermute | solution.py:26
  360.6 16.1 %collective-permute-start.24 = (f32[128,6]{1,0:T(8,128)S(1)}, f32[128,6]{1,0:T(8,128)S(1)}, u32[]{:S(2)}, u32[]{:S(2)}) collective-permute-start(f32[128,6]{1,0:T(8,128)S(1)} %add_add_fusion.2), channel_id=1, source_target_pairs={{0,8},{8,0},{16,24},{24,16},{1,9},{9,1},{17,25},{25,17},{2,10},{10... | collective-permute-start | bytes 9224 | tf_op jit(solution)/shard_map/ppermute | solution.py:26
Sparse Core Ops, SparseCore 0:
  125.7 167.6 all-reduce.1

commit v2 on v1

v2 whole, which is shorter than its diff:
```python
import functools

import jax
import jax.numpy as jnp
from jax import lax
from jax.experimental import pallas as pl
from jax.experimental.pallas import tpu as pltpu
from jax.sharding import PartitionSpec as P

F32 = jnp.float32
BF16 = jnp.bfloat16
LIMIT = 44 << 20
SLOTS = 4
VMEM = pl.BlockSpec(memory_space=pltpu.VMEM)
ANY = pl.BlockSpec(memory_space=pl.ANY)


def block_of(size, most):
    while size % most:
        most //= 2
    return most


def swap(x, axis, bits):
    n = lax.axis_size(axis)
    return lax.ppermute(x, axis, [(i, i ^ bits) for i in range(n)])


def tree(parts):
    while len(parts) > 1:
        parts = [parts[i] + parts[i + 1] for i in range(0, len(parts), 2)]
    return parts[0]


def sum_direct(x, axis, unit=1):
    n = lax.axis_size(axis)
    return tree([x if k == 0 else swap(x, axis, k) for k in range(0, n, unit)])


def sum_marker(x):
    return sum_direct(x + swap(x, "marker", 1), "marker", 2)


def denoise(signal, precision, shrink, logit_base):
    energy = shrink * precision * signal * signal
    weight = jax.nn.sigmoid(logit_base + 0.5 * energy)
    return (shrink * weight * signal, shrink * weight * (1.0 + (1.0 - weight) * energy))


def stream(place, held, sems, total, prepare, use):
    slots = held.shape[0]

    def copy(c):
        slot = lax.rem(c, slots)
        return pltpu.make_async_copy(place(c), held.at[slot], sems.at[slot])

    for c in range(min(slots, total)):
        copy(c).start()
    prepare()

    def step(c, carry):
        copy(c).wait()
        use(c, held.at[lax.rem(c, slots)])

        @pl.when(c + slots < total)
        def _():
            copy(c + slots).start()

        return carry

    lax.fori_loop(0, total, step, 0)


def ring(rows, columns):
    return [pltpu.VMEM((SLOTS, rows, columns), BF16), pltpu.SemaphoreType.DMA((SLOTS,))]


def forward_loop(g, rows, total, held, sems, off, span, pieces, wide, fresh, prepare):
    people = g.shape[0]
    slots, pb, kb = held.shape
    steps, blocks = span // kb, people // pb

    def place(c):
        k, i = c // blocks, lax.rem(c, blocks)
        col = off[k // steps] * span + lax.rem(k, steps) * kb
        return g.at[pl.ds(pl.multiple_of(i * pb, pb), pb), pl.ds(pl.multiple_of(col, kb), kb)]

    def use(c, slot):
        k, i = c // blocks, lax.rem(c, blocks)
        d = rows[:, pl.ds(pl.multiple_of(k * kb, kb), kb)]
        here = pl.ds(pl.multiple_of(i * pb, pb), pb)
        across = (((1,), (1,)), ((), ()))
        if wide:
            at = (here, slice(None))
            value = lax.dot_general(slot[...], d, across, preferred_element_type=F32)
        else:
            at = (slice(None), here)
            value = lax.dot_general(d, slot[...], across, preferred_element_type=F32)
        if fresh:

            @pl.when(k == 0)
            def _():
                total[at] = value

            @pl.when(k > 0)
            def _():
                total[at] += value

        else:
            total[at] += value

    stream(place, held, sems, pieces * steps * blocks, prepare, use)


def split_people(out, total, t):
    n, r, share = out.shape
    for b in range(n):
        value = total[b * share : (b + 1) * share, :].T
        high = value.astype(BF16)
        out[b, : r - t, :] = high
        if t:
            out[b, r - t :, :] = (value[:t] - high[:t].astype(F32)).astype(BF16)


def prior(cols):
    inclusion, ratio, precision = [cols[:, j : j + 1] for j in range(3)]
    shrink = ratio / (1.0 + ratio)
    base = jnp.log(inclusion / (1.0 - inclusion)) + 0.5 * jnp.log(1.0 - shrink)
    return precision, shrink, base


def slope_body(message, cols, out):
    _, slopes = denoise(message[...], *prior(cols))
    out[...] = jnp.sum(slopes, axis=1, keepdims=True)


def slope_sum(message, cols):
    return pl.pallas_call(
        slope_body,
        in_specs=[VMEM, VMEM],
        out_specs=VMEM,
        out_shape=jax.ShapeDtypeStruct((message.shape[0], 1), F32),
        compiler_params=pltpu.CompilerParams(vmem_limit_bytes=LIMIT),
        name="slope_sum",
    )(message, cols)


def first_body(markers, off, message, cols, slopes, probes, g, out, centre, rows, held, sems, total):
    t = message.shape[0]

    def prepare():
        slope = slopes[...] / markers
        first, _ = denoise(message[...], *prior(cols))
        made = (first - slope * message[...]) / (1.0 - slope)
        centre[...] = made
        rows[:t, :] = made.astype(BF16)
        rows[t:, :] = probes[...].astype(BF16)

    forward_loop(g, rows, total, held, sems, off, g.shape[1], 1, True, True, prepare)
    split_people(out, total, t)


def cost(rows, people, markers):
    return pl.CostEstimate(
        flops=2 * rows * people * markers, transcendentals=0, bytes_accessed=2 * people * markers
    )


def first_forward(message, cols, slopes, probes, genotypes, columns):
    people, markers = genotypes.shape
    t = message.shape[0]
    r = t + probes.shape[0]
    pb, kb = block_of(people, 1024), block_of(markers, 2048)
    return pl.pallas_call(
        functools.partial(first_body, markers * columns),
        grid_spec=pltpu.PrefetchScalarGridSpec(
            num_scalar_prefetch=1,
            grid=(),
            in_specs=[VMEM, VMEM, VMEM, VMEM, ANY],
            out_specs=[VMEM, VMEM],
            scratch_shapes=[
                pltpu.VMEM((r, markers), BF16),
                *ring(pb, kb),
                pltpu.VMEM((people, r), F32),
            ],
        ),
        out_shape=[
            jax.ShapeDtypeStruct((columns, r + t, people // columns), BF16),
            jax.ShapeDtypeStruct(message.shape, F32),
        ],
        compiler_params=pltpu.CompilerParams(vmem_limit_bytes=LIMIT),
        cost_estimate=cost(r, people, markers),
        name="first_forward",
    )(jnp.zeros((1,), jnp.int32), message, cols, slopes, probes, genotypes)


def narrow_body(n, unit, with_acc, off, *refs):
    refs = list(refs)
    pieces = [refs.pop(0) for _ in range(n)]
    acc = refs.pop(0) if with_acc else None
    g, out, rows, held, sems = refs
    span = pieces[0].shape[1]

    def prepare():
        for j in range(n):
            rows[:, j * span : (j + 1) * span] = pieces[j][...]
        if with_acc:
            out[...] = acc[...]

    count = n * span // unit
    forward_loop(g, rows, out, held, sems, off, unit, count, False, not with_acc, prepare)


def narrow_forward(pieces, places, acc, genotypes, name):
    people = genotypes.shape[0]
    n, (t, span) = len(pieces), pieces[0].shape
    unit = n * span // places.shape[0]
    pb, kb = block_of(people, 1024), block_of(unit, 2048)
    operands = [*pieces, *([] if acc is None else [acc]), genotypes]
    return pl.pallas_call(
        functools.partial(narrow_body, n, unit, acc is not None),
        grid_spec=pltpu.PrefetchScalarGridSpec(
            num_scalar_prefetch=1,
            grid=(),
            in_specs=[VMEM] * (len(operands) - 1) + [ANY],
            out_specs=VMEM,
            scratch_shapes=[pltpu.VMEM((t, n * span), BF16), *ring(pb, kb)],
        ),
        out_shape=jax.ShapeDtypeStruct((t, people), F32),
        compiler_params=pltpu.CompilerParams(vmem_limit_bytes=LIMIT),
        cost_estimate=cost(t, people, n * span),
        name=name,
    )(places, *operands)


def wide_body(n, half, with_acc, off, *refs):
    refs = list(refs)
    pieces = [refs.pop(0) for _ in range(n)]
    probes = refs.pop(0)
    acc = refs.pop(0) if with_acc else None
    if with_acc:
        g, out, rows, held, sems, total = refs
    else:
        g, total, rows, held, sems = refs
    t, unit = pieces[0].shape[0], pieces[0].shape[1] // 2

    def prepare():
        for j in range(n):
            here = slice(j * unit, (j + 1) * unit)
            rows[:t, here] = pieces[j][:, half * unit : (half + 1) * unit]
            there = pl.multiple_of((off[j] - half * n) * unit, unit)
            rows[t:, here] = probes[:, pl.ds(there, unit)]
        if with_acc:
            total[...] = acc[...]

    forward_loop(g, rows, total, held, sems, off, unit, n, True, not with_acc, prepare)
    if with_acc:
        split_people(out, total, 0)


def wide_forward(pieces, probes, places, half, acc, genotypes, columns, name):
    people = genotypes.shape[0]
    n, t, unit = len(pieces), pieces[0].shape[0], pieces[0].shape[1] // 2
    r = t + probes.shape[0]
    pb, kb = block_of(people, 1024), block_of(unit, 2048)
    operands = [*pieces, probes, *([] if acc is None else [acc]), genotypes]
    scratch = [pltpu.VMEM((r, n * unit), BF16), *ring(pb, kb)]
    if acc is None:
        shape = jax.ShapeDtypeStruct((people, r), F32)
    else:
        shape = jax.ShapeDtypeStruct((columns, r, people // columns), BF16)
        scratch.append(pltpu.VMEM((people, r), F32))
    return pl.pallas_call(
        functools.partial(wide_body, n, half, acc is not None),
        grid_spec=pltpu.PrefetchScalarGridSpec(
            num_scalar_prefetch=1,
            grid=(),
            in_specs=[VMEM] * (len(operands) - 1) + [ANY],
            out_specs=VMEM,
            scratch_shapes=scratch,
        ),
        out_shape=shape,
        compiler_params=pltpu.CompilerParams(vmem_limit_bytes=LIMIT),
        cost_estimate=cost(r, people, n * unit),
        name=name,
    )(places, *operands)


def backward_loop(g, rows, total, held, sems, off, span, pieces):
    people = g.shape[0]
    slots, pk, mb = held.shape
    steps, blocks = span // mb, people // pk

    def place(c):
        k, i = c // blocks, lax.rem(c, blocks)
        col = off[k // steps] * span + lax.rem(k, steps) * mb
        return g.at[pl.ds(pl.multiple_of(i * pk, pk), pk), pl.ds(pl.multiple_of(col, mb), mb)]

    def use(c, slot):
        k, i = c // blocks, lax.rem(c, blocks)
        here = pl.ds(pl.multiple_of(k * mb, mb), mb)
        d = rows[:, pl.ds(pl.multiple_of(i * pk, pk), pk)]
        value = jnp.dot(d, slot[...], preferred_element_type=F32)

        @pl.when(i == 0)
        def _():
            total[:, here] = value

        @pl.when(i > 0)
        def _():
            total[:, here] += value

    stream(place, held, sems, pieces * steps * blocks, lambda: None, use)


def back_body(n, unit, t, base, off, rows, g, *refs):
    refs = list(refs)
    held, sems = refs[-2:]
    if t == rows.shape[0]:
        outs, total = refs[:-3], refs[-3]
    else:
        outs, (whole, total, made, sent) = refs[:-6], refs[-6:-2]
    backward_loop(g, rows, total, held, sems, off, unit, n)
    copies = []
    if t != rows.shape[0]:
        made[...] = total[t:, :].astype(BF16)
        for j in range(n):
            cols = pl.ds(pl.multiple_of((off[j] - base) * unit, unit), unit)
            copies.append(
                pltpu.make_async_copy(
                    made.at[:, pl.ds(j * unit, unit)], whole.at[:, cols], sent.at[j]
                )
            )
            copies[-1].start()
    span = outs[0].shape[1]
    for j, out in enumerate(outs):
        out[...] = total[:t, j * span : (j + 1) * span]
    for copy in copies:
        copy.wait()


def backward(rows, places, genotypes, unit, t, base, arrays, name):
    people = genotypes.shape[0]
    r, n = rows.shape[0], places.shape[0]
    pk, mb = block_of(people, 1024), block_of(unit, 2048)
    out_specs = [VMEM] * arrays
    out_shape = [jax.ShapeDtypeStruct((t, n * unit // arrays), F32)] * arrays
    scratch = [pltpu.VMEM((r, n * unit), F32)]
    if t != r:
        out_specs.append(ANY)
        out_shape.append(jax.ShapeDtypeStruct((r - t, n * unit), BF16))
        scratch += [pltpu.VMEM((r - t, n * unit), BF16), pltpu.SemaphoreType.DMA((n,))]
    return pl.pallas_call(
        functools.partial(back_body, n, unit, t, base),
        grid_spec=pltpu.PrefetchScalarGridSpec(
            num_scalar_prefetch=1,
            grid=(),
            in_specs=[VMEM, ANY],
            out_specs=out_specs,
            scratch_shapes=[*scratch, *ring(pk, mb)],
        ),
        out_shape=out_shape,
        compiler_params=pltpu.CompilerParams(vmem_limit_bytes=LIMIT),
        cost_estimate=cost(r, people, n * unit),
        name=name,
    )(places, rows, genotypes)


def finish_body(n, copies, off, sums, wide_cols, cols, centre, *refs):
    start_hi, back_hi, low = refs[:n], refs[n : 2 * n], refs[2 * n : 3 * n]
    estimate, lmmse = refs[3 * n :]
    t, unit = start_hi[0].shape[0], start_hi[0].shape[1] // 2
    norm_start, du, uu, xx, xw, ww = [sums[:, j : j + 1] for j in range(6)]
    tau, gamma = wide_cols[:, 0:1], wide_cols[:, 1:2]
    second_precision, slab_var, odds = [cols[:, j : j + 1] for j in range(3)]

    step_0 = norm_start / (tau * du + gamma * norm_start)
    left, b = 1.0 - step_0 * gamma, step_0 * tau
    norm_next = left * left * norm_start - 2.0 * left * b * du + b * b * uu
    a = left + norm_next / norm_start
    dir_norm = a * a * norm_start - 2.0 * a * b * du + b * b * uu
    dir_square = a * a * xx - 2.0 * a * b * xw + b * b * ww
    step_1 = norm_next / (tau * dir_square + gamma * dir_norm)

    start_coef = (step_0 + step_1 * a)[:t]
    back_coef = (step_1 * b)[:t]
    dots = step_0 * norm_start + step_1 * (a * norm_start - b * du)
    probe_dot = sum(dots[i * t : (i + 1) * t] for i in range(1, copies))
    probe_norm = sum(norm_start[i * t : (i + 1) * t] for i in range(1, copies))
    second_slope = second_precision * probe_dot / (probe_norm + 1e-06)
    next_precision = second_precision * (1.0 - second_slope) / second_slope
    next_shrink = slab_var * next_precision / (1.0 + slab_var * next_precision)
    next_base = odds + 0.5 * jnp.log(1.0 - next_shrink)
    for j, half in [(j, half) for j in range(n) for half in range(2)]:
        here = pl.ds(pl.multiple_of((half * n + off[j]) * unit, unit), unit)
        part = slice(half * unit, (half + 1) * unit)
        start = start_hi[j][:, part].astype(F32) + low[j][:t, part].astype(F32)
        back = back_hi[j][:, part].astype(F32) + low[j][t:, part].astype(F32)
        middle = centre[:, here]
        made = middle + start_coef * start - back_coef * back
        lmmse[:, here] = made
        next_message = (made - second_slope * middle) / (1.0 - second_slope)
        value, _ = denoise(next_message, next_precision, next_shrink, next_base)
        estimate[:, here] = value


def finish(places, sums, wide_cols, cols, centre, start_hi, back_hi, low):
    n = len(low)
    shape = jax.ShapeDtypeStruct(centre.shape, F32)
    copies = sums.shape[0] // centre.shape[0]
    operands = [sums, wide_cols, cols, centre, *start_hi, *back_hi, *low]
    return pl.pallas_call(
        functools.partial(finish_body, n, copies),
        grid_spec=pltpu.PrefetchScalarGridSpec(
            num_scalar_prefetch=1, grid=(), in_specs=[VMEM] * len(operands), out_specs=[VMEM, VMEM]
        ),
        out_shape=[shape, shape],
        compiler_params=pltpu.CompilerParams(vmem_limit_bytes=LIMIT),
        name="finish",
    )(places, *operands)


def per_device(
    genotypes, phenotypes, message, probes, inclusion, slab_ratio, input_precision, noise_precision
):
    samples, columns = lax.axis_size("sample"), lax.axis_size("marker")
    people_here, markers_here = genotypes.shape
    people, markers = people_here * samples, markers_here * columns
    traits = message.shape[0]
    copies = probes.shape[0] // traits + 1
    me, column = lax.axis_index("sample"), lax.axis_index("marker")
    unit, share = markers_here // (2 * samples), people_here // columns
    order = jnp.arange(samples, dtype=jnp.int32) ^ me
    some = samples // 2
    near, far = [jnp.stack([o, o + samples], axis=1).reshape(-1) for o in (order[:some], order[some:])]

    cols = jnp.stack([inclusion, slab_ratio, input_precision], axis=1)
    slopes = sum_marker(slope_sum(message, cols))
    value, centre = first_forward(message, cols, slopes, probes, genotypes, columns)
    kept_x = jnp.sum(lax.all_to_all(value, "marker", 0, 0).astype(F32), axis=0)
    kept_x, low_x = kept_x[: traits * copies], kept_x[traits * copies :]
    own = lax.dynamic_slice_in_dim(phenotypes, column * share, share, 1) - (kept_x[:traits] + low_x)
    rows = jnp.concatenate([own, kept_x[traits:]], axis=0).astype(BF16)
    rows = lax.all_gather(rows, "marker", axis=1, tiled=True)
    starts, probe_back = [], []
    for half in range(2):
        *parts, whole = backward(
            rows, order + half * samples, genotypes, unit, traits, half * samples, samples, f"first_back_{half}"
        )
        starts.append([swap(part, "sample", k) if k else part for k, part in enumerate(parts)])
        if half:
            whole = lax.psum_scatter(whole, "sample", scatter_dimension=1, tiled=True)
            probe_back.append(lax.all_gather(whole, "sample", axis=1, tiled=True))
        else:
            probe_back.append(lax.psum(whole, "sample"))
    scale = (noise_precision / people)[:, None]
    start = scale * jnp.concatenate([tree(parts) for parts in starts], axis=1)
    start_high = lax.reduce_precision(start, 8, 7)
    start_low = (start - start_high).astype(BF16)
    start_high = start_high.astype(BF16)

    start_pieces = [swap(start_high, "sample", k) if k else start_high for k in range(samples)]
    value = narrow_forward(start_pieces[:some], near, None, genotypes, "second_forward_near")
    value = narrow_forward(start_pieces[some:], far, value, genotypes, "second_forward_far")
    value = sum_marker(value)
    kept_s = lax.dynamic_slice_in_dim(value, column * share, share, 1)
    rows = value.astype(BF16)
    parts = backward(rows, far, genotypes, unit, traits, 0, some, "second_back_far")
    sent = [swap(part, "sample", k + some) for k, part in enumerate(parts)]
    parts = backward(rows, near, genotypes, unit, traits, 0, some, "second_back_near")
    back = tree([swap(part, "sample", k) if k else part for k, part in enumerate(parts)] + sent)
    back_high = lax.reduce_precision(back, 8, 7)
    back_low = (back - back_high).astype(BF16)
    back_high = back_high.astype(BF16)
    back_pieces = [swap(back_high, "sample", k) if k else back_high for k in range(samples)]
    low = jnp.concatenate([start_low, back_low], axis=0)
    low, *back_pieces = lax.optimization_barrier((low, *back_pieces))
    low_pieces = [swap(low, "sample", k) if k else low for k in range(samples)]

    total = wide_forward(
        back_pieces, probe_back[0], order, 0, None, genotypes, columns, "third_forward_0"
    )
    total, *low_pieces = lax.optimization_barrier((total, *low_pieces))
    value = wide_forward(
        back_pieces, probe_back[1], order + samples, 1, total, genotypes, columns, "third_forward_1"
    )
    last = jnp.sum(lax.all_to_all(value, "marker", 0, 0).astype(F32), axis=0)
    before = jnp.concatenate([kept_s, kept_x[traits:]], axis=0)

    def own_units(*halves):
        return jnp.concatenate(
            [lax.dynamic_slice_in_dim(x, me * unit, unit, 1) for x in halves], axis=1
        )

    def three(d, u):
        return jnp.stack([jnp.sum(d * d, 1), jnp.sum(d * u, 1), jnp.sum(u * u, 1)], axis=1)

    probes_here = own_units(probes[:, : samples * unit], probes[:, samples * unit :])
    norms = jnp.concatenate(
        [three(start, back), three(probes_here, own_units(*probe_back).astype(F32))], axis=0
    )
    sums = jnp.concatenate([norms, three(before, last)], axis=1)
    sums = sum_direct(sum_marker(sums), "sample")

    first_slope = slopes[:, 0] / markers
    second_precision = input_precision * (1.0 - first_slope) / first_slope
    odds = jnp.log(inclusion / (1.0 - inclusion))
    wide_cols = jnp.stack(
        [jnp.tile(noise_precision / people, copies), jnp.tile(second_precision, copies)], axis=1
    )
    cols = jnp.stack([second_precision, slab_ratio / input_precision, odds], axis=1)
    return tuple(
        finish(order, sums, wide_cols, cols, centre, start_pieces, back_pieces, low_pieces)
    )


def solution(mesh):
    return jax.shard_map(
        per_device,
        mesh=mesh,
        in_specs=(
            P("sample", "marker"),
            P(None, "sample"),
            P(None, "marker"),
            P(None, "marker"),
            P(),
            P(),
            P(),
            P(),
        ),
        out_specs=(P(None, "marker"), P(None, "marker")),
        check_vma=False,
    )
```

time: 392 us -> 376 us (0.959)
  waiting for transfers between devices: 157 us -> 124 us
  starting transfers between devices: 51.1 us -> 68 us
  local copies, waits for them, and re-layouts: 7.22 us -> 17.7 us
  other arithmetic: 14.8 us -> 4.87 us
    psum x1, waiting for transfers between devices: 54.9 us -> 0.01 us  [per_device(): probe_back.append(lax.psum(whole, 'sample'))]
    ppermute x30 -> x33, waiting for transfers between devices: 75.9 us -> 97.5 us  [swap(): return lax.ppermute(x, axis, [(i, i ^ bits) for i in range(n)])]
    ppermute x30 -> x33, starting transfers between devices: 43.5 us -> 59.9 us  [swap(): return lax.ppermute(x, axis, [(i, i ^ bits) for i in range(n)])]
    all_gather x0 -> x1, waiting for transfers between devices: none -> 9.56 us  [per_device(): probe_back.append(lax.all_gather(whole, 'sample', axis=1, tiled=True))]
    all_to_all x2, waiting for transfers between devices: 26.7 us -> 17.2 us  [the longest x1 10.3 us: per_device(): kept_x = jnp.sum(lax.all_to_all(value, 'marker', 0, 0).astype(F32), axis=0)]
    dynamic_slice x0 -> x3, local copies, waits for them, and re-layouts: none -> 5.1 us  [own_units(): lax.dynamic_slice_in_dim(x, me * unit, unit, 1)]
    unnamed x18 -> x28, local copies, waits for them, and re-layouts: 5.12 us -> 7.96 us
    pallas_call x9 -> x10, Pallas kernels: 131 us -> 132 us  [the longest x4 52.7 us: backward(): pl.pallas_call(functools.partial(back_body, n, unit, t, base), grid_spec=...]
  transfers between devices with their start and end apart: 33 -> 38, of which waited for: 23 -> 23; matrix products, arithmetic and copies ran while one was open for 2% -> 3% of each run, Pallas kernels for 20% -> 21%
where the time goes in v2:
time: 376 us; the launch traced here: 375 us
  Pallas kernels  136 us (36%)
  waiting for transfers between devices  124 us (33%)
  starting transfers between devices  68 us (18%)
  local copies, waits for them, and re-layouts  17.7 us (5%)
  between operations  14.2 us (4%)
  blocking collectives  9.95 us (3%)
  other arithmetic  4.87 us (1%)
    ppermute x33, waiting for transfers between devices, swap(): return lax.ppermute(x, axis, [(i, i ^ bits) for i in range(n)])  97.5 us
    ppermute x33, starting transfers between devices, swap(): return lax.ppermute(x, axis, [(i, i ^ bits) for i in range(n)])  59.9 us
    pallas_call x4, Pallas kernels, backward(): pl.pallas_call(functools.partial(back_body, n, unit, t, base), grid_spec=...  52.7 us
    pallas_call x2, Pallas kernels, wide_forward(): pl.pallas_call(functools.partial(wide_body, n, half, acc is not None), gr...  27.3 us
    pallas_call x2, Pallas kernels, narrow_forward(): pl.pallas_call(functools.partial(narrow_body, n, unit, acc is not None),...  26.3 us
    pallas_call x1, Pallas kernels, first_forward(): pl.pallas_call(functools.partial(first_body, markers * columns), grid_spe...  24.6 us
    all_to_all x1, waiting for transfers between devices, per_device(): kept_x = jnp.sum(lax.all_to_all(value, 'marker', 0, 0).astype(F32), axis=0)  10.3 us
    all_gather x1, blocking collectives, per_device(): rows = lax.all_gather(rows, 'marker', axis=1, tiled=True)  9.95 us
  transfers between devices with their start and end apart: 38, of which 23 were waited for; matrix products, arithmetic and copies ran while one was open for 3% of the time, Pallas kernels for 21%

profile of v2, /device:TPU:0, one launch (start us, length us, event | category | flops | bytes accessed | tf_op | source)
XLA Modules:
  0.0 375.0 jit_solution(1373641084694422464)
XLA Ops:
  11.2 3.8 %collective-permute-start.3 = (f32[16,1]{1,0:T(8,128)S(1)}, f32[16,1]{1,0:T(8,128)S(1)}, u32[]{:S(2)}, u32[]{:S(2)}) collective-permute-start(f32[16,1]{1,0:T(8,128)S(1)} %add.100), channel_id=1, source_target_pairs={{0,6},{1,7},{2,4},{3,5},{4,2},{5,3},{6,0},{7,1},{8,14},{9,15},{10,... | collective-permute-start | bytes 200 | tf_op jit(solution)/shard_map/ppermute | solution.py:26
  16.6 2.0 collective-permute-done.2
  19.8 3.1 copy-done
  22.9 24.6 %first_forward.1 = (bf16[8,144,256]{2,1,0:T(8,128)(2,1)}, f32[16,16384]{1,0:T(8,128)S(1)}) custom-call(s32[1]{0:T(128)} %constant.9.clone.1.off, f32[16,16384]{1,0:T(8,128)S(1)} %copy-done.1, f32[16,3]{1,0:T(8,128)S(1)} %copy.49.cols, f32[16,1]{1,0:T(8,128)S(1)} %get-tuple-element.64.slopes, f32[112,16384]{1,0:T(8,128)S(1)} %copy-done, ...), custom_call_target="tpu_custom_call" | custom-call | flops 8589934592 | bytes 67108864 | tf_op jit(solution)/shard_map/first_forward/pallas_call | solution.py:174
  47.5 3.6 all-to-all-start
  51.1 10.3 %all-to-all-done = bf16[8,144,256]{2,1,0:T(8,128)(2,1)S(1)} async-done(((bf16[8,144,256]{2,1,0:T(8,128)(2,1)}), bf16[8,144,256]{2,1,0:T(8,128)(2,1)S(1)}, u32[]{:S(2)}, u32[]{:S(2)}) %all-to-all-start) | async-done | bytes 589856 | tf_op jit(solution)/shard_map/all_to_all | solution.py:440
  62.3 9.9 %all_gather.6.rows = bf16[128,2048]{1,0:T(8,128)(2,1)S(1)} all-gather(bf16[128,256]{1,0:T(8,128)(2,1)S(1)} %pad_maximum_fusion.4), channel_id=1, replica_groups=mesh['sample'=4,'marker'=8] {'marker'}, dimensions={1}, use_global_device_ids=true | all-gather | bytes 589824 | tf_op jit(solution)/shard_map/all_gather | solution.py:444
  72.3 13.9 %first_back_1.1 = (f32[16,2048]{1,0:T(8,128)S(1)}, f32[16,2048]{1,0:T(8,128)S(1)}, f32[16,2048]{1,0:T(8,128)S(1)}, f32[16,2048]{1,0:T(8,128)S(1)}, bf16[112,8192]{1,0:T(8,128)(2,1)}) custom-call(s32[4]{0:T(128)S(1)} %broadcast_add_fusion.off, bf16[128,2048]{1,0:T(8,128)(2,1)S(1)} %all_gather.6.rows, bf16[2048,16384]{1,0:T(8,128)(2,1)} %refs_6_.1), custom_call_target="tpu_custom_call" | custom-call | flops 4294967296 | bytes 33554432 | tf_op jit(solution)/shard_map/first_back_1/pallas_call | solution.py:353
  86.8 1.6 collective-permute-start.7
  88.4 2.6 collective-permute-start.8
  91.2 14.2 %first_back_0.1 = (f32[16,2048]{1,0:T(8,128)S(1)}, f32[16,2048]{1,0:T(8,128)S(1)}, f32[16,2048]{1,0:T(8,128)S(1)}, f32[16,2048]{1,0:T(8,128)S(1)}, bf16[112,8192]{1,0:T(8,128)(2,1)}) custom-call(s32[4]{0:T(128)S(1)} %iota_xor_fusion.off, bf16[128,2048]{1,0:T(8,128)(2,1)S(1)} %all_gather.6.rows, bf16[2048,16384]{1,0:T(8,128)(2,1)} %refs_6_.1), custom_call_target="tpu_custom_call" | custom-call | flops 4294967296 | bytes 33554432 | tf_op jit(solution)/shard_map/first_back_0/pallas_call | solution.py:353
  106.1 3.5 collective-permute-start.5
  109.9 8.8 %collective-permute-done.4 = f32[16,2048]{1,0:T(8,128)S(1)} collective-permute-done((f32[16,2048]{1,0:T(8,128)S(1)}, f32[16,2048]{1,0:T(8,128)S(1)}, u32[]{:S(2)}, u32[]{:S(2)}) %collective-permute-start.4) | collective-permute-done | bytes 131104 | tf_op jit(solution)/shard_map/ppermute | solution.py:26
  118.7 11.3 %collective-permute-done.5 = f32[16,2048]{1,0:T(8,128)S(1)} collective-permute-done((f32[16,2048]{1,0:T(8,128)S(1)}, f32[16,2048]{1,0:T(8,128)S(1)}, u32[]{:S(2)}, u32[]{:S(2)}) %collective-permute-start.5) | collective-permute-done | bytes 131104 | tf_op jit(solution)/shard_map/ppermute | solution.py:26
  130.2 9.5 %collective-permute-start.12 = (bf16[16,4096]{1,0:T(8,128)(2,1)S(1)}, bf16[16,4096]{1,0:T(8,128)(2,1)S(1)}, u32[]{:S(2)}, u32[]{:S(2)}) collective-permute-start(bf16[16,4096]{1,0:T(8,128)(2,1)S(1)} %get-tuple-element.71.refs_0_), channel_id=1, source_target_pairs={{0,8},{8,0},{16,24},{24,16},{1,9},{9,1},{17,25},{25,17},{2,10},{10... | collective-permute-start | bytes 393224 | tf_op jit(solution)/shard_map/ppermute | solution.py:26
  139.8 3.4 collective-permute-start.11
  145.0 13.0 %second_forward_near.1.refs_2_ = f32[16,2048]{1,0:T(8,128)S(1)} custom-call(s32[4]{0:T(128)S(1)} %reshape.15.off, bf16[16,4096]{1,0:T(8,128)(2,1)S(1)} %get-tuple-element.71.refs_0_, bf16[16,4096]{1,0:T(8,128)(2,1)S(1)} %collective-permute-done.12.refs_1_, bf16[2048,16384]{1,0:T(8,128)(2,1)} %refs_6_.1), custom_call_target="tpu_custom_call" | custom-call | flops 536870912 | bytes 33554432 | tf_op jit(solution)/shard_map/second_forward_near/pallas_call | solution.py:220
  158.0 13.4 %second_forward_far.1 = f32[16,2048]{1,0:T(8,128)S(1)} custom-call(s32[4]{0:T(128)S(1)} %reshape.16.off, bf16[16,4096]{1,0:T(8,128)(2,1)S(1)} %collective-permute-done.10.refs_0_.refs_2_, bf16[16,4096]{1,0:T(8,128)(2,1)S(1)} %collective-permute-done.11.refs_1_.refs_3_, f32[16,2048]{1,0:T(8,128)S(1)} %second_forward_near.1.refs_2_, bf16[2048,16384]{1,0:T(8,128)(2,1)} %refs_6_.1), custom_call_target="tpu_custom_call" | custom-call | flops 536870912 | bytes 33554432 | tf_op jit(solution)/shard_map/second_forward_far/pallas_call | solution.py:220
  171.5 3.8 %fusion.9 = (f32[112,8192]{1,0:T(8,128)}, f32[112,8192]{1,0:T(8,128)}) fusion(f32[112,16384]{1,0:T(8,128)S(1)} %bitcast.26), kind=kLoop, calls=%fused_computation.61 | loop fusion | bytes 14680064 | tf_op jit(solution)/shard_map/slice | solution.py:498
  175.3 1.5 collective-permute-start.16
  176.8 1.5 collective-permute-start.15
  178.8 2.9 constant_dynamic-slice_fusion.3
  182.6 2.3 collective-permute-done.15
  185.0 12.4 %second_back_far.1 = (f32[16,4096]{1,0:T(8,128)S(1)}, f32[16,4096]{1,0:T(8,128)S(1)}) custom-call(s32[4]{0:T(128)S(1)} %reshape.16.off, bf16[16,2048]{1,0:T(8,128)(2,1)S(1)} %get-tuple-element.66.rows, bf16[2048,16384]{1,0:T(8,128)(2,1)} %refs_6_.1), custom_call_target="tpu_custom_call" | custom-call | flops 536870912 | bytes 33554432 | tf_op jit(solution)/shard_map/second_back_far/pallas_call | solution.py:353
  197.4 1.9 collective-permute-start.18
  199.3 1.5 collective-permute-start.19
  200.8 12.3 %second_back_near.1 = (f32[16,4096]{1,0:T(8,128)S(1)}, f32[16,4096]{1,0:T(8,128)S(1)}) custom-call(s32[4]{0:T(128)S(1)} %reshape.15.off, bf16[16,2048]{1,0:T(8,128)(2,1)S(1)} %get-tuple-element.66.rows, bf16[2048,16384]{1,0:T(8,128)(2,1)} %refs_6_.1), custom_call_target="tpu_custom_call" | custom-call | flops 536870912 | bytes 33554432 | tf_op jit(solution)/shard_map/second_back_near/pallas_call | solution.py:353
  213.6 17.8 %collective-permute-done.18 = f32[16,4096]{1,0:T(8,128)S(1)} collective-permute-done((f32[16,4096]{1,0:T(8,128)S(1)}, f32[16,4096]{1,0:T(8,128)S(1)}, u32[]{:S(2)}, u32[]{:S(2)}) %collective-permute-start.18) | collective-permute-done | bytes 262176 | tf_op jit(solution)/shard_map/ppermute | solution.py:26
  231.4 9.6 %collective-permute-done.17 = f32[16,4096]{1,0:T(8,128)S(1)} collective-permute-done((f32[16,4096]{1,0:T(8,128)S(1)}, f32[16,4096]{1,0:T(8,128)S(1)}, u32[]{:S(2)}, u32[]{:S(2)}) %collective-permute-start.17) | collective-permute-done | bytes 262176 | tf_op jit(solution)/shard_map/ppermute | solution.py:26
  241.3 2.3 collective-permute-start.22
  243.6 11.0 %collective-permute-start.21 = (bf16[16,4096]{1,0:T(8,128)(2,1)S(1)}, bf16[16,4096]{1,0:T(8,128)(2,1)S(1)}, u32[]{:S(2)}, u32[]{:S(2)}) collective-permute-start(bf16[16,4096]{1,0:T(8,128)(2,1)S(1)} %get-tuple-element.43.refs_0_.refs_4_), channel_id=1, source_target_pairs={{0,16},{8,24},{16,0},{24,8},{1,17},{9,25},{17,1},{25,9},{2,18},{10... | collective-permute-start | bytes 393224 | tf_op jit(solution)/shard_map/ppermute | solution.py:26
  254.7 9.5 %collective-permute-done.21.refs_2_.refs_6_ = bf16[16,4096]{1,0:T(8,128)(2,1)S(1)} collective-permute-done((bf16[16,4096]{1,0:T(8,128)(2,1)S(1)}, bf16[16,4096]{1,0:T(8,128)(2,1)S(1)}, u32[]{:S(2)}, u32[]{:S(2)}) %collective-permute-start.21) | collective-permute-done | bytes 131104 | tf_op jit(solution)/shard_map/ppermute | solution.py:26
  264.2 2.1 collective-permute-start.25
  266.3 2.3 collective-permute-start.23
  268.6 1.5 copy-done.2
  270.1 13.3 %third_forward_0.1.refs_5_ = f32[2048,128]{1,0:T(8,128)S(1)} custom-call(s32[4]{0:T(128)S(1)} %iota_xor_fusion.off, bf16[16,4096]{1,0:T(8,128)(2,1)S(1)} %get-tuple-element.43.refs_0_.refs_4_, bf16[16,4096]{1,0:T(8,128)(2,1)S(1)} %collective-permute-done.20.refs_1_.refs_5_, bf16[16,4096]{1,0:T(8,128)(2,1)S(1)} %collective-permute-done.21.refs_2_.refs_6_, ...), custom_call_target="tpu_custom_call" | custom-call | flops 4294967296 | bytes 33554432 | tf_op jit(solution)/shard_map/third_forward_0/pallas_call | solution.py:273
  283.4 24.3 %collective-permute-done.24.refs_10_ = bf16[32,4096]{1,0:T(8,128)(2,1)} collective-permute-done((bf16[32,4096]{1,0:T(8,128)(2,1)S(1)}, bf16[32,4096]{1,0:T(8,128)(2,1)}, u32[]{:S(2)}, u32[]{:S(2)}) %collective-permute-start.24) | collective-permute-done | bytes 262176 | tf_op jit(solution)/shard_map/ppermute | solution.py:26
  307.8 9.6 %all-gather.2.cloned.1.call-done.refs_4_ = bf16[112,8192]{1,0:T(8,128)(2,1)} async-done(((bf16[112,2048]{1,0:T(8,128)(2,1)}), bf16[112,8192]{1,0:T(8,128)(2,1)}) %all-gather.2.cloned.1.call-update) | async-done | bytes 1835024 | tf_op jit(solution)/shard_map/all_gather | solution.py:453
  317.3 1.5 copy-done.3
  318.8 14.0 %third_forward_1.1 = bf16[8,128,256]{2,1,0:T(8,128)(2,1)} custom-call(s32[4]{0:T(128)S(1)} %broadcast_add_fusion.off, bf16[16,4096]{1,0:T(8,128)(2,1)S(1)} %get-tuple-element.43.refs_0_.refs_4_, bf16[16,4096]{1,0:T(8,128)(2,1)S(1)} %collective-permute-done.20.refs_1_.refs_5_, bf16[16,4096]{1,0:T(8,128)(2,1)S(1)} %collective-permute-done.21.refs_2_.refs_6_, ...), custom_call_target="tpu_custom_call" | custom-call | flops 4294967296 | bytes 33554432 | tf_op jit(solution)/shard_map/third_forward_1/pallas_call | solution.py:273
  332.8 4.3 %all-to-all-start.1 = ((bf16[8,128,256]{2,1,0:T(8,128)(2,1)}), bf16[8,128,256]{2,1,0:T(8,128)(2,1)}, u32[]{:S(2)}, u32[]{:S(2)}) async-start(bf16[8,128,256]{2,1,0:T(8,128)(2,1)} %third_forward_1.1), calls=%async_computation.2 | async-start | bytes 1048576 | tf_op jit(solution)/shard_map/all_to_all | solution.py:487
  340.0 6.9 %all-to-all-done.1 = bf16[8,128,256]{2,1,0:T(8,128)(2,1)} async-done(((bf16[8,128,256]{2,1,0:T(8,128)(2,1)}), bf16[8,128,256]{2,1,0:T(8,128)(2,1)}, u32[]{:S(2)}, u32[]{:S(2)}) %all-to-all-start.1) | async-done | bytes 524320 | tf_op jit(solution)/shard_map/all_to_all | solution.py:487
  351.8 1.5 collective-permute-start.27
  353.4 2.2 collective-permute-done.29
  356.1 2.1 collective-permute-start.32
  358.2 2.3 collective-permute-start.30
  360.7 2.1 collective-permute-done.32
  364.2 4.3 %finish.1 = (f32[16,16384]{1,0:T(8,128)}, f32[16,16384]{1,0:T(8,128)}) custom-call(s32[4]{0:T(128)S(1)} %iota_xor_fusion.off, f32[128,6]{1,0:T(8,128)S(1)} %add_add_fusion.4.sums, f32[128,2]{1,0:T(8,128)S(1)} %copy.54.wide_cols, f32[16,3]{1,0:T(8,128)S(1)} %copy.55.cols, f32[16,16384]{1,0:T(8,128)S(1)} %get-tuple-element.49.centre, ...), custom_call_target="tpu_custom_call" | custom-call | tf_op jit(solution)/shard_map/finish/pallas_call | solution.py:412
  (122 shorter events, 24.0 us)
Async XLA Ops:
  9.9 1.3 collective-permute-start
  11.2 5.4 %collective-permute-start.3 = (f32[16,1]{1,0:T(8,128)S(1)}, f32[16,1]{1,0:T(8,128)S(1)}, u32[]{:S(2)}, u32[]{:S(2)}) collective-permute-start(f32[16,1]{1,0:T(8,128)S(1)} %add.100), channel_id=1, source_target_pairs={{0,6},{1,7},{2,4},{3,5},{4,2},{5,3},{6,0},{7,1},{8,14},{9,15},{10,... | collective-permute-start | bytes 200 | tf_op jit(solution)/shard_map/ppermute | solution.py:26
  15.0 3.7 collective-permute-start.2
  15.5 3.7 collective-permute-start.1
  19.8 3.1 copy-start
  47.5 13.9 %all-to-all-start = ((bf16[8,144,256]{2,1,0:T(8,128)(2,1)}), bf16[8,144,256]{2,1,0:T(8,128)(2,1)S(1)}, u32[]{:S(2)}, u32[]{:S(2)}) async-start(bf16[8,144,256]{2,1,0:T(8,128)(2,1)} %get-tuple-element.28), calls=%async_computation | async-start | bytes 1179648 | tf_op jit(solution)/shard_map/all_to_all | solution.py:440
  51.0 130.8 %reduce-scatter.2.cloned.1.call-start = ((), (), s32[]{:S(2)}) async-start(), calls=%async_computation.4 | async-start | bytes 2293760 | tf_op jit(solution)/shard_map/reduce_scatter | solution.py:452
  61.5 152.1 %copy-start.6 = (f32[144,256]{1,0:T(8,128)}, f32[144,256]{1,0:T(8,128)S(1)}, u32[]{:S(2)}) copy-start(f32[144,256]{1,0:T(8,128)S(1)} %convert_reduce_fusion) | copy-start | bytes 442372
  86.2 182.4 %all-reduce.2.cloned.1.call-start = ((), (), s32[]{:S(2)}) async-start(), calls=%async_computation.3 | async-start | bytes 3670016 | tf_op jit(solution)/shard_map/psum | solution.py:455
  86.8 22.8 %collective-permute-start.7 = (f32[16,2048]{1,0:T(8,128)S(1)}, f32[16,2048]{1,0:T(8,128)S(1)}, u32[]{:S(2)}, u32[]{:S(2)}) collective-permute-start(f32[16,2048]{1,0:T(8,128)S(1)} %get-tuple-element.34), channel_id=1, source_target_pairs={{0,8},{8,0},{16,24},{24,16},{1,9},{9,1},{17,25},{25,17},{2,10},{10... | collective-permute-start | bytes 393224 | tf_op jit(solution)/shard_map/ppermute | solution.py:26
  88.4 21.4 %collective-permute-start.8 = (f32[16,2048]{1,0:T(8,128)S(1)}, f32[16,2048]{1,0:T(8,128)S(1)}, u32[]{:S(2)}, u32[]{:S(2)}) collective-permute-start(f32[16,2048]{1,0:T(8,128)S(1)} %get-tuple-element.35), channel_id=1, source_target_pairs={{0,16},{8,24},{16,0},{24,8},{1,17},{9,25},{17,1},{25,9},{2,18},{10... | collective-permute-start | bytes 393224 | tf_op jit(solution)/shard_map/ppermute | solution.py:26
  91.0 18.8 %collective-permute-start.9 = (f32[16,2048]{1,0:T(8,128)S(1)}, f32[16,2048]{1,0:T(8,128)S(1)}, u32[]{:S(2)}, u32[]{:S(2)}) collective-permute-start(f32[16,2048]{1,0:T(8,128)S(1)} %get-tuple-element.36), channel_id=1, source_target_pairs={{0,24},{8,16},{16,8},{24,0},{1,25},{9,17},{17,9},{25,1},{2,26},{10... | collective-permute-start | bytes 393224 | tf_op jit(solution)/shard_map/ppermute | solution.py:26
  105.4 13.3 %collective-permute-start.4 = (f32[16,2048]{1,0:T(8,128)S(1)}, f32[16,2048]{1,0:T(8,128)S(1)}, u32[]{:S(2)}, u32[]{:S(2)}) collective-permute-start(f32[16,2048]{1,0:T(8,128)S(1)} %get-tuple-element.30), channel_id=1, source_target_pairs={{0,8},{8,0},{16,24},{24,16},{1,9},{9,1},{17,25},{25,17},{2,10},{10... | collective-permute-start | bytes 393224 | tf_op jit(solution)/shard_map/ppermute | solution.py:26
  106.1 23.9 %collective-permute-start.5 = (f32[16,2048]{1,0:T(8,128)S(1)}, f32[16,2048]{1,0:T(8,128)S(1)}, u32[]{:S(2)}, u32[]{:S(2)}) collective-permute-start(f32[16,2048]{1,0:T(8,128)S(1)} %get-tuple-element.31), channel_id=1, source_target_pairs={{0,16},{8,24},{16,0},{24,8},{1,17},{9,25},{17,1},{25,9},{2,18},{10... | collective-permute-start | bytes 393224 | tf_op jit(solution)/shard_map/ppermute | solution.py:26
  109.6 20.4 %collective-permute-start.6 = (f32[16,2048]{1,0:T(8,128)S(1)}, f32[16,2048]{1,0:T(8,128)S(1)}, u32[]{:S(2)}, u32[]{:S(2)}) collective-permute-start(f32[16,2048]{1,0:T(8,128)S(1)} %get-tuple-element.32), channel_id=1, source_target_pairs={{0,24},{8,16},{16,8},{24,0},{1,25},{9,17},{17,9},{25,1},{2,26},{10... | collective-permute-start | bytes 393224 | tf_op jit(solution)/shard_map/ppermute | solution.py:26
  130.2 14.8 %collective-permute-start.12 = (bf16[16,4096]{1,0:T(8,128)(2,1)S(1)}, bf16[16,4096]{1,0:T(8,128)(2,1)S(1)}, u32[]{:S(2)}, u32[]{:S(2)}) collective-permute-start(bf16[16,4096]{1,0:T(8,128)(2,1)S(1)} %get-tuple-element.71.refs_0_), channel_id=1, source_target_pairs={{0,8},{8,0},{16,24},{24,16},{1,9},{9,1},{17,25},{25,17},{2,10},{10... | collective-permute-start | bytes 393224 | tf_op jit(solution)/shard_map/ppermute | solution.py:26
  139.8 18.2 %collective-permute-start.11 = (bf16[16,4096]{1,0:T(8,128)(2,1)S(1)}, bf16[16,4096]{1,0:T(8,128)(2,1)S(1)}, u32[]{:S(2)}, u32[]{:S(2)}) collective-permute-start(bf16[16,4096]{1,0:T(8,128)(2,1)S(1)} %get-tuple-element.71.refs_0_), channel_id=1, source_target_pairs={{0,24},{8,16},{16,8},{24,0},{1,25},{9,17},{17,9},{25,1},{2,26},{10... | collective-permute-start | bytes 393224 | tf_op jit(solution)/shard_map/ppermute | solution.py:26
  143.1 14.9 %collective-permute-start.10 = (bf16[16,4096]{1,0:T(8,128)(2,1)S(1)}, bf16[16,4096]{1,0:T(8,128)(2,1)S(1)}, u32[]{:S(2)}, u32[]{:S(2)}) collective-permute-start(bf16[16,4096]{1,0:T(8,128)(2,1)S(1)} %get-tuple-element.71.refs_0_), channel_id=1, source_target_pairs={{0,16},{8,24},{16,0},{24,8},{1,17},{9,25},{17,1},{25,9},{2,18},{10... | collective-permute-start | bytes 393224 | tf_op jit(solution)/shard_map/ppermute | solution.py:26
  143.5 173.8 %all-gather.2.cloned.1.call-start = ((), (), s32[]{:S(2)}) async-start(), calls=%async_computation.5 | async-start | bytes 2293760 | tf_op jit(solution)/shard_map/all_gather | solution.py:453
  145.0 26.5 %slice-start = ((s8[7340032]{0:T(1024)(128)(4,1)}), s8[4194304]{0:T(1024)(128)(4,1)S(1)}, s32[]{:S(2)}) async-start(s8[7340032]{0:T(1024)(128)(4,1)} %bitcast.25), calls=%async_computation.6 | async-start | bytes 8388608
  158.0 13.5 %slice-start.1 = ((s8[7340032]{0:T(1024)(128)(4,1)}), s8[3145728]{0:T(1024)(128)(4,1)S(1)}, s32[]{:S(2)}) async-start(s8[7340032]{0:T(1024)(128)(4,1)} %bitcast.25), calls=%async_computation.7 | async-start | bytes 6291456
  171.4 3.9 %collective-permute-start.13 = (f32[16,2048]{1,0:T(8,128)S(1)}, f32[16,2048]{1,0:T(8,128)S(1)}, u32[]{:S(2)}, u32[]{:S(2)}) collective-permute-start(f32[16,2048]{1,0:T(8,128)S(1)} %second_forward_far.1), channel_id=1, source_target_pairs={{0,1},{1,0},{2,3},{3,2},{4,5},{5,4},{6,7},{7,6},{8,9},{9,8},{10,11... | collective-permute-start | bytes 393224 | tf_op jit(solution)/shard_map/ppermute | solution.py:26
  175.3 7.3 %collective-permute-start.16 = (f32[16,2048]{1,0:T(8,128)S(1)}, f32[16,2048]{1,0:T(8,128)S(1)}, u32[]{:S(2)}, u32[]{:S(2)}) collective-permute-start(f32[16,2048]{1,0:T(8,128)S(1)} %add.114), channel_id=1, source_target_pairs={{0,6},{1,7},{2,4},{3,5},{4,2},{5,3},{6,0},{7,1},{8,14},{9,15},{10,... | collective-permute-start | bytes 393224 | tf_op jit(solution)/shard_map/ppermute | solution.py:26
  176.8 8.1 %collective-permute-start.15 = (f32[16,2048]{1,0:T(8,128)S(1)}, f32[16,2048]{1,0:T(8,128)S(1)}, u32[]{:S(2)}, u32[]{:S(2)}) collective-permute-start(f32[16,2048]{1,0:T(8,128)S(1)} %add.114), channel_id=1, source_target_pairs={{0,4},{1,5},{2,6},{3,7},{4,0},{5,1},{6,2},{7,3},{8,12},{9,13},{10,... | collective-permute-start | bytes 393224 | tf_op jit(solution)/shard_map/ppermute | solution.py:26
  178.3 6.7 %collective-permute-start.14 = (f32[16,2048]{1,0:T(8,128)S(1)}, f32[16,2048]{1,0:T(8,128)S(1)}, u32[]{:S(2)}, u32[]{:S(2)}) collective-permute-start(f32[16,2048]{1,0:T(8,128)S(1)} %add.114), channel_id=1, source_target_pairs={{0,2},{1,3},{2,0},{3,1},{4,6},{5,7},{6,4},{7,5},{8,10},{9,11},{10,... | collective-permute-start | bytes 393224 | tf_op jit(solution)/shard_map/ppermute | solution.py:26
  197.4 33.9 %collective-permute-start.18 = (f32[16,4096]{1,0:T(8,128)S(1)}, f32[16,4096]{1,0:T(8,128)S(1)}, u32[]{:S(2)}, u32[]{:S(2)}) collective-permute-start(f32[16,4096]{1,0:T(8,128)S(1)} %get-tuple-element.39), channel_id=1, source_target_pairs={{0,16},{8,24},{16,0},{24,8},{1,17},{9,25},{17,1},{25,9},{2,18},{10... | collective-permute-start | bytes 786440 | tf_op jit(solution)/shard_map/ppermute | solution.py:26
  199.3 14.2 %copy-start.10 = (f32[16]{0:T(128)S(1)}, f32[16]{0:T(128)}, u32[]{:S(2)}) copy-start(f32[16]{0:T(128)} %param.12) | copy-start | bytes 196
  199.3 32.0 %collective-permute-start.19 = (f32[16,4096]{1,0:T(8,128)S(1)}, f32[16,4096]{1,0:T(8,128)S(1)}, u32[]{:S(2)}, u32[]{:S(2)}) collective-permute-start(f32[16,4096]{1,0:T(8,128)S(1)} %get-tuple-element.40), channel_id=1, source_target_pairs={{0,24},{8,16},{16,8},{24,0},{1,25},{9,17},{17,9},{25,1},{2,26},{10... | collective-permute-start | bytes 786440 | tf_op jit(solution)/shard_map/ppermute | solution.py:26
  213.1 27.9 %collective-permute-start.17 = (f32[16,4096]{1,0:T(8,128)S(1)}, f32[16,4096]{1,0:T(8,128)S(1)}, u32[]{:S(2)}, u32[]{:S(2)}) collective-permute-start(f32[16,4096]{1,0:T(8,128)S(1)} %get-tuple-element.38), channel_id=1, source_target_pairs={{0,8},{8,0},{16,24},{24,16},{1,9},{9,1},{17,25},{25,17},{2,10},{10... | collective-permute-start | bytes 786440 | tf_op jit(solution)/shard_map/ppermute | solution.py:26
  241.3 13.4 %collective-permute-start.22 = (bf16[16,4096]{1,0:T(8,128)(2,1)S(1)}, bf16[16,4096]{1,0:T(8,128)(2,1)S(1)}, u32[]{:S(2)}, u32[]{:S(2)}) collective-permute-start(bf16[16,4096]{1,0:T(8,128)(2,1)S(1)} %get-tuple-element.43.refs_0_.refs_4_), channel_id=1, source_target_pairs={{0,24},{8,16},{16,8},{24,0},{1,25},{9,17},{17,9},{25,1},{2,26},{10... | collective-permute-start | bytes 393224 | tf_op jit(solution)/shard_map/ppermute | solution.py:26
  243.6 20.6 %collective-permute-start.21 = (bf16[16,4096]{1,0:T(8,128)(2,1)S(1)}, bf16[16,4096]{1,0:T(8,128)(2,1)S(1)}, u32[]{:S(2)}, u32[]{:S(2)}) collective-permute-start(bf16[16,4096]{1,0:T(8,128)(2,1)S(1)} %get-tuple-element.43.refs_0_.refs_4_), channel_id=1, source_target_pairs={{0,16},{8,24},{16,0},{24,8},{1,17},{9,25},{17,1},{25,9},{2,18},{10... | collective-permute-start | bytes 393224 | tf_op jit(solution)/shard_map/ppermute | solution.py:26
  254.7 9.5 %collective-permute-start.20 = (bf16[16,4096]{1,0:T(8,128)(2,1)S(1)}, bf16[16,4096]{1,0:T(8,128)(2,1)S(1)}, u32[]{:S(2)}, u32[]{:S(2)}) collective-permute-start(bf16[16,4096]{1,0:T(8,128)(2,1)S(1)} %get-tuple-element.43.refs_0_.refs_4_), channel_id=1, source_target_pairs={{0,8},{8,0},{16,24},{24,16},{1,9},{9,1},{17,25},{25,17},{2,10},{10... | collective-permute-start | bytes 393224 | tf_op jit(solution)/shard_map/ppermute | solution.py:26
  264.2 19.2 %collective-permute-start.25 = (bf16[32,4096]{1,0:T(8,128)(2,1)S(1)}, bf16[32,4096]{1,0:T(8,128)(2,1)}, u32[]{:S(2)}, u32[]{:S(2)}) collective-permute-start(bf16[32,4096]{1,0:T(8,128)(2,1)S(1)} %pad_maximum_fusion.2.refs_8_), channel_id=1, source_target_pairs={{0,24},{8,16},{16,8},{24,0},{1,25},{9,17},{17,9},{25,1},{2,26},{10... | collective-permute-start | bytes 786440 | tf_op jit(solution)/shard_map/ppermute | solution.py:26
  266.3 41.5 %collective-permute-start.24 = (bf16[32,4096]{1,0:T(8,128)(2,1)S(1)}, bf16[32,4096]{1,0:T(8,128)(2,1)}, u32[]{:S(2)}, u32[]{:S(2)}) collective-permute-start(bf16[32,4096]{1,0:T(8,128)(2,1)S(1)} %pad_maximum_fusion.2.refs_8_), channel_id=1, source_target_pairs={{0,16},{8,24},{16,0},{24,8},{1,17},{9,25},{17,1},{25,9},{2,18},{10... | collective-permute-start | bytes 786440 | tf_op jit(solution)/shard_map/ppermute | solution.py:26
  266.3 41.5 %collective-permute-start.23 = (bf16[32,4096]{1,0:T(8,128)(2,1)S(1)}, bf16[32,4096]{1,0:T(8,128)(2,1)}, u32[]{:S(2)}, u32[]{:S(2)}) collective-permute-start(bf16[32,4096]{1,0:T(8,128)(2,1)S(1)} %pad_maximum_fusion.2.refs_8_), channel_id=1, source_target_pairs={{0,8},{8,0},{16,24},{24,16},{1,9},{9,1},{17,25},{25,17},{2,10},{10... | collective-permute-start | bytes 786440 | tf_op jit(solution)/shard_map/ppermute | solution.py:26
  332.8 6.5 %copy-start.4 = (f32[112,2048]{1,0:T(8,128)S(1)}, f32[112,2048]{1,0:T(8,128)}, u32[]{:S(2)}) copy-start(f32[112,2048]{1,0:T(8,128)} %get-tuple-element.82) | copy-start | bytes 2752516
  332.8 14.0 %all-to-all-start.1 = ((bf16[8,128,256]{2,1,0:T(8,128)(2,1)}), bf16[8,128,256]{2,1,0:T(8,128)(2,1)}, u32[]{:S(2)}, u32[]{:S(2)}) async-start(bf16[8,128,256]{2,1,0:T(8,128)(2,1)} %third_forward_1.1), calls=%async_computation.2 | async-start | bytes 1048576 | tf_op jit(solution)/shard_map/all_to_all | solution.py:487
  339.3 8.7 %slice-start.2 = ((f32[144,256]{1,0:T(8,128)}), f32[112,256]{1,0:T(8,128)S(1)}, s32[]{:S(2)}) async-start(f32[144,256]{1,0:T(8,128)} %copy-done.6), calls=%async_computation.8 | async-start | bytes 229376 | tf_op jit(solution)/shard_map/slice | solution.py:443
  339.4 9.1 %copy-start.7 = (f32[16]{0:T(128)S(1)}, f32[16]{0:T(128)}, u32[]{:S(2)}) copy-start(f32[16]{0:T(128)} %param.14) | copy-start | bytes 196
  339.4 9.1 %copy-start.8 = (f32[16]{0:T(128)S(1)}, f32[16]{0:T(128)}, u32[]{:S(2)}) copy-start(f32[16]{0:T(128)} %param.13) | copy-start | bytes 196
  339.4 9.1 %copy-start.9 = (f32[16]{0:T(128)S(1)}, f32[16]{0:T(128)}, u32[]{:S(2)}) copy-start(f32[16]{0:T(128)} %get-tuple-element.63) | copy-start | bytes 196
  348.4 1.3 collective-permute-start.26
  349.7 5.8 %collective-permute-start.29 = (f32[128,6]{1,0:T(8,128)S(1)}, f32[128,6]{1,0:T(8,128)S(1)}, u32[]{:S(2)}, u32[]{:S(2)}) collective-permute-start(f32[128,6]{1,0:T(8,128)S(1)} %add.122), channel_id=1, source_target_pairs={{0,6},{1,7},{2,4},{3,5},{4,2},{5,3},{6,0},{7,1},{8,14},{9,15},{10,... | collective-permute-start | bytes 9224 | tf_op jit(solution)/shard_map/ppermute | solution.py:26
  350.3 5.3 %collective-permute-start.28 = (f32[128,6]{1,0:T(8,128)S(1)}, f32[128,6]{1,0:T(8,128)S(1)}, u32[]{:S(2)}, u32[]{:S(2)}) collective-permute-start(f32[128,6]{1,0:T(8,128)S(1)} %add.122), channel_id=1, source_target_pairs={{0,4},{1,5},{2,6},{3,7},{4,0},{5,1},{6,2},{7,3},{8,12},{9,13},{10,... | collective-permute-start | bytes 9224 | tf_op jit(solution)/shard_map/ppermute | solution.py:26
  351.8 4.3 %collective-permute-start.27 = (f32[128,6]{1,0:T(8,128)S(1)}, f32[128,6]{1,0:T(8,128)S(1)}, u32[]{:S(2)}, u32[]{:S(2)}) collective-permute-start(f32[128,6]{1,0:T(8,128)S(1)} %add.122), channel_id=1, source_target_pairs={{0,2},{1,3},{2,0},{3,1},{4,6},{5,7},{6,4},{7,5},{8,10},{9,11},{10,... | collective-permute-start | bytes 9224 | tf_op jit(solution)/shard_map/ppermute | solution.py:26
  356.1 6.7 %collective-permute-start.32 = (f32[128,6]{1,0:T(8,128)S(1)}, f32[128,6]{1,0:T(8,128)S(1)}, u32[]{:S(2)}, u32[]{:S(2)}) collective-permute-start(f32[128,6]{1,0:T(8,128)S(1)} %add_add_fusion.5), channel_id=1, source_target_pairs={{0,24},{8,16},{16,8},{24,0},{1,25},{9,17},{17,9},{25,1},{2,26},{10... | collective-permute-start | bytes 9224 | tf_op jit(solution)/shard_map/ppermute | solution.py:26
  358.2 6.0 %collective-permute-start.31 = (f32[128,6]{1,0:T(8,128)S(1)}, f32[128,6]{1,0:T(8,128)S(1)}, u32[]{:S(2)}, u32[]{:S(2)}) collective-permute-start(f32[128,6]{1,0:T(8,128)S(1)} %add_add_fusion.5), channel_id=1, source_target_pairs={{0,16},{8,24},{16,0},{24,8},{1,17},{9,25},{17,1},{25,9},{2,18},{10... | collective-permute-start | bytes 9224 | tf_op jit(solution)/shard_map/ppermute | solution.py:26
  358.2 6.0 %collective-permute-start.30 = (f32[128,6]{1,0:T(8,128)S(1)}, f32[128,6]{1,0:T(8,128)S(1)}, u32[]{:S(2)}, u32[]{:S(2)}) collective-permute-start(f32[128,6]{1,0:T(8,128)S(1)} %add_add_fusion.5), channel_id=1, source_target_pairs={{0,8},{8,0},{16,24},{24,16},{1,9},{9,1},{17,25},{25,17},{2,10},{10... | collective-permute-start | bytes 9224 | tf_op jit(solution)/shard_map/ppermute | solution.py:26
  (5 other events, 7.2 us)
Sparse Core Ops, SparseCore 0:
  86.3 58.9 reduce-scatter.1
  147.7 112.9 all-reduce.1
  262.3 55.0 all-gather.1

commit v3 on v2

--- a/solution.py
+++ b/solution.py
@@ -75,14 +75,14 @@
     return [pltpu.VMEM((SLOTS, rows, columns), BF16), pltpu.SemaphoreType.DMA((SLOTS,))]
 
 
-def forward_loop(g, rows, total, held, sems, off, span, pieces, wide, fresh, prepare):
+def forward_loop(g, rows, total, held, sems, unit_at, span, pieces, wide, fresh, prepare):
     people = g.shape[0]
     slots, pb, kb = held.shape
     steps, blocks = span // kb, people // pb
 
     def place(c):
         k, i = c // blocks, lax.rem(c, blocks)
-        col = off[k // steps] * span + lax.rem(k, steps) * kb
+        col = unit_at(k // steps) * span + lax.rem(k, steps) * kb
         return g.at[pl.ds(pl.multiple_of(i * pb, pb), pb), pl.ds(pl.multiple_of(col, kb), kb)]
 
     def use(c, slot):
@@ -156,7 +156,7 @@
         rows[:t, :] = made.astype(BF16)
         rows[t:, :] = probes[...].astype(BF16)
 
-    forward_loop(g, rows, total, held, sems, off, g.shape[1], 1, True, True, prepare)
+    forward_loop(g, rows, total, held, sems, lambda j: j, g.shape[1], 1, True, True, prepare)
     split_people(out, total, t)
 
 
@@ -208,7 +208,9 @@
             out[...] = acc[...]
 
     count = n * span // unit
-    forward_loop(g, rows, out, held, sems, off, unit, count, False, not with_acc, prepare)
+    forward_loop(
+        g, rows, out, held, sems, lambda j: off[j], unit, count, False, not with_acc, prepare
+    )
 
 
 def narrow_forward(pieces, places, acc, genotypes, name):
@@ -233,37 +235,50 @@
     )(places, *operands)
 
 
-def wide_body(n, half, with_acc, off, *refs):
+def wide_body(n, half, chunks, with_acc, off, *refs):
     refs = list(refs)
     pieces = [refs.pop(0) for _ in range(n)]
-    probes = refs.pop(0)
+    inner = [refs.pop(0) for _ in range(chunks)]
+    outer = [refs.pop(0) for _ in range(chunks)]
     acc = refs.pop(0) if with_acc else None
     if with_acc:
         g, out, rows, held, sems, total = refs
     else:
         g, total, rows, held, sems = refs
     t, unit = pieces[0].shape[0], pieces[0].shape[1] // 2
+    span = inner[0].shape[1]
 
     def prepare():
         for j in range(n):
-            here = slice(j * unit, (j + 1) * unit)
+            here = pl.ds(pl.multiple_of(off[j] * unit, unit), unit)
             rows[:t, here] = pieces[j][:, half * unit : (half + 1) * unit]
-            there = pl.multiple_of((off[j] - half * n) * unit, unit)
-            rows[t:, here] = probes[:, pl.ds(there, unit)]
+        for j in range(chunks):
+            here = slice(j * span, (j + 1) * span)
+
+            @pl.when(off[n] == 1)
+            def _():
+                rows[t:, here] = inner[j][...]
+
+            @pl.when(off[n] == 0)
+            def _():
+                rows[t:, here] = outer[j][...]
+
         if with_acc:
             total[...] = acc[...]
 
-    forward_loop(g, rows, total, held, sems, off, unit, n, True, not with_acc, prepare)
+    forward_loop(
+        g, rows, total, held, sems, lambda j: half * n + j, unit, n, True, not with_acc, prepare
+    )
     if with_acc:
         split_people(out, total, 0)
 
 
-def wide_forward(pieces, probes, places, half, acc, genotypes, columns, name):
+def wide_forward(pieces, inner, outer, places, half, acc, genotypes, columns, name):
     people = genotypes.shape[0]
     n, t, unit = len(pieces), pieces[0].shape[0], pieces[0].shape[1] // 2
-    r = t + probes.shape[0]
+    r = t + inner[0].shape[0]
     pb, kb = block_of(people, 1024), block_of(unit, 2048)
-    operands = [*pieces, probes, *([] if acc is None else [acc]), genotypes]
+    operands = [*pieces, *inner, *outer, *([] if acc is None else [acc]), genotypes]
     scratch = [pltpu.VMEM((r, n * unit), BF16), *ring(pb, kb)]
     if acc is None:
         shape = jax.ShapeDtypeStruct((people, r), F32)
@@ -271,7 +286,7 @@
         shape = jax.ShapeDtypeStruct((columns, r, people // columns), BF16)
         scratch.append(pltpu.VMEM((people, r), F32))
     return pl.pallas_call(
-        functools.partial(wide_body, n, half, acc is not None),
+        functools.partial(wide_body, n, half, len(inner), acc is not None),
         grid_spec=pltpu.PrefetchScalarGridSpec(
             num_scalar_prefetch=1,
             grid=(),
@@ -319,19 +334,28 @@
     if t == rows.shape[0]:
         outs, total = refs[:-3], refs[-3]
     else:
-        outs, (whole, total, made, sent) = refs[:-6], refs[-6:-2]
+        outs, (lower, upper, total, made, sent) = refs[:-7], refs[-7:-2]
     backward_loop(g, rows, total, held, sems, off, unit, n)
     copies = []
     if t != rows.shape[0]:
         made[...] = total[t:, :].astype(BF16)
         for j in range(n):
-            cols = pl.ds(pl.multiple_of((off[j] - base) * unit, unit), unit)
-            copies.append(
-                pltpu.make_async_copy(
-                    made.at[:, pl.ds(j * unit, unit)], whole.at[:, cols], sent.at[j]
-                )
-            )
-            copies[-1].start()
+            place = off[j] - base
+            part = made.at[:, pl.ds(j * unit, unit)]
+
+            def copy(whole, first):
+                cols = pl.ds(pl.multiple_of((place - first) * unit, unit), unit)
+                return pltpu.make_async_copy(part, whole.at[:, cols], sent.at[j])
+
+            @pl.when(place < n // 2)
+            def _():
+                copy(lower, 0).start()
+
+            @pl.when(place >= n // 2)
+            def _():
+                copy(upper, n // 2).start()
+
+            copies.append(pltpu.make_async_copy(part, lower.at[:, pl.ds(0, unit)], sent.at[j]))
     span = outs[0].shape[1]
     for j, out in enumerate(outs):
         out[...] = total[:t, j * span : (j + 1) * span]
@@ -347,8 +371,8 @@
     out_shape = [jax.ShapeDtypeStruct((t, n * unit // arrays), F32)] * arrays
     scratch = [pltpu.VMEM((r, n * unit), F32)]
     if t != r:
-        out_specs.append(ANY)
-        out_shape.append(jax.ShapeDtypeStruct((r - t, n * unit), BF16))
+        out_specs += [ANY] * 2
+        out_shape += [jax.ShapeDtypeStruct((r - t, n * unit // 2), BF16)] * 2
         scratch += [pltpu.VMEM((r - t, n * unit), BF16), pltpu.SemaphoreType.DMA((n,))]
     return pl.pallas_call(
         functools.partial(back_body, n, unit, t, base),
@@ -441,18 +465,34 @@
     kept_x, low_x = kept_x[: traits * copies], kept_x[traits * copies :]
     own = lax.dynamic_slice_in_dim(phenotypes, column * share, share, 1) - (kept_x[:traits] + low_x)
     rows = jnp.concatenate([own, kept_x[traits:]], axis=0).astype(BF16)
+    pred_x = rows[traits:].astype(F32)
     rows = lax.all_gather(rows, "marker", axis=1, tiled=True)
-    starts, probe_back = [], []
+    starts, chunks = [], []
     for half in range(2):
-        *parts, whole = backward(
+        *parts, lower, upper = backward(
             rows, order + half * samples, genotypes, unit, traits, half * samples, samples, f"first_back_{half}"
         )
         starts.append([swap(part, "sample", k) if k else part for k, part in enumerate(parts)])
-        if half:
-            whole = lax.psum_scatter(whole, "sample", scatter_dimension=1, tiled=True)
-            probe_back.append(lax.all_gather(whole, "sample", axis=1, tiled=True))
-        else:
-            probe_back.append(lax.psum(whole, "sample"))
+        chunks += [lower, upper]
+        rows, *_ = lax.optimization_barrier((rows, lower))
+
+    def add(x, y):
+        return (x.astype(F32) + y.astype(F32)).astype(BF16)
+
+    def inward(c):
+        return add(chunks[c], lax.ppermute(chunks[c], "sample", [(0, 1), (3, 2)]))
+
+    def across(x):
+        return add(x, lax.ppermute(x, "sample", [(1, 2), (2, 1)]))
+
+    def outward(x):
+        return lax.ppermute(x, "sample", [(1, 0), (2, 3)])
+
+    def tie(values, *others):
+        return lax.optimization_barrier((tuple(values), others))[0]
+
+    pair, full, ends = [None] * 4, [None] * 4, [None] * 4
+    pair[0] = inward(0)
     scale = (noise_precision / people)[:, None]
     start = scale * jnp.concatenate([tree(parts) for parts in starts], axis=1)
     start_high = lax.reduce_precision(start, 8, 7)
@@ -460,47 +500,64 @@
     start_high = start_high.astype(BF16)
 
     start_pieces = [swap(start_high, "sample", k) if k else start_high for k in range(samples)]
+    start_pieces[0], start_pieces[1], chunks[1] = tie(
+        (start_pieces[0], start_pieces[1], chunks[1]), pair[0], start_high
+    )
+    full[0], pair[1] = across(pair[0]), inward(1)
     value = narrow_forward(start_pieces[:some], near, None, genotypes, "second_forward_near")
     value = narrow_forward(start_pieces[some:], far, value, genotypes, "second_forward_far")
+    value, chunks[2] = tie((value, chunks[2]), full[0], pair[1])
+    ends[0], full[1], pair[2] = outward(full[0]), across(pair[1]), inward(2)
     value = sum_marker(value)
     kept_s = lax.dynamic_slice_in_dim(value, column * share, share, 1)
     rows = value.astype(BF16)
     parts = backward(rows, far, genotypes, unit, traits, 0, some, "second_back_far")
     sent = [swap(part, "sample", k + some) for k, part in enumerate(parts)]
+    rows, chunks[3] = tie((rows, chunks[3]), full[1], pair[2], ends[0], *parts)
+    ends[1], full[2], pair[3] = outward(full[1]), across(pair[2]), inward(3)
     parts = backward(rows, near, genotypes, unit, traits, 0, some, "second_back_near")
     back = tree([swap(part, "sample", k) if k else part for k, part in enumerate(parts)] + sent)
     back_high = lax.reduce_precision(back, 8, 7)
     back_low = (back - back_high).astype(BF16)
     back_high = back_high.astype(BF16)
+    (back_high,) = tie((back_high,), full[2], pair[3], ends[1])
+    ends[2], full[3] = outward(full[2]), across(pair[3])
     back_pieces = [swap(back_high, "sample", k) if k else back_high for k in range(samples)]
-    low = jnp.concatenate([start_low, back_low], axis=0)
-    low, *back_pieces = lax.optimization_barrier((low, *back_pieces))
+    back_pieces = tie(back_pieces, full[3], ends[2])
+    ends[3] = outward(full[3])
+
+    inner = ((me == 1) | (me == 2)).astype(jnp.int32)
+    places = jnp.concatenate([order, inner[None]])
+    total = wide_forward(
+        back_pieces, full[:2], ends[:2], places, 0, None, genotypes, columns, "third_forward_0"
+    )
+    total, low = tie((total, jnp.concatenate([start_low, back_low], axis=0)), ends[3], total)
     low_pieces = [swap(low, "sample", k) if k else low for k in range(samples)]
-
-    total = wide_forward(
-        back_pieces, probe_back[0], order, 0, None, genotypes, columns, "third_forward_0"
-    )
-    total, *low_pieces = lax.optimization_barrier((total, *low_pieces))
     value = wide_forward(
-        back_pieces, probe_back[1], order + samples, 1, total, genotypes, columns, "third_forward_1"
-    )
+        back_pieces, full[2:], ends[2:], places, 1, total, genotypes, columns, "third_forward_1"
+    )
+    (value,) = tie((value,), *low_pieces)
     last = jnp.sum(lax.all_to_all(value, "marker", 0, 0).astype(F32), axis=0)
     before = jnp.concatenate([kept_s, kept_x[traits:]], axis=0)
 
-    def own_units(*halves):
-        return jnp.concatenate(
-            [lax.dynamic_slice_in_dim(x, me * unit, unit, 1) for x in halves], axis=1
-        )
-
-    def three(d, u):
-        return jnp.stack([jnp.sum(d * d, 1), jnp.sum(d * u, 1), jnp.sum(u * u, 1)], axis=1)
-
-    probes_here = own_units(probes[:, : samples * unit], probes[:, samples * unit :])
+    def dot(x, y):
+        return jnp.sum(x * y, axis=1)
+
+    probes_here = [
+        lax.dynamic_slice_in_dim(probes, (half * samples + me) * unit, unit, 1) for half in range(2)
+    ]
+    kept_p, last_p = kept_x[traits:], last[traits:]
     norms = jnp.concatenate(
-        [three(start, back), three(probes_here, own_units(*probe_back).astype(F32))], axis=0
-    )
-    sums = jnp.concatenate([norms, three(before, last)], axis=1)
-    sums = sum_direct(sum_marker(sums), "sample")
+        [
+            jnp.stack([dot(start, start), dot(start, back), dot(back, back)], axis=1),
+            jnp.stack(
+                [sum(dot(p, p) for p in probes_here), dot(kept_p, pred_x), dot(last_p, pred_x)], axis=1
+            ),
+        ],
+        axis=0,
+    )
+    squares = jnp.stack([dot(before, before), dot(before, last), dot(last, last)], axis=1)
+    sums = sum_direct(sum_marker(jnp.concatenate([norms, squares], axis=1)), "sample")
 
     first_slope = slopes[:, 0] / markers
     second_precision = input_precision * (1.0 - first_slope) / first_slope

time: 376 us -> 379 us (level)
  starting transfers between devices: 68 us -> 92.8 us
  between operations: 14.2 us -> 1.4 us
  local copies, waits for them, and re-layouts: 17.7 us -> 6.07 us
  other arithmetic: 4.87 us -> 15.8 us
  waiting for transfers between devices: 124 us -> 119 us
    ppermute x0 -> x12, starting transfers between devices: none -> 20.3 us  [the longest x4 12 us: inward(): return add(chunks[c], lax.ppermute(chunks[c], 'sample', [(0, 1), (3, 2)]))]
    ppermute x0 -> x12, waiting for transfers between devices: none -> 11.8 us  [the longest x4 11.7 us: outward(): return lax.ppermute(x, 'sample', [(1, 0), (2, 3)])]
    all_gather x1 -> x0, waiting for transfers between devices: 9.56 us -> none  [per_device(): probe_back.append(lax.all_gather(whole, 'sample', axis=1, tiled=True))]
    ppermute x33, waiting for transfers between devices: 97.5 us -> 90.2 us  [swap(): return lax.ppermute(x, axis, [(i, i ^ bits) for i in range(n)])]
    convert_element_type x1 -> x9, other arithmetic: 0.03 us -> 6.46 us  [the longest x8 6.43 us: add(): return (x.astype(F32) + y.astype(F32)).astype(BF16)]
    dynamic_slice x3 -> x0, local copies, waits for them, and re-layouts: 5.1 us -> none  [own_units(): lax.dynamic_slice_in_dim(x, me * unit, unit, 1)]
    ppermute x33, starting transfers between devices: 59.9 us -> 64.8 us  [swap(): return lax.ppermute(x, axis, [(i, i ^ bits) for i in range(n)])]
    unnamed x28 -> x54, local copies, waits for them, and re-layouts: 7.96 us -> 4.42 us
  transfers between devices with their start and end apart: 38 -> 47, of which waited for: 23 -> 27; matrix products, arithmetic and copies ran while one was open for 3% -> 3% of each run, Pallas kernels for 21% -> 24%
where the time goes in v3:
time: 379 us
  Pallas kernels  133 us (35%)
  waiting for transfers between devices  119 us (31%)
  starting transfers between devices  92.8 us (24%)
  other arithmetic  15.8 us (4%)
  blocking collectives  9.95 us (3%)
  local copies, waits for them, and re-layouts  6.07 us (2%)
    ppermute x33, waiting for transfers between devices, swap(): return lax.ppermute(x, axis, [(i, i ^ bits) for i in range(n)])  90.2 us
    ppermute x33, starting transfers between devices, swap(): return lax.ppermute(x, axis, [(i, i ^ bits) for i in range(n)])  64.8 us
    pallas_call x4, Pallas kernels, backward(): pl.pallas_call(functools.partial(back_body, n, unit, t, base), grid_spec=...  52.2 us
    pallas_call x2, Pallas kernels, wide_forward(): pl.pallas_call(functools.partial(wide_body, n, half, len(inner), acc is n...  27.2 us
    pallas_call x2, Pallas kernels, narrow_forward(): pl.pallas_call(functools.partial(narrow_body, n, unit, acc is not None),...  25.4 us
    pallas_call x1, Pallas kernels, first_forward(): pl.pallas_call(functools.partial(first_body, markers * columns), grid_spe...  24.5 us
    ppermute x4, starting transfers between devices, inward(): return add(chunks[c], lax.ppermute(chunks[c], 'sample', [(0, 1), (3, 2)]))  12 us
    ppermute x4, waiting for transfers between devices, outward(): return lax.ppermute(x, 'sample', [(1, 0), (2, 3)])  11.7 us
  transfers between devices with their start and end apart: 47, of which 27 were waited for; matrix products, arithmetic and copies ran while one was open for 3% of the time, Pallas kernels for 24%

profile of v3, /device:TPU:0, one launch (start us, length us, event | category | flops | bytes accessed | tf_op | source)
XLA Modules:
  0.0 378.5 jit_solution(4365299623487386747)
XLA Ops:
  4.7 2.8 collective-permute-start.1
  9.2 2.0 collective-permute-done.2
  11.2 2.4 collective-permute-done.3
  14.3 3.1 copy-done
  17.4 24.5 %first_forward.1 = (bf16[8,144,256]{2,1,0:T(8,128)(2,1)}, f32[16,16384]{1,0:T(8,128)S(1)}) custom-call(s32[1]{0:T(128)} %constant.8.clone.1.off, f32[16,16384]{1,0:T(8,128)S(1)} %copy-done.2, f32[16,3]{1,0:T(8,128)S(1)} %copy.49.cols, f32[16,1]{1,0:T(8,128)S(1)} %get-tuple-element.81.slopes, f32[112,16384]{1,0:T(8,128)S(1)} %copy-done, ...), custom_call_target="tpu_custom_call" | custom-call | flops 8589934592 | bytes 67108864 | tf_op jit(solution)/shard_map/first_forward/pallas_call | solution.py:174
  41.9 3.6 all-to-all-start
  45.5 10.3 %all-to-all-done = bf16[8,144,256]{2,1,0:T(8,128)(2,1)S(1)} async-done(((bf16[8,144,256]{2,1,0:T(8,128)(2,1)}), bf16[8,144,256]{2,1,0:T(8,128)(2,1)S(1)}, u32[]{:S(2)}, u32[]{:S(2)}) %all-to-all-start) | async-done | bytes 589856 | tf_op jit(solution)/shard_map/all_to_all | solution.py:464
  56.8 9.9 %all_gather.3.rows = bf16[128,2048]{1,0:T(8,128)(2,1)S(1)} all-gather(bf16[128,256]{1,0:T(8,128)(2,1)S(1)} %pad_maximum_fusion.2), channel_id=1, replica_groups=mesh['sample'=4,'marker'=8] {'marker'}, dimensions={1}, use_global_device_ids=true | all-gather | bytes 589824 | tf_op jit(solution)/shard_map/all_gather | solution.py:469
  66.7 12.8 %first_back_0.1 = (f32[16,2048]{1,0:T(8,128)S(1)}, f32[16,2048]{1,0:T(8,128)S(1)}, f32[16,2048]{1,0:T(8,128)S(1)}, f32[16,2048]{1,0:T(8,128)S(1)}, bf16[112,4096...) custom-call(s32[4]{0:T(128)S(1)} %iota_xor_fusion.off, bf16[128,2048]{1,0:T(8,128)(2,1)S(1)} %all_gather.3.rows, ...), custom_call_target="tpu_custom_call" | custom-call | flops 4294967296 | bytes 33554432 | tf_op jit(solution)/shard_map/first_back_0/pallas_call | solution.py:377
  79.5 3.5 collective-permute-start.13
  83.1 3.0 collective-permute-start.5
  87.5 13.6 %first_back_1.1 = (f32[16,2048]{1,0:T(8,128)S(1)}, f32[16,2048]{1,0:T(8,128)S(1)}, f32[16,2048]{1,0:T(8,128)S(1)}, f32[16,2048]{1,0:T(8,128)S(1)}, bf16[112,4096...) custom-call(s32[4]{0:T(128)S(1)} %broadcast_add_fusion.off, bf16[128,2048]{1,0:T(8,128)(2,1)S(1)} %all_gather.3.rows, ...), custom_call_target="tpu_custom_call" | custom-call | flops 4294967296 | bytes 33554432 | tf_op jit(solution)/shard_map/first_back_1/pallas_call | solution.py:377
  101.1 5.3 %collective-permute-done.4 = f32[16,2048]{1,0:T(8,128)S(1)} collective-permute-done((f32[16,2048]{1,0:T(8,128)S(1)}, f32[16,2048]{1,0:T(8,128)S(1)}, u32[]{:S(2)}, u32[]{:S(2)}) %collective-permute-start.4) | collective-permute-done | bytes 131104 | tf_op jit(solution)/shard_map/ppermute | solution.py:26
  106.5 3.5 collective-permute-start.8
  111.8 3.3 collective-permute-done.6
  115.1 2.8 collective-permute-done.8
  117.9 5.1 %collective-permute-done.9 = f32[16,2048]{1,0:T(8,128)S(1)} collective-permute-done((f32[16,2048]{1,0:T(8,128)S(1)}, f32[16,2048]{1,0:T(8,128)S(1)}, u32[]{:S(2)}, u32[]{:S(2)}) %collective-permute-start.9) | collective-permute-done | bytes 131104 | tf_op jit(solution)/shard_map/ppermute | solution.py:26
  123.8 3.2 collective-permute-start.12
  128.2 2.5 collective-permute-done.12.refs_1_
  130.7 4.6 %collective-permute-start.15 = (bf16[112,4096]{1,0:T(8,128)(2,1)S(1)}, bf16[112,4096]{1,0:T(8,128)(2,1)}, u32[]{:S(2)}, u32[]{:S(2)}) collective-permute-start(bf16[112,4096]{1,0:T(8,128)(2,1)S(1)} %get-tuple-element.51), channel_id=1, source_target_pairs={{0,8},{24,16},{1,9},{25,17},{2,10},{26,18},{3,11},{27,19},{4,12},{... | collective-permute-start | bytes 2752520 | tf_op jit(solution)/shard_map/ppermute | solution.py:483
  137.9 12.7 %second_forward_near.1.refs_2_ = f32[16,2048]{1,0:T(8,128)S(1)} custom-call(s32[4]{0:T(128)S(1)} %reshape.27.off, bf16[16,4096]{1,0:T(8,128)(2,1)S(1)} %get-tuple-element.48.refs_0_, bf16[16,4096]{1,0:T(8,128)(2,1)S(1)} %collective-permute-done.12.refs_1_, bf16[2048,16384]{1,0:T(8,128)(2,1)} %refs_9_.1), custom_call_target="tpu_custom_call" | custom-call | flops 536870912 | bytes 33554432 | tf_op jit(solution)/shard_map/second_forward_near/pallas_call | solution.py:222
  150.6 6.9 %collective-permute-done.10.refs_0_.refs_2_ = bf16[16,4096]{1,0:T(8,128)(2,1)S(1)} collective-permute-done((bf16[16,4096]{1,0:T(8,128)(2,1)S(1)}, bf16[16,4096]{1,0:T(8,128)(2,1)S(1)}, u32[]{:S(2)}, u32[]{:S(2)}) %collective-permute-start.10) | collective-permute-done | bytes 131104 | tf_op jit(solution)/shard_map/ppermute | solution.py:26
  157.5 3.3 collective-permute-done.11.refs_1_.refs_3_
  160.8 12.7 %second_forward_far.1 = f32[16,2048]{1,0:T(8,128)S(1)} custom-call(s32[4]{0:T(128)S(1)} %reshape.28.off, bf16[16,4096]{1,0:T(8,128)(2,1)S(1)} %collective-permute-done.10.refs_0_.refs_2_, bf16[16,4096]{1,0:T(8,128)(2,1)S(1)} %collective-permute-done.11.refs_1_.refs_3_, f32[16,2048]{1,0:T(8,128)S(1)} %second_forward_near.1.refs_2_, bf16[2048,16384]{1,0:T(8,128)(2,1)} %refs_9_.1), custom_call_target="tpu_custom_call" | custom-call | flops 536870912 | bytes 33554432 | tf_op jit(solution)/shard_map/second_forward_far/pallas_call | solution.py:222
  185.6 2.2 collective-permute-done.18
  188.5 13.0 %second_back_far.1 = (f32[16,4096]{1,0:T(8,128)}, f32[16,4096]{1,0:T(8,128)}) custom-call(s32[4]{0:T(128)S(1)} %reshape.28.off, bf16[16,2048]{1,0:T(8,128)(2,1)S(1)} %get-tuple-element.57.rows, bf16[2048,16384]{1,0:T(8,128)(2,1)} %refs_9_.1), custom_call_target="tpu_custom_call" | custom-call | flops 536870912 | bytes 33554432 | tf_op jit(solution)/shard_map/second_back_far/pallas_call | solution.py:377
  202.8 4.4 %collective-permute-done.22.refs_6_ = bf16[112,4096]{1,0:T(8,128)(2,1)S(1)} collective-permute-done((bf16[112,4096]{1,0:T(8,128)(2,1)S(1)}, bf16[112,4096]{1,0:T(8,128)(2,1)S(1)}, u32[]{:S(2)}, u32[]{:S(2)}) %collective-permute-start.22) | collective-permute-done | bytes 917536 | tf_op jit(solution)/shard_map/ppermute | solution.py:489
  207.2 2.5 collective-permute-start.27
  209.7 2.5 collective-permute-start.25
  212.2 12.9 %second_back_near.1 = (f32[16,4096]{1,0:T(8,128)S(1)}, f32[16,4096]{1,0:T(8,128)}) custom-call(s32[4]{0:T(128)S(1)} %reshape.27.off, bf16[16,2048]{1,0:T(8,128)(2,1)S(1)} %get-tuple-element.57.rows, bf16[2048,16384]{1,0:T(8,128)(2,1)} %refs_9_.1), custom_call_target="tpu_custom_call" | custom-call | flops 536870912 | bytes 33554432 | tf_op jit(solution)/shard_map/second_back_near/pallas_call | solution.py:377
  227.0 8.6 %collective-permute-done.24 = f32[16,4096]{1,0:T(8,128)} collective-permute-done((f32[16,4096]{1,0:T(8,128)}, f32[16,4096]{1,0:T(8,128)}, u32[]{:S(2)}, u32[]{:S(2)}) %collective-permute-start.24) | collective-permute-done | bytes 262176 | tf_op jit(solution)/shard_map/ppermute | solution.py:26
  236.9 7.3 %collective-permute-done.25 = f32[16,4096]{1,0:T(8,128)} collective-permute-done((f32[16,4096]{1,0:T(8,128)}, f32[16,4096]{1,0:T(8,128)}, u32[]{:S(2)}, u32[]{:S(2)}) %collective-permute-start.25) | collective-permute-done | bytes 262176 | tf_op jit(solution)/shard_map/ppermute | solution.py:26
  244.2 2.0 multiply_reduce_fusion.4
  251.9 7.3 %collective-permute-done.28.refs_7_ = bf16[112,4096]{1,0:T(8,128)(2,1)S(1)} collective-permute-done((bf16[112,4096]{1,0:T(8,128)(2,1)S(1)}, bf16[112,4096]{1,0:T(8,128)(2,1)S(1)}, u32[]{:S(2)}, u32[]{:S(2)}) %collective-permute-start.28) | collective-permute-done | bytes 917536 | tf_op jit(solution)/shard_map/ppermute | solution.py:489
  259.2 21.4 %collective-permute-start.29 = (bf16[16,4096]{1,0:T(8,128)(2,1)S(1)}, bf16[16,4096]{1,0:T(8,128)(2,1)S(1)}, u32[]{:S(2)}, u32[]{:S(2)}) collective-permute-start(bf16[16,4096]{1,0:T(8,128)(2,1)S(1)} %get-tuple-element.62.refs_0_.refs_4_), channel_id=1, source_target_pairs={{0,8},{8,0},{16,24},{24,16},{1,9},{9,1},{17,25},{25,17},{2,10},{10... | collective-permute-start | bytes 393224 | tf_op jit(solution)/shard_map/ppermute | solution.py:26
  280.7 2.4 collective-permute-start.31
  283.1 24.6 %collective-permute-done.29.refs_1_.refs_5_ = bf16[16,4096]{1,0:T(8,128)(2,1)S(1)} collective-permute-done((bf16[16,4096]{1,0:T(8,128)(2,1)S(1)}, bf16[16,4096]{1,0:T(8,128)(2,1)S(1)}, u32[]{:S(2)}, u32[]{:S(2)}) %collective-permute-start.29) | collective-permute-done | bytes 131104 | tf_op jit(solution)/shard_map/ppermute | solution.py:26
  307.8 13.3 %third_forward_0.1.refs_8_ = f32[2048,128]{1,0:T(8,128)S(1)} custom-call(s32[5]{0:T(128)S(1)} %pad_add_fusion.2.off, bf16[16,4096]{1,0:T(8,128)(2,1)S(1)} %get-tuple-element.62.refs_0_.refs_4_, bf16[16,4096]{1,0:T(8,128)(2,1)S(1)} %collective-permute-done.29.refs_1_.refs_5_, bf16[16,4096]{1,0:T(8,128)(2,1)S(1)} %collective-permute-done.30.refs_2_.refs_6_, ...), custom_call_target="tpu_custom_call" | custom-call | flops 4294967296 | bytes 33554432 | tf_op jit(solution)/shard_map/third_forward_0/pallas_call | solution.py:288
  323.2 2.4 collective-permute-start.37
  325.6 13.9 %third_forward_1.1 = bf16[8,128,256]{2,1,0:T(8,128)(2,1)} custom-call(s32[5]{0:T(128)S(1)} %pad_add_fusion.2.off, bf16[16,4096]{1,0:T(8,128)(2,1)S(1)} %get-tuple-element.62.refs_0_.refs_4_, bf16[16,4096]{1,0:T(8,128)(2,1)S(1)} %collective-permute-done.29.refs_1_.refs_5_, bf16[16,4096]{1,0:T(8,128)(2,1)S(1)} %collective-permute-done.30.refs_2_.refs_6_, ...), custom_call_target="tpu_custom_call" | custom-call | flops 4294967296 | bytes 33554432 | tf_op jit(solution)/shard_map/third_forward_1/pallas_call | solution.py:288
  339.5 2.1 collective-permute-done.36.refs_10_
  341.7 4.1 %all-to-all-start.1 = ((bf16[8,128,256]{2,1,0:T(8,128)(2,1)}), bf16[8,128,256]{2,1,0:T(8,128)(2,1)}, u32[]{:S(2)}, u32[]{:S(2)}) async-start(bf16[8,128,256]{2,1,0:T(8,128)(2,1)} %third_forward_1.1), calls=%async_computation.1 | async-start | bytes 1048576 | tf_op jit(solution)/shard_map/all_to_all | solution.py:540
  348.5 7.1 %all-to-all-done.1 = bf16[8,128,256]{2,1,0:T(8,128)(2,1)} async-done(((bf16[8,128,256]{2,1,0:T(8,128)(2,1)}), bf16[8,128,256]{2,1,0:T(8,128)(2,1)}, u32[]{:S(2)}, u32[]{:S(2)}) %all-to-all-start.1) | async-done | bytes 524320 | tf_op jit(solution)/shard_map/all_to_all | solution.py:540
  359.7 2.4 collective-permute-start.41
  364.9 4.0 %collective-permute-start.42 = (f32[128,6]{1,0:T(8,128)S(1)}, f32[128,6]{1,0:T(8,128)S(1)}, u32[]{:S(2)}, u32[]{:S(2)}) collective-permute-start(f32[128,6]{1,0:T(8,128)S(1)} %add_add_fusion.5), channel_id=1, source_target_pairs={{0,8},{8,0},{16,24},{24,16},{1,9},{9,1},{17,25},{25,17},{2,10},{10... | collective-permute-start | bytes 9224 | tf_op jit(solution)/shard_map/ppermute | solution.py:26
  368.9 2.4 collective-permute-start.44
  371.5 3.8 %collective-permute-done.43 = f32[128,6]{1,0:T(8,128)S(1)} collective-permute-done((f32[128,6]{1,0:T(8,128)S(1)}, f32[128,6]{1,0:T(8,128)S(1)}, u32[]{:S(2)}, u32[]{:S(2)}) %collective-permute-start.43) | collective-permute-done | bytes 3104 | tf_op jit(solution)/shard_map/ppermute | solution.py:26
  375.4 3.2 finish.1
  (167 shorter events, 49.9 us)
Async XLA Ops:
  3.4 1.3 collective-permute-start
  4.7 4.5 %collective-permute-start.1 = (f32[16,1]{1,0:T(8,128)S(1)}, f32[16,1]{1,0:T(8,128)S(1)}, u32[]{:S(2)}, u32[]{:S(2)}) collective-permute-start(f32[16,1]{1,0:T(8,128)S(1)} %add.135), channel_id=1, source_target_pairs={{0,2},{1,3},{2,0},{3,1},{4,6},{5,7},{6,4},{7,5},{8,10},{9,11},{10,... | collective-permute-start | bytes 200 | tf_op jit(solution)/shard_map/ppermute | solution.py:26
  7.5 3.7 collective-permute-start.2
  9.0 4.5 %collective-permute-start.3 = (f32[16,1]{1,0:T(8,128)S(1)}, f32[16,1]{1,0:T(8,128)S(1)}, u32[]{:S(2)}, u32[]{:S(2)}) collective-permute-start(f32[16,1]{1,0:T(8,128)S(1)} %add.135), channel_id=1, source_target_pairs={{0,6},{1,7},{2,4},{3,5},{4,2},{5,3},{6,0},{7,1},{8,14},{9,15},{10,... | collective-permute-start | bytes 200 | tf_op jit(solution)/shard_map/ppermute | solution.py:26
  41.9 13.9 %all-to-all-start = ((bf16[8,144,256]{2,1,0:T(8,128)(2,1)}), bf16[8,144,256]{2,1,0:T(8,128)(2,1)S(1)}, u32[]{:S(2)}, u32[]{:S(2)}) async-start(bf16[8,144,256]{2,1,0:T(8,128)(2,1)} %get-tuple-element.36), calls=%async_computation | async-start | bytes 1179648 | tf_op jit(solution)/shard_map/all_to_all | solution.py:464
  79.5 47.5 %collective-permute-start.13 = (bf16[112,4096]{1,0:T(8,128)(2,1)S(1)}, bf16[112,4096]{1,0:T(8,128)(2,1)S(1)}, u32[]{:S(2)}, u32[]{:S(2)}) collective-permute-start(bf16[112,4096]{1,0:T(8,128)(2,1)S(1)} %get-tuple-element.41), channel_id=1, source_target_pairs={{0,8},{24,16},{1,9},{25,17},{2,10},{26,18},{3,11},{27,19},{4,12},{... | collective-permute-start | bytes 2752520 | tf_op jit(solution)/shard_map/ppermute | solution.py:483
  83.0 23.4 %collective-permute-start.4 = (f32[16,2048]{1,0:T(8,128)S(1)}, f32[16,2048]{1,0:T(8,128)S(1)}, u32[]{:S(2)}, u32[]{:S(2)}) collective-permute-start(f32[16,2048]{1,0:T(8,128)S(1)} %get-tuple-element.38), channel_id=1, source_target_pairs={{0,8},{8,0},{16,24},{24,16},{1,9},{9,1},{17,25},{25,17},{2,10},{10... | collective-permute-start | bytes 393224 | tf_op jit(solution)/shard_map/ppermute | solution.py:26
  83.1 26.8 %collective-permute-start.5 = (f32[16,2048]{1,0:T(8,128)S(1)}, f32[16,2048]{1,0:T(8,128)S(1)}, u32[]{:S(2)}, u32[]{:S(2)}) collective-permute-start(f32[16,2048]{1,0:T(8,128)S(1)} %get-tuple-element.39), channel_id=1, source_target_pairs={{0,16},{8,24},{16,0},{24,8},{1,17},{9,25},{17,1},{25,9},{2,18},{10... | collective-permute-start | bytes 393224 | tf_op jit(solution)/shard_map/ppermute | solution.py:26
  86.1 28.9 %collective-permute-start.6 = (f32[16,2048]{1,0:T(8,128)S(1)}, f32[16,2048]{1,0:T(8,128)S(1)}, u32[]{:S(2)}, u32[]{:S(2)}) collective-permute-start(f32[16,2048]{1,0:T(8,128)S(1)} %get-tuple-element.40), channel_id=1, source_target_pairs={{0,24},{8,16},{16,8},{24,0},{1,25},{9,17},{17,9},{25,1},{2,26},{10... | collective-permute-start | bytes 393224 | tf_op jit(solution)/shard_map/ppermute | solution.py:26
  101.1 14.0 %collective-permute-start.7 = (f32[16,2048]{1,0:T(8,128)S(1)}, f32[16,2048]{1,0:T(8,128)S(1)}, u32[]{:S(2)}, u32[]{:S(2)}) collective-permute-start(f32[16,2048]{1,0:T(8,128)S(1)} %get-tuple-element.44), channel_id=1, source_target_pairs={{0,8},{8,0},{16,24},{24,16},{1,9},{9,1},{17,25},{25,17},{2,10},{10... | collective-permute-start | bytes 393224 | tf_op jit(solution)/shard_map/ppermute | solution.py:26
  106.5 11.4 %collective-permute-start.8 = (f32[16,2048]{1,0:T(8,128)S(1)}, f32[16,2048]{1,0:T(8,128)S(1)}, u32[]{:S(2)}, u32[]{:S(2)}) collective-permute-start(f32[16,2048]{1,0:T(8,128)S(1)} %get-tuple-element.45), channel_id=1, source_target_pairs={{0,16},{8,24},{16,0},{24,8},{1,17},{9,25},{17,1},{25,9},{2,18},{10... | collective-permute-start | bytes 393224 | tf_op jit(solution)/shard_map/ppermute | solution.py:26
  109.9 13.1 %collective-permute-start.9 = (f32[16,2048]{1,0:T(8,128)S(1)}, f32[16,2048]{1,0:T(8,128)S(1)}, u32[]{:S(2)}, u32[]{:S(2)}) collective-permute-start(f32[16,2048]{1,0:T(8,128)S(1)} %get-tuple-element.46), channel_id=1, source_target_pairs={{0,24},{8,16},{16,8},{24,0},{1,25},{9,17},{17,9},{25,1},{2,26},{10... | collective-permute-start | bytes 393224 | tf_op jit(solution)/shard_map/ppermute | solution.py:26
  123.8 6.9 %collective-permute-start.12 = (bf16[16,4096]{1,0:T(8,128)(2,1)S(1)}, bf16[16,4096]{1,0:T(8,128)(2,1)S(1)}, u32[]{:S(2)}, u32[]{:S(2)}) collective-permute-start(bf16[16,4096]{1,0:T(8,128)(2,1)S(1)} %get-tuple-element.48.refs_0_), channel_id=1, source_target_pairs={{0,8},{8,0},{16,24},{24,16},{1,9},{9,1},{17,25},{25,17},{2,10},{10... | collective-permute-start | bytes 393224 | tf_op jit(solution)/shard_map/ppermute | solution.py:26
  130.7 42.8 %collective-permute-start.15 = (bf16[112,4096]{1,0:T(8,128)(2,1)S(1)}, bf16[112,4096]{1,0:T(8,128)(2,1)}, u32[]{:S(2)}, u32[]{:S(2)}) collective-permute-start(bf16[112,4096]{1,0:T(8,128)(2,1)S(1)} %get-tuple-element.51), channel_id=1, source_target_pairs={{0,8},{24,16},{1,9},{25,17},{2,10},{26,18},{3,11},{27,19},{4,12},{... | collective-permute-start | bytes 2752520 | tf_op jit(solution)/shard_map/ppermute | solution.py:483
  135.4 22.1 %collective-permute-start.10 = (bf16[16,4096]{1,0:T(8,128)(2,1)S(1)}, bf16[16,4096]{1,0:T(8,128)(2,1)S(1)}, u32[]{:S(2)}, u32[]{:S(2)}) collective-permute-start(bf16[16,4096]{1,0:T(8,128)(2,1)S(1)} %get-tuple-element.48.refs_0_), channel_id=1, source_target_pairs={{0,16},{8,24},{16,0},{24,8},{1,17},{9,25},{17,1},{25,9},{2,18},{10... | collective-permute-start | bytes 393224 | tf_op jit(solution)/shard_map/ppermute | solution.py:26
  135.4 25.4 %collective-permute-start.11 = (bf16[16,4096]{1,0:T(8,128)(2,1)S(1)}, bf16[16,4096]{1,0:T(8,128)(2,1)S(1)}, u32[]{:S(2)}, u32[]{:S(2)}) collective-permute-start(bf16[16,4096]{1,0:T(8,128)(2,1)S(1)} %get-tuple-element.48.refs_0_), channel_id=1, source_target_pairs={{0,24},{8,16},{16,8},{24,0},{1,25},{9,17},{17,9},{25,1},{2,26},{10... | collective-permute-start | bytes 393224 | tf_op jit(solution)/shard_map/ppermute | solution.py:26
  137.2 37.9 %collective-permute-start.14 = (bf16[112,4096]{1,0:T(8,128)(2,1)}, bf16[112,4096]{1,0:T(8,128)(2,1)S(1)}, u32[]{:S(2)}, u32[]{:S(2)}) collective-permute-start(bf16[112,4096]{1,0:T(8,128)(2,1)} %add_convert_fusion.7), channel_id=1, source_target_pairs={{8,16},{16,8},{9,17},{17,9},{10,18},{18,10},{11,19},{19,11},{12,20... | collective-permute-start | bytes 2752520 | tf_op jit(solution)/shard_map/ppermute | solution.py:486
  175.4 26.1 %collective-permute-start.21 = (bf16[112,4096]{1,0:T(8,128)(2,1)S(1)}, bf16[112,4096]{1,0:T(8,128)(2,1)S(1)}, u32[]{:S(2)}, u32[]{:S(2)}) collective-permute-start(bf16[112,4096]{1,0:T(8,128)(2,1)S(1)} %get-tuple-element.54), channel_id=1, source_target_pairs={{0,8},{24,16},{1,9},{25,17},{2,10},{26,18},{3,11},{27,19},{4,12},{... | collective-permute-start | bytes 2752520 | tf_op jit(solution)/shard_map/ppermute | solution.py:483
  176.7 1.4 collective-permute-start.16
  178.2 6.0 %collective-permute-start.17 = (f32[16,2048]{1,0:T(8,128)S(1)}, f32[16,2048]{1,0:T(8,128)S(1)}, u32[]{:S(2)}, u32[]{:S(2)}) collective-permute-start(f32[16,2048]{1,0:T(8,128)S(1)} %add.152), channel_id=1, source_target_pairs={{0,2},{1,3},{2,0},{3,1},{4,6},{5,7},{6,4},{7,5},{8,10},{9,11},{10,... | collective-permute-start | bytes 393224 | tf_op jit(solution)/shard_map/ppermute | solution.py:26
  179.7 8.1 %collective-permute-start.18 = (f32[16,2048]{1,0:T(8,128)S(1)}, f32[16,2048]{1,0:T(8,128)S(1)}, u32[]{:S(2)}, u32[]{:S(2)}) collective-permute-start(f32[16,2048]{1,0:T(8,128)S(1)} %add.152), channel_id=1, source_target_pairs={{0,4},{1,5},{2,6},{3,7},{4,0},{5,1},{6,2},{7,3},{8,12},{9,13},{10,... | collective-permute-start | bytes 393224 | tf_op jit(solution)/shard_map/ppermute | solution.py:26
  180.3 7.5 %collective-permute-start.19 = (f32[16,2048]{1,0:T(8,128)S(1)}, f32[16,2048]{1,0:T(8,128)S(1)}, u32[]{:S(2)}, u32[]{:S(2)}) collective-permute-start(f32[16,2048]{1,0:T(8,128)S(1)} %add.152), channel_id=1, source_target_pairs={{0,6},{1,7},{2,4},{3,5},{4,2},{5,3},{6,0},{7,1},{8,14},{9,15},{10,... | collective-permute-start | bytes 393224 | tf_op jit(solution)/shard_map/ppermute | solution.py:26
  181.7 20.9 %collective-permute-start.20 = (bf16[112,4096]{1,0:T(8,128)(2,1)S(1)}, bf16[112,4096]{1,0:T(8,128)(2,1)S(1)}, u32[]{:S(2)}, u32[]{:S(2)}) collective-permute-start(bf16[112,4096]{1,0:T(8,128)(2,1)S(1)} %add_convert_fusion.5), channel_id=1, source_target_pairs={{8,16},{16,8},{9,17},{17,9},{10,18},{18,10},{11,19},{19,11},{12,20... | collective-permute-start | bytes 2752520 | tf_op jit(solution)/shard_map/ppermute | solution.py:486
  184.1 23.1 %collective-permute-start.22 = (bf16[112,4096]{1,0:T(8,128)(2,1)S(1)}, bf16[112,4096]{1,0:T(8,128)(2,1)S(1)}, u32[]{:S(2)}, u32[]{:S(2)}) collective-permute-start(bf16[112,4096]{1,0:T(8,128)(2,1)S(1)} %add_convert_fusion.6.refs_4_), channel_id=1, source_target_pairs={{8,0},{16,24},{9,1},{17,25},{10,2},{18,26},{11,3},{19,27},{12,4},{... | collective-permute-start | bytes 2752520 | tf_op jit(solution)/shard_map/ppermute | solution.py:489
  207.2 38.9 %collective-permute-start.27 = (bf16[112,4096]{1,0:T(8,128)(2,1)}, bf16[112,4096]{1,0:T(8,128)(2,1)}, u32[]{:S(2)}, u32[]{:S(2)}) collective-permute-start(bf16[112,4096]{1,0:T(8,128)(2,1)} %get-tuple-element.60), channel_id=1, source_target_pairs={{0,8},{24,16},{1,9},{25,17},{2,10},{26,18},{3,11},{27,19},{4,12},{... | collective-permute-start | bytes 2752520 | tf_op jit(solution)/shard_map/ppermute | solution.py:483
  209.7 25.8 %collective-permute-start.24 = (f32[16,4096]{1,0:T(8,128)}, f32[16,4096]{1,0:T(8,128)}, u32[]{:S(2)}, u32[]{:S(2)}) collective-permute-start(f32[16,4096]{1,0:T(8,128)} %get-tuple-element.55), channel_id=1, source_target_pairs={{0,16},{8,24},{16,0},{24,8},{1,17},{9,25},{17,1},{25,9},{2,18},{10... | collective-permute-start | bytes 786440 | tf_op jit(solution)/shard_map/ppermute | solution.py:26
  209.7 34.4 %collective-permute-start.25 = (f32[16,4096]{1,0:T(8,128)}, f32[16,4096]{1,0:T(8,128)}, u32[]{:S(2)}, u32[]{:S(2)}) collective-permute-start(f32[16,4096]{1,0:T(8,128)} %get-tuple-element.56), channel_id=1, source_target_pairs={{0,24},{8,16},{16,8},{24,0},{1,25},{9,17},{17,9},{25,1},{2,26},{10... | collective-permute-start | bytes 786440 | tf_op jit(solution)/shard_map/ppermute | solution.py:26
  225.1 19.1 %collective-permute-start.23 = (f32[16,4096]{1,0:T(8,128)}, f32[16,4096]{1,0:T(8,128)}, u32[]{:S(2)}, u32[]{:S(2)}) collective-permute-start(f32[16,4096]{1,0:T(8,128)} %get-tuple-element.59), channel_id=1, source_target_pairs={{0,8},{8,0},{16,24},{24,16},{1,9},{9,1},{17,25},{25,17},{2,10},{10... | collective-permute-start | bytes 786440 | tf_op jit(solution)/shard_map/ppermute | solution.py:26
  226.3 22.4 %collective-permute-start.26 = (bf16[112,4096]{1,0:T(8,128)(2,1)}, bf16[112,4096]{1,0:T(8,128)(2,1)S(1)}, u32[]{:S(2)}, u32[]{:S(2)}) collective-permute-start(bf16[112,4096]{1,0:T(8,128)(2,1)} %add_convert_fusion.3), channel_id=1, source_target_pairs={{8,16},{16,8},{9,17},{17,9},{10,18},{18,10},{11,19},{19,11},{12,20... | collective-permute-start | bytes 2752520 | tf_op jit(solution)/shard_map/ppermute | solution.py:486
  235.6 23.6 %collective-permute-start.28 = (bf16[112,4096]{1,0:T(8,128)(2,1)S(1)}, bf16[112,4096]{1,0:T(8,128)(2,1)S(1)}, u32[]{:S(2)}, u32[]{:S(2)}) collective-permute-start(bf16[112,4096]{1,0:T(8,128)(2,1)S(1)} %add_convert_fusion.4.refs_5_), channel_id=1, source_target_pairs={{8,0},{16,24},{9,1},{17,25},{10,2},{18,26},{11,3},{19,27},{12,4},{... | collective-permute-start | bytes 2752520 | tf_op jit(solution)/shard_map/ppermute | solution.py:489
  247.9 2.4 collective-permute-start.32
  248.9 58.9 %copy-start.6 = (bf16[112,4096]{1,0:T(8,128)(2,1)S(1)}, bf16[112,4096]{1,0:T(8,128)(2,1)}, u32[]{:S(2)}) copy-start(bf16[112,4096]{1,0:T(8,128)(2,1)} %copy-done.5) | copy-start | bytes 2752516
  248.9 58.9 %collective-permute-start.33 = (bf16[112,4096]{1,0:T(8,128)(2,1)S(1)}, bf16[112,4096]{1,0:T(8,128)(2,1)S(1)}, u32[]{:S(2)}, u32[]{:S(2)}) collective-permute-start(bf16[112,4096]{1,0:T(8,128)(2,1)S(1)} %add_convert_fusion.2.refs_4_), channel_id=1, source_target_pairs={{8,0},{16,24},{9,1},{17,25},{10,2},{18,26},{11,3},{19,27},{12,4},{... | collective-permute-start | bytes 2752520 | tf_op jit(solution)/shard_map/ppermute | solution.py:489
  250.6 70.5 %collective-permute-start.34 = (bf16[112,4096]{1,0:T(8,128)(2,1)S(1)}, bf16[112,4096]{1,0:T(8,128)(2,1)S(1)}, u32[]{:S(2)}, u32[]{:S(2)}) collective-permute-start(bf16[112,4096]{1,0:T(8,128)(2,1)S(1)} %add_convert_fusion.refs_5_), channel_id=1, source_target_pairs={{8,0},{16,24},{9,1},{17,25},{10,2},{18,26},{11,3},{19,27},{12,4},{... | collective-permute-start | bytes 2752520 | tf_op jit(solution)/shard_map/ppermute | solution.py:489
  259.2 48.6 %collective-permute-start.29 = (bf16[16,4096]{1,0:T(8,128)(2,1)S(1)}, bf16[16,4096]{1,0:T(8,128)(2,1)S(1)}, u32[]{:S(2)}, u32[]{:S(2)}) collective-permute-start(bf16[16,4096]{1,0:T(8,128)(2,1)S(1)} %get-tuple-element.62.refs_0_.refs_4_), channel_id=1, source_target_pairs={{0,8},{8,0},{16,24},{24,16},{1,9},{9,1},{17,25},{25,17},{2,10},{10... | collective-permute-start | bytes 393224 | tf_op jit(solution)/shard_map/ppermute | solution.py:26
  280.7 27.1 %collective-permute-start.30 = (bf16[16,4096]{1,0:T(8,128)(2,1)S(1)}, bf16[16,4096]{1,0:T(8,128)(2,1)S(1)}, u32[]{:S(2)}, u32[]{:S(2)}) collective-permute-start(bf16[16,4096]{1,0:T(8,128)(2,1)S(1)} %get-tuple-element.62.refs_0_.refs_4_), channel_id=1, source_target_pairs={{0,16},{8,24},{16,0},{24,8},{1,17},{9,25},{17,1},{25,9},{2,18},{10... | collective-permute-start | bytes 393224 | tf_op jit(solution)/shard_map/ppermute | solution.py:26
  280.7 27.1 %collective-permute-start.31 = (bf16[16,4096]{1,0:T(8,128)(2,1)S(1)}, bf16[16,4096]{1,0:T(8,128)(2,1)S(1)}, u32[]{:S(2)}, u32[]{:S(2)}) collective-permute-start(bf16[16,4096]{1,0:T(8,128)(2,1)S(1)} %get-tuple-element.62.refs_0_.refs_4_), channel_id=1, source_target_pairs={{0,24},{8,16},{16,8},{24,0},{1,25},{9,17},{17,9},{25,1},{2,26},{10... | collective-permute-start | bytes 393224 | tf_op jit(solution)/shard_map/ppermute | solution.py:26
  321.1 18.4 %collective-permute-start.35 = (bf16[32,4096]{1,0:T(8,128)(2,1)S(1)}, bf16[32,4096]{1,0:T(8,128)(2,1)S(1)}, u32[]{:S(2)}, u32[]{:S(2)}) collective-permute-start(bf16[32,4096]{1,0:T(8,128)(2,1)S(1)} %pad_maximum_fusion.refs_8_), channel_id=1, source_target_pairs={{0,8},{8,0},{16,24},{24,16},{1,9},{9,1},{17,25},{25,17},{2,10},{10... | collective-permute-start | bytes 786440 | tf_op jit(solution)/shard_map/ppermute | solution.py:26
  321.2 20.5 %collective-permute-start.36 = (bf16[32,4096]{1,0:T(8,128)(2,1)S(1)}, bf16[32,4096]{1,0:T(8,128)(2,1)S(1)}, u32[]{:S(2)}, u32[]{:S(2)}) collective-permute-start(bf16[32,4096]{1,0:T(8,128)(2,1)S(1)} %pad_maximum_fusion.refs_8_), channel_id=1, source_target_pairs={{0,16},{8,24},{16,0},{24,8},{1,17},{9,25},{17,1},{25,9},{2,18},{10... | collective-permute-start | bytes 786440 | tf_op jit(solution)/shard_map/ppermute | solution.py:26
  323.2 18.5 %collective-permute-start.37 = (bf16[32,4096]{1,0:T(8,128)(2,1)S(1)}, bf16[32,4096]{1,0:T(8,128)(2,1)S(1)}, u32[]{:S(2)}, u32[]{:S(2)}) collective-permute-start(bf16[32,4096]{1,0:T(8,128)(2,1)S(1)} %pad_maximum_fusion.refs_8_), channel_id=1, source_target_pairs={{0,24},{8,16},{16,8},{24,0},{1,25},{9,17},{17,9},{25,1},{2,26},{10... | collective-permute-start | bytes 786440 | tf_op jit(solution)/shard_map/ppermute | solution.py:26
  341.7 13.9 %all-to-all-start.1 = ((bf16[8,128,256]{2,1,0:T(8,128)(2,1)}), bf16[8,128,256]{2,1,0:T(8,128)(2,1)}, u32[]{:S(2)}, u32[]{:S(2)}) async-start(bf16[8,128,256]{2,1,0:T(8,128)(2,1)} %third_forward_1.1), calls=%async_computation.1 | async-start | bytes 1048576 | tf_op jit(solution)/shard_map/all_to_all | solution.py:540
  357.2 1.3 collective-permute-start.38
  358.5 4.4 %collective-permute-start.39 = (f32[128,6]{1,0:T(8,128)S(1)}, f32[128,6]{1,0:T(8,128)S(1)}, u32[]{:S(2)}, u32[]{:S(2)}) collective-permute-start(f32[128,6]{1,0:T(8,128)S(1)} %add.169), channel_id=1, source_target_pairs={{0,2},{1,3},{2,0},{3,1},{4,6},{5,7},{6,4},{7,5},{8,10},{9,11},{10,... | collective-permute-start | bytes 9224 | tf_op jit(solution)/shard_map/ppermute | solution.py:26
  359.1 5.0 %collective-permute-start.40 = (f32[128,6]{1,0:T(8,128)S(1)}, f32[128,6]{1,0:T(8,128)S(1)}, u32[]{:S(2)}, u32[]{:S(2)}) collective-permute-start(f32[128,6]{1,0:T(8,128)S(1)} %add.169), channel_id=1, source_target_pairs={{0,4},{1,5},{2,6},{3,7},{4,0},{5,1},{6,2},{7,3},{8,12},{9,13},{10,... | collective-permute-start | bytes 9224 | tf_op jit(solution)/shard_map/ppermute | solution.py:26
  359.7 5.2 %collective-permute-start.41 = (f32[128,6]{1,0:T(8,128)S(1)}, f32[128,6]{1,0:T(8,128)S(1)}, u32[]{:S(2)}, u32[]{:S(2)}) collective-permute-start(f32[128,6]{1,0:T(8,128)S(1)} %add.169), channel_id=1, source_target_pairs={{0,6},{1,7},{2,4},{3,5},{4,2},{5,3},{6,0},{7,1},{8,14},{9,15},{10,... | collective-permute-start | bytes 9224 | tf_op jit(solution)/shard_map/ppermute | solution.py:26
  364.9 6.6 %collective-permute-start.42 = (f32[128,6]{1,0:T(8,128)S(1)}, f32[128,6]{1,0:T(8,128)S(1)}, u32[]{:S(2)}, u32[]{:S(2)}) collective-permute-start(f32[128,6]{1,0:T(8,128)S(1)} %add_add_fusion.5), channel_id=1, source_target_pairs={{0,8},{8,0},{16,24},{24,16},{1,9},{9,1},{17,25},{25,17},{2,10},{10... | collective-permute-start | bytes 9224 | tf_op jit(solution)/shard_map/ppermute | solution.py:26
  368.9 6.5 %collective-permute-start.43 = (f32[128,6]{1,0:T(8,128)S(1)}, f32[128,6]{1,0:T(8,128)S(1)}, u32[]{:S(2)}, u32[]{:S(2)}) collective-permute-start(f32[128,6]{1,0:T(8,128)S(1)} %add_add_fusion.5), channel_id=1, source_target_pairs={{0,16},{8,24},{16,0},{24,8},{1,17},{9,25},{17,1},{25,9},{2,18},{10... | collective-permute-start | bytes 9224 | tf_op jit(solution)/shard_map/ppermute | solution.py:26
  368.9 6.4 %collective-permute-start.44 = (f32[128,6]{1,0:T(8,128)S(1)}, f32[128,6]{1,0:T(8,128)S(1)}, u32[]{:S(2)}, u32[]{:S(2)}) collective-permute-start(f32[128,6]{1,0:T(8,128)S(1)} %add_add_fusion.5), channel_id=1, source_target_pairs={{0,24},{8,16},{16,8},{24,0},{1,25},{9,17},{17,9},{25,1},{2,26},{10... | collective-permute-start | bytes 9224 | tf_op jit(solution)/shard_map/ppermute | solution.py:26
  (26 other events, 454.6 us)

commit v4 on v3

--- a/solution.py
+++ b/solution.py
@@ -154,7 +154,7 @@
         made = (first - slope * message[...]) / (1.0 - slope)
         centre[...] = made
         rows[:t, :] = made.astype(BF16)
-        rows[t:, :] = probes[...].astype(BF16)
+        rows[t:, :] = probes[...]
 
     forward_loop(g, rows, total, held, sems, lambda j: j, g.shape[1], 1, True, True, prepare)
     split_people(out, total, t)
@@ -235,7 +235,7 @@
     )(places, *operands)
 
 
-def wide_body(n, half, chunks, with_acc, off, *refs):
+def wide_body(n, begin, chunks, with_acc, off, *refs):
     refs = list(refs)
     pieces = [refs.pop(0) for _ in range(n)]
     inner = [refs.pop(0) for _ in range(chunks)]
@@ -247,11 +247,17 @@
         g, total, rows, held, sems = refs
     t, unit = pieces[0].shape[0], pieces[0].shape[1] // 2
     span = inner[0].shape[1]
+    count = chunks * span // unit
 
     def prepare():
-        for j in range(n):
-            here = pl.ds(pl.multiple_of(off[j] * unit, unit), unit)
-            rows[:t, here] = pieces[j][:, half * unit : (half + 1) * unit]
+        for j, half in [(j, half) for j in range(n) for half in range(2)]:
+            place = half * n + off[j] - begin
+
+            @pl.when((place >= 0) & (place < count))
+            def _():
+                here = pl.ds(pl.multiple_of(place * unit, unit), unit)
+                rows[:t, here] = pieces[j][:, half * unit : (half + 1) * unit]
+
         for j in range(chunks):
             here = slice(j * span, (j + 1) * span)
 
@@ -267,26 +273,27 @@
             total[...] = acc[...]
 
     forward_loop(
-        g, rows, total, held, sems, lambda j: half * n + j, unit, n, True, not with_acc, prepare
+        g, rows, total, held, sems, lambda j: begin + j, unit, count, True, not with_acc, prepare
     )
     if with_acc:
         split_people(out, total, 0)
 
 
-def wide_forward(pieces, inner, outer, places, half, acc, genotypes, columns, name):
+def wide_forward(pieces, inner, outer, places, begin, acc, genotypes, columns, name):
     people = genotypes.shape[0]
     n, t, unit = len(pieces), pieces[0].shape[0], pieces[0].shape[1] // 2
     r = t + inner[0].shape[0]
     pb, kb = block_of(people, 1024), block_of(unit, 2048)
     operands = [*pieces, *inner, *outer, *([] if acc is None else [acc]), genotypes]
-    scratch = [pltpu.VMEM((r, n * unit), BF16), *ring(pb, kb)]
+    span = len(inner) * inner[0].shape[1]
+    scratch = [pltpu.VMEM((r, span), BF16), *ring(pb, kb)]
     if acc is None:
         shape = jax.ShapeDtypeStruct((people, r), F32)
     else:
         shape = jax.ShapeDtypeStruct((columns, r, people // columns), BF16)
         scratch.append(pltpu.VMEM((people, r), F32))
     return pl.pallas_call(
-        functools.partial(wide_body, n, half, len(inner), acc is not None),
+        functools.partial(wide_body, n, begin, len(inner), acc is not None),
         grid_spec=pltpu.PrefetchScalarGridSpec(
             num_scalar_prefetch=1,
             grid=(),
@@ -296,7 +303,7 @@
         ),
         out_shape=shape,
         compiler_params=pltpu.CompilerParams(vmem_limit_bytes=LIMIT),
-        cost_estimate=cost(r, people, n * unit),
+        cost_estimate=cost(r, people, span),
         name=name,
     )(places, *operands)
 
@@ -459,8 +466,11 @@
     near, far = [jnp.stack([o, o + samples], axis=1).reshape(-1) for o in (order[:some], order[some:])]
 
     cols = jnp.stack([inclusion, slab_ratio, input_precision], axis=1)
-    slopes = sum_marker(slope_sum(message, cols))
-    value, centre = first_forward(message, cols, slopes, probes, genotypes, columns)
+    slopes = slope_sum(message, cols)
+    slopes = slopes + swap(slopes, "marker", 1)
+    probes_b = lax.optimization_barrier((probes, slopes))[0].astype(BF16)
+    slopes = sum_direct(slopes, "marker", 2)
+    value, centre = first_forward(message, cols, slopes, probes_b, genotypes, columns)
     kept_x = jnp.sum(lax.all_to_all(value, "marker", 0, 0).astype(F32), axis=0)
     kept_x, low_x = kept_x[: traits * copies], kept_x[traits * copies :]
     own = lax.dynamic_slice_in_dim(phenotypes, column * share, share, 1) - (kept_x[:traits] + low_x)
@@ -479,17 +489,21 @@
     def add(x, y):
         return (x.astype(F32) + y.astype(F32)).astype(BF16)
 
-    def inward(c):
-        return add(chunks[c], lax.ppermute(chunks[c], "sample", [(0, 1), (3, 2)]))
-
-    def across(x):
-        return add(x, lax.ppermute(x, "sample", [(1, 2), (2, 1)]))
+    def tie(values, *others):
+        return lax.optimization_barrier((tuple(values), others))[0]
+
+    def hop(x, pairs, *others):
+        y = lax.ppermute(x, "sample", pairs)
+        return add(*tie((x, y), *others))
+
+    def inward(c, *others):
+        return hop(chunks[c], [(0, 1), (3, 2)], *others)
+
+    def across(x, *others):
+        return hop(x, [(1, 2), (2, 1)], *others)
 
     def outward(x):
         return lax.ppermute(x, "sample", [(1, 0), (2, 3)])
-
-    def tie(values, *others):
-        return lax.optimization_barrier((tuple(values), others))[0]
 
     pair, full, ends = [None] * 4, [None] * 4, [None] * 4
     pair[0] = inward(0)
@@ -503,41 +517,43 @@
     start_pieces[0], start_pieces[1], chunks[1] = tie(
         (start_pieces[0], start_pieces[1], chunks[1]), pair[0], start_high
     )
-    full[0], pair[1] = across(pair[0]), inward(1)
     value = narrow_forward(start_pieces[:some], near, None, genotypes, "second_forward_near")
-    value = narrow_forward(start_pieces[some:], far, value, genotypes, "second_forward_far")
+    value, *start_pieces = tie((value, *start_pieces))
+    full[0], pair[1] = across(pair[0], value), inward(1, value)
     value, chunks[2] = tie((value, chunks[2]), full[0], pair[1])
     ends[0], full[1], pair[2] = outward(full[0]), across(pair[1]), inward(2)
+    value = narrow_forward(start_pieces[some:], far, value, genotypes, "second_forward_far")
+    value, chunks[3] = tie((value, chunks[3]), full[1], pair[2], ends[0])
+    ends[1], full[2], pair[3] = outward(full[1]), across(pair[2]), inward(3)
     value = sum_marker(value)
     kept_s = lax.dynamic_slice_in_dim(value, column * share, share, 1)
     rows = value.astype(BF16)
     parts = backward(rows, far, genotypes, unit, traits, 0, some, "second_back_far")
     sent = [swap(part, "sample", k + some) for k, part in enumerate(parts)]
-    rows, chunks[3] = tie((rows, chunks[3]), full[1], pair[2], ends[0], *parts)
-    ends[1], full[2], pair[3] = outward(full[1]), across(pair[2]), inward(3)
+    (rows,) = tie((rows,), full[2], pair[3], ends[1], *parts)
+    ends[2] = outward(full[2])
     parts = backward(rows, near, genotypes, unit, traits, 0, some, "second_back_near")
-    back = tree([swap(part, "sample", k) if k else part for k, part in enumerate(parts)] + sent)
+    sent = [swap(part, "sample", k) if k else part for k, part in enumerate(parts)] + sent
+    back = tree(list(tie(sent, ends[2])))
     back_high = lax.reduce_precision(back, 8, 7)
     back_low = (back - back_high).astype(BF16)
     back_high = back_high.astype(BF16)
-    (back_high,) = tie((back_high,), full[2], pair[3], ends[1])
-    ends[2], full[3] = outward(full[2]), across(pair[3])
     back_pieces = [swap(back_high, "sample", k) if k else back_high for k in range(samples)]
-    back_pieces = tie(back_pieces, full[3], ends[2])
+    full[3] = across(pair[3], *back_pieces)
     ends[3] = outward(full[3])
 
     inner = ((me == 1) | (me == 2)).astype(jnp.int32)
     places = jnp.concatenate([order, inner[None]])
     total = wide_forward(
-        back_pieces, full[:2], ends[:2], places, 0, None, genotypes, columns, "third_forward_0"
-    )
-    total, low = tie((total, jnp.concatenate([start_low, back_low], axis=0)), ends[3], total)
+        back_pieces, full[:3], ends[:3], places, 0, None, genotypes, columns, "third_forward_0"
+    )
+    total, low = tie((total, jnp.concatenate([start_low, back_low], axis=0)), ends[3])
     low_pieces = [swap(low, "sample", k) if k else low for k in range(samples)]
     value = wide_forward(
-        back_pieces, full[2:], ends[2:], places, 1, total, genotypes, columns, "third_forward_1"
-    )
-    (value,) = tie((value,), *low_pieces)
-    last = jnp.sum(lax.all_to_all(value, "marker", 0, 0).astype(F32), axis=0)
+        back_pieces, full[3:], ends[3:], places, 3 * some, total, genotypes, columns, "third_forward_1"
+    )
+    (last,) = tie((lax.all_to_all(value, "marker", 0, 0),), *low_pieces)
+    last = jnp.sum(last.astype(F32), axis=0)
     before = jnp.concatenate([kept_s, kept_x[traits:]], axis=0)
 
     def dot(x, y):

time: 379 us -> 368 us (0.971)
  waiting for transfers between devices: 119 us -> 110 us
  starting transfers between devices: 92.8 us -> 83.9 us
  other arithmetic: 15.8 us -> 23.6 us
    ppermute x33, starting transfers between devices: 64.8 us -> 50.9 us  [swap(): return lax.ppermute(x, axis, [(i, i ^ bits) for i in range(n)])]
    ppermute x4, waiting for transfers between devices: 11.7 us -> 3.83 us  [outward(): return lax.ppermute(x, 'sample', [(1, 0), (2, 3)])]
    all_to_all x1, waiting for transfers between devices: 7.07 us -> 0.01 us  [per_device(): last, = tie((lax.all_to_all(value, 'marker', 0, 0),), *low_pieces)]
    ppermute x8, starting transfers between devices: 14.8 us -> 20.1 us  [hop(): y = lax.ppermute(x, 'sample', pairs)]
    ppermute x33, waiting for transfers between devices: 90.2 us -> 94.4 us  [swap(): return lax.ppermute(x, axis, [(i, i ^ bits) for i in range(n)])]
  transfers between devices with their start and end apart: 47 -> 47, of which waited for: 27 -> 23; matrix products, arithmetic and copies ran while one was open for 3% -> 5% of each run, Pallas kernels for 24% -> 23%
where the time goes in v4:
time: 368 us; the launch traced here: 367 us
  Pallas kernels  134 us (36%)
  waiting for transfers between devices  110 us (30%)
  starting transfers between devices  83.9 us (23%)
  other arithmetic  23.6 us (6%)
  blocking collectives  9.94 us (3%)
  local copies, waits for them, and re-layouts  4.48 us (1%)
    ppermute x33, waiting for transfers between devices, swap(): return lax.ppermute(x, axis, [(i, i ^ bits) for i in range(n)])  94.4 us
    pallas_call x4, Pallas kernels, backward(): pl.pallas_call(functools.partial(back_body, n, unit, t, base), grid_spec=...  51.4 us
    ppermute x33, starting transfers between devices, swap(): return lax.ppermute(x, axis, [(i, i ^ bits) for i in range(n)])  50.9 us
    pallas_call x2, Pallas kernels, wide_forward(): pl.pallas_call(functools.partial(wide_body, n, begin, len(inner), acc is...  28.6 us
    pallas_call x2, Pallas kernels, narrow_forward(): pl.pallas_call(functools.partial(narrow_body, n, unit, acc is not None),...  25.4 us
    pallas_call x1, Pallas kernels, first_forward(): pl.pallas_call(functools.partial(first_body, markers * columns), grid_spe...  24.5 us
    ppermute x8, starting transfers between devices, hop(): y = lax.ppermute(x, 'sample', pairs)  20.1 us
    all_to_all x1, waiting for transfers between devices, per_device(): kept_x = jnp.sum(lax.all_to_all(value, 'marker', 0, 0).astype(F32), axis=0)  10.3 us
  transfers between devices with their start and end apart: 47, of which 23 were waited for; matrix products, arithmetic and copies ran while one was open for 5% of the time, Pallas kernels for 23%

profile of v4, /device:TPU:0, one launch (start us, length us, event | category | flops | bytes accessed | tf_op | source)
XLA Modules:
  0.0 366.7 jit_solution(12656500178446259840)
XLA Ops:
  4.7 2.8 collective-permute-start.1
  9.1 3.5 convert_element_type.101.probes
  14.2 24.5 %first_forward.1 = (bf16[8,144,256]{2,1,0:T(8,128)(2,1)}, f32[16,16384]{1,0:T(8,128)S(1)}) custom-call(s32[1]{0:T(128)} %constant.8.clone.1.off, f32[16,16384]{1,0:T(8,128)S(1)} %copy-done, f32[16,3]{1,0:T(8,128)S(1)} %copy.49.cols, f32[16,1]{1,0:T(8,128)S(1)} %get-tuple-element.125.slopes, bf16[112,16384]{1,0:T(8,128)(2,1)S(1)} %convert_element_type.101.probes, ...), custom_call_target="tpu_custom_call" | custom-call | flops 8589934592 | bytes 67108864 | tf_op jit(solution)/shard_map/first_forward/pallas_call | solution.py:174
  39.7 3.5 all-to-all-start
  43.3 10.3 %all-to-all-done = bf16[8,144,256]{2,1,0:T(8,128)(2,1)S(1)} async-done(((bf16[8,144,256]{2,1,0:T(8,128)(2,1)}), bf16[8,144,256]{2,1,0:T(8,128)(2,1)S(1)}, u32[]{:S(2)}, u32[]{:S(2)}) %all-to-all-start) | async-done | bytes 589856 | tf_op jit(solution)/shard_map/all_to_all | solution.py:474
  54.5 9.9 %all_gather.3.rows = bf16[128,2048]{1,0:T(8,128)(2,1)S(1)} all-gather(bf16[128,256]{1,0:T(8,128)(2,1)S(1)} %pad_maximum_fusion.2), channel_id=1, replica_groups=mesh['sample'=4,'marker'=8] {'marker'}, dimensions={1}, use_global_device_ids=true | all-gather | bytes 589824 | tf_op jit(solution)/shard_map/all_gather | solution.py:479
  64.4 12.7 %first_back_0.1 = (f32[16,2048]{1,0:T(8,128)S(1)}, f32[16,2048]{1,0:T(8,128)S(1)}, f32[16,2048]{1,0:T(8,128)S(1)}, f32[16,2048]{1,0:T(8,128)S(1)}, bf16[112,4096...) custom-call(s32[4]{0:T(128)S(1)} %iota_xor_fusion.off, bf16[128,2048]{1,0:T(8,128)(2,1)S(1)} %all_gather.3.rows, ...), custom_call_target="tpu_custom_call" | custom-call | flops 4294967296 | bytes 33554432 | tf_op jit(solution)/shard_map/first_back_0/pallas_call | solution.py:384
  77.2 3.5 collective-permute-start.11
  80.8 3.0 collective-permute-start.5
  85.2 12.7 %first_back_1.1 = (f32[16,2048]{1,0:T(8,128)S(1)}, f32[16,2048]{1,0:T(8,128)S(1)}, f32[16,2048]{1,0:T(8,128)S(1)}, f32[16,2048]{1,0:T(8,128)S(1)}, bf16[112,4096...) custom-call(s32[4]{0:T(128)S(1)} %broadcast_add_fusion.off, bf16[128,2048]{1,0:T(8,128)(2,1)S(1)} %all_gather.3.rows, ...), custom_call_target="tpu_custom_call" | custom-call | flops 4294967296 | bytes 33554432 | tf_op jit(solution)/shard_map/first_back_1/pallas_call | solution.py:384
  98.0 6.1 %collective-permute-done.4 = f32[16,2048]{1,0:T(8,128)S(1)} collective-permute-done((f32[16,2048]{1,0:T(8,128)S(1)}, f32[16,2048]{1,0:T(8,128)S(1)}, u32[]{:S(2)}, u32[]{:S(2)}) %collective-permute-start.4) | collective-permute-done | bytes 131104 | tf_op jit(solution)/shard_map/ppermute | solution.py:26
  104.2 3.5 collective-permute-start.8
  109.5 3.3 collective-permute-done.6
  112.8 2.8 collective-permute-done.8
  115.6 5.1 %collective-permute-done.9 = f32[16,2048]{1,0:T(8,128)S(1)} collective-permute-done((f32[16,2048]{1,0:T(8,128)S(1)}, f32[16,2048]{1,0:T(8,128)S(1)}, u32[]{:S(2)}, u32[]{:S(2)}) %collective-permute-start.9) | collective-permute-done | bytes 131104 | tf_op jit(solution)/shard_map/ppermute | solution.py:26
  121.5 3.2 collective-permute-start.10
  125.0 3.4 collective-permute-done.10.refs_1_
  128.4 4.6 %collective-permute-start.15 = (bf16[112,4096]{1,0:T(8,128)(2,1)S(1)}, bf16[112,4096]{1,0:T(8,128)(2,1)}, u32[]{:S(2)}, u32[]{:S(2)}) collective-permute-start(bf16[112,4096]{1,0:T(8,128)(2,1)S(1)} %get-tuple-element.82), channel_id=1, source_target_pairs={{0,8},{24,16},{1,9},{25,17},{2,10},{26,18},{3,11},{27,19},{4,12},{... | collective-permute-start | bytes 2752520 | tf_op jit(solution)/shard_map/ppermute | solution.py:496
  136.5 12.7 %second_forward_near.1.refs_2_ = f32[16,2048]{1,0:T(8,128)S(1)} custom-call(s32[4]{0:T(128)S(1)} %reshape.27.off, bf16[16,4096]{1,0:T(8,128)(2,1)S(1)} %get-tuple-element.112.refs_0_, bf16[16,4096]{1,0:T(8,128)(2,1)S(1)} %collective-permute-done.10.refs_1_, bf16[2048,16384]{1,0:T(8,128)(2,1)} %refs_7_.1), custom_call_target="tpu_custom_call" | custom-call | flops 536870912 | bytes 33554432 | tf_op jit(solution)/shard_map/second_forward_near/pallas_call | solution.py:222
  149.2 14.9 %collective-permute-done.12.refs_0_.refs_2_ = bf16[16,4096]{1,0:T(8,128)(2,1)S(1)} collective-permute-done((bf16[16,4096]{1,0:T(8,128)(2,1)S(1)}, bf16[16,4096]{1,0:T(8,128)(2,1)S(1)}, u32[]{:S(2)}, u32[]{:S(2)}) %collective-permute-start.12) | collective-permute-done | bytes 131104 | tf_op jit(solution)/shard_map/ppermute | solution.py:26
  164.1 2.5 add_convert_fusion.5
  167.9 4.8 %collective-permute-start.17 = (bf16[112,4096]{1,0:T(8,128)(2,1)S(1)}, bf16[112,4096]{1,0:T(8,128)(2,1)}, u32[]{:S(2)}, u32[]{:S(2)}) collective-permute-start(bf16[112,4096]{1,0:T(8,128)(2,1)S(1)} %get-tuple-element.89), channel_id=1, source_target_pairs={{0,8},{24,16},{1,9},{25,17},{2,10},{26,18},{3,11},{27,19},{4,12},{... | collective-permute-start | bytes 2752520 | tf_op jit(solution)/shard_map/ppermute | solution.py:496
  175.8 12.7 %second_forward_far.1 = f32[16,2048]{1,0:T(8,128)S(1)} custom-call(s32[4]{0:T(128)S(1)} %reshape.28.off, bf16[16,4096]{1,0:T(8,128)(2,1)S(1)} %collective-permute-done.12.refs_0_.refs_2_, bf16[16,4096]{1,0:T(8,128)(2,1)S(1)} %collective-permute-done.13.refs_1_.refs_3_, f32[16,2048]{1,0:T(8,128)S(1)} %second_forward_near.1.refs_2_, bf16[2048,16384]{1,0:T(8,128)(2,1)} %refs_7_.1), custom_call_target="tpu_custom_call" | custom-call | flops 536870912 | bytes 33554432 | tf_op jit(solution)/shard_map/second_forward_far/pallas_call | solution.py:222
  192.6 3.6 collective-permute-done.18.refs_7_
  196.3 2.6 collective-permute-start.24
  204.6 2.4 collective-permute-done.20
  208.3 2.4 collective-permute-done.21
  211.4 13.0 %second_back_far.1 = (f32[16,4096]{1,0:T(8,128)}, f32[16,4096]{1,0:T(8,128)}) custom-call(s32[4]{0:T(128)S(1)} %reshape.28.off, bf16[16,2048]{1,0:T(8,128)(2,1)S(1)} %get-tuple-element.99.rows, bf16[2048,16384]{1,0:T(8,128)(2,1)} %refs_7_.1), custom_call_target="tpu_custom_call" | custom-call | flops 536870912 | bytes 33554432 | tf_op jit(solution)/shard_map/second_back_far/pallas_call | solution.py:384
  224.4 2.0 collective-permute-start.27
  230.7 12.9 %second_back_near.1 = (f32[16,4096]{1,0:T(8,128)S(1)}, f32[16,4096]{1,0:T(8,128)}) custom-call(s32[4]{0:T(128)S(1)} %reshape.27.off, bf16[16,2048]{1,0:T(8,128)(2,1)S(1)} %get-tuple-element.99.rows, bf16[2048,16384]{1,0:T(8,128)(2,1)} %refs_7_.1), custom_call_target="tpu_custom_call" | custom-call | flops 536870912 | bytes 33554432 | tf_op jit(solution)/shard_map/second_back_near/pallas_call | solution.py:384
  243.6 3.4 collective-permute-start.26
  248.4 18.8 %collective-permute-done.26 = f32[16,4096]{1,0:T(8,128)} collective-permute-done((f32[16,4096]{1,0:T(8,128)}, f32[16,4096]{1,0:T(8,128)}, u32[]{:S(2)}, u32[]{:S(2)}) %collective-permute-start.26) | collective-permute-done | bytes 262176 | tf_op jit(solution)/shard_map/ppermute | solution.py:26
  268.8 2.0 collective-permute-start.31
  270.8 2.4 collective-permute-start.32
  273.2 2.3 multiply_reduce_fusion
  275.6 5.3 %collective-permute-done.31.refs_2_.refs_6_ = bf16[16,4096]{1,0:T(8,128)(2,1)S(1)} collective-permute-done((bf16[16,4096]{1,0:T(8,128)(2,1)S(1)}, bf16[16,4096]{1,0:T(8,128)(2,1)S(1)}, u32[]{:S(2)}, u32[]{:S(2)}) %collective-permute-start.31) | collective-permute-done | bytes 131104 | tf_op jit(solution)/shard_map/ppermute | solution.py:26
  283.1 19.7 %third_forward_0.1.refs_6_ = f32[2048,128]{1,0:T(8,128)S(1)} custom-call(s32[5]{0:T(128)S(1)} %pad_add_fusion.2.off, bf16[16,4096]{1,0:T(8,128)(2,1)S(1)} %get-tuple-element.132.refs_0_.refs_4_, bf16[16,4096]{1,0:T(8,128)(2,1)S(1)} %collective-permute-done.30.refs_1_.refs_5_, bf16[16,4096]{1,0:T(8,128)(2,1)S(1)} %collective-permute-done.31.refs_2_.refs_6_, ...), custom_call_target="tpu_custom_call" | custom-call | flops 6442450944 | bytes 50331648 | tf_op jit(solution)/shard_map/third_forward_0/pallas_call | solution.py:295
  303.0 8.8 %third_forward_1.1 = bf16[8,128,256]{2,1,0:T(8,128)(2,1)} custom-call(s32[5]{0:T(128)S(1)} %pad_add_fusion.2.off, bf16[16,4096]{1,0:T(8,128)(2,1)S(1)} %get-tuple-element.132.refs_0_.refs_4_, bf16[16,4096]{1,0:T(8,128)(2,1)S(1)} %collective-permute-done.30.refs_1_.refs_5_, bf16[16,4096]{1,0:T(8,128)(2,1)S(1)} %collective-permute-done.31.refs_2_.refs_6_, ...), custom_call_target="tpu_custom_call" | custom-call | flops 2147483648 | bytes 16777216 | tf_op jit(solution)/shard_map/third_forward_1/pallas_call | solution.py:295
  311.9 4.3 %all-to-all-start.1 = ((bf16[8,128,256]{2,1,0:T(8,128)(2,1)}), bf16[8,128,256]{2,1,0:T(8,128)(2,1)}, u32[]{:S(2)}, u32[]{:S(2)}) async-start(bf16[8,128,256]{2,1,0:T(8,128)(2,1)} %third_forward_1.1), calls=%async_computation.1 | async-start | bytes 1048576 | tf_op jit(solution)/shard_map/all_to_all | solution.py:555
  316.2 2.8 collective-permute-start.35
  319.0 2.4 collective-permute-start.37
  322.8 7.5 %collective-permute-done.35.refs_9_ = bf16[32,4096]{1,0:T(8,128)(2,1)S(1)} collective-permute-done((bf16[32,4096]{1,0:T(8,128)(2,1)S(1)}, bf16[32,4096]{1,0:T(8,128)(2,1)S(1)}, u32[]{:S(2)}, u32[]{:S(2)}) %collective-permute-start.35) | collective-permute-done | bytes 262176 | tf_op jit(solution)/shard_map/ppermute | solution.py:26
  330.2 10.1 %collective-permute-done.36.refs_10_ = bf16[32,4096]{1,0:T(8,128)(2,1)S(1)} collective-permute-done((bf16[32,4096]{1,0:T(8,128)(2,1)S(1)}, bf16[32,4096]{1,0:T(8,128)(2,1)S(1)}, u32[]{:S(2)}, u32[]{:S(2)}) %collective-permute-start.36) | collective-permute-done | bytes 262176 | tf_op jit(solution)/shard_map/ppermute | solution.py:26
  349.5 2.4 collective-permute-done.41
  351.9 5.2 %collective-permute-start.42 = (f32[128,6]{1,0:T(8,128)S(1)}, f32[128,6]{1,0:T(8,128)S(1)}, u32[]{:S(2)}, u32[]{:S(2)}) collective-permute-start(f32[128,6]{1,0:T(8,128)S(1)} %add_add_fusion.5), channel_id=1, source_target_pairs={{0,8},{8,0},{16,24},{24,16},{1,9},{9,1},{17,25},{25,17},{2,10},{10... | collective-permute-start | bytes 9224 | tf_op jit(solution)/shard_map/ppermute | solution.py:26
  357.1 2.4 collective-permute-start.44
  359.7 3.7 %collective-permute-done.43 = f32[128,6]{1,0:T(8,128)S(1)} collective-permute-done((f32[128,6]{1,0:T(8,128)S(1)}, f32[128,6]{1,0:T(8,128)S(1)}, u32[]{:S(2)}, u32[]{:S(2)}) %collective-permute-start.43) | collective-permute-done | bytes 3104 | tf_op jit(solution)/shard_map/ppermute | solution.py:26
  363.5 3.2 finish.1
  (170 shorter events, 53.5 us)
Async XLA Ops:
  3.4 1.3 collective-permute-start
  4.7 7.9 %collective-permute-start.1 = (f32[16,1]{1,0:T(8,128)S(1)}, f32[16,1]{1,0:T(8,128)S(1)}, u32[]{:S(2)}, u32[]{:S(2)}) collective-permute-start(f32[16,1]{1,0:T(8,128)S(1)} %add.135), channel_id=1, source_target_pairs={{0,2},{1,3},{2,0},{3,1},{4,6},{5,7},{6,4},{7,5},{8,10},{9,11},{10,... | collective-permute-start | bytes 200 | tf_op jit(solution)/shard_map/ppermute | solution.py:26
  7.5 5.0 %collective-permute-start.2 = (f32[16,1]{1,0:T(8,128)S(1)}, f32[16,1]{1,0:T(8,128)S(1)}, u32[]{:S(2)}, u32[]{:S(2)}) collective-permute-start(f32[16,1]{1,0:T(8,128)S(1)} %add.135), channel_id=1, source_target_pairs={{0,4},{1,5},{2,6},{3,7},{4,0},{5,1},{6,2},{7,3},{8,12},{9,13},{10,... | collective-permute-start | bytes 200 | tf_op jit(solution)/shard_map/ppermute | solution.py:26
  9.0 4.5 %collective-permute-start.3 = (f32[16,1]{1,0:T(8,128)S(1)}, f32[16,1]{1,0:T(8,128)S(1)}, u32[]{:S(2)}, u32[]{:S(2)}) collective-permute-start(f32[16,1]{1,0:T(8,128)S(1)} %add.135), channel_id=1, source_target_pairs={{0,6},{1,7},{2,4},{3,5},{4,2},{5,3},{6,0},{7,1},{8,14},{9,15},{10,... | collective-permute-start | bytes 200 | tf_op jit(solution)/shard_map/ppermute | solution.py:26
  39.7 13.9 %all-to-all-start = ((bf16[8,144,256]{2,1,0:T(8,128)(2,1)}), bf16[8,144,256]{2,1,0:T(8,128)(2,1)S(1)}, u32[]{:S(2)}, u32[]{:S(2)}) async-start(bf16[8,144,256]{2,1,0:T(8,128)(2,1)} %get-tuple-element.59), calls=%async_computation | async-start | bytes 1179648 | tf_op jit(solution)/shard_map/all_to_all | solution.py:474
  77.2 47.5 %collective-permute-start.11 = (bf16[112,4096]{1,0:T(8,128)(2,1)S(1)}, bf16[112,4096]{1,0:T(8,128)(2,1)S(1)}, u32[]{:S(2)}, u32[]{:S(2)}) collective-permute-start(bf16[112,4096]{1,0:T(8,128)(2,1)S(1)} %get-tuple-element.71), channel_id=1, source_target_pairs={{0,8},{24,16},{1,9},{25,17},{2,10},{26,18},{3,11},{27,19},{4,12},{... | collective-permute-start | bytes 2752520 | tf_op jit(solution)/shard_map/ppermute | solution.py:496
  80.7 23.4 %collective-permute-start.4 = (f32[16,2048]{1,0:T(8,128)S(1)}, f32[16,2048]{1,0:T(8,128)S(1)}, u32[]{:S(2)}, u32[]{:S(2)}) collective-permute-start(f32[16,2048]{1,0:T(8,128)S(1)} %get-tuple-element.61), channel_id=1, source_target_pairs={{0,8},{8,0},{16,24},{24,16},{1,9},{9,1},{17,25},{25,17},{2,10},{10... | collective-permute-start | bytes 393224 | tf_op jit(solution)/shard_map/ppermute | solution.py:26
  80.8 26.8 %collective-permute-start.5 = (f32[16,2048]{1,0:T(8,128)S(1)}, f32[16,2048]{1,0:T(8,128)S(1)}, u32[]{:S(2)}, u32[]{:S(2)}) collective-permute-start(f32[16,2048]{1,0:T(8,128)S(1)} %get-tuple-element.62), channel_id=1, source_target_pairs={{0,16},{8,24},{16,0},{24,8},{1,17},{9,25},{17,1},{25,9},{2,18},{10... | collective-permute-start | bytes 393224 | tf_op jit(solution)/shard_map/ppermute | solution.py:26
  83.8 28.9 %collective-permute-start.6 = (f32[16,2048]{1,0:T(8,128)S(1)}, f32[16,2048]{1,0:T(8,128)S(1)}, u32[]{:S(2)}, u32[]{:S(2)}) collective-permute-start(f32[16,2048]{1,0:T(8,128)S(1)} %get-tuple-element.63), channel_id=1, source_target_pairs={{0,24},{8,16},{16,8},{24,0},{1,25},{9,17},{17,9},{25,1},{2,26},{10... | collective-permute-start | bytes 393224 | tf_op jit(solution)/shard_map/ppermute | solution.py:26
  98.0 14.8 %collective-permute-start.7 = (f32[16,2048]{1,0:T(8,128)S(1)}, f32[16,2048]{1,0:T(8,128)S(1)}, u32[]{:S(2)}, u32[]{:S(2)}) collective-permute-start(f32[16,2048]{1,0:T(8,128)S(1)} %get-tuple-element.67), channel_id=1, source_target_pairs={{0,8},{8,0},{16,24},{24,16},{1,9},{9,1},{17,25},{25,17},{2,10},{10... | collective-permute-start | bytes 393224 | tf_op jit(solution)/shard_map/ppermute | solution.py:26
  104.2 11.4 %collective-permute-start.8 = (f32[16,2048]{1,0:T(8,128)S(1)}, f32[16,2048]{1,0:T(8,128)S(1)}, u32[]{:S(2)}, u32[]{:S(2)}) collective-permute-start(f32[16,2048]{1,0:T(8,128)S(1)} %get-tuple-element.68), channel_id=1, source_target_pairs={{0,16},{8,24},{16,0},{24,8},{1,17},{9,25},{17,1},{25,9},{2,18},{10... | collective-permute-start | bytes 393224 | tf_op jit(solution)/shard_map/ppermute | solution.py:26
  107.6 13.1 %collective-permute-start.9 = (f32[16,2048]{1,0:T(8,128)S(1)}, f32[16,2048]{1,0:T(8,128)S(1)}, u32[]{:S(2)}, u32[]{:S(2)}) collective-permute-start(f32[16,2048]{1,0:T(8,128)S(1)} %get-tuple-element.69), channel_id=1, source_target_pairs={{0,24},{8,16},{16,8},{24,0},{1,25},{9,17},{17,9},{25,1},{2,26},{10... | collective-permute-start | bytes 393224 | tf_op jit(solution)/shard_map/ppermute | solution.py:26
  121.5 6.9 %collective-permute-start.10 = (bf16[16,4096]{1,0:T(8,128)(2,1)S(1)}, bf16[16,4096]{1,0:T(8,128)(2,1)S(1)}, u32[]{:S(2)}, u32[]{:S(2)}) collective-permute-start(bf16[16,4096]{1,0:T(8,128)(2,1)S(1)} %get-tuple-element.112.refs_0_), channel_id=1, source_target_pairs={{0,8},{8,0},{16,24},{24,16},{1,9},{9,1},{17,25},{25,17},{2,10},{10... | collective-permute-start | bytes 393224 | tf_op jit(solution)/shard_map/ppermute | solution.py:26
  128.4 35.6 %collective-permute-start.15 = (bf16[112,4096]{1,0:T(8,128)(2,1)S(1)}, bf16[112,4096]{1,0:T(8,128)(2,1)}, u32[]{:S(2)}, u32[]{:S(2)}) collective-permute-start(bf16[112,4096]{1,0:T(8,128)(2,1)S(1)} %get-tuple-element.82), channel_id=1, source_target_pairs={{0,8},{24,16},{1,9},{25,17},{2,10},{26,18},{3,11},{27,19},{4,12},{... | collective-permute-start | bytes 2752520 | tf_op jit(solution)/shard_map/ppermute | solution.py:496
  133.0 31.1 %collective-permute-start.14 = (bf16[112,4096]{1,0:T(8,128)(2,1)S(1)}, bf16[112,4096]{1,0:T(8,128)(2,1)}, u32[]{:S(2)}, u32[]{:S(2)}) collective-permute-start(bf16[112,4096]{1,0:T(8,128)(2,1)S(1)} %add_convert_fusion.7), channel_id=1, source_target_pairs={{8,16},{16,8},{9,17},{17,9},{10,18},{18,10},{11,19},{19,11},{12,20... | collective-permute-start | bytes 2752520 | tf_op jit(solution)/shard_map/ppermute | solution.py:496
  134.7 29.4 %collective-permute-start.12 = (bf16[16,4096]{1,0:T(8,128)(2,1)S(1)}, bf16[16,4096]{1,0:T(8,128)(2,1)S(1)}, u32[]{:S(2)}, u32[]{:S(2)}) collective-permute-start(bf16[16,4096]{1,0:T(8,128)(2,1)S(1)} %get-tuple-element.112.refs_0_), channel_id=1, source_target_pairs={{0,16},{8,24},{16,0},{24,8},{1,17},{9,25},{17,1},{25,9},{2,18},{10... | collective-permute-start | bytes 393224 | tf_op jit(solution)/shard_map/ppermute | solution.py:26
  134.9 29.1 %collective-permute-start.13 = (bf16[16,4096]{1,0:T(8,128)(2,1)S(1)}, bf16[16,4096]{1,0:T(8,128)(2,1)S(1)}, u32[]{:S(2)}, u32[]{:S(2)}) collective-permute-start(bf16[16,4096]{1,0:T(8,128)(2,1)S(1)} %get-tuple-element.112.refs_0_), channel_id=1, source_target_pairs={{0,24},{8,16},{16,8},{24,0},{1,25},{9,17},{17,9},{25,1},{2,26},{10... | collective-permute-start | bytes 393224 | tf_op jit(solution)/shard_map/ppermute | solution.py:26
  167.9 21.5 %collective-permute-start.17 = (bf16[112,4096]{1,0:T(8,128)(2,1)S(1)}, bf16[112,4096]{1,0:T(8,128)(2,1)}, u32[]{:S(2)}, u32[]{:S(2)}) collective-permute-start(bf16[112,4096]{1,0:T(8,128)(2,1)S(1)} %get-tuple-element.89), channel_id=1, source_target_pairs={{0,8},{24,16},{1,9},{25,17},{2,10},{26,18},{3,11},{27,19},{4,12},{... | collective-permute-start | bytes 2752520 | tf_op jit(solution)/shard_map/ppermute | solution.py:496
  172.7 16.8 %collective-permute-start.16 = (bf16[112,4096]{1,0:T(8,128)(2,1)}, bf16[112,4096]{1,0:T(8,128)(2,1)}, u32[]{:S(2)}, u32[]{:S(2)}) collective-permute-start(bf16[112,4096]{1,0:T(8,128)(2,1)} %add_convert_fusion.5), channel_id=1, source_target_pairs={{8,16},{16,8},{9,17},{17,9},{10,18},{18,10},{11,19},{19,11},{12,20... | collective-permute-start | bytes 2752520 | tf_op jit(solution)/shard_map/ppermute | solution.py:496
  174.4 21.8 %collective-permute-start.18 = (bf16[112,4096]{1,0:T(8,128)(2,1)S(1)}, bf16[112,4096]{1,0:T(8,128)(2,1)S(1)}, u32[]{:S(2)}, u32[]{:S(2)}) collective-permute-start(bf16[112,4096]{1,0:T(8,128)(2,1)S(1)} %add_convert_fusion.6.refs_4_), channel_id=1, source_target_pairs={{8,0},{16,24},{9,1},{17,25},{10,2},{18,26},{11,3},{19,27},{12,4},{... | collective-permute-start | bytes 2752520 | tf_op jit(solution)/shard_map/ppermute | solution.py:506
  196.3 31.5 %collective-permute-start.24 = (bf16[112,4096]{1,0:T(8,128)(2,1)S(1)}, bf16[112,4096]{1,0:T(8,128)(2,1)S(1)}, u32[]{:S(2)}, u32[]{:S(2)}) collective-permute-start(bf16[112,4096]{1,0:T(8,128)(2,1)S(1)} %copy-done.9), channel_id=1, source_target_pairs={{0,8},{24,16},{1,9},{25,17},{2,10},{26,18},{3,11},{27,19},{4,12},{... | collective-permute-start | bytes 2752520 | tf_op jit(solution)/shard_map/ppermute | solution.py:496
  198.9 28.9 %collective-permute-start.23 = (bf16[112,4096]{1,0:T(8,128)(2,1)S(1)}, bf16[112,4096]{1,0:T(8,128)(2,1)S(1)}, u32[]{:S(2)}, u32[]{:S(2)}) collective-permute-start(bf16[112,4096]{1,0:T(8,128)(2,1)S(1)} %add_convert_fusion.3), channel_id=1, source_target_pairs={{8,16},{16,8},{9,17},{17,9},{10,18},{18,10},{11,19},{19,11},{12,20... | collective-permute-start | bytes 2752520 | tf_op jit(solution)/shard_map/ppermute | solution.py:496
  199.6 1.4 collective-permute-start.19
  201.1 6.0 %collective-permute-start.20 = (f32[16,2048]{1,0:T(8,128)S(1)}, f32[16,2048]{1,0:T(8,128)S(1)}, u32[]{:S(2)}, u32[]{:S(2)}) collective-permute-start(f32[16,2048]{1,0:T(8,128)S(1)} %add.154), channel_id=1, source_target_pairs={{0,2},{1,3},{2,0},{3,1},{4,6},{5,7},{6,4},{7,5},{8,10},{9,11},{10,... | collective-permute-start | bytes 393224 | tf_op jit(solution)/shard_map/ppermute | solution.py:26
  202.6 8.1 %collective-permute-start.21 = (f32[16,2048]{1,0:T(8,128)S(1)}, f32[16,2048]{1,0:T(8,128)S(1)}, u32[]{:S(2)}, u32[]{:S(2)}) collective-permute-start(f32[16,2048]{1,0:T(8,128)S(1)} %add.154), channel_id=1, source_target_pairs={{0,4},{1,5},{2,6},{3,7},{4,0},{5,1},{6,2},{7,3},{8,12},{9,13},{10,... | collective-permute-start | bytes 393224 | tf_op jit(solution)/shard_map/ppermute | solution.py:26
  203.2 7.5 %collective-permute-start.22 = (f32[16,2048]{1,0:T(8,128)S(1)}, f32[16,2048]{1,0:T(8,128)S(1)}, u32[]{:S(2)}, u32[]{:S(2)}) collective-permute-start(f32[16,2048]{1,0:T(8,128)S(1)} %add.154), channel_id=1, source_target_pairs={{0,6},{1,7},{2,4},{3,5},{4,2},{5,3},{6,0},{7,1},{8,14},{9,15},{10,... | collective-permute-start | bytes 393224 | tf_op jit(solution)/shard_map/ppermute | solution.py:26
  207.1 23.6 %collective-permute-start.25 = (bf16[112,4096]{1,0:T(8,128)(2,1)S(1)}, bf16[112,4096]{1,0:T(8,128)(2,1)S(1)}, u32[]{:S(2)}, u32[]{:S(2)}) collective-permute-start(bf16[112,4096]{1,0:T(8,128)(2,1)S(1)} %add_convert_fusion.4.refs_5_), channel_id=1, source_target_pairs={{8,0},{16,24},{9,1},{17,25},{10,2},{18,26},{11,3},{19,27},{12,4},{... | collective-permute-start | bytes 2752520 | tf_op jit(solution)/shard_map/ppermute | solution.py:506
  224.4 24.0 %collective-permute-start.27 = (f32[16,4096]{1,0:T(8,128)}, f32[16,4096]{1,0:T(8,128)}, u32[]{:S(2)}, u32[]{:S(2)}) collective-permute-start(f32[16,4096]{1,0:T(8,128)} %get-tuple-element.97), channel_id=1, source_target_pairs={{0,16},{8,24},{16,0},{24,8},{1,17},{9,25},{17,1},{25,9},{2,18},{10... | collective-permute-start | bytes 786440 | tf_op jit(solution)/shard_map/ppermute | solution.py:26
  226.4 21.9 %collective-permute-start.28 = (f32[16,4096]{1,0:T(8,128)}, f32[16,4096]{1,0:T(8,128)}, u32[]{:S(2)}, u32[]{:S(2)}) collective-permute-start(f32[16,4096]{1,0:T(8,128)} %get-tuple-element.98), channel_id=1, source_target_pairs={{0,24},{8,16},{16,8},{24,0},{1,25},{9,17},{17,9},{25,1},{2,26},{10... | collective-permute-start | bytes 786440 | tf_op jit(solution)/shard_map/ppermute | solution.py:26
  228.0 39.1 %collective-permute-start.29 = (bf16[112,4096]{1,0:T(8,128)(2,1)S(1)}, bf16[112,4096]{1,0:T(8,128)(2,1)}, u32[]{:S(2)}, u32[]{:S(2)}) collective-permute-start(bf16[112,4096]{1,0:T(8,128)(2,1)S(1)} %add_convert_fusion.2.refs_6_), channel_id=1, source_target_pairs={{8,0},{16,24},{9,1},{17,25},{10,2},{18,26},{11,3},{19,27},{12,4},{... | collective-permute-start | bytes 2752520 | tf_op jit(solution)/shard_map/ppermute | solution.py:506
  243.6 23.5 %collective-permute-start.26 = (f32[16,4096]{1,0:T(8,128)}, f32[16,4096]{1,0:T(8,128)}, u32[]{:S(2)}, u32[]{:S(2)}) collective-permute-start(f32[16,4096]{1,0:T(8,128)} %get-tuple-element.101), channel_id=1, source_target_pairs={{0,8},{8,0},{16,24},{24,16},{1,9},{9,1},{17,25},{25,17},{2,10},{10... | collective-permute-start | bytes 786440 | tf_op jit(solution)/shard_map/ppermute | solution.py:26
  247.6 27.9 %collective-permute-start.33 = (bf16[112,4096]{1,0:T(8,128)(2,1)}, bf16[112,4096]{1,0:T(8,128)(2,1)S(1)}, u32[]{:S(2)}, u32[]{:S(2)}) collective-permute-start(bf16[112,4096]{1,0:T(8,128)(2,1)} %add_convert_fusion.1), channel_id=1, source_target_pairs={{8,16},{16,8},{9,17},{17,9},{10,18},{18,10},{11,19},{19,11},{12,20... | collective-permute-start | bytes 2752520 | tf_op jit(solution)/shard_map/ppermute | solution.py:496
  268.8 6.8 %collective-permute-start.30 = (bf16[16,4096]{1,0:T(8,128)(2,1)S(1)}, bf16[16,4096]{1,0:T(8,128)(2,1)S(1)}, u32[]{:S(2)}, u32[]{:S(2)}) collective-permute-start(bf16[16,4096]{1,0:T(8,128)(2,1)S(1)} %get-tuple-element.132.refs_0_.refs_4_), channel_id=1, source_target_pairs={{0,8},{8,0},{16,24},{24,16},{1,9},{9,1},{17,25},{25,17},{2,10},{10... | collective-permute-start | bytes 393224 | tf_op jit(solution)/shard_map/ppermute | solution.py:26
  268.8 12.0 %collective-permute-start.31 = (bf16[16,4096]{1,0:T(8,128)(2,1)S(1)}, bf16[16,4096]{1,0:T(8,128)(2,1)S(1)}, u32[]{:S(2)}, u32[]{:S(2)}) collective-permute-start(bf16[16,4096]{1,0:T(8,128)(2,1)S(1)} %get-tuple-element.132.refs_0_.refs_4_), channel_id=1, source_target_pairs={{0,16},{8,24},{16,0},{24,8},{1,17},{9,25},{17,1},{25,9},{2,18},{10... | collective-permute-start | bytes 393224 | tf_op jit(solution)/shard_map/ppermute | solution.py:26
  270.8 10.1 %collective-permute-start.32 = (bf16[16,4096]{1,0:T(8,128)(2,1)S(1)}, bf16[16,4096]{1,0:T(8,128)(2,1)S(1)}, u32[]{:S(2)}, u32[]{:S(2)}) collective-permute-start(bf16[16,4096]{1,0:T(8,128)(2,1)S(1)} %get-tuple-element.132.refs_0_.refs_4_), channel_id=1, source_target_pairs={{0,24},{8,16},{16,8},{24,0},{1,25},{9,17},{17,9},{25,1},{2,26},{10... | collective-permute-start | bytes 393224 | tf_op jit(solution)/shard_map/ppermute | solution.py:26
  281.1 21.8 %collective-permute-start.34 = (bf16[112,4096]{1,0:T(8,128)(2,1)S(1)}, bf16[112,4096]{1,0:T(8,128)(2,1)S(1)}, u32[]{:S(2)}, u32[]{:S(2)}) collective-permute-start(bf16[112,4096]{1,0:T(8,128)(2,1)S(1)} %add_convert_fusion.refs_4_), channel_id=1, source_target_pairs={{8,0},{16,24},{9,1},{17,25},{10,2},{18,26},{11,3},{19,27},{12,4},{... | collective-permute-start | bytes 2752520 | tf_op jit(solution)/shard_map/ppermute | solution.py:506
  311.8 51.6 %copy-start.2 = (f32[16,16384]{1,0:T(8,128)S(1)}, f32[16,16384]{1,0:T(8,128)}, u32[]{:S(2)}) copy-start(f32[16,16384]{1,0:T(8,128)} %copy-done.1) | copy-start | bytes 3145732
  311.9 28.5 %all-to-all-start.1 = ((bf16[8,128,256]{2,1,0:T(8,128)(2,1)}), bf16[8,128,256]{2,1,0:T(8,128)(2,1)}, u32[]{:S(2)}, u32[]{:S(2)}) async-start(bf16[8,128,256]{2,1,0:T(8,128)(2,1)} %third_forward_1.1), calls=%async_computation.1 | async-start | bytes 1048576 | tf_op jit(solution)/shard_map/all_to_all | solution.py:555
  316.2 14.0 %collective-permute-start.35 = (bf16[32,4096]{1,0:T(8,128)(2,1)S(1)}, bf16[32,4096]{1,0:T(8,128)(2,1)S(1)}, u32[]{:S(2)}, u32[]{:S(2)}) collective-permute-start(bf16[32,4096]{1,0:T(8,128)(2,1)S(1)} %copy-done.3), channel_id=1, source_target_pairs={{0,8},{8,0},{16,24},{24,16},{1,9},{9,1},{17,25},{25,17},{2,10},{10... | collective-permute-start | bytes 786440 | tf_op jit(solution)/shard_map/ppermute | solution.py:26
  319.0 21.3 %collective-permute-start.36 = (bf16[32,4096]{1,0:T(8,128)(2,1)S(1)}, bf16[32,4096]{1,0:T(8,128)(2,1)S(1)}, u32[]{:S(2)}, u32[]{:S(2)}) collective-permute-start(bf16[32,4096]{1,0:T(8,128)(2,1)S(1)} %copy-done.3), channel_id=1, source_target_pairs={{0,16},{8,24},{16,0},{24,8},{1,17},{9,25},{17,1},{25,9},{2,18},{10... | collective-permute-start | bytes 786440 | tf_op jit(solution)/shard_map/ppermute | solution.py:26
  319.0 21.3 %collective-permute-start.37 = (bf16[32,4096]{1,0:T(8,128)(2,1)S(1)}, bf16[32,4096]{1,0:T(8,128)(2,1)S(1)}, u32[]{:S(2)}, u32[]{:S(2)}) collective-permute-start(bf16[32,4096]{1,0:T(8,128)(2,1)S(1)} %copy-done.3), channel_id=1, source_target_pairs={{0,24},{8,16},{16,8},{24,0},{1,25},{9,17},{17,9},{25,1},{2,26},{10... | collective-permute-start | bytes 786440 | tf_op jit(solution)/shard_map/ppermute | solution.py:26
  342.0 1.3 collective-permute-start.38
  343.3 4.3 %collective-permute-start.39 = (f32[128,6]{1,0:T(8,128)S(1)}, f32[128,6]{1,0:T(8,128)S(1)}, u32[]{:S(2)}, u32[]{:S(2)}) collective-permute-start(f32[128,6]{1,0:T(8,128)S(1)} %add.169), channel_id=1, source_target_pairs={{0,2},{1,3},{2,0},{3,1},{4,6},{5,7},{6,4},{7,5},{8,10},{9,11},{10,... | collective-permute-start | bytes 9224 | tf_op jit(solution)/shard_map/ppermute | solution.py:26
  345.2 4.3 %collective-permute-start.40 = (f32[128,6]{1,0:T(8,128)S(1)}, f32[128,6]{1,0:T(8,128)S(1)}, u32[]{:S(2)}, u32[]{:S(2)}) collective-permute-start(f32[128,6]{1,0:T(8,128)S(1)} %add.169), channel_id=1, source_target_pairs={{0,4},{1,5},{2,6},{3,7},{4,0},{5,1},{6,2},{7,3},{8,12},{9,13},{10,... | collective-permute-start | bytes 9224 | tf_op jit(solution)/shard_map/ppermute | solution.py:26
  346.7 5.2 %collective-permute-start.41 = (f32[128,6]{1,0:T(8,128)S(1)}, f32[128,6]{1,0:T(8,128)S(1)}, u32[]{:S(2)}, u32[]{:S(2)}) collective-permute-start(f32[128,6]{1,0:T(8,128)S(1)} %add.169), channel_id=1, source_target_pairs={{0,6},{1,7},{2,4},{3,5},{4,2},{5,3},{6,0},{7,1},{8,14},{9,15},{10,... | collective-permute-start | bytes 9224 | tf_op jit(solution)/shard_map/ppermute | solution.py:26
  351.9 7.8 %collective-permute-start.42 = (f32[128,6]{1,0:T(8,128)S(1)}, f32[128,6]{1,0:T(8,128)S(1)}, u32[]{:S(2)}, u32[]{:S(2)}) collective-permute-start(f32[128,6]{1,0:T(8,128)S(1)} %add_add_fusion.5), channel_id=1, source_target_pairs={{0,8},{8,0},{16,24},{24,16},{1,9},{9,1},{17,25},{25,17},{2,10},{10... | collective-permute-start | bytes 9224 | tf_op jit(solution)/shard_map/ppermute | solution.py:26
  357.1 6.4 %collective-permute-start.43 = (f32[128,6]{1,0:T(8,128)S(1)}, f32[128,6]{1,0:T(8,128)S(1)}, u32[]{:S(2)}, u32[]{:S(2)}) collective-permute-start(f32[128,6]{1,0:T(8,128)S(1)} %add_add_fusion.5), channel_id=1, source_target_pairs={{0,16},{8,24},{16,0},{24,8},{1,17},{9,25},{17,1},{25,9},{2,18},{10... | collective-permute-start | bytes 9224 | tf_op jit(solution)/shard_map/ppermute | solution.py:26
  357.1 6.4 %collective-permute-start.44 = (f32[128,6]{1,0:T(8,128)S(1)}, f32[128,6]{1,0:T(8,128)S(1)}, u32[]{:S(2)}, u32[]{:S(2)}) collective-permute-start(f32[128,6]{1,0:T(8,128)S(1)} %add_add_fusion.5), channel_id=1, source_target_pairs={{0,24},{8,16},{16,8},{24,0},{1,25},{9,17},{17,9},{25,1},{2,26},{10... | collective-permute-start | bytes 9224 | tf_op jit(solution)/shard_map/ppermute | solution.py:26
  (27 other events, 562.2 us)

commit v5 on v4

--- a/solution.py
+++ b/solution.py
@@ -246,8 +246,10 @@
     else:
         g, total, rows, held, sems = refs
     t, unit = pieces[0].shape[0], pieces[0].shape[1] // 2
-    span = inner[0].shape[1]
-    count = chunks * span // unit
+    ends = [0]
+    for x in inner:
+        ends.append(ends[-1] + x.shape[1])
+    count = ends[-1] // unit
 
     def prepare():
         for j, half in [(j, half) for j in range(n) for half in range(2)]:
@@ -259,7 +261,7 @@
                 rows[:t, here] = pieces[j][:, half * unit : (half + 1) * unit]
 
         for j in range(chunks):
-            here = slice(j * span, (j + 1) * span)
+            here = slice(ends[j], ends[j + 1])
 
             @pl.when(off[n] == 1)
             def _():
@@ -285,7 +287,7 @@
     r = t + inner[0].shape[0]
     pb, kb = block_of(people, 1024), block_of(unit, 2048)
     operands = [*pieces, *inner, *outer, *([] if acc is None else [acc]), genotypes]
-    span = len(inner) * inner[0].shape[1]
+    span = sum(x.shape[1] for x in inner)
     scratch = [pltpu.VMEM((r, span), BF16), *ring(pb, kb)]
     if acc is None:
         shape = jax.ShapeDtypeStruct((people, r), F32)
@@ -335,7 +337,7 @@
     stream(place, held, sems, pieces * steps * blocks, lambda: None, use)
 
 
-def back_body(n, unit, t, base, off, rows, g, *refs):
+def back_body(n, unit, t, base, cut, off, rows, g, *refs):
     refs = list(refs)
     held, sems = refs[-2:]
     if t == rows.shape[0]:
@@ -354,13 +356,13 @@
                 cols = pl.ds(pl.multiple_of((place - first) * unit, unit), unit)
                 return pltpu.make_async_copy(part, whole.at[:, cols], sent.at[j])
 
-            @pl.when(place < n // 2)
+            @pl.when(place < cut)
             def _():
                 copy(lower, 0).start()
 
-            @pl.when(place >= n // 2)
+            @pl.when(place >= cut)
             def _():
-                copy(upper, n // 2).start()
+                copy(upper, cut).start()
 
             copies.append(pltpu.make_async_copy(part, lower.at[:, pl.ds(0, unit)], sent.at[j]))
     span = outs[0].shape[1]
@@ -370,7 +372,7 @@
         copy.wait()
 
 
-def backward(rows, places, genotypes, unit, t, base, arrays, name):
+def backward(rows, places, genotypes, unit, t, base, cut, arrays, name):
     people = genotypes.shape[0]
     r, n = rows.shape[0], places.shape[0]
     pk, mb = block_of(people, 1024), block_of(unit, 2048)
@@ -379,10 +381,10 @@
     scratch = [pltpu.VMEM((r, n * unit), F32)]
     if t != r:
         out_specs += [ANY] * 2
-        out_shape += [jax.ShapeDtypeStruct((r - t, n * unit // 2), BF16)] * 2
+        out_shape += [jax.ShapeDtypeStruct((r - t, c * unit), BF16) for c in (cut, n - cut)]
         scratch += [pltpu.VMEM((r - t, n * unit), BF16), pltpu.SemaphoreType.DMA((n,))]
     return pl.pallas_call(
-        functools.partial(back_body, n, unit, t, base),
+        functools.partial(back_body, n, unit, t, base, cut),
         grid_spec=pltpu.PrefetchScalarGridSpec(
             num_scalar_prefetch=1,
             grid=(),
@@ -425,8 +427,8 @@
     for j, half in [(j, half) for j in range(n) for half in range(2)]:
         here = pl.ds(pl.multiple_of((half * n + off[j]) * unit, unit), unit)
         part = slice(half * unit, (half + 1) * unit)
-        start = start_hi[j][:, part].astype(F32) + low[j][:t, part].astype(F32)
-        back = back_hi[j][:, part].astype(F32) + low[j][t:, part].astype(F32)
+        start = start_hi[j][:, part].astype(F32) + low[j][:, part].astype(F32)
+        back = back_hi[j][:, part].astype(F32)
         middle = centre[:, here]
         made = middle + start_coef * start - back_coef * back
         lmmse[:, here] = made
@@ -478,13 +480,15 @@
     pred_x = rows[traits:].astype(F32)
     rows = lax.all_gather(rows, "marker", axis=1, tiled=True)
     starts, chunks = [], []
-    for half in range(2):
+    for half, cut in enumerate((samples - 1, some)):
+        base = half * samples
         *parts, lower, upper = backward(
-            rows, order + half * samples, genotypes, unit, traits, half * samples, samples, f"first_back_{half}"
+            rows, order + base, genotypes, unit, traits, base, cut, samples, f"first_back_{half}"
         )
         starts.append([swap(part, "sample", k) if k else part for k, part in enumerate(parts)])
         chunks += [lower, upper]
         rows, *_ = lax.optimization_barrier((rows, lower))
+    chunks = [chunks[0], jnp.concatenate(chunks[1:3], axis=1), chunks[3]]
 
     def add(x, y):
         return (x.astype(F32) + y.astype(F32)).astype(BF16)
@@ -505,7 +509,7 @@
     def outward(x):
         return lax.ppermute(x, "sample", [(1, 0), (2, 3)])
 
-    pair, full, ends = [None] * 4, [None] * 4, [None] * 4
+    pair, full, ends = [None] * 3, [None] * 3, [None] * 3
     pair[0] = inward(0)
     scale = (noise_precision / people)[:, None]
     start = scale * jnp.concatenate([tree(parts) for parts in starts], axis=1)
@@ -514,43 +518,36 @@
     start_high = start_high.astype(BF16)
 
     start_pieces = [swap(start_high, "sample", k) if k else start_high for k in range(samples)]
-    start_pieces[0], start_pieces[1], chunks[1] = tie(
-        (start_pieces[0], start_pieces[1], chunks[1]), pair[0], start_high
-    )
-    value = narrow_forward(start_pieces[:some], near, None, genotypes, "second_forward_near")
-    value, *start_pieces = tie((value, *start_pieces))
-    full[0], pair[1] = across(pair[0], value), inward(1, value)
+    *start_pieces, pair[0], chunks[1] = tie((*start_pieces, pair[0], chunks[1]))
+    full[0], pair[1] = across(pair[0]), inward(1)
+    both = jnp.concatenate([near, far])
+    value = narrow_forward(start_pieces, both, None, genotypes, "second_forward")
     value, chunks[2] = tie((value, chunks[2]), full[0], pair[1])
     ends[0], full[1], pair[2] = outward(full[0]), across(pair[1]), inward(2)
-    value = narrow_forward(start_pieces[some:], far, value, genotypes, "second_forward_far")
-    value, chunks[3] = tie((value, chunks[3]), full[1], pair[2], ends[0])
-    ends[1], full[2], pair[3] = outward(full[1]), across(pair[2]), inward(3)
     value = sum_marker(value)
     kept_s = lax.dynamic_slice_in_dim(value, column * share, share, 1)
     rows = value.astype(BF16)
-    parts = backward(rows, far, genotypes, unit, traits, 0, some, "second_back_far")
+    parts = backward(rows, far, genotypes, unit, traits, 0, 0, some, "second_back_far")
     sent = [swap(part, "sample", k + some) for k, part in enumerate(parts)]
-    (rows,) = tie((rows,), full[2], pair[3], ends[1], *parts)
+    (rows,) = tie((rows,), full[1], pair[2], ends[0], *parts)
+    ends[1] = outward(full[1])
+    parts = backward(rows, near, genotypes, unit, traits, 0, 0, some, "second_back_near")
+    sent = [swap(part, "sample", k) if k else part for k, part in enumerate(parts)] + sent
+    back_high = tree(list(tie(sent, ends[1]))).astype(BF16)
+    back = back_high.astype(F32)
+    back_pieces = [swap(back_high, "sample", k) if k else back_high for k in range(samples)]
+    full[2] = across(pair[2], *back_pieces)
     ends[2] = outward(full[2])
-    parts = backward(rows, near, genotypes, unit, traits, 0, some, "second_back_near")
-    sent = [swap(part, "sample", k) if k else part for k, part in enumerate(parts)] + sent
-    back = tree(list(tie(sent, ends[2])))
-    back_high = lax.reduce_precision(back, 8, 7)
-    back_low = (back - back_high).astype(BF16)
-    back_high = back_high.astype(BF16)
-    back_pieces = [swap(back_high, "sample", k) if k else back_high for k in range(samples)]
-    full[3] = across(pair[3], *back_pieces)
-    ends[3] = outward(full[3])
 
     inner = ((me == 1) | (me == 2)).astype(jnp.int32)
     places = jnp.concatenate([order, inner[None]])
     total = wide_forward(
-        back_pieces, full[:3], ends[:3], places, 0, None, genotypes, columns, "third_forward_0"
-    )
-    total, low = tie((total, jnp.concatenate([start_low, back_low], axis=0)), ends[3])
-    low_pieces = [swap(low, "sample", k) if k else low for k in range(samples)]
+        back_pieces, full[:2], ends[:2], places, 0, None, genotypes, columns, "third_forward_0"
+    )
+    (start_low,) = tie((start_low,), total)
+    low_pieces = [swap(start_low, "sample", k) if k else start_low for k in range(samples)]
     value = wide_forward(
-        back_pieces, full[3:], ends[3:], places, 3 * some, total, genotypes, columns, "third_forward_1"
+        back_pieces, full[2:], ends[2:], places, 3 * some, total, genotypes, columns, "third_forward_1"
     )
     (last,) = tie((lax.all_to_all(value, "marker", 0, 0),), *low_pieces)
     last = jnp.sum(last.astype(F32), axis=0)

time: 368 us -> 367 us (level)
  waiting for transfers between devices: 110 us -> 119 us
  other arithmetic: 23.6 us -> 18.5 us
  Pallas kernels: 134 us -> 130 us
    ppermute x8 -> x6, waiting for transfers between devices: 1.02 us -> 17.3 us  [hop(): y = lax.ppermute(x, 'sample', pairs)]
    ppermute x4 -> x3, waiting for transfers between devices: 3.83 us -> 0.01 us  [outward(): return lax.ppermute(x, 'sample', [(1, 0), (2, 3)])]
    pallas_call x2 -> x1, Pallas kernels: 25.4 us -> 22.3 us  [narrow_forward(): pl.pallas_call(functools.partial(narrow_body, n, unit, acc is not None),...]
    convert_element_type x8 -> x6, other arithmetic: 8.79 us -> 5.85 us  [add(): return (x.astype(F32) + y.astype(F32)).astype(BF16)]
    ppermute x8 -> x6, starting transfers between devices: 20.1 us -> 19.1 us  [hop(): y = lax.ppermute(x, 'sample', pairs)]
  transfers between devices with their start and end apart: 47 -> 44, of which waited for: 23 -> 25; matrix products, arithmetic and copies ran while one was open for 5% -> 4% of each run, Pallas kernels for 23% -> 21%
where the time goes in v5:
time: 367 us; the launch traced here: 366 us
  Pallas kernels  130 us (35%)
  waiting for transfers between devices  119 us (32%)
  starting transfers between devices  82.6 us (23%)
  other arithmetic  18.5 us (5%)
  blocking collectives  9.95 us (3%)
  local copies, waits for them, and re-layouts  5.3 us (1%)
    ppermute x33, waiting for transfers between devices, swap(): return lax.ppermute(x, axis, [(i, i ^ bits) for i in range(n)])  91 us
    ppermute x33, starting transfers between devices, swap(): return lax.ppermute(x, axis, [(i, i ^ bits) for i in range(n)])  52.3 us
    pallas_call x4, Pallas kernels, backward(): pl.pallas_call(functools.partial(back_body, n, unit, t, base, cut), grid_...  49.9 us
    pallas_call x2, Pallas kernels, wide_forward(): pl.pallas_call(functools.partial(wide_body, n, begin, len(inner), acc is...  28.9 us
    pallas_call x1, Pallas kernels, first_forward(): pl.pallas_call(functools.partial(first_body, markers * columns), grid_spe...  24.5 us
    pallas_call x1, Pallas kernels, narrow_forward(): pl.pallas_call(functools.partial(narrow_body, n, unit, acc is not None),...  22.3 us
    ppermute x6, starting transfers between devices, hop(): y = lax.ppermute(x, 'sample', pairs)  19.1 us
    ppermute x6, waiting for transfers between devices, hop(): y = lax.ppermute(x, 'sample', pairs)  17.3 us
  transfers between devices with their start and end apart: 44, of which 25 were waited for; matrix products, arithmetic and copies ran while one was open for 4% of the time, Pallas kernels for 21%

profile of v5, /device:TPU:0, one launch (start us, length us, event | category | flops | bytes accessed | tf_op | source)
XLA Modules:
  0.0 365.9 jit_solution(3626431626709667017)
XLA Ops:
  4.7 2.8 collective-permute-start.1
  9.1 3.5 convert_element_type.83.probes
  14.3 24.5 %first_forward.1 = (bf16[8,144,256]{2,1,0:T(8,128)(2,1)}, f32[16,16384]{1,0:T(8,128)S(1)}) custom-call(s32[1]{0:T(128)} %constant.8.clone.1.off, f32[16,16384]{1,0:T(8,128)S(1)} %copy-done, f32[16,3]{1,0:T(8,128)S(1)} %copy.49.cols, f32[16,1]{1,0:T(8,128)S(1)} %get-tuple-element.107.slopes, bf16[112,16384]{1,0:T(8,128)(2,1)S(1)} %convert_element_type.83.probes, ...), custom_call_target="tpu_custom_call" | custom-call | flops 8589934592 | bytes 67108864 | tf_op jit(solution)/shard_map/first_forward/pallas_call | solution.py:174
  39.8 3.5 all-to-all-start
  43.4 10.3 %all-to-all-done = bf16[8,144,256]{2,1,0:T(8,128)(2,1)S(1)} async-done(((bf16[8,144,256]{2,1,0:T(8,128)(2,1)}), bf16[8,144,256]{2,1,0:T(8,128)(2,1)S(1)}, u32[]{:S(2)}, u32[]{:S(2)}) %all-to-all-start) | async-done | bytes 589856 | tf_op jit(solution)/shard_map/all_to_all | solution.py:476
  54.6 9.9 %all_gather.3.rows = bf16[128,2048]{1,0:T(8,128)(2,1)S(1)} all-gather(bf16[128,256]{1,0:T(8,128)(2,1)S(1)} %pad_maximum_fusion.2), channel_id=1, replica_groups=mesh['sample'=4,'marker'=8] {'marker'}, dimensions={1}, use_global_device_ids=true | all-gather | bytes 589824 | tf_op jit(solution)/shard_map/all_gather | solution.py:481
  64.5 12.8 %first_back_0.1 = (f32[16,2048]{1,0:T(8,128)S(1)}, f32[16,2048]{1,0:T(8,128)S(1)}, f32[16,2048]{1,0:T(8,128)S(1)}, f32[16,2048]{1,0:T(8,128)S(1)}, bf16[112,6144...) custom-call(s32[4]{0:T(128)S(1)} %iota_xor_fusion.off, bf16[128,2048]{1,0:T(8,128)(2,1)S(1)} %all_gather.3.rows, ...), custom_call_target="tpu_custom_call" | custom-call | flops 4294967296 | bytes 33554432 | tf_op jit(solution)/shard_map/first_back_0/pallas_call | solution.py:386
  77.3 3.6 collective-permute-start.13
  81.0 3.0 collective-permute-start.5
  85.3 12.8 %first_back_1.1 = (f32[16,2048]{1,0:T(8,128)S(1)}, f32[16,2048]{1,0:T(8,128)S(1)}, f32[16,2048]{1,0:T(8,128)S(1)}, f32[16,2048]{1,0:T(8,128)S(1)}, bf16[112,4096...) custom-call(s32[4]{0:T(128)S(1)} %broadcast_add_fusion.off, bf16[128,2048]{1,0:T(8,128)(2,1)S(1)} %all_gather.3.rows, ...), custom_call_target="tpu_custom_call" | custom-call | flops 4294967296 | bytes 33554432 | tf_op jit(solution)/shard_map/first_back_1/pallas_call | solution.py:386
  99.6 14.6 %collective-permute-done.4 = f32[16,2048]{1,0:T(8,128)S(1)} collective-permute-done((f32[16,2048]{1,0:T(8,128)S(1)}, f32[16,2048]{1,0:T(8,128)S(1)}, u32[]{:S(2)}, u32[]{:S(2)}) %collective-permute-start.4) | collective-permute-done | bytes 131104 | tf_op jit(solution)/shard_map/ppermute | solution.py:26
  114.1 3.5 collective-permute-start.8
  117.6 1.8 collective-permute-start.9
  119.4 3.3 collective-permute-done.6
  122.8 2.8 collective-permute-done.8
  125.6 5.1 %collective-permute-done.9 = f32[16,2048]{1,0:T(8,128)S(1)} collective-permute-done((f32[16,2048]{1,0:T(8,128)S(1)}, f32[16,2048]{1,0:T(8,128)S(1)}, u32[]{:S(2)}, u32[]{:S(2)}) %collective-permute-start.9) | collective-permute-done | bytes 131104 | tf_op jit(solution)/shard_map/ppermute | solution.py:26
  131.5 3.2 collective-permute-start.10
  134.7 2.4 collective-permute-start.12
  137.4 2.0 collective-permute-done.10.refs_1_
  139.4 7.9 %collective-permute-done.11.refs_2_ = bf16[16,4096]{1,0:T(8,128)(2,1)S(1)} collective-permute-done((bf16[16,4096]{1,0:T(8,128)(2,1)S(1)}, bf16[16,4096]{1,0:T(8,128)(2,1)S(1)}, u32[]{:S(2)}, u32[]{:S(2)}) %collective-permute-start.11) | collective-permute-done | bytes 131104 | tf_op jit(solution)/shard_map/ppermute | solution.py:26
  147.3 5.4 %collective-permute-start.15 = (bf16[112,6144]{1,0:T(8,128)(2,1)}, bf16[112,6144]{1,0:T(8,128)(2,1)}, u32[]{:S(2)}, u32[]{:S(2)}) collective-permute-start(bf16[112,6144]{1,0:T(8,128)(2,1)} %pad_maximum_fusion), channel_id=1, source_target_pairs={{0,8},{24,16},{1,9},{25,17},{2,10},{26,18},{3,11},{27,19},{4,12},{... | collective-permute-start | bytes 4128776 | tf_op jit(solution)/shard_map/ppermute | solution.py:500
  155.0 22.3 %second_forward.1 = f32[16,2048]{1,0:T(8,128)S(1)} custom-call(s32[8]{0:T(128)S(1)} %pad_add_fusion.2.off, bf16[16,4096]{1,0:T(8,128)(2,1)S(1)} %get-tuple-element.65.refs_0_, bf16[16,4096]{1,0:T(8,128)(2,1)S(1)} %collective-permute-done.10.refs_1_, bf16[16,4096]{1,0:T(8,128)(2,1)S(1)} %collective-permute-done.11.refs_2_, ...), custom_call_target="tpu_custom_call" | custom-call | flops 1073741824 | bytes 67108864 | tf_op jit(solution)/shard_map/second_forward/pallas_call | solution.py:222
  177.4 3.3 collective-permute-done.15
  180.7 2.2 add_convert_fusion.1
  185.4 6.9 %collective-permute-start.21 = (bf16[112,4096]{1,0:T(8,128)(2,1)S(1)}, bf16[112,4096]{1,0:T(8,128)(2,1)S(1)}, u32[]{:S(2)}, u32[]{:S(2)}) collective-permute-start(bf16[112,4096]{1,0:T(8,128)(2,1)S(1)} %get-tuple-element.80), channel_id=1, source_target_pairs={{0,8},{24,16},{1,9},{25,17},{2,10},{26,18},{3,11},{27,19},{4,12},{... | collective-permute-start | bytes 2752520 | tf_op jit(solution)/shard_map/ppermute | solution.py:500
  195.9 14.0 %collective-permute-done.21 = bf16[112,4096]{1,0:T(8,128)(2,1)S(1)} collective-permute-done((bf16[112,4096]{1,0:T(8,128)(2,1)S(1)}, bf16[112,4096]{1,0:T(8,128)(2,1)S(1)}, u32[]{:S(2)}, u32[]{:S(2)}) %collective-permute-start.21) | collective-permute-done | bytes 917536 | tf_op jit(solution)/shard_map/ppermute | solution.py:500
  214.0 1.8 collective-permute-done.19
  216.5 12.2 %second_back_far.1 = (f32[16,4096]{1,0:T(8,128)S(1)}, f32[16,4096]{1,0:T(8,128)S(1)}) custom-call(s32[4]{0:T(128)S(1)} %reshape.28.off, bf16[16,2048]{1,0:T(8,128)(2,1)S(1)} %get-tuple-element.84.rows, bf16[2048,16384]{1,0:T(8,128)(2,1)} %refs_7_.1), custom_call_target="tpu_custom_call" | custom-call | flops 536870912 | bytes 33554432 | tf_op jit(solution)/shard_map/second_back_far/pallas_call | solution.py:386
  228.7 8.3 %collective-permute-start.24 = (f32[16,4096]{1,0:T(8,128)S(1)}, f32[16,4096]{1,0:T(8,128)S(1)}, u32[]{:S(2)}, u32[]{:S(2)}) collective-permute-start(f32[16,4096]{1,0:T(8,128)S(1)} %get-tuple-element.82), channel_id=1, source_target_pairs={{0,16},{8,24},{16,0},{24,8},{1,17},{9,25},{17,1},{25,9},{2,18},{10... | collective-permute-start | bytes 786440 | tf_op jit(solution)/shard_map/ppermute | solution.py:26
  238.1 12.2 %second_back_near.1 = (f32[16,4096]{1,0:T(8,128)S(1)}, f32[16,4096]{1,0:T(8,128)S(1)}) custom-call(s32[4]{0:T(128)S(1)} %reshape.27.off, bf16[16,2048]{1,0:T(8,128)(2,1)S(1)} %get-tuple-element.84.rows, bf16[2048,16384]{1,0:T(8,128)(2,1)} %refs_7_.1), custom_call_target="tpu_custom_call" | custom-call | flops 536870912 | bytes 33554432 | tf_op jit(solution)/shard_map/second_back_near/pallas_call | solution.py:386
  250.4 10.8 %collective-permute-done.24 = f32[16,4096]{1,0:T(8,128)S(1)} collective-permute-done((f32[16,4096]{1,0:T(8,128)S(1)}, f32[16,4096]{1,0:T(8,128)S(1)}, u32[]{:S(2)}, u32[]{:S(2)}) %collective-permute-start.24) | collective-permute-done | bytes 262176 | tf_op jit(solution)/shard_map/ppermute | solution.py:26
  261.3 11.9 %collective-permute-done.23 = f32[16,4096]{1,0:T(8,128)S(1)} collective-permute-done((f32[16,4096]{1,0:T(8,128)S(1)}, f32[16,4096]{1,0:T(8,128)S(1)}, u32[]{:S(2)}, u32[]{:S(2)}) %collective-permute-start.23) | collective-permute-done | bytes 262176 | tf_op jit(solution)/shard_map/ppermute | solution.py:26
  274.1 3.2 collective-permute-start.28
  278.5 2.8 collective-permute-done.27.refs_1_.refs_5_
  281.2 6.0 %collective-permute-done.28.refs_2_.refs_6_ = bf16[16,4096]{1,0:T(8,128)(2,1)S(1)} collective-permute-done((bf16[16,4096]{1,0:T(8,128)(2,1)S(1)}, bf16[16,4096]{1,0:T(8,128)(2,1)S(1)}, u32[]{:S(2)}, u32[]{:S(2)}) %collective-permute-start.28) | collective-permute-done | bytes 131104 | tf_op jit(solution)/shard_map/ppermute | solution.py:26
  289.7 2.3 multiply_reduce_fusion
  293.5 18.6 %third_forward_0.1.refs_6_ = f32[2048,128]{1,0:T(8,128)S(1)} custom-call(s32[5]{0:T(128)S(1)} %pad_add_fusion.3.off, bf16[16,4096]{1,0:T(8,128)(2,1)S(1)} %get-tuple-element.108.refs_0_.refs_4_, bf16[16,4096]{1,0:T(8,128)(2,1)S(1)} %collective-permute-done.27.refs_1_.refs_5_, bf16[16,4096]{1,0:T(8,128)(2,1)S(1)} %collective-permute-done.28.refs_2_.refs_6_, ...), custom_call_target="tpu_custom_call" | custom-call | flops 6442450944 | bytes 50331648 | tf_op jit(solution)/shard_map/third_forward_0/pallas_call | solution.py:297
  312.1 10.3 %third_forward_1.1 = bf16[8,128,256]{2,1,0:T(8,128)(2,1)} custom-call(s32[5]{0:T(128)S(1)} %pad_add_fusion.3.off, bf16[16,4096]{1,0:T(8,128)(2,1)S(1)} %get-tuple-element.108.refs_0_.refs_4_, bf16[16,4096]{1,0:T(8,128)(2,1)S(1)} %collective-permute-done.27.refs_1_.refs_5_, bf16[16,4096]{1,0:T(8,128)(2,1)S(1)} %collective-permute-done.28.refs_2_.refs_6_, ...), custom_call_target="tpu_custom_call" | custom-call | flops 2147483648 | bytes 16777216 | tf_op jit(solution)/shard_map/third_forward_1/pallas_call | solution.py:297
  322.5 3.6 all-to-all-start.1
  326.2 3.6 collective-permute-start.32
  333.1 2.8 collective-permute-done.32.refs_9_
  335.9 6.8 %collective-permute-done.33.refs_10_ = bf16[16,4096]{1,0:T(8,128)(2,1)S(1)} collective-permute-done((bf16[16,4096]{1,0:T(8,128)(2,1)S(1)}, bf16[16,4096]{1,0:T(8,128)(2,1)S(1)}, u32[]{:S(2)}, u32[]{:S(2)}) %collective-permute-start.33) | collective-permute-done | bytes 131104 | tf_op jit(solution)/shard_map/ppermute | solution.py:26
  344.6 1.9 collective-permute-start.36
  349.0 1.9 collective-permute-done.37
  350.8 2.4 collective-permute-done.38
  353.2 2.4 collective-permute-start.39
  358.3 3.2 collective-permute-done.40
  362.8 3.1 finish.1
  (165 shorter events, 44.9 us)
Async XLA Ops:
  3.4 1.3 collective-permute-start
  4.7 7.9 %collective-permute-start.1 = (f32[16,1]{1,0:T(8,128)S(1)}, f32[16,1]{1,0:T(8,128)S(1)}, u32[]{:S(2)}, u32[]{:S(2)}) collective-permute-start(f32[16,1]{1,0:T(8,128)S(1)} %add.129), channel_id=1, source_target_pairs={{0,2},{1,3},{2,0},{3,1},{4,6},{5,7},{6,4},{7,5},{8,10},{9,11},{10,... | collective-permute-start | bytes 200 | tf_op jit(solution)/shard_map/ppermute | solution.py:26
  7.5 5.0 %collective-permute-start.2 = (f32[16,1]{1,0:T(8,128)S(1)}, f32[16,1]{1,0:T(8,128)S(1)}, u32[]{:S(2)}, u32[]{:S(2)}) collective-permute-start(f32[16,1]{1,0:T(8,128)S(1)} %add.129), channel_id=1, source_target_pairs={{0,4},{1,5},{2,6},{3,7},{4,0},{5,1},{6,2},{7,3},{8,12},{9,13},{10,... | collective-permute-start | bytes 200 | tf_op jit(solution)/shard_map/ppermute | solution.py:26
  9.0 4.5 %collective-permute-start.3 = (f32[16,1]{1,0:T(8,128)S(1)}, f32[16,1]{1,0:T(8,128)S(1)}, u32[]{:S(2)}, u32[]{:S(2)}) collective-permute-start(f32[16,1]{1,0:T(8,128)S(1)} %add.129), channel_id=1, source_target_pairs={{0,6},{1,7},{2,4},{3,5},{4,2},{5,3},{6,0},{7,1},{8,14},{9,15},{10,... | collective-permute-start | bytes 200 | tf_op jit(solution)/shard_map/ppermute | solution.py:26
  39.8 13.9 %all-to-all-start = ((bf16[8,144,256]{2,1,0:T(8,128)(2,1)}), bf16[8,144,256]{2,1,0:T(8,128)(2,1)S(1)}, u32[]{:S(2)}, u32[]{:S(2)}) async-start(bf16[8,144,256]{2,1,0:T(8,128)(2,1)} %get-tuple-element.50), calls=%async_computation | async-start | bytes 1179648 | tf_op jit(solution)/shard_map/all_to_all | solution.py:476
  77.3 59.8 %collective-permute-start.13 = (bf16[112,6144]{1,0:T(8,128)(2,1)S(1)}, bf16[112,6144]{1,0:T(8,128)(2,1)S(1)}, u32[]{:S(2)}, u32[]{:S(2)}) collective-permute-start(bf16[112,6144]{1,0:T(8,128)(2,1)S(1)} %get-tuple-element.61), channel_id=1, source_target_pairs={{0,8},{24,16},{1,9},{25,17},{2,10},{26,18},{3,11},{27,19},{4,12},{... | collective-permute-start | bytes 4128776 | tf_op jit(solution)/shard_map/ppermute | solution.py:500
  80.9 33.2 %collective-permute-start.4 = (f32[16,2048]{1,0:T(8,128)S(1)}, f32[16,2048]{1,0:T(8,128)S(1)}, u32[]{:S(2)}, u32[]{:S(2)}) collective-permute-start(f32[16,2048]{1,0:T(8,128)S(1)} %get-tuple-element.52), channel_id=1, source_target_pairs={{0,8},{8,0},{16,24},{24,16},{1,9},{9,1},{17,25},{25,17},{2,10},{10... | collective-permute-start | bytes 393224 | tf_op jit(solution)/shard_map/ppermute | solution.py:26
  81.0 36.6 %collective-permute-start.5 = (f32[16,2048]{1,0:T(8,128)S(1)}, f32[16,2048]{1,0:T(8,128)S(1)}, u32[]{:S(2)}, u32[]{:S(2)}) collective-permute-start(f32[16,2048]{1,0:T(8,128)S(1)} %get-tuple-element.53), channel_id=1, source_target_pairs={{0,16},{8,24},{16,0},{24,8},{1,17},{9,25},{17,1},{25,9},{2,18},{10... | collective-permute-start | bytes 393224 | tf_op jit(solution)/shard_map/ppermute | solution.py:26
  84.0 38.7 %collective-permute-start.6 = (f32[16,2048]{1,0:T(8,128)S(1)}, f32[16,2048]{1,0:T(8,128)S(1)}, u32[]{:S(2)}, u32[]{:S(2)}) collective-permute-start(f32[16,2048]{1,0:T(8,128)S(1)} %get-tuple-element.54), channel_id=1, source_target_pairs={{0,24},{8,16},{16,8},{24,0},{1,25},{9,17},{17,9},{25,1},{2,26},{10... | collective-permute-start | bytes 393224 | tf_op jit(solution)/shard_map/ppermute | solution.py:26
  98.1 87.2 %copy-start.7 = (bf16[112,4096]{1,0:T(8,128)(2,1)}, bf16[112,4096]{1,0:T(8,128)(2,1)S(1)}, u32[]{:S(2)}) copy-start(bf16[112,4096]{1,0:T(8,128)(2,1)S(1)} %get-tuple-element.80) | copy-start | bytes 2752516
  98.1 24.6 %collective-permute-start.7 = (f32[16,2048]{1,0:T(8,128)S(1)}, f32[16,2048]{1,0:T(8,128)S(1)}, u32[]{:S(2)}, u32[]{:S(2)}) collective-permute-start(f32[16,2048]{1,0:T(8,128)S(1)} %get-tuple-element.58), channel_id=1, source_target_pairs={{0,8},{8,0},{16,24},{24,16},{1,9},{9,1},{17,25},{25,17},{2,10},{10... | collective-permute-start | bytes 393224 | tf_op jit(solution)/shard_map/ppermute | solution.py:26
  114.1 11.5 %collective-permute-start.8 = (f32[16,2048]{1,0:T(8,128)S(1)}, f32[16,2048]{1,0:T(8,128)S(1)}, u32[]{:S(2)}, u32[]{:S(2)}) collective-permute-start(f32[16,2048]{1,0:T(8,128)S(1)} %get-tuple-element.59), channel_id=1, source_target_pairs={{0,16},{8,24},{16,0},{24,8},{1,17},{9,25},{17,1},{25,9},{2,18},{10... | collective-permute-start | bytes 393224 | tf_op jit(solution)/shard_map/ppermute | solution.py:26
  117.6 13.1 %collective-permute-start.9 = (f32[16,2048]{1,0:T(8,128)S(1)}, f32[16,2048]{1,0:T(8,128)S(1)}, u32[]{:S(2)}, u32[]{:S(2)}) collective-permute-start(f32[16,2048]{1,0:T(8,128)S(1)} %get-tuple-element.60), channel_id=1, source_target_pairs={{0,24},{8,16},{16,8},{24,0},{1,25},{9,17},{17,9},{25,1},{2,26},{10... | collective-permute-start | bytes 393224 | tf_op jit(solution)/shard_map/ppermute | solution.py:26
  131.5 7.9 %collective-permute-start.10 = (bf16[16,4096]{1,0:T(8,128)(2,1)S(1)}, bf16[16,4096]{1,0:T(8,128)(2,1)S(1)}, u32[]{:S(2)}, u32[]{:S(2)}) collective-permute-start(bf16[16,4096]{1,0:T(8,128)(2,1)S(1)} %get-tuple-element.65.refs_0_), channel_id=1, source_target_pairs={{0,8},{8,0},{16,24},{24,16},{1,9},{9,1},{17,25},{25,17},{2,10},{10... | collective-permute-start | bytes 393224 | tf_op jit(solution)/shard_map/ppermute | solution.py:26
  134.7 12.6 %collective-permute-start.11 = (bf16[16,4096]{1,0:T(8,128)(2,1)S(1)}, bf16[16,4096]{1,0:T(8,128)(2,1)S(1)}, u32[]{:S(2)}, u32[]{:S(2)}) collective-permute-start(bf16[16,4096]{1,0:T(8,128)(2,1)S(1)} %get-tuple-element.65.refs_0_), channel_id=1, source_target_pairs={{0,16},{8,24},{16,0},{24,8},{1,17},{9,25},{17,1},{25,9},{2,18},{10... | collective-permute-start | bytes 393224 | tf_op jit(solution)/shard_map/ppermute | solution.py:26
  134.7 12.6 %collective-permute-start.12 = (bf16[16,4096]{1,0:T(8,128)(2,1)S(1)}, bf16[16,4096]{1,0:T(8,128)(2,1)S(1)}, u32[]{:S(2)}, u32[]{:S(2)}) collective-permute-start(bf16[16,4096]{1,0:T(8,128)(2,1)S(1)} %get-tuple-element.65.refs_0_), channel_id=1, source_target_pairs={{0,24},{8,16},{16,8},{24,0},{1,25},{9,17},{17,9},{25,1},{2,26},{10... | collective-permute-start | bytes 393224 | tf_op jit(solution)/shard_map/ppermute | solution.py:26
  137.4 39.9 %copy-start.14 = (bf16[112,6144]{1,0:T(8,128)(2,1)}, bf16[112,6144]{1,0:T(8,128)(2,1)S(1)}, u32[]{:S(2)}) copy-start(bf16[112,6144]{1,0:T(8,128)(2,1)S(1)} %add_convert_fusion.3) | copy-start | bytes 4128772
  147.3 33.4 %collective-permute-start.15 = (bf16[112,6144]{1,0:T(8,128)(2,1)}, bf16[112,6144]{1,0:T(8,128)(2,1)}, u32[]{:S(2)}, u32[]{:S(2)}) collective-permute-start(bf16[112,6144]{1,0:T(8,128)(2,1)} %pad_maximum_fusion), channel_id=1, source_target_pairs={{0,8},{24,16},{1,9},{25,17},{2,10},{26,18},{3,11},{27,19},{4,12},{... | collective-permute-start | bytes 4128776 | tf_op jit(solution)/shard_map/ppermute | solution.py:500
  152.7 28.0 %collective-permute-start.14 = (bf16[112,6144]{1,0:T(8,128)(2,1)S(1)}, bf16[112,6144]{1,0:T(8,128)(2,1)}, u32[]{:S(2)}, u32[]{:S(2)}) collective-permute-start(bf16[112,6144]{1,0:T(8,128)(2,1)S(1)} %add_convert_fusion.3), channel_id=1, source_target_pairs={{8,16},{16,8},{9,17},{17,9},{10,18},{18,10},{11,19},{19,11},{12,20... | collective-permute-start | bytes 4128776 | tf_op jit(solution)/shard_map/ppermute | solution.py:500
  182.9 28.5 %collective-permute-start.20 = (bf16[112,6144]{1,0:T(8,128)(2,1)S(1)}, bf16[112,6144]{1,0:T(8,128)(2,1)S(1)}, u32[]{:S(2)}, u32[]{:S(2)}) collective-permute-start(bf16[112,6144]{1,0:T(8,128)(2,1)S(1)} %add_convert_fusion.1), channel_id=1, source_target_pairs={{8,16},{16,8},{9,17},{17,9},{10,18},{18,10},{11,19},{19,11},{12,20... | collective-permute-start | bytes 4128776 | tf_op jit(solution)/shard_map/ppermute | solution.py:500
  185.4 24.6 %collective-permute-start.21 = (bf16[112,4096]{1,0:T(8,128)(2,1)S(1)}, bf16[112,4096]{1,0:T(8,128)(2,1)S(1)}, u32[]{:S(2)}, u32[]{:S(2)}) collective-permute-start(bf16[112,4096]{1,0:T(8,128)(2,1)S(1)} %get-tuple-element.80), channel_id=1, source_target_pairs={{0,8},{24,16},{1,9},{25,17},{2,10},{26,18},{3,11},{27,19},{4,12},{... | collective-permute-start | bytes 2752520 | tf_op jit(solution)/shard_map/ppermute | solution.py:500
  192.2 1.6 collective-permute-start.16
  192.3 45.8 %collective-permute-start.22 = (bf16[112,6144]{1,0:T(8,128)(2,1)S(1)}, bf16[112,6144]{1,0:T(8,128)(2,1)S(1)}, u32[]{:S(2)}, u32[]{:S(2)}) collective-permute-start(bf16[112,6144]{1,0:T(8,128)(2,1)S(1)} %add_convert_fusion.2.refs_4_), channel_id=1, source_target_pairs={{8,0},{16,24},{9,1},{17,25},{10,2},{18,26},{11,3},{19,27},{12,4},{... | collective-permute-start | bytes 4128776 | tf_op jit(solution)/shard_map/ppermute | solution.py:510
  193.8 19.4 %collective-permute-start.17 = (f32[16,2048]{1,0:T(8,128)S(1)}, f32[16,2048]{1,0:T(8,128)S(1)}, u32[]{:S(2)}, u32[]{:S(2)}) collective-permute-start(f32[16,2048]{1,0:T(8,128)S(1)} %add.146), channel_id=1, source_target_pairs={{0,2},{1,3},{2,0},{3,1},{4,6},{5,7},{6,4},{7,5},{8,10},{9,11},{10,... | collective-permute-start | bytes 393224 | tf_op jit(solution)/shard_map/ppermute | solution.py:26
  195.4 18.6 %collective-permute-start.18 = (f32[16,2048]{1,0:T(8,128)S(1)}, f32[16,2048]{1,0:T(8,128)S(1)}, u32[]{:S(2)}, u32[]{:S(2)}) collective-permute-start(f32[16,2048]{1,0:T(8,128)S(1)} %add.146), channel_id=1, source_target_pairs={{0,4},{1,5},{2,6},{3,7},{4,0},{5,1},{6,2},{7,3},{8,12},{9,13},{10,... | collective-permute-start | bytes 393224 | tf_op jit(solution)/shard_map/ppermute | solution.py:26
  209.9 5.9 %collective-permute-start.19 = (f32[16,2048]{1,0:T(8,128)S(1)}, f32[16,2048]{1,0:T(8,128)S(1)}, u32[]{:S(2)}, u32[]{:S(2)}) collective-permute-start(f32[16,2048]{1,0:T(8,128)S(1)} %add.146), channel_id=1, source_target_pairs={{0,6},{1,7},{2,4},{3,5},{4,2},{5,3},{6,0},{7,1},{8,14},{9,15},{10,... | collective-permute-start | bytes 393224 | tf_op jit(solution)/shard_map/ppermute | solution.py:26
  211.7 61.4 %collective-permute-start.26 = (bf16[112,6144]{1,0:T(8,128)(2,1)S(1)}, bf16[112,6144]{1,0:T(8,128)(2,1)S(1)}, u32[]{:S(2)}, u32[]{:S(2)}) collective-permute-start(bf16[112,6144]{1,0:T(8,128)(2,1)S(1)} %add_convert_fusion.refs_5_), channel_id=1, source_target_pairs={{8,0},{16,24},{9,1},{17,25},{10,2},{18,26},{11,3},{19,27},{12,4},{... | collective-permute-start | bytes 4128776 | tf_op jit(solution)/shard_map/ppermute | solution.py:510
  213.3 65.2 %collective-permute-start.30 = (bf16[112,4096]{1,0:T(8,128)(2,1)S(1)}, bf16[112,4096]{1,0:T(8,128)(2,1)S(1)}, u32[]{:S(2)}, u32[]{:S(2)}) collective-permute-start(bf16[112,4096]{1,0:T(8,128)(2,1)S(1)} %add_convert_fusion.5), channel_id=1, source_target_pairs={{8,16},{16,8},{9,17},{17,9},{10,18},{18,10},{11,19},{19,11},{12,20... | collective-permute-start | bytes 2752520 | tf_op jit(solution)/shard_map/ppermute | solution.py:500
  228.7 32.6 %collective-permute-start.24 = (f32[16,4096]{1,0:T(8,128)S(1)}, f32[16,4096]{1,0:T(8,128)S(1)}, u32[]{:S(2)}, u32[]{:S(2)}) collective-permute-start(f32[16,4096]{1,0:T(8,128)S(1)} %get-tuple-element.82), channel_id=1, source_target_pairs={{0,16},{8,24},{16,0},{24,8},{1,17},{9,25},{17,1},{25,9},{2,18},{10... | collective-permute-start | bytes 786440 | tf_op jit(solution)/shard_map/ppermute | solution.py:26
  236.9 24.3 %collective-permute-start.25 = (f32[16,4096]{1,0:T(8,128)S(1)}, f32[16,4096]{1,0:T(8,128)S(1)}, u32[]{:S(2)}, u32[]{:S(2)}) collective-permute-start(f32[16,4096]{1,0:T(8,128)S(1)} %get-tuple-element.83), channel_id=1, source_target_pairs={{0,24},{8,16},{16,8},{24,0},{1,25},{9,17},{17,9},{25,1},{2,26},{10... | collective-permute-start | bytes 786440 | tf_op jit(solution)/shard_map/ppermute | solution.py:26
  250.3 22.8 %collective-permute-start.23 = (f32[16,4096]{1,0:T(8,128)S(1)}, f32[16,4096]{1,0:T(8,128)S(1)}, u32[]{:S(2)}, u32[]{:S(2)}) collective-permute-start(f32[16,4096]{1,0:T(8,128)S(1)} %get-tuple-element.86), channel_id=1, source_target_pairs={{0,8},{8,0},{16,24},{24,16},{1,9},{9,1},{17,25},{25,17},{2,10},{10... | collective-permute-start | bytes 786440 | tf_op jit(solution)/shard_map/ppermute | solution.py:26
  274.1 7.2 %collective-permute-start.27 = (bf16[16,4096]{1,0:T(8,128)(2,1)S(1)}, bf16[16,4096]{1,0:T(8,128)(2,1)S(1)}, u32[]{:S(2)}, u32[]{:S(2)}) collective-permute-start(bf16[16,4096]{1,0:T(8,128)(2,1)S(1)} %get-tuple-element.108.refs_0_.refs_4_), channel_id=1, source_target_pairs={{0,8},{8,0},{16,24},{24,16},{1,9},{9,1},{17,25},{25,17},{2,10},{10... | collective-permute-start | bytes 393224 | tf_op jit(solution)/shard_map/ppermute | solution.py:26
  274.1 13.2 %collective-permute-start.28 = (bf16[16,4096]{1,0:T(8,128)(2,1)S(1)}, bf16[16,4096]{1,0:T(8,128)(2,1)S(1)}, u32[]{:S(2)}, u32[]{:S(2)}) collective-permute-start(bf16[16,4096]{1,0:T(8,128)(2,1)S(1)} %get-tuple-element.108.refs_0_.refs_4_), channel_id=1, source_target_pairs={{0,16},{8,24},{16,0},{24,8},{1,17},{9,25},{17,1},{25,9},{2,18},{10... | collective-permute-start | bytes 393224 | tf_op jit(solution)/shard_map/ppermute | solution.py:26
  277.3 10.0 %collective-permute-start.29 = (bf16[16,4096]{1,0:T(8,128)(2,1)S(1)}, bf16[16,4096]{1,0:T(8,128)(2,1)S(1)}, u32[]{:S(2)}, u32[]{:S(2)}) collective-permute-start(bf16[16,4096]{1,0:T(8,128)(2,1)S(1)} %get-tuple-element.108.refs_0_.refs_4_), channel_id=1, source_target_pairs={{0,24},{8,16},{16,8},{24,0},{1,25},{9,17},{17,9},{25,1},{2,26},{10... | collective-permute-start | bytes 393224 | tf_op jit(solution)/shard_map/ppermute | solution.py:26
  288.4 23.7 %collective-permute-start.31 = (bf16[112,4096]{1,0:T(8,128)(2,1)}, bf16[112,4096]{1,0:T(8,128)(2,1)}, u32[]{:S(2)}, u32[]{:S(2)}) collective-permute-start(bf16[112,4096]{1,0:T(8,128)(2,1)} %add_convert_fusion.4.refs_4_), channel_id=1, source_target_pairs={{8,0},{16,24},{9,1},{17,25},{10,2},{18,26},{11,3},{19,27},{12,4},{... | collective-permute-start | bytes 2752520 | tf_op jit(solution)/shard_map/ppermute | solution.py:510
  322.5 20.3 %all-to-all-start.1 = ((bf16[8,128,256]{2,1,0:T(8,128)(2,1)}), bf16[8,128,256]{2,1,0:T(8,128)(2,1)S(1)}, u32[]{:S(2)}, u32[]{:S(2)}) async-start(bf16[8,128,256]{2,1,0:T(8,128)(2,1)} %third_forward_1.1), calls=%async_computation.1 | async-start | bytes 1048576 | tf_op jit(solution)/shard_map/all_to_all | solution.py:552
  326.1 36.6 %copy-start.6 = (f32[16,16384]{1,0:T(8,128)S(1)}, f32[16,16384]{1,0:T(8,128)}, u32[]{:S(2)}) copy-start(f32[16,16384]{1,0:T(8,128)} %copy-done.5) | copy-start | bytes 3145732
  326.1 36.6 %copy-start.10 = (bf16[16,4096]{1,0:T(8,128)(2,1)S(1)}, bf16[16,4096]{1,0:T(8,128)(2,1)}, u32[]{:S(2)}) copy-start(bf16[16,4096]{1,0:T(8,128)(2,1)} %copy-done.9) | copy-start | bytes 393220
  326.2 9.7 %collective-permute-start.32 = (bf16[16,4096]{1,0:T(8,128)(2,1)S(1)}, bf16[16,4096]{1,0:T(8,128)(2,1)S(1)}, u32[]{:S(2)}, u32[]{:S(2)}) collective-permute-start(bf16[16,4096]{1,0:T(8,128)(2,1)S(1)} %copy-done.13), channel_id=1, source_target_pairs={{0,8},{8,0},{16,24},{24,16},{1,9},{9,1},{17,25},{25,17},{2,10},{10... | collective-permute-start | bytes 393224 | tf_op jit(solution)/shard_map/ppermute | solution.py:26
  329.8 12.9 %collective-permute-start.33 = (bf16[16,4096]{1,0:T(8,128)(2,1)S(1)}, bf16[16,4096]{1,0:T(8,128)(2,1)S(1)}, u32[]{:S(2)}, u32[]{:S(2)}) collective-permute-start(bf16[16,4096]{1,0:T(8,128)(2,1)S(1)} %copy-done.13), channel_id=1, source_target_pairs={{0,16},{8,24},{16,0},{24,8},{1,17},{9,25},{17,1},{25,9},{2,18},{10... | collective-permute-start | bytes 393224 | tf_op jit(solution)/shard_map/ppermute | solution.py:26
  330.8 11.9 %collective-permute-start.34 = (bf16[16,4096]{1,0:T(8,128)(2,1)S(1)}, bf16[16,4096]{1,0:T(8,128)(2,1)S(1)}, u32[]{:S(2)}, u32[]{:S(2)}) collective-permute-start(bf16[16,4096]{1,0:T(8,128)(2,1)S(1)} %copy-done.13), channel_id=1, source_target_pairs={{0,24},{8,16},{16,8},{24,0},{1,25},{9,17},{17,9},{25,1},{2,26},{10... | collective-permute-start | bytes 393224 | tf_op jit(solution)/shard_map/ppermute | solution.py:26
  343.3 1.3 collective-permute-start.35
  344.6 4.3 %collective-permute-start.36 = (f32[128,6]{1,0:T(8,128)S(1)}, f32[128,6]{1,0:T(8,128)S(1)}, u32[]{:S(2)}, u32[]{:S(2)}) collective-permute-start(f32[128,6]{1,0:T(8,128)S(1)} %add.161), channel_id=1, source_target_pairs={{0,2},{1,3},{2,0},{3,1},{4,6},{5,7},{6,4},{7,5},{8,10},{9,11},{10,... | collective-permute-start | bytes 9224 | tf_op jit(solution)/shard_map/ppermute | solution.py:26
  346.6 4.3 %collective-permute-start.37 = (f32[128,6]{1,0:T(8,128)S(1)}, f32[128,6]{1,0:T(8,128)S(1)}, u32[]{:S(2)}, u32[]{:S(2)}) collective-permute-start(f32[128,6]{1,0:T(8,128)S(1)} %add.161), channel_id=1, source_target_pairs={{0,4},{1,5},{2,6},{3,7},{4,0},{5,1},{6,2},{7,3},{8,12},{9,13},{10,... | collective-permute-start | bytes 9224 | tf_op jit(solution)/shard_map/ppermute | solution.py:26
  348.0 5.2 %collective-permute-start.38 = (f32[128,6]{1,0:T(8,128)S(1)}, f32[128,6]{1,0:T(8,128)S(1)}, u32[]{:S(2)}, u32[]{:S(2)}) collective-permute-start(f32[128,6]{1,0:T(8,128)S(1)} %add.161), channel_id=1, source_target_pairs={{0,6},{1,7},{2,4},{3,5},{4,2},{5,3},{6,0},{7,1},{8,14},{9,15},{10,... | collective-permute-start | bytes 9224 | tf_op jit(solution)/shard_map/ppermute | solution.py:26
  353.2 5.1 %collective-permute-start.39 = (f32[128,6]{1,0:T(8,128)S(1)}, f32[128,6]{1,0:T(8,128)S(1)}, u32[]{:S(2)}, u32[]{:S(2)}) collective-permute-start(f32[128,6]{1,0:T(8,128)S(1)} %add_add_fusion.4), channel_id=1, source_target_pairs={{0,8},{8,0},{16,24},{24,16},{1,9},{9,1},{17,25},{25,17},{2,10},{10... | collective-permute-start | bytes 9224 | tf_op jit(solution)/shard_map/ppermute | solution.py:26
  355.6 5.9 %collective-permute-start.40 = (f32[128,6]{1,0:T(8,128)S(1)}, f32[128,6]{1,0:T(8,128)S(1)}, u32[]{:S(2)}, u32[]{:S(2)}) collective-permute-start(f32[128,6]{1,0:T(8,128)S(1)} %add_add_fusion.4), channel_id=1, source_target_pairs={{0,16},{8,24},{16,0},{24,8},{1,17},{9,25},{17,1},{25,9},{2,18},{10... | collective-permute-start | bytes 9224 | tf_op jit(solution)/shard_map/ppermute | solution.py:26
  356.5 6.2 %collective-permute-start.41 = (f32[128,6]{1,0:T(8,128)S(1)}, f32[128,6]{1,0:T(8,128)S(1)}, u32[]{:S(2)}, u32[]{:S(2)}) collective-permute-start(f32[128,6]{1,0:T(8,128)S(1)} %add_add_fusion.4), channel_id=1, source_target_pairs={{0,24},{8,16},{16,8},{24,0},{1,25},{9,17},{17,9},{25,1},{2,26},{10... | collective-permute-start | bytes 9224 | tf_op jit(solution)/shard_map/ppermute | solution.py:26
  (26 other events, 436.5 us)

commit v6 on v5

--- a/solution.py
+++ b/solution.py
@@ -235,11 +235,11 @@
     )(places, *operands)
 
 
-def wide_body(n, begin, chunks, with_acc, off, *refs):
+def wide_body(n, begin, chunks, chosen, with_acc, off, *refs):
     refs = list(refs)
     pieces = [refs.pop(0) for _ in range(n)]
     inner = [refs.pop(0) for _ in range(chunks)]
-    outer = [refs.pop(0) for _ in range(chunks)]
+    outer = [refs.pop(0) if j in chosen else None for j in range(chunks)]
     acc = refs.pop(0) if with_acc else None
     if with_acc:
         g, out, rows, held, sems, total = refs
@@ -262,6 +262,9 @@
 
         for j in range(chunks):
             here = slice(ends[j], ends[j + 1])
+            if outer[j] is None:
+                rows[t:, here] = inner[j][...]
+                continue
 
             @pl.when(off[n] == 1)
             def _():
@@ -286,6 +289,8 @@
     n, t, unit = len(pieces), pieces[0].shape[0], pieces[0].shape[1] // 2
     r = t + inner[0].shape[0]
     pb, kb = block_of(people, 1024), block_of(unit, 2048)
+    chosen = [j for j, x in enumerate(outer) if x is not None]
+    outer = [outer[j] for j in chosen]
     operands = [*pieces, *inner, *outer, *([] if acc is None else [acc]), genotypes]
     span = sum(x.shape[1] for x in inner)
     scratch = [pltpu.VMEM((r, span), BF16), *ring(pb, kb)]
@@ -295,7 +300,7 @@
         shape = jax.ShapeDtypeStruct((columns, r, people // columns), BF16)
         scratch.append(pltpu.VMEM((people, r), F32))
     return pl.pallas_call(
-        functools.partial(wide_body, n, begin, len(inner), acc is not None),
+        functools.partial(wide_body, n, begin, len(inner), chosen, acc is not None),
         grid_spec=pltpu.PrefetchScalarGridSpec(
             num_scalar_prefetch=1,
             grid=(),
@@ -343,7 +348,8 @@
     if t == rows.shape[0]:
         outs, total = refs[:-3], refs[-3]
     else:
-        outs, (lower, upper, total, made, sent) = refs[:-7], refs[-7:-2]
+        total, made, sent = refs[-5:-2]
+        outs, (lower, upper) = (refs[:-7], refs[-7:-5]) if cut < n else (refs[:-6], [refs[-6]] * 2)
     backward_loop(g, rows, total, held, sems, off, unit, n)
     copies = []
     if t != rows.shape[0]:
@@ -380,8 +386,9 @@
     out_shape = [jax.ShapeDtypeStruct((t, n * unit // arrays), F32)] * arrays
     scratch = [pltpu.VMEM((r, n * unit), F32)]
     if t != r:
-        out_specs += [ANY] * 2
-        out_shape += [jax.ShapeDtypeStruct((r - t, c * unit), BF16) for c in (cut, n - cut)]
+        sizes = [c for c in (cut, n - cut) if c]
+        out_specs += [ANY] * len(sizes)
+        out_shape += [jax.ShapeDtypeStruct((r - t, c * unit), BF16) for c in sizes]
         scratch += [pltpu.VMEM((r - t, n * unit), BF16), pltpu.SemaphoreType.DMA((n,))]
     return pl.pallas_call(
         functools.partial(back_body, n, unit, t, base, cut),
@@ -403,6 +410,7 @@
     start_hi, back_hi, low = refs[:n], refs[n : 2 * n], refs[2 * n : 3 * n]
     estimate, lmmse = refs[3 * n :]
     t, unit = start_hi[0].shape[0], start_hi[0].shape[1] // 2
+    sums = sums[...].T
     norm_start, du, uu, xx, xw, ww = [sums[:, j : j + 1] for j in range(6)]
     tau, gamma = wide_cols[:, 0:1], wide_cols[:, 1:2]
     second_precision, slab_var, odds = [cols[:, j : j + 1] for j in range(3)]
@@ -440,7 +448,7 @@
 def finish(places, sums, wide_cols, cols, centre, start_hi, back_hi, low):
     n = len(low)
     shape = jax.ShapeDtypeStruct(centre.shape, F32)
-    copies = sums.shape[0] // centre.shape[0]
+    copies = sums.shape[1] // centre.shape[0]
     operands = [sums, wide_cols, cols, centre, *start_hi, *back_hi, *low]
     return pl.pallas_call(
         functools.partial(finish_body, n, copies),
@@ -480,15 +488,17 @@
     pred_x = rows[traits:].astype(F32)
     rows = lax.all_gather(rows, "marker", axis=1, tiled=True)
     starts, chunks = [], []
-    for half, cut in enumerate((samples - 1, some)):
+    for half, cut in enumerate((samples, some)):
         base = half * samples
-        *parts, lower, upper = backward(
+        outs = backward(
             rows, order + base, genotypes, unit, traits, base, cut, samples, f"first_back_{half}"
         )
+        parts = outs[:samples]
         starts.append([swap(part, "sample", k) if k else part for k, part in enumerate(parts)])
-        chunks += [lower, upper]
-        rows, *_ = lax.optimization_barrier((rows, lower))
-    chunks = [chunks[0], jnp.concatenate(chunks[1:3], axis=1), chunks[3]]
+        chunks += outs[samples:]
+        rows, *_ = lax.optimization_barrier((rows, outs[-1]))
+
+    first_half = lax.psum_scatter(chunks[0], "sample", scatter_dimension=1, tiled=True)
 
     def add(x, y):
         return (x.astype(F32) + y.astype(F32)).astype(BF16)
@@ -510,7 +520,6 @@
         return lax.ppermute(x, "sample", [(1, 0), (2, 3)])
 
     pair, full, ends = [None] * 3, [None] * 3, [None] * 3
-    pair[0] = inward(0)
     scale = (noise_precision / people)[:, None]
     start = scale * jnp.concatenate([tree(parts) for parts in starts], axis=1)
     start_high = lax.reduce_precision(start, 8, 7)
@@ -518,18 +527,20 @@
     start_high = start_high.astype(BF16)
 
     start_pieces = [swap(start_high, "sample", k) if k else start_high for k in range(samples)]
-    *start_pieces, pair[0], chunks[1] = tie((*start_pieces, pair[0], chunks[1]))
-    full[0], pair[1] = across(pair[0]), inward(1)
+    *start_pieces, chunks[1], chunks[2], first_half = tie((*start_pieces, chunks[1], chunks[2], first_half))
+    first_half = lax.all_gather(first_half, "sample", axis=1, tiled=True)
+    pair[1] = inward(1)
     both = jnp.concatenate([near, far])
     value = narrow_forward(start_pieces, both, None, genotypes, "second_forward")
-    value, chunks[2] = tie((value, chunks[2]), full[0], pair[1])
-    ends[0], full[1], pair[2] = outward(full[0]), across(pair[1]), inward(2)
+    value, pair[1], chunks[2], start_low = tie((value, pair[1], chunks[2], start_low))
+    full[1], pair[2] = across(pair[1]), inward(2)
+    low_pieces = [swap(start_low, "sample", k) if k else start_low for k in range(samples)]
     value = sum_marker(value)
     kept_s = lax.dynamic_slice_in_dim(value, column * share, share, 1)
     rows = value.astype(BF16)
     parts = backward(rows, far, genotypes, unit, traits, 0, 0, some, "second_back_far")
     sent = [swap(part, "sample", k + some) for k, part in enumerate(parts)]
-    (rows,) = tie((rows,), full[1], pair[2], ends[0], *parts)
+    (rows,) = tie((rows,), full[1], pair[2], *low_pieces, first_half, *parts)
     ends[1] = outward(full[1])
     parts = backward(rows, near, genotypes, unit, traits, 0, 0, some, "second_back_near")
     sent = [swap(part, "sample", k) if k else part for k, part in enumerate(parts)] + sent
@@ -542,14 +553,12 @@
     inner = ((me == 1) | (me == 2)).astype(jnp.int32)
     places = jnp.concatenate([order, inner[None]])
     total = wide_forward(
-        back_pieces, full[:2], ends[:2], places, 0, None, genotypes, columns, "third_forward_0"
-    )
-    (start_low,) = tie((start_low,), total)
-    low_pieces = [swap(start_low, "sample", k) if k else start_low for k in range(samples)]
+        back_pieces, [first_half, full[1]], [None, ends[1]], places, 0, None, genotypes, columns, "third_forward_0"
+    )
     value = wide_forward(
         back_pieces, full[2:], ends[2:], places, 3 * some, total, genotypes, columns, "third_forward_1"
     )
-    (last,) = tie((lax.all_to_all(value, "marker", 0, 0),), *low_pieces)
+    last = lax.all_to_all(value, "marker", 0, 0)
     last = jnp.sum(last.astype(F32), axis=0)
     before = jnp.concatenate([kept_s, kept_x[traits:]], axis=0)
 
@@ -562,15 +571,14 @@
     kept_p, last_p = kept_x[traits:], last[traits:]
     norms = jnp.concatenate(
         [
-            jnp.stack([dot(start, start), dot(start, back), dot(back, back)], axis=1),
-            jnp.stack(
-                [sum(dot(p, p) for p in probes_here), dot(kept_p, pred_x), dot(last_p, pred_x)], axis=1
-            ),
+            jnp.stack([dot(start, start), dot(start, back), dot(back, back)]),
+            jnp.stack([sum(dot(p, p) for p in probes_here), dot(kept_p, pred_x), dot(last_p, pred_x)]),
         ],
-        axis=0,
-    )
-    squares = jnp.stack([dot(before, before), dot(before, last), dot(last, last)], axis=1)
-    sums = sum_direct(sum_marker(jnp.concatenate([norms, squares], axis=1)), "sample")
+        axis=1,
+    )
+    squares = jnp.stack([dot(before, before), dot(before, last), dot(last, last)])
+    sums = jnp.concatenate([norms, squares, jnp.zeros((2, norms.shape[1]), F32)], axis=0)
+    sums = sum_direct(sum_marker(sums), "sample")
 
     first_slope = slopes[:, 0] / markers
     second_precision = input_precision * (1.0 - first_slope) / first_slope

time: 367 us -> 380 us (1.035)
  between operations: 1.4 us -> 14.7 us
  waiting for transfers between devices: 119 us -> 111 us
    ppermute x33, waiting for transfers between devices: 91 us -> 68.6 us  [swap(): return lax.ppermute(x, axis, [(i, i ^ bits) for i in range(n)])]
    ppermute x33, starting transfers between devices: 52.3 us -> 63.9 us  [swap(): return lax.ppermute(x, axis, [(i, i ^ bits) for i in range(n)])]
    ppermute x6 -> x4, starting transfers between devices: 19.1 us -> 10.7 us  [hop(): y = lax.ppermute(x, 'sample', pairs)]
    ppermute x6 -> x4, waiting for transfers between devices: 17.3 us -> 24.9 us  [hop(): y = lax.ppermute(x, 'sample', pairs)]
    all_to_all x1, waiting for transfers between devices: 0.01 us -> 6.87 us  [per_device(): last = lax.all_to_all(value, 'marker', 0, 0)]
    convert_element_type x6 -> x4, other arithmetic: 5.85 us -> 7.99 us  [add(): return (x.astype(F32) + y.astype(F32)).astype(BF16)]
  transfers between devices with their start and end apart: 44 -> 43, of which waited for: 25 -> 18; matrix products, arithmetic and copies ran while one was open for 4% -> 4% of each run, Pallas kernels for 21% -> 21%
where the time goes in v6:
time: 380 us; the launch traced here: 379 us
  Pallas kernels  133 us (35%)
  waiting for transfers between devices  111 us (29%)
  starting transfers between devices  84.5 us (22%)
  other arithmetic  20 us (5%)
  between operations  14.7 us (4%)
  blocking collectives  9.94 us (3%)
  local copies, waits for them, and re-layouts  6.14 us (2%)
    ppermute x33, waiting for transfers between devices, swap(): return lax.ppermute(x, axis, [(i, i ^ bits) for i in range(n)])  68.6 us
    ppermute x33, starting transfers between devices, swap(): return lax.ppermute(x, axis, [(i, i ^ bits) for i in range(n)])  63.9 us
    pallas_call x4, Pallas kernels, backward(): pl.pallas_call(functools.partial(back_body, n, unit, t, base, cut), grid_...  52.8 us
    pallas_call x2, Pallas kernels, wide_forward(): pl.pallas_call(functools.partial(wide_body, n, begin, len(inner), chosen,...  28.6 us
    ppermute x4, waiting for transfers between devices, hop(): y = lax.ppermute(x, 'sample', pairs)  24.9 us
    pallas_call x1, Pallas kernels, first_forward(): pl.pallas_call(functools.partial(first_body, markers * columns), grid_spe...  24.5 us
    pallas_call x1, Pallas kernels, narrow_forward(): pl.pallas_call(functools.partial(narrow_body, n, unit, acc is not None),...  22.3 us
    ppermute x4, starting transfers between devices, hop(): y = lax.ppermute(x, 'sample', pairs)  10.7 us
  transfers between devices with their start and end apart: 43, of which 18 were waited for; matrix products, arithmetic and copies ran while one was open for 4% of the time, Pallas kernels for 21%

profile of v6, /device:TPU:0, one launch (start us, length us, event | category | flops | bytes accessed | tf_op | source)
XLA Modules:
  0.0 379.1 jit_solution(2071174506497375806)
XLA Ops:
  11.2 2.8 collective-permute-start.1
  14.1 1.5 collective-permute-start.2
  15.6 3.5 convert_element_type.65.probes
  20.8 24.5 %first_forward.1 = (bf16[8,144,256]{2,1,0:T(8,128)(2,1)}, f32[16,16384]{1,0:T(8,128)S(1)}) custom-call(s32[1]{0:T(128)} %constant.7.clone.1.off, f32[16,16384]{1,0:T(8,128)S(1)} %copy-done, f32[16,3]{1,0:T(8,128)S(1)} %copy.31.cols, f32[16,1]{1,0:T(8,128)S(1)} %get-tuple-element.99.slopes, bf16[112,16384]{1,0:T(8,128)(2,1)S(1)} %convert_element_type.65.probes, ...), custom_call_target="tpu_custom_call" | custom-call | flops 8589934592 | bytes 67108864 | tf_op jit(solution)/shard_map/first_forward/pallas_call | solution.py:174
  45.3 3.6 all-to-all-start
  48.9 10.3 %all-to-all-done = bf16[8,144,256]{2,1,0:T(8,128)(2,1)S(1)} async-done(((bf16[8,144,256]{2,1,0:T(8,128)(2,1)}), bf16[8,144,256]{2,1,0:T(8,128)(2,1)S(1)}, u32[]{:S(2)}, u32[]{:S(2)}) %all-to-all-start) | async-done | bytes 589856 | tf_op jit(solution)/shard_map/all_to_all | solution.py:484
  60.1 9.9 %all_gather.6.rows = bf16[128,2048]{1,0:T(8,128)(2,1)S(1)} all-gather(bf16[128,256]{1,0:T(8,128)(2,1)S(1)} %pad_maximum_fusion.1), channel_id=1, replica_groups=mesh['sample'=4,'marker'=8] {'marker'}, dimensions={1}, use_global_device_ids=true | all-gather | bytes 589824 | tf_op jit(solution)/shard_map/all_gather | solution.py:489
  70.1 14.5 %first_back_0.1 = (f32[16,2048]{1,0:T(8,128)S(1)}, f32[16,2048]{1,0:T(8,128)}, f32[16,2048]{1,0:T(8,128)}, f32[16,2048]{1,0:T(8,128)}, bf16[112,8192]{1,0:T(8,128)(2,1)}) custom-call(s32[4]{0:T(128)S(1)} %iota_xor_fusion.off, bf16[128,2048]{1,0:T(8,128)(2,1)S(1)} %all_gather.6.rows, bf16[2048,16384]{1,0:T(8,128)(2,1)} %refs_7_.3), custom_call_target="tpu_custom_call" | custom-call | flops 4294967296 | bytes 33554432 | tf_op jit(solution)/shard_map/first_back_0/pallas_call | solution.py:393
  85.3 1.6 collective-permute-start.4
  86.9 2.6 collective-permute-start.5
  89.7 13.1 %first_back_1.1 = (f32[16,2048]{1,0:T(8,128)S(1)}, f32[16,2048]{1,0:T(8,128)S(1)}, f32[16,2048]{1,0:T(8,128)S(1)}, f32[16,2048]{1,0:T(8,128)S(1)}, bf16[112,4096...) custom-call(s32[4]{0:T(128)S(1)} %broadcast_add_fusion.off, bf16[128,2048]{1,0:T(8,128)(2,1)S(1)} %all_gather.6.rows, ...), custom_call_target="tpu_custom_call" | custom-call | flops 4294967296 | bytes 33554432 | tf_op jit(solution)/shard_map/first_back_1/pallas_call | solution.py:393
  103.5 3.5 collective-permute-start.8
  107.3 7.3 %collective-permute-done.7 = f32[16,2048]{1,0:T(8,128)S(1)} collective-permute-done((f32[16,2048]{1,0:T(8,128)S(1)}, f32[16,2048]{1,0:T(8,128)S(1)}, u32[]{:S(2)}, u32[]{:S(2)}) %collective-permute-start.7) | collective-permute-done | bytes 131104 | tf_op jit(solution)/shard_map/ppermute | solution.py:26
  114.6 14.2 %collective-permute-done.8 = f32[16,2048]{1,0:T(8,128)S(1)} collective-permute-done((f32[16,2048]{1,0:T(8,128)S(1)}, f32[16,2048]{1,0:T(8,128)S(1)}, u32[]{:S(2)}, u32[]{:S(2)}) %collective-permute-start.8) | collective-permute-done | bytes 131104 | tf_op jit(solution)/shard_map/ppermute | solution.py:26
  129.6 9.3 %collective-permute-start.10 = (bf16[16,4096]{1,0:T(8,128)(2,1)S(1)}, bf16[16,4096]{1,0:T(8,128)(2,1)S(1)}, u32[]{:S(2)}, u32[]{:S(2)}) collective-permute-start(bf16[16,4096]{1,0:T(8,128)(2,1)S(1)} %get-tuple-element.59.refs_0_), channel_id=1, source_target_pairs={{0,8},{8,0},{16,24},{24,16},{1,9},{9,1},{17,25},{25,17},{2,10},{10... | collective-permute-start | bytes 393224 | tf_op jit(solution)/shard_map/ppermute | solution.py:26
  138.9 1.9 collective-permute-start.11
  142.3 2.2 collective-permute-done.10.refs_1_
  144.4 7.6 %collective-permute-done.11.refs_2_ = bf16[16,4096]{1,0:T(8,128)(2,1)S(1)} collective-permute-done((bf16[16,4096]{1,0:T(8,128)(2,1)S(1)}, bf16[16,4096]{1,0:T(8,128)(2,1)S(1)}, u32[]{:S(2)}, u32[]{:S(2)}) %collective-permute-start.11) | collective-permute-done | bytes 131104 | tf_op jit(solution)/shard_map/ppermute | solution.py:26
  152.1 5.3 %collective-permute-start.13 = (bf16[112,4096]{1,0:T(8,128)(2,1)S(1)}, bf16[112,4096]{1,0:T(8,128)(2,1)}, u32[]{:S(2)}, u32[]{:S(2)}) collective-permute-start(bf16[112,4096]{1,0:T(8,128)(2,1)S(1)} %get-tuple-element.64), channel_id=1, source_target_pairs={{0,8},{24,16},{1,9},{25,17},{2,10},{26,18},{3,11},{27,19},{4,12},{... | collective-permute-start | bytes 2752520 | tf_op jit(solution)/shard_map/ppermute | solution.py:510
  157.9 22.3 %second_forward.1 = f32[16,2048]{1,0:T(8,128)S(1)} custom-call(s32[8]{0:T(128)S(1)} %pad_add_fusion.2.off, bf16[16,4096]{1,0:T(8,128)(2,1)S(1)} %get-tuple-element.59.refs_0_, bf16[16,4096]{1,0:T(8,128)(2,1)S(1)} %collective-permute-done.10.refs_1_, bf16[16,4096]{1,0:T(8,128)(2,1)S(1)} %collective-permute-done.11.refs_2_, ...), custom_call_target="tpu_custom_call" | custom-call | flops 1073741824 | bytes 67108864 | tf_op jit(solution)/shard_map/second_forward/pallas_call | solution.py:222
  180.2 2.3 add_convert_fusion.3
  182.6 2.2 collective-permute-start.19
  184.8 1.6 collective-permute-start.18
  187.9 1.6 collective-permute-start.15
  190.0 24.9 %collective-permute-done.19 = bf16[112,4096]{1,0:T(8,128)(2,1)} collective-permute-done((bf16[112,4096]{1,0:T(8,128)(2,1)S(1)}, bf16[112,4096]{1,0:T(8,128)(2,1)}, u32[]{:S(2)}, u32[]{:S(2)}) %collective-permute-start.19) | collective-permute-done | bytes 917536 | tf_op jit(solution)/shard_map/ppermute | solution.py:510
  215.2 1.7 add_convert_fusion.2.refs_5_
  218.2 2.3 add_convert_fusion.1
  220.5 13.3 %collective-permute-start.21 = (bf16[16,4096]{1,0:T(8,128)(2,1)}, bf16[16,4096]{1,0:T(8,128)(2,1)S(1)}, u32[]{:S(2)}, u32[]{:S(2)}) collective-permute-start(bf16[16,4096]{1,0:T(8,128)(2,1)} %get-tuple-element.74.refs_8_), channel_id=1, source_target_pairs={{0,16},{8,24},{16,0},{24,8},{1,17},{9,25},{17,1},{25,9},{2,18},{10... | collective-permute-start | bytes 393224 | tf_op jit(solution)/shard_map/ppermute | solution.py:26
  233.9 1.6 collective-permute-start.30
  236.2 13.0 %second_back_far.1 = (f32[16,4096]{1,0:T(8,128)}, f32[16,4096]{1,0:T(8,128)}) custom-call(s32[4]{0:T(128)S(1)} %reshape.28.off, bf16[16,2048]{1,0:T(8,128)(2,1)S(1)} %get-tuple-element.78.rows, bf16[2048,16384]{1,0:T(8,128)(2,1)} %refs_7_.3), custom_call_target="tpu_custom_call" | custom-call | flops 536870912 | bytes 33554432 | tf_op jit(solution)/shard_map/second_back_far/pallas_call | solution.py:393
  249.2 2.6 collective-permute-start.24
  253.2 12.2 %second_back_near.1 = (f32[16,4096]{1,0:T(8,128)S(1)}, f32[16,4096]{1,0:T(8,128)S(1)}) custom-call(s32[4]{0:T(128)S(1)} %reshape.27.off, bf16[16,2048]{1,0:T(8,128)(2,1)S(1)} %get-tuple-element.78.rows, bf16[2048,16384]{1,0:T(8,128)(2,1)} %refs_7_.3), custom_call_target="tpu_custom_call" | custom-call | flops 536870912 | bytes 33554432 | tf_op jit(solution)/shard_map/second_back_near/pallas_call | solution.py:393
  266.1 18.1 %collective-permute-done.24 = f32[16,4096]{1,0:T(8,128)} collective-permute-done((f32[16,4096]{1,0:T(8,128)}, f32[16,4096]{1,0:T(8,128)}, u32[]{:S(2)}, u32[]{:S(2)}) %collective-permute-start.24) | collective-permute-done | bytes 262176 | tf_op jit(solution)/shard_map/ppermute | solution.py:26
  284.2 2.2 multiply_reduce_fusion.2
  286.4 5.1 %collective-permute-start.27 = (bf16[16,4096]{1,0:T(8,128)(2,1)S(1)}, bf16[16,4096]{1,0:T(8,128)(2,1)S(1)}, u32[]{:S(2)}, u32[]{:S(2)}) collective-permute-start(bf16[16,4096]{1,0:T(8,128)(2,1)S(1)} %get-tuple-element.100.refs_0_.refs_4_), channel_id=1, source_target_pairs={{0,8},{8,0},{16,24},{24,16},{1,9},{9,1},{17,25},{25,17},{2,10},{10... | collective-permute-start | bytes 393224 | tf_op jit(solution)/shard_map/ppermute | solution.py:26
  293.9 1.7 collective-permute-done.27.refs_1_.refs_5_
  295.6 8.0 %collective-permute-done.28.refs_2_.refs_6_ = bf16[16,4096]{1,0:T(8,128)(2,1)S(1)} collective-permute-done((bf16[16,4096]{1,0:T(8,128)(2,1)S(1)}, bf16[16,4096]{1,0:T(8,128)(2,1)S(1)}, u32[]{:S(2)}, u32[]{:S(2)}) %collective-permute-start.28) | collective-permute-done | bytes 131104 | tf_op jit(solution)/shard_map/ppermute | solution.py:26
  303.6 1.7 add_convert_fusion.refs_4_
  309.3 18.6 %third_forward_0.1.refs_6_ = f32[2048,128]{1,0:T(8,128)S(1)} custom-call(s32[5]{0:T(128)S(1)} %pad_add_fusion.3.off, bf16[16,4096]{1,0:T(8,128)(2,1)S(1)} %get-tuple-element.100.refs_0_.refs_4_, bf16[16,4096]{1,0:T(8,128)(2,1)S(1)} %collective-permute-done.27.refs_1_.refs_5_, bf16[16,4096]{1,0:T(8,128)(2,1)S(1)} %collective-permute-done.28.refs_2_.refs_6_, ...), custom_call_target="tpu_custom_call" | custom-call | flops 6442450944 | bytes 50331648 | tf_op jit(solution)/shard_map/third_forward_0/pallas_call | solution.py:302
  327.9 10.0 %third_forward_1.1 = bf16[8,128,256]{2,1,0:T(8,128)(2,1)} custom-call(s32[5]{0:T(128)S(1)} %pad_add_fusion.3.off, bf16[16,4096]{1,0:T(8,128)(2,1)S(1)} %get-tuple-element.100.refs_0_.refs_4_, bf16[16,4096]{1,0:T(8,128)(2,1)S(1)} %collective-permute-done.27.refs_1_.refs_5_, bf16[16,4096]{1,0:T(8,128)(2,1)S(1)} %collective-permute-done.28.refs_2_.refs_6_, ...), custom_call_target="tpu_custom_call" | custom-call | flops 2147483648 | bytes 16777216 | tf_op jit(solution)/shard_map/third_forward_1/pallas_call | solution.py:302
  338.0 3.6 all-to-all-start.1
  341.8 1.8 multiply_reduce_fusion
  344.4 6.9 %all-to-all-done.1 = bf16[8,128,256]{2,1,0:T(8,128)(2,1)S(1)} async-done(((bf16[8,128,256]{2,1,0:T(8,128)(2,1)}), bf16[8,128,256]{2,1,0:T(8,128)(2,1)S(1)}, u32[]{:S(2)}, u32[]{:S(2)}) %all-to-all-start.1) | async-done | bytes 524320 | tf_op jit(solution)/shard_map/all_to_all | solution.py:561
  354.1 2.4 collective-permute-start.35
  358.6 3.6 collective-permute-start.36
  362.7 1.9 collective-permute-start.38
  364.8 1.9 collective-permute-done.37
  368.2 4.1 %finish.1 = (f32[16,16384]{1,0:T(8,128)}, f32[16,16384]{1,0:T(8,128)}) custom-call(s32[4]{0:T(128)S(1)} %iota_xor_fusion.off, f32[8,128]{1,0:T(8,128)S(1)} %add_add_fusion.4.sums, f32[128,2]{1,0:T(8,128)S(1)} %copy.34.wide_cols, f32[16,3]{1,0:T(8,128)S(1)} %copy.35.cols, f32[16,16384]{1,0:T(8,128)S(1)} %get-tuple-element.87.centre, ...), custom_call_target="tpu_custom_call" | custom-call | tf_op jit(solution)/shard_map/finish/pallas_call | solution.py:453
  (163 shorter events, 32.0 us)
Async XLA Ops:
  9.9 1.3 collective-permute-start
  11.2 7.9 %collective-permute-start.1 = (f32[16,1]{1,0:T(8,128)S(1)}, f32[16,1]{1,0:T(8,128)S(1)}, u32[]{:S(2)}, u32[]{:S(2)}) collective-permute-start(f32[16,1]{1,0:T(8,128)S(1)} %add.125), channel_id=1, source_target_pairs={{0,2},{1,3},{2,0},{3,1},{4,6},{5,7},{6,4},{7,5},{8,10},{9,11},{10,... | collective-permute-start | bytes 200 | tf_op jit(solution)/shard_map/ppermute | solution.py:26
  14.1 5.0 %collective-permute-start.2 = (f32[16,1]{1,0:T(8,128)S(1)}, f32[16,1]{1,0:T(8,128)S(1)}, u32[]{:S(2)}, u32[]{:S(2)}) collective-permute-start(f32[16,1]{1,0:T(8,128)S(1)} %add.125), channel_id=1, source_target_pairs={{0,4},{1,5},{2,6},{3,7},{4,0},{5,1},{6,2},{7,3},{8,12},{9,13},{10,... | collective-permute-start | bytes 200 | tf_op jit(solution)/shard_map/ppermute | solution.py:26
  15.6 4.5 %collective-permute-start.3 = (f32[16,1]{1,0:T(8,128)S(1)}, f32[16,1]{1,0:T(8,128)S(1)}, u32[]{:S(2)}, u32[]{:S(2)}) collective-permute-start(f32[16,1]{1,0:T(8,128)S(1)} %add.125), channel_id=1, source_target_pairs={{0,6},{1,7},{2,4},{3,5},{4,2},{5,3},{6,0},{7,1},{8,14},{9,15},{10,... | collective-permute-start | bytes 200 | tf_op jit(solution)/shard_map/ppermute | solution.py:26
  45.3 13.9 %all-to-all-start = ((bf16[8,144,256]{2,1,0:T(8,128)(2,1)}), bf16[8,144,256]{2,1,0:T(8,128)(2,1)S(1)}, u32[]{:S(2)}, u32[]{:S(2)}) async-start(bf16[8,144,256]{2,1,0:T(8,128)(2,1)} %get-tuple-element.46), calls=%async_computation | async-start | bytes 1179648 | tf_op jit(solution)/shard_map/all_to_all | solution.py:484
  48.9 103.2 %reduce-scatter.2.cloned.1.call-start = ((), (), s32[]{:S(2)}) async-start(), calls=%async_computation.3 | async-start | bytes 2293760 | tf_op jit(solution)/shard_map/reduce_scatter | solution.py:501
  84.6 168.5 %all-gather.2.cloned.1.call-start = ((), (), s32[]{:S(2)}) async-start(), calls=%async_computation.4 | async-start | bytes 2293760 | tf_op jit(solution)/shard_map/all_gather | solution.py:531
  85.3 21.8 %collective-permute-start.4 = (f32[16,2048]{1,0:T(8,128)}, f32[16,2048]{1,0:T(8,128)S(1)}, u32[]{:S(2)}, u32[]{:S(2)}) collective-permute-start(f32[16,2048]{1,0:T(8,128)} %get-tuple-element.48), channel_id=1, source_target_pairs={{0,8},{8,0},{16,24},{24,16},{1,9},{9,1},{17,25},{25,17},{2,10},{10... | collective-permute-start | bytes 393224 | tf_op jit(solution)/shard_map/ppermute | solution.py:26
  86.9 20.4 %collective-permute-start.5 = (f32[16,2048]{1,0:T(8,128)}, f32[16,2048]{1,0:T(8,128)S(1)}, u32[]{:S(2)}, u32[]{:S(2)}) collective-permute-start(f32[16,2048]{1,0:T(8,128)} %get-tuple-element.49), channel_id=1, source_target_pairs={{0,16},{8,24},{16,0},{24,8},{1,17},{9,25},{17,1},{25,9},{2,18},{10... | collective-permute-start | bytes 393224 | tf_op jit(solution)/shard_map/ppermute | solution.py:26
  89.4 17.8 %collective-permute-start.6 = (f32[16,2048]{1,0:T(8,128)}, f32[16,2048]{1,0:T(8,128)S(1)}, u32[]{:S(2)}, u32[]{:S(2)}) collective-permute-start(f32[16,2048]{1,0:T(8,128)} %get-tuple-element.50), channel_id=1, source_target_pairs={{0,24},{8,16},{16,8},{24,0},{1,25},{9,17},{17,9},{25,1},{2,26},{10... | collective-permute-start | bytes 393224 | tf_op jit(solution)/shard_map/ppermute | solution.py:26
  102.8 79.8 %copy-start.4 = (bf16[112,4096]{1,0:T(8,128)(2,1)}, bf16[112,4096]{1,0:T(8,128)(2,1)S(1)}, u32[]{:S(2)}) copy-start(bf16[112,4096]{1,0:T(8,128)(2,1)S(1)} %get-tuple-element.72) | copy-start | bytes 2752516
  102.8 11.8 %collective-permute-start.7 = (f32[16,2048]{1,0:T(8,128)S(1)}, f32[16,2048]{1,0:T(8,128)S(1)}, u32[]{:S(2)}, u32[]{:S(2)}) collective-permute-start(f32[16,2048]{1,0:T(8,128)S(1)} %get-tuple-element.54), channel_id=1, source_target_pairs={{0,8},{8,0},{16,24},{24,16},{1,9},{9,1},{17,25},{25,17},{2,10},{10... | collective-permute-start | bytes 393224 | tf_op jit(solution)/shard_map/ppermute | solution.py:26
  103.5 25.2 %collective-permute-start.8 = (f32[16,2048]{1,0:T(8,128)S(1)}, f32[16,2048]{1,0:T(8,128)S(1)}, u32[]{:S(2)}, u32[]{:S(2)}) collective-permute-start(f32[16,2048]{1,0:T(8,128)S(1)} %get-tuple-element.55), channel_id=1, source_target_pairs={{0,16},{8,24},{16,0},{24,8},{1,17},{9,25},{17,1},{25,9},{2,18},{10... | collective-permute-start | bytes 393224 | tf_op jit(solution)/shard_map/ppermute | solution.py:26
  107.0 21.8 %collective-permute-start.9 = (f32[16,2048]{1,0:T(8,128)S(1)}, f32[16,2048]{1,0:T(8,128)S(1)}, u32[]{:S(2)}, u32[]{:S(2)}) collective-permute-start(f32[16,2048]{1,0:T(8,128)S(1)} %get-tuple-element.56), channel_id=1, source_target_pairs={{0,24},{8,16},{16,8},{24,0},{1,25},{9,17},{17,9},{25,1},{2,26},{10... | collective-permute-start | bytes 393224 | tf_op jit(solution)/shard_map/ppermute | solution.py:26
  107.3 44.7 %copy-start.18 = (f32[16,2048]{1,0:T(8,128)}, f32[16,2048]{1,0:T(8,128)S(1)}, u32[]{:S(2)}) copy-start(f32[16,2048]{1,0:T(8,128)S(1)} %add_add_fusion.2) | copy-start | bytes 393220
  129.6 14.8 %collective-permute-start.10 = (bf16[16,4096]{1,0:T(8,128)(2,1)S(1)}, bf16[16,4096]{1,0:T(8,128)(2,1)S(1)}, u32[]{:S(2)}, u32[]{:S(2)}) collective-permute-start(bf16[16,4096]{1,0:T(8,128)(2,1)S(1)} %get-tuple-element.59.refs_0_), channel_id=1, source_target_pairs={{0,8},{8,0},{16,24},{24,16},{1,9},{9,1},{17,25},{25,17},{2,10},{10... | collective-permute-start | bytes 393224 | tf_op jit(solution)/shard_map/ppermute | solution.py:26
  138.9 13.1 %collective-permute-start.11 = (bf16[16,4096]{1,0:T(8,128)(2,1)S(1)}, bf16[16,4096]{1,0:T(8,128)(2,1)S(1)}, u32[]{:S(2)}, u32[]{:S(2)}) collective-permute-start(bf16[16,4096]{1,0:T(8,128)(2,1)S(1)} %get-tuple-element.59.refs_0_), channel_id=1, source_target_pairs={{0,16},{8,24},{16,0},{24,8},{1,17},{9,25},{17,1},{25,9},{2,18},{10... | collective-permute-start | bytes 393224 | tf_op jit(solution)/shard_map/ppermute | solution.py:26
  140.8 11.2 %collective-permute-start.12 = (bf16[16,4096]{1,0:T(8,128)(2,1)S(1)}, bf16[16,4096]{1,0:T(8,128)(2,1)S(1)}, u32[]{:S(2)}, u32[]{:S(2)}) collective-permute-start(bf16[16,4096]{1,0:T(8,128)(2,1)S(1)} %get-tuple-element.59.refs_0_), channel_id=1, source_target_pairs={{0,24},{8,16},{16,8},{24,0},{1,25},{9,17},{17,9},{25,1},{2,26},{10... | collective-permute-start | bytes 393224 | tf_op jit(solution)/shard_map/ppermute | solution.py:26
  144.4 35.8 %copy-start.6 = (bf16[16,4096]{1,0:T(8,128)(2,1)}, bf16[16,4096]{1,0:T(8,128)(2,1)S(1)}, u32[]{:S(2)}) copy-start(bf16[16,4096]{1,0:T(8,128)(2,1)S(1)} %collective-permute-done.10.refs_1_) | copy-start | bytes 393220
  152.1 28.2 %collective-permute-start.13 = (bf16[112,4096]{1,0:T(8,128)(2,1)S(1)}, bf16[112,4096]{1,0:T(8,128)(2,1)}, u32[]{:S(2)}, u32[]{:S(2)}) collective-permute-start(bf16[112,4096]{1,0:T(8,128)(2,1)S(1)} %get-tuple-element.64), channel_id=1, source_target_pairs={{0,8},{24,16},{1,9},{25,17},{2,10},{26,18},{3,11},{27,19},{4,12},{... | collective-permute-start | bytes 2752520 | tf_op jit(solution)/shard_map/ppermute | solution.py:510
  182.6 32.3 %collective-permute-start.19 = (bf16[112,4096]{1,0:T(8,128)(2,1)S(1)}, bf16[112,4096]{1,0:T(8,128)(2,1)}, u32[]{:S(2)}, u32[]{:S(2)}) collective-permute-start(bf16[112,4096]{1,0:T(8,128)(2,1)S(1)} %get-tuple-element.72), channel_id=1, source_target_pairs={{0,8},{24,16},{1,9},{25,17},{2,10},{26,18},{3,11},{27,19},{4,12},{... | collective-permute-start | bytes 2752520 | tf_op jit(solution)/shard_map/ppermute | solution.py:510
  184.8 30.4 %collective-permute-start.18 = (bf16[112,4096]{1,0:T(8,128)(2,1)}, bf16[112,4096]{1,0:T(8,128)(2,1)}, u32[]{:S(2)}, u32[]{:S(2)}) collective-permute-start(bf16[112,4096]{1,0:T(8,128)(2,1)} %add_convert_fusion.3), channel_id=1, source_target_pairs={{8,16},{16,8},{9,17},{17,9},{10,18},{18,10},{11,19},{19,11},{12,20... | collective-permute-start | bytes 2752520 | tf_op jit(solution)/shard_map/ppermute | solution.py:510
  186.4 31.8 %copy-start.5 = (bf16[112,4096]{1,0:T(8,128)(2,1)S(1)}, bf16[112,4096]{1,0:T(8,128)(2,1)}, u32[]{:S(2)}) copy-start(bf16[112,4096]{1,0:T(8,128)(2,1)} %copy-done.4) | copy-start | bytes 2752516
  186.4 1.4 collective-permute-start.14
  186.5 62.6 %collective-permute-start.20 = (bf16[16,4096]{1,0:T(8,128)(2,1)}, bf16[16,4096]{1,0:T(8,128)(2,1)S(1)}, u32[]{:S(2)}, u32[]{:S(2)}) collective-permute-start(bf16[16,4096]{1,0:T(8,128)(2,1)} %get-tuple-element.74.refs_8_), channel_id=1, source_target_pairs={{0,8},{8,0},{16,24},{24,16},{1,9},{9,1},{17,25},{25,17},{2,10},{10... | collective-permute-start | bytes 393224 | tf_op jit(solution)/shard_map/ppermute | solution.py:26
  187.9 32.7 %collective-permute-start.15 = (f32[16,2048]{1,0:T(8,128)S(1)}, f32[16,2048]{1,0:T(8,128)S(1)}, u32[]{:S(2)}, u32[]{:S(2)}) collective-permute-start(f32[16,2048]{1,0:T(8,128)S(1)} %add.140), channel_id=1, source_target_pairs={{0,2},{1,3},{2,0},{3,1},{4,6},{5,7},{6,4},{7,5},{8,10},{9,11},{10,... | collective-permute-start | bytes 393224 | tf_op jit(solution)/shard_map/ppermute | solution.py:26
  189.4 44.5 %collective-permute-start.16 = (f32[16,2048]{1,0:T(8,128)S(1)}, f32[16,2048]{1,0:T(8,128)S(1)}, u32[]{:S(2)}, u32[]{:S(2)}) collective-permute-start(f32[16,2048]{1,0:T(8,128)S(1)} %add.140), channel_id=1, source_target_pairs={{0,4},{1,5},{2,6},{3,7},{4,0},{5,1},{6,2},{7,3},{8,12},{9,13},{10,... | collective-permute-start | bytes 393224 | tf_op jit(solution)/shard_map/ppermute | solution.py:26
  214.9 19.0 %collective-permute-start.17 = (f32[16,2048]{1,0:T(8,128)S(1)}, f32[16,2048]{1,0:T(8,128)S(1)}, u32[]{:S(2)}, u32[]{:S(2)}) collective-permute-start(f32[16,2048]{1,0:T(8,128)S(1)} %add.140), channel_id=1, source_target_pairs={{0,6},{1,7},{2,4},{3,5},{4,2},{5,3},{6,0},{7,1},{8,14},{9,15},{10,... | collective-permute-start | bytes 393224 | tf_op jit(solution)/shard_map/ppermute | solution.py:26
  216.9 67.3 %collective-permute-start.26 = (bf16[112,4096]{1,0:T(8,128)(2,1)S(1)}, bf16[112,4096]{1,0:T(8,128)(2,1)S(1)}, u32[]{:S(2)}, u32[]{:S(2)}) collective-permute-start(bf16[112,4096]{1,0:T(8,128)(2,1)S(1)} %add_convert_fusion.2.refs_5_), channel_id=1, source_target_pairs={{8,0},{16,24},{9,1},{17,25},{10,2},{18,26},{11,3},{19,27},{12,4},{... | collective-permute-start | bytes 2752520 | tf_op jit(solution)/shard_map/ppermute | solution.py:520
  220.5 31.3 %collective-permute-start.21 = (bf16[16,4096]{1,0:T(8,128)(2,1)}, bf16[16,4096]{1,0:T(8,128)(2,1)S(1)}, u32[]{:S(2)}, u32[]{:S(2)}) collective-permute-start(bf16[16,4096]{1,0:T(8,128)(2,1)} %get-tuple-element.74.refs_8_), channel_id=1, source_target_pairs={{0,16},{8,24},{16,0},{24,8},{1,17},{9,25},{17,1},{25,9},{2,18},{10... | collective-permute-start | bytes 393224 | tf_op jit(solution)/shard_map/ppermute | solution.py:26
  233.9 19.3 %collective-permute-start.22 = (bf16[16,4096]{1,0:T(8,128)(2,1)}, bf16[16,4096]{1,0:T(8,128)(2,1)S(1)}, u32[]{:S(2)}, u32[]{:S(2)}) collective-permute-start(bf16[16,4096]{1,0:T(8,128)(2,1)} %get-tuple-element.74.refs_8_), channel_id=1, source_target_pairs={{0,24},{8,16},{16,8},{24,0},{1,25},{9,17},{17,9},{25,1},{2,26},{10... | collective-permute-start | bytes 393224 | tf_op jit(solution)/shard_map/ppermute | solution.py:26
  233.9 60.0 %collective-permute-start.30 = (bf16[112,4096]{1,0:T(8,128)(2,1)}, bf16[112,4096]{1,0:T(8,128)(2,1)}, u32[]{:S(2)}, u32[]{:S(2)}) collective-permute-start(bf16[112,4096]{1,0:T(8,128)(2,1)} %add_convert_fusion.1), channel_id=1, source_target_pairs={{8,16},{16,8},{9,17},{17,9},{10,18},{18,10},{11,19},{19,11},{12,20... | collective-permute-start | bytes 2752520 | tf_op jit(solution)/shard_map/ppermute | solution.py:510
  249.2 35.0 %collective-permute-start.24 = (f32[16,4096]{1,0:T(8,128)}, f32[16,4096]{1,0:T(8,128)}, u32[]{:S(2)}, u32[]{:S(2)}) collective-permute-start(f32[16,4096]{1,0:T(8,128)} %get-tuple-element.76), channel_id=1, source_target_pairs={{0,16},{8,24},{16,0},{24,8},{1,17},{9,25},{17,1},{25,9},{2,18},{10... | collective-permute-start | bytes 786440 | tf_op jit(solution)/shard_map/ppermute | solution.py:26
  251.8 32.4 %collective-permute-start.25 = (f32[16,4096]{1,0:T(8,128)}, f32[16,4096]{1,0:T(8,128)}, u32[]{:S(2)}, u32[]{:S(2)}) collective-permute-start(f32[16,4096]{1,0:T(8,128)} %get-tuple-element.77), channel_id=1, source_target_pairs={{0,24},{8,16},{16,8},{24,0},{1,25},{9,17},{17,9},{25,1},{2,26},{10... | collective-permute-start | bytes 786440 | tf_op jit(solution)/shard_map/ppermute | solution.py:26
  253.2 31.1 %copy-start.21 = (f32[16,2048]{1,0:T(8,128)S(1)}, f32[16,2048]{1,0:T(8,128)}, u32[]{:S(2)}) copy-start(f32[16,2048]{1,0:T(8,128)} %copy-done.20) | copy-start | bytes 393220
  265.4 18.8 %collective-permute-start.23 = (f32[16,4096]{1,0:T(8,128)S(1)}, f32[16,4096]{1,0:T(8,128)S(1)}, u32[]{:S(2)}, u32[]{:S(2)}) collective-permute-start(f32[16,4096]{1,0:T(8,128)S(1)} %get-tuple-element.80), channel_id=1, source_target_pairs={{0,8},{8,0},{16,24},{24,16},{1,9},{9,1},{17,25},{25,17},{2,10},{10... | collective-permute-start | bytes 786440 | tf_op jit(solution)/shard_map/ppermute | solution.py:26
  286.4 9.2 %collective-permute-start.27 = (bf16[16,4096]{1,0:T(8,128)(2,1)S(1)}, bf16[16,4096]{1,0:T(8,128)(2,1)S(1)}, u32[]{:S(2)}, u32[]{:S(2)}) collective-permute-start(bf16[16,4096]{1,0:T(8,128)(2,1)S(1)} %get-tuple-element.100.refs_0_.refs_4_), channel_id=1, source_target_pairs={{0,8},{8,0},{16,24},{24,16},{1,9},{9,1},{17,25},{25,17},{2,10},{10... | collective-permute-start | bytes 393224 | tf_op jit(solution)/shard_map/ppermute | solution.py:26
  291.5 12.1 %collective-permute-start.28 = (bf16[16,4096]{1,0:T(8,128)(2,1)S(1)}, bf16[16,4096]{1,0:T(8,128)(2,1)S(1)}, u32[]{:S(2)}, u32[]{:S(2)}) collective-permute-start(bf16[16,4096]{1,0:T(8,128)(2,1)S(1)} %get-tuple-element.100.refs_0_.refs_4_), channel_id=1, source_target_pairs={{0,16},{8,24},{16,0},{24,8},{1,17},{9,25},{17,1},{25,9},{2,18},{10... | collective-permute-start | bytes 393224 | tf_op jit(solution)/shard_map/ppermute | solution.py:26
  292.4 11.2 %collective-permute-start.29 = (bf16[16,4096]{1,0:T(8,128)(2,1)S(1)}, bf16[16,4096]{1,0:T(8,128)(2,1)S(1)}, u32[]{:S(2)}, u32[]{:S(2)}) collective-permute-start(bf16[16,4096]{1,0:T(8,128)(2,1)S(1)} %get-tuple-element.100.refs_0_.refs_4_), channel_id=1, source_target_pairs={{0,24},{8,16},{16,8},{24,0},{1,25},{9,17},{17,9},{25,1},{2,26},{10... | collective-permute-start | bytes 393224 | tf_op jit(solution)/shard_map/ppermute | solution.py:26
  305.3 22.6 %collective-permute-start.31 = (bf16[112,4096]{1,0:T(8,128)(2,1)S(1)}, bf16[112,4096]{1,0:T(8,128)(2,1)}, u32[]{:S(2)}, u32[]{:S(2)}) collective-permute-start(bf16[112,4096]{1,0:T(8,128)(2,1)S(1)} %add_convert_fusion.refs_4_), channel_id=1, source_target_pairs={{8,0},{16,24},{9,1},{17,25},{10,2},{18,26},{11,3},{19,27},{12,4},{... | collective-permute-start | bytes 2752520 | tf_op jit(solution)/shard_map/ppermute | solution.py:520
  338.0 13.3 %all-to-all-start.1 = ((bf16[8,128,256]{2,1,0:T(8,128)(2,1)}), bf16[8,128,256]{2,1,0:T(8,128)(2,1)S(1)}, u32[]{:S(2)}, u32[]{:S(2)}) async-start(bf16[8,128,256]{2,1,0:T(8,128)(2,1)} %third_forward_1.1), calls=%async_computation.2 | async-start | bytes 1048576 | tf_op jit(solution)/shard_map/all_to_all | solution.py:561
  351.7 1.2 collective-permute-start.32
  353.0 3.6 collective-permute-start.33
  353.5 3.6 collective-permute-start.34
  354.1 4.5 %collective-permute-start.35 = (f32[8,128]{1,0:T(8,128)S(1)}, f32[8,128]{1,0:T(8,128)S(1)}, u32[]{:S(2)}, u32[]{:S(2)}) collective-permute-start(f32[8,128]{1,0:T(8,128)S(1)} %add.155), channel_id=1, source_target_pairs={{0,6},{1,7},{2,4},{3,5},{4,2},{5,3},{6,0},{7,1},{8,14},{9,15},{10,... | collective-permute-start | bytes 12296 | tf_op jit(solution)/shard_map/ppermute | solution.py:26
  358.6 6.2 %collective-permute-start.36 = (f32[8,128]{1,0:T(8,128)S(1)}, f32[8,128]{1,0:T(8,128)S(1)}, u32[]{:S(2)}, u32[]{:S(2)}) collective-permute-start(f32[8,128]{1,0:T(8,128)S(1)} %add_add_fusion.5), channel_id=1, source_target_pairs={{0,8},{8,0},{16,24},{24,16},{1,9},{9,1},{17,25},{25,17},{2,10},{10... | collective-permute-start | bytes 12296 | tf_op jit(solution)/shard_map/ppermute | solution.py:26
  362.2 4.5 %collective-permute-start.37 = (f32[8,128]{1,0:T(8,128)S(1)}, f32[8,128]{1,0:T(8,128)S(1)}, u32[]{:S(2)}, u32[]{:S(2)}) collective-permute-start(f32[8,128]{1,0:T(8,128)S(1)} %add_add_fusion.5), channel_id=1, source_target_pairs={{0,16},{8,24},{16,0},{24,8},{1,17},{9,25},{17,1},{25,9},{2,18},{10... | collective-permute-start | bytes 12296 | tf_op jit(solution)/shard_map/ppermute | solution.py:26
  362.7 5.4 %collective-permute-start.38 = (f32[8,128]{1,0:T(8,128)S(1)}, f32[8,128]{1,0:T(8,128)S(1)}, u32[]{:S(2)}, u32[]{:S(2)}) collective-permute-start(f32[8,128]{1,0:T(8,128)S(1)} %add_add_fusion.5), channel_id=1, source_target_pairs={{0,24},{8,16},{16,8},{24,0},{1,25},{9,17},{17,9},{25,1},{2,26},{10... | collective-permute-start | bytes 12296 | tf_op jit(solution)/shard_map/ppermute | solution.py:26
  (25 other events, 428.3 us)
Sparse Core Ops, SparseCore 0:
  84.8 57.9 reduce-scatter.1
  186.5 56.9 all-gather.1

commit v7 on v6

--- a/solution.py
+++ b/solution.py
@@ -527,20 +527,23 @@
     start_high = start_high.astype(BF16)
 
     start_pieces = [swap(start_high, "sample", k) if k else start_high for k in range(samples)]
-    *start_pieces, chunks[1], chunks[2], first_half = tie((*start_pieces, chunks[1], chunks[2], first_half))
+    *start_pieces, chunks[1], chunks[2], start_low, first_half = tie(
+        (*start_pieces, chunks[1], chunks[2], start_low, first_half)
+    )
     first_half = lax.all_gather(first_half, "sample", axis=1, tiled=True)
     pair[1] = inward(1)
+    low_pieces = [swap(start_low, "sample", k) if k else start_low for k in range(samples)]
     both = jnp.concatenate([near, far])
     value = narrow_forward(start_pieces, both, None, genotypes, "second_forward")
-    value, pair[1], chunks[2], start_low = tie((value, pair[1], chunks[2], start_low))
-    full[1], pair[2] = across(pair[1]), inward(2)
-    low_pieces = [swap(start_low, "sample", k) if k else start_low for k in range(samples)]
+    value, pair[1], chunks[2], *low_pieces = tie((value, pair[1], chunks[2], *low_pieces))
     value = sum_marker(value)
     kept_s = lax.dynamic_slice_in_dim(value, column * share, share, 1)
     rows = value.astype(BF16)
+    (rows,) = tie((rows,), first_half)
     parts = backward(rows, far, genotypes, unit, traits, 0, 0, some, "second_back_far")
     sent = [swap(part, "sample", k + some) for k, part in enumerate(parts)]
-    (rows,) = tie((rows,), full[1], pair[2], *low_pieces, first_half, *parts)
+    full[1], pair[2] = across(pair[1], *parts), inward(2, *parts)
+    (rows,) = tie((rows,), full[1], pair[2], *parts)
     ends[1] = outward(full[1])
     parts = backward(rows, near, genotypes, unit, traits, 0, 0, some, "second_back_near")
     sent = [swap(part, "sample", k) if k else part for k, part in enumerate(parts)] + sent

time: 380 us -> 379 us (level)
  starting transfers between devices: 84.5 us -> 77.1 us
  waiting for transfers between devices: 111 us -> 118 us
    ppermute x33, waiting for transfers between devices: 68.6 us -> 94.2 us  [swap(): return lax.ppermute(x, axis, [(i, i ^ bits) for i in range(n)])]
    ppermute x4, waiting for transfers between devices: 24.9 us -> 6.43 us  [hop(): y = lax.ppermute(x, 'sample', pairs)]
    ppermute x33, starting transfers between devices: 63.9 us -> 57.1 us  [swap(): return lax.ppermute(x, axis, [(i, i ^ bits) for i in range(n)])]
  transfers between devices with their start and end apart: 43 -> 43, of which waited for: 18 -> 25; matrix products, arithmetic and copies ran while one was open for 4% -> 4% of each run, Pallas kernels for 21% -> 21%
where the time goes in v7:
time: 379 us; the launch traced here: 378 us
  Pallas kernels  133 us (35%)
  waiting for transfers between devices  118 us (31%)
  starting transfers between devices  77.1 us (20%)
  other arithmetic  16.6 us (4%)
  between operations  14.7 us (4%)
  blocking collectives  9.95 us (3%)
  local copies, waits for them, and re-layouts  8.61 us (2%)
    ppermute x33, waiting for transfers between devices, swap(): return lax.ppermute(x, axis, [(i, i ^ bits) for i in range(n)])  94.2 us
    ppermute x33, starting transfers between devices, swap(): return lax.ppermute(x, axis, [(i, i ^ bits) for i in range(n)])  57.1 us
    pallas_call x4, Pallas kernels, backward(): pl.pallas_call(functools.partial(back_body, n, unit, t, base, cut), grid_...  52.1 us
    pallas_call x2, Pallas kernels, wide_forward(): pl.pallas_call(functools.partial(wide_body, n, begin, len(inner), chosen,...  28.6 us
    pallas_call x1, Pallas kernels, first_forward(): pl.pallas_call(functools.partial(first_body, markers * columns), grid_spe...  24.5 us
    pallas_call x1, Pallas kernels, narrow_forward(): pl.pallas_call(functools.partial(narrow_body, n, unit, acc is not None),...  22.5 us
    all_to_all x1, waiting for transfers between devices, per_device(): kept_x = jnp.sum(lax.all_to_all(value, 'marker', 0, 0).astype(F32), axis=0)  10.3 us
    ppermute x4, starting transfers between devices, hop(): y = lax.ppermute(x, 'sample', pairs)  10.2 us
  transfers between devices with their start and end apart: 43, of which 25 were waited for; matrix products, arithmetic and copies ran while one was open for 4% of the time, Pallas kernels for 21%

profile of v7, /device:TPU:0, one launch (start us, length us, event | category | flops | bytes accessed | tf_op | source)
XLA Modules:
  0.0 377.6 jit_solution(8192179676479665910)
XLA Ops:
  11.2 2.8 collective-permute-start.1
  15.6 3.5 convert_element_type.65.probes
  20.8 24.5 %first_forward.1 = (bf16[8,144,256]{2,1,0:T(8,128)(2,1)}, f32[16,16384]{1,0:T(8,128)S(1)}) custom-call(s32[1]{0:T(128)} %constant.7.clone.1.off, f32[16,16384]{1,0:T(8,128)S(1)} %copy-done, f32[16,3]{1,0:T(8,128)S(1)} %copy.31.cols, f32[16,1]{1,0:T(8,128)S(1)} %get-tuple-element.109.slopes, bf16[112,16384]{1,0:T(8,128)(2,1)S(1)} %convert_element_type.65.probes, ...), custom_call_target="tpu_custom_call" | custom-call | flops 8589934592 | bytes 67108864 | tf_op jit(solution)/shard_map/first_forward/pallas_call | solution.py:174
  45.4 3.6 all-to-all-start
  49.0 10.3 %all-to-all-done = bf16[8,144,256]{2,1,0:T(8,128)(2,1)S(1)} async-done(((bf16[8,144,256]{2,1,0:T(8,128)(2,1)}), bf16[8,144,256]{2,1,0:T(8,128)(2,1)S(1)}, u32[]{:S(2)}, u32[]{:S(2)}) %all-to-all-start) | async-done | bytes 589856 | tf_op jit(solution)/shard_map/all_to_all | solution.py:484
  60.2 9.9 %all_gather.6.rows = bf16[128,2048]{1,0:T(8,128)(2,1)S(1)} all-gather(bf16[128,256]{1,0:T(8,128)(2,1)S(1)} %pad_maximum_fusion.1), channel_id=1, replica_groups=mesh['sample'=4,'marker'=8] {'marker'}, dimensions={1}, use_global_device_ids=true | all-gather | bytes 589824 | tf_op jit(solution)/shard_map/all_gather | solution.py:489
  70.1 14.5 %first_back_0.1 = (f32[16,2048]{1,0:T(8,128)S(1)}, f32[16,2048]{1,0:T(8,128)}, f32[16,2048]{1,0:T(8,128)}, f32[16,2048]{1,0:T(8,128)}, bf16[112,8192]{1,0:T(8,128)(2,1)}) custom-call(s32[4]{0:T(128)S(1)} %iota_xor_fusion.off, bf16[128,2048]{1,0:T(8,128)(2,1)S(1)} %all_gather.6.rows, bf16[2048,16384]{1,0:T(8,128)(2,1)} %refs_7_.3), custom_call_target="tpu_custom_call" | custom-call | flops 4294967296 | bytes 33554432 | tf_op jit(solution)/shard_map/first_back_0/pallas_call | solution.py:393
  86.9 2.6 collective-permute-start.5
  89.7 13.1 %first_back_1.1 = (f32[16,2048]{1,0:T(8,128)S(1)}, f32[16,2048]{1,0:T(8,128)S(1)}, f32[16,2048]{1,0:T(8,128)S(1)}, f32[16,2048]{1,0:T(8,128)S(1)}, bf16[112,4096...) custom-call(s32[4]{0:T(128)S(1)} %broadcast_add_fusion.off, bf16[128,2048]{1,0:T(8,128)(2,1)S(1)} %all_gather.6.rows, ...), custom_call_target="tpu_custom_call" | custom-call | flops 4294967296 | bytes 33554432 | tf_op jit(solution)/shard_map/first_back_1/pallas_call | solution.py:393
  103.6 3.5 collective-permute-start.8
  107.4 7.3 %collective-permute-done.7 = f32[16,2048]{1,0:T(8,128)S(1)} collective-permute-done((f32[16,2048]{1,0:T(8,128)S(1)}, f32[16,2048]{1,0:T(8,128)S(1)}, u32[]{:S(2)}, u32[]{:S(2)}) %collective-permute-start.7) | collective-permute-done | bytes 131104 | tf_op jit(solution)/shard_map/ppermute | solution.py:26
  114.7 14.2 %collective-permute-done.8 = f32[16,2048]{1,0:T(8,128)S(1)} collective-permute-done((f32[16,2048]{1,0:T(8,128)S(1)}, f32[16,2048]{1,0:T(8,128)S(1)}, u32[]{:S(2)}, u32[]{:S(2)}) %collective-permute-start.8) | collective-permute-done | bytes 131104 | tf_op jit(solution)/shard_map/ppermute | solution.py:26
  129.7 9.3 %collective-permute-start.10 = (bf16[16,4096]{1,0:T(8,128)(2,1)S(1)}, bf16[16,4096]{1,0:T(8,128)(2,1)S(1)}, u32[]{:S(2)}, u32[]{:S(2)}) collective-permute-start(bf16[16,4096]{1,0:T(8,128)(2,1)S(1)} %get-tuple-element.64.refs_0_), channel_id=1, source_target_pairs={{0,8},{8,0},{16,24},{24,16},{1,9},{9,1},{17,25},{25,17},{2,10},{10... | collective-permute-start | bytes 393224 | tf_op jit(solution)/shard_map/ppermute | solution.py:26
  139.0 1.9 collective-permute-start.11
  142.3 2.1 collective-permute-done.10.refs_1_
  144.5 7.6 %collective-permute-done.11.refs_2_ = bf16[16,4096]{1,0:T(8,128)(2,1)S(1)} collective-permute-done((bf16[16,4096]{1,0:T(8,128)(2,1)S(1)}, bf16[16,4096]{1,0:T(8,128)(2,1)S(1)}, u32[]{:S(2)}, u32[]{:S(2)}) %collective-permute-start.11) | collective-permute-done | bytes 131104 | tf_op jit(solution)/shard_map/ppermute | solution.py:26
  152.1 5.3 %collective-permute-start.13 = (bf16[112,4096]{1,0:T(8,128)(2,1)S(1)}, bf16[112,4096]{1,0:T(8,128)(2,1)}, u32[]{:S(2)}, u32[]{:S(2)}) collective-permute-start(bf16[112,4096]{1,0:T(8,128)(2,1)S(1)} %get-tuple-element.69), channel_id=1, source_target_pairs={{0,8},{24,16},{1,9},{25,17},{2,10},{26,18},{3,11},{27,19},{4,12},{... | collective-permute-start | bytes 2752520 | tf_op jit(solution)/shard_map/ppermute | solution.py:510
  160.4 3.0 collective-permute-start.15
  164.8 22.5 %second_forward.1 = f32[16,2048]{1,0:T(8,128)S(1)} custom-call(s32[8]{0:T(128)S(1)} %pad_add_fusion.2.off, bf16[16,4096]{1,0:T(8,128)(2,1)S(1)} %get-tuple-element.64.refs_0_, bf16[16,4096]{1,0:T(8,128)(2,1)S(1)} %collective-permute-done.10.refs_1_, bf16[16,4096]{1,0:T(8,128)(2,1)S(1)} %collective-permute-done.11.refs_2_, ...), custom_call_target="tpu_custom_call" | custom-call | flops 1073741824 | bytes 67108864 | tf_op jit(solution)/shard_map/second_forward/pallas_call | solution.py:222
  187.4 6.4 %collective-permute-done.13 = bf16[112,4096]{1,0:T(8,128)(2,1)} collective-permute-done((bf16[112,4096]{1,0:T(8,128)(2,1)S(1)}, bf16[112,4096]{1,0:T(8,128)(2,1)}, u32[]{:S(2)}, u32[]{:S(2)}) %collective-permute-start.13) | collective-permute-done | bytes 917536 | tf_op jit(solution)/shard_map/ppermute | solution.py:510
  193.8 2.4 add_convert_fusion.3
  196.2 3.3 collective-permute-done.14.refs_9_
  199.6 5.2 %collective-permute-done.15.refs_10_ = bf16[16,4096]{1,0:T(8,128)(2,1)S(1)} collective-permute-done((bf16[16,4096]{1,0:T(8,128)(2,1)}, bf16[16,4096]{1,0:T(8,128)(2,1)S(1)}, u32[]{:S(2)}, u32[]{:S(2)}) %collective-permute-start.15) | collective-permute-done | bytes 131104 | tf_op jit(solution)/shard_map/ppermute | solution.py:26
  204.8 6.6 %collective-permute-done.16.refs_11_ = bf16[16,4096]{1,0:T(8,128)(2,1)S(1)} collective-permute-done((bf16[16,4096]{1,0:T(8,128)(2,1)}, bf16[16,4096]{1,0:T(8,128)(2,1)S(1)}, u32[]{:S(2)}, u32[]{:S(2)}) %collective-permute-start.16) | collective-permute-done | bytes 131104 | tf_op jit(solution)/shard_map/ppermute | solution.py:26
  211.3 2.2 collective-permute-start.22
  218.2 1.8 collective-permute-start.20
  220.1 2.3 collective-permute-done.18
  222.4 3.9 %collective-permute-done.19 = f32[16,2048]{1,0:T(8,128)S(1)} collective-permute-done((f32[16,2048]{1,0:T(8,128)S(1)}, f32[16,2048]{1,0:T(8,128)S(1)}, u32[]{:S(2)}, u32[]{:S(2)}) %collective-permute-start.19) | collective-permute-done | bytes 131104 | tf_op jit(solution)/shard_map/ppermute | solution.py:26
  226.9 12.2 %second_back_far.1 = (f32[16,4096]{1,0:T(8,128)S(1)}, f32[16,4096]{1,0:T(8,128)S(1)}) custom-call(s32[4]{0:T(128)S(1)} %reshape.28.off, bf16[16,2048]{1,0:T(8,128)(2,1)S(1)} %get-tuple-element.84.rows, bf16[2048,16384]{1,0:T(8,128)(2,1)} %refs_7_.3), custom_call_target="tpu_custom_call" | custom-call | flops 536870912 | bytes 33554432 | tf_op jit(solution)/shard_map/second_back_far/pallas_call | solution.py:393
  239.2 1.7 add_convert_fusion.2.refs_5_
  244.8 12.2 %second_back_near.1 = (f32[16,4096]{1,0:T(8,128)S(1)}, f32[16,4096]{1,0:T(8,128)S(1)}) custom-call(s32[4]{0:T(128)S(1)} %reshape.27.off, bf16[16,2048]{1,0:T(8,128)(2,1)S(1)} %get-tuple-element.84.rows, bf16[2048,16384]{1,0:T(8,128)(2,1)} %refs_7_.3), custom_call_target="tpu_custom_call" | custom-call | flops 536870912 | bytes 33554432 | tf_op jit(solution)/shard_map/second_back_near/pallas_call | solution.py:393
  257.0 4.8 %collective-permute-start.23 = (f32[16,4096]{1,0:T(8,128)S(1)}, f32[16,4096]{1,0:T(8,128)S(1)}, u32[]{:S(2)}, u32[]{:S(2)}) collective-permute-start(f32[16,4096]{1,0:T(8,128)S(1)} %get-tuple-element.86), channel_id=1, source_target_pairs={{0,8},{8,0},{16,24},{24,16},{1,9},{9,1},{17,25},{25,17},{2,10},{10... | collective-permute-start | bytes 786440 | tf_op jit(solution)/shard_map/ppermute | solution.py:26
  262.5 1.8 collective-permute-start.25
  264.2 6.3 %collective-permute-done.23 = f32[16,4096]{1,0:T(8,128)S(1)} collective-permute-done((f32[16,4096]{1,0:T(8,128)S(1)}, f32[16,4096]{1,0:T(8,128)S(1)}, u32[]{:S(2)}, u32[]{:S(2)}) %collective-permute-start.23) | collective-permute-done | bytes 262176 | tf_op jit(solution)/shard_map/ppermute | solution.py:26
  270.6 17.5 %collective-permute-done.24 = f32[16,4096]{1,0:T(8,128)S(1)} collective-permute-done((f32[16,4096]{1,0:T(8,128)S(1)}, f32[16,4096]{1,0:T(8,128)S(1)}, u32[]{:S(2)}, u32[]{:S(2)}) %collective-permute-start.24) | collective-permute-done | bytes 262176 | tf_op jit(solution)/shard_map/ppermute | solution.py:26
  288.9 3.9 %collective-permute-start.27 = (bf16[16,4096]{1,0:T(8,128)(2,1)S(1)}, bf16[16,4096]{1,0:T(8,128)(2,1)S(1)}, u32[]{:S(2)}, u32[]{:S(2)}) collective-permute-start(bf16[16,4096]{1,0:T(8,128)(2,1)S(1)} %get-tuple-element.110.refs_0_.refs_4_), channel_id=1, source_target_pairs={{0,8},{8,0},{16,24},{24,16},{1,9},{9,1},{17,25},{25,17},{2,10},{10... | collective-permute-start | bytes 393224 | tf_op jit(solution)/shard_map/ppermute | solution.py:26
  293.2 2.0 collective-permute-start.29
  296.5 7.1 %collective-permute-done.28.refs_2_.refs_6_ = bf16[16,4096]{1,0:T(8,128)(2,1)S(1)} collective-permute-done((bf16[16,4096]{1,0:T(8,128)(2,1)S(1)}, bf16[16,4096]{1,0:T(8,128)(2,1)S(1)}, u32[]{:S(2)}, u32[]{:S(2)}) %collective-permute-start.28) | collective-permute-done | bytes 131104 | tf_op jit(solution)/shard_map/ppermute | solution.py:26
  307.9 18.6 %third_forward_0.1.refs_6_ = f32[2048,128]{1,0:T(8,128)S(1)} custom-call(s32[5]{0:T(128)S(1)} %pad_add_fusion.3.off, bf16[16,4096]{1,0:T(8,128)(2,1)S(1)} %get-tuple-element.110.refs_0_.refs_4_, bf16[16,4096]{1,0:T(8,128)(2,1)S(1)} %collective-permute-done.27.refs_1_.refs_5_, bf16[16,4096]{1,0:T(8,128)(2,1)S(1)} %collective-permute-done.28.refs_2_.refs_6_, ...), custom_call_target="tpu_custom_call" | custom-call | flops 6442450944 | bytes 50331648 | tf_op jit(solution)/shard_map/third_forward_0/pallas_call | solution.py:302
  326.8 10.0 %third_forward_1.1 = bf16[8,128,256]{2,1,0:T(8,128)(2,1)} custom-call(s32[5]{0:T(128)S(1)} %pad_add_fusion.3.off, bf16[16,4096]{1,0:T(8,128)(2,1)S(1)} %get-tuple-element.110.refs_0_.refs_4_, bf16[16,4096]{1,0:T(8,128)(2,1)S(1)} %collective-permute-done.27.refs_1_.refs_5_, bf16[16,4096]{1,0:T(8,128)(2,1)S(1)} %collective-permute-done.28.refs_2_.refs_6_, ...), custom_call_target="tpu_custom_call" | custom-call | flops 2147483648 | bytes 16777216 | tf_op jit(solution)/shard_map/third_forward_1/pallas_call | solution.py:302
  336.8 3.6 all-to-all-start.1
  340.7 1.8 multiply_reduce_fusion
  343.3 6.8 %all-to-all-done.1 = bf16[8,128,256]{2,1,0:T(8,128)(2,1)S(1)} async-done(((bf16[8,128,256]{2,1,0:T(8,128)(2,1)}), bf16[8,128,256]{2,1,0:T(8,128)(2,1)S(1)}, u32[]{:S(2)}, u32[]{:S(2)}) %all-to-all-start.1) | async-done | bytes 524320 | tf_op jit(solution)/shard_map/all_to_all | solution.py:564
  353.0 2.4 collective-permute-start.35
  357.5 3.3 collective-permute-start.36
  361.2 1.9 collective-permute-start.38
  363.4 1.9 collective-permute-done.37
  366.7 4.1 %finish.1 = (f32[16,16384]{1,0:T(8,128)}, f32[16,16384]{1,0:T(8,128)}) custom-call(s32[4]{0:T(128)S(1)} %iota_xor_fusion.off, f32[8,128]{1,0:T(8,128)S(1)} %add_add_fusion.4.sums, f32[128,2]{1,0:T(8,128)S(1)} %copy.34.wide_cols, f32[16,3]{1,0:T(8,128)S(1)} %copy.35.cols, f32[16,16384]{1,0:T(8,128)S(1)} %get-tuple-element.93.centre, ...), custom_call_target="tpu_custom_call" | custom-call | tf_op jit(solution)/shard_map/finish/pallas_call | solution.py:453
  (163 shorter events, 43.2 us)
Async XLA Ops:
  9.9 1.3 collective-permute-start
  11.2 7.9 %collective-permute-start.1 = (f32[16,1]{1,0:T(8,128)S(1)}, f32[16,1]{1,0:T(8,128)S(1)}, u32[]{:S(2)}, u32[]{:S(2)}) collective-permute-start(f32[16,1]{1,0:T(8,128)S(1)} %add.125), channel_id=1, source_target_pairs={{0,2},{1,3},{2,0},{3,1},{4,6},{5,7},{6,4},{7,5},{8,10},{9,11},{10,... | collective-permute-start | bytes 200 | tf_op jit(solution)/shard_map/ppermute | solution.py:26
  14.1 5.0 %collective-permute-start.2 = (f32[16,1]{1,0:T(8,128)S(1)}, f32[16,1]{1,0:T(8,128)S(1)}, u32[]{:S(2)}, u32[]{:S(2)}) collective-permute-start(f32[16,1]{1,0:T(8,128)S(1)} %add.125), channel_id=1, source_target_pairs={{0,4},{1,5},{2,6},{3,7},{4,0},{5,1},{6,2},{7,3},{8,12},{9,13},{10,... | collective-permute-start | bytes 200 | tf_op jit(solution)/shard_map/ppermute | solution.py:26
  15.6 4.5 %collective-permute-start.3 = (f32[16,1]{1,0:T(8,128)S(1)}, f32[16,1]{1,0:T(8,128)S(1)}, u32[]{:S(2)}, u32[]{:S(2)}) collective-permute-start(f32[16,1]{1,0:T(8,128)S(1)} %add.125), channel_id=1, source_target_pairs={{0,6},{1,7},{2,4},{3,5},{4,2},{5,3},{6,0},{7,1},{8,14},{9,15},{10,... | collective-permute-start | bytes 200 | tf_op jit(solution)/shard_map/ppermute | solution.py:26
  45.4 13.9 %all-to-all-start = ((bf16[8,144,256]{2,1,0:T(8,128)(2,1)}), bf16[8,144,256]{2,1,0:T(8,128)(2,1)S(1)}, u32[]{:S(2)}, u32[]{:S(2)}) async-start(bf16[8,144,256]{2,1,0:T(8,128)(2,1)} %get-tuple-element.51), calls=%async_computation | async-start | bytes 1179648 | tf_op jit(solution)/shard_map/all_to_all | solution.py:484
  48.9 103.2 %reduce-scatter.2.cloned.1.call-start = ((), (), s32[]{:S(2)}) async-start(), calls=%async_computation.3 | async-start | bytes 2293760 | tf_op jit(solution)/shard_map/reduce_scatter | solution.py:501
  84.7 142.2 %all-gather.2.cloned.1.call-start = ((), (), s32[]{:S(2)}) async-start(), calls=%async_computation.4 | async-start | bytes 2293760 | tf_op jit(solution)/shard_map/all_gather | solution.py:533
  85.3 21.8 %collective-permute-start.4 = (f32[16,2048]{1,0:T(8,128)}, f32[16,2048]{1,0:T(8,128)S(1)}, u32[]{:S(2)}, u32[]{:S(2)}) collective-permute-start(f32[16,2048]{1,0:T(8,128)} %get-tuple-element.53), channel_id=1, source_target_pairs={{0,8},{8,0},{16,24},{24,16},{1,9},{9,1},{17,25},{25,17},{2,10},{10... | collective-permute-start | bytes 393224 | tf_op jit(solution)/shard_map/ppermute | solution.py:26
  86.9 20.4 %collective-permute-start.5 = (f32[16,2048]{1,0:T(8,128)}, f32[16,2048]{1,0:T(8,128)S(1)}, u32[]{:S(2)}, u32[]{:S(2)}) collective-permute-start(f32[16,2048]{1,0:T(8,128)} %get-tuple-element.54), channel_id=1, source_target_pairs={{0,16},{8,24},{16,0},{24,8},{1,17},{9,25},{17,1},{25,9},{2,18},{10... | collective-permute-start | bytes 393224 | tf_op jit(solution)/shard_map/ppermute | solution.py:26
  89.5 17.8 %collective-permute-start.6 = (f32[16,2048]{1,0:T(8,128)}, f32[16,2048]{1,0:T(8,128)S(1)}, u32[]{:S(2)}, u32[]{:S(2)}) collective-permute-start(f32[16,2048]{1,0:T(8,128)} %get-tuple-element.55), channel_id=1, source_target_pairs={{0,24},{8,16},{16,8},{24,0},{1,25},{9,17},{17,9},{25,1},{2,26},{10... | collective-permute-start | bytes 393224 | tf_op jit(solution)/shard_map/ppermute | solution.py:26
  102.9 108.4 %copy-start.4 = (bf16[112,4096]{1,0:T(8,128)(2,1)}, bf16[112,4096]{1,0:T(8,128)(2,1)S(1)}, u32[]{:S(2)}) copy-start(bf16[112,4096]{1,0:T(8,128)(2,1)S(1)} %get-tuple-element.82) | copy-start | bytes 2752516
  102.9 11.8 %collective-permute-start.7 = (f32[16,2048]{1,0:T(8,128)S(1)}, f32[16,2048]{1,0:T(8,128)S(1)}, u32[]{:S(2)}, u32[]{:S(2)}) collective-permute-start(f32[16,2048]{1,0:T(8,128)S(1)} %get-tuple-element.59), channel_id=1, source_target_pairs={{0,8},{8,0},{16,24},{24,16},{1,9},{9,1},{17,25},{25,17},{2,10},{10... | collective-permute-start | bytes 393224 | tf_op jit(solution)/shard_map/ppermute | solution.py:26
  103.6 25.2 %collective-permute-start.8 = (f32[16,2048]{1,0:T(8,128)S(1)}, f32[16,2048]{1,0:T(8,128)S(1)}, u32[]{:S(2)}, u32[]{:S(2)}) collective-permute-start(f32[16,2048]{1,0:T(8,128)S(1)} %get-tuple-element.60), channel_id=1, source_target_pairs={{0,16},{8,24},{16,0},{24,8},{1,17},{9,25},{17,1},{25,9},{2,18},{10... | collective-permute-start | bytes 393224 | tf_op jit(solution)/shard_map/ppermute | solution.py:26
  107.1 21.7 %collective-permute-start.9 = (f32[16,2048]{1,0:T(8,128)S(1)}, f32[16,2048]{1,0:T(8,128)S(1)}, u32[]{:S(2)}, u32[]{:S(2)}) collective-permute-start(f32[16,2048]{1,0:T(8,128)S(1)} %get-tuple-element.61), channel_id=1, source_target_pairs={{0,24},{8,16},{16,8},{24,0},{1,25},{9,17},{17,9},{25,1},{2,26},{10... | collective-permute-start | bytes 393224 | tf_op jit(solution)/shard_map/ppermute | solution.py:26
  129.7 14.8 %collective-permute-start.10 = (bf16[16,4096]{1,0:T(8,128)(2,1)S(1)}, bf16[16,4096]{1,0:T(8,128)(2,1)S(1)}, u32[]{:S(2)}, u32[]{:S(2)}) collective-permute-start(bf16[16,4096]{1,0:T(8,128)(2,1)S(1)} %get-tuple-element.64.refs_0_), channel_id=1, source_target_pairs={{0,8},{8,0},{16,24},{24,16},{1,9},{9,1},{17,25},{25,17},{2,10},{10... | collective-permute-start | bytes 393224 | tf_op jit(solution)/shard_map/ppermute | solution.py:26
  139.0 13.1 %collective-permute-start.11 = (bf16[16,4096]{1,0:T(8,128)(2,1)S(1)}, bf16[16,4096]{1,0:T(8,128)(2,1)S(1)}, u32[]{:S(2)}, u32[]{:S(2)}) collective-permute-start(bf16[16,4096]{1,0:T(8,128)(2,1)S(1)} %get-tuple-element.64.refs_0_), channel_id=1, source_target_pairs={{0,16},{8,24},{16,0},{24,8},{1,17},{9,25},{17,1},{25,9},{2,18},{10... | collective-permute-start | bytes 393224 | tf_op jit(solution)/shard_map/ppermute | solution.py:26
  140.9 11.2 %collective-permute-start.12 = (bf16[16,4096]{1,0:T(8,128)(2,1)S(1)}, bf16[16,4096]{1,0:T(8,128)(2,1)S(1)}, u32[]{:S(2)}, u32[]{:S(2)}) collective-permute-start(bf16[16,4096]{1,0:T(8,128)(2,1)S(1)} %get-tuple-element.64.refs_0_), channel_id=1, source_target_pairs={{0,24},{8,16},{16,8},{24,0},{1,25},{9,17},{17,9},{25,1},{2,26},{10... | collective-permute-start | bytes 393224 | tf_op jit(solution)/shard_map/ppermute | solution.py:26
  144.5 42.9 %copy-start.6 = (bf16[16,4096]{1,0:T(8,128)(2,1)}, bf16[16,4096]{1,0:T(8,128)(2,1)S(1)}, u32[]{:S(2)}) copy-start(bf16[16,4096]{1,0:T(8,128)(2,1)S(1)} %collective-permute-done.10.refs_1_) | copy-start | bytes 393220
  152.1 35.3 %copy-start.8 = (bf16[16,4096]{1,0:T(8,128)(2,1)}, bf16[16,4096]{1,0:T(8,128)(2,1)S(1)}, u32[]{:S(2)}) copy-start(bf16[16,4096]{1,0:T(8,128)(2,1)S(1)} %collective-permute-done.11.refs_2_) | copy-start | bytes 393220
  152.1 35.3 %copy-start.10 = (bf16[16,4096]{1,0:T(8,128)(2,1)}, bf16[16,4096]{1,0:T(8,128)(2,1)S(1)}, u32[]{:S(2)}) copy-start(bf16[16,4096]{1,0:T(8,128)(2,1)S(1)} %collective-permute-done.12.refs_3_) | copy-start | bytes 393220
  152.1 41.7 %collective-permute-start.13 = (bf16[112,4096]{1,0:T(8,128)(2,1)S(1)}, bf16[112,4096]{1,0:T(8,128)(2,1)}, u32[]{:S(2)}, u32[]{:S(2)}) collective-permute-start(bf16[112,4096]{1,0:T(8,128)(2,1)S(1)} %get-tuple-element.69), channel_id=1, source_target_pairs={{0,8},{24,16},{1,9},{25,17},{2,10},{26,18},{3,11},{27,19},{4,12},{... | collective-permute-start | bytes 2752520 | tf_op jit(solution)/shard_map/ppermute | solution.py:510
  160.4 39.1 %collective-permute-start.14 = (bf16[16,4096]{1,0:T(8,128)(2,1)}, bf16[16,4096]{1,0:T(8,128)(2,1)S(1)}, u32[]{:S(2)}, u32[]{:S(2)}) collective-permute-start(bf16[16,4096]{1,0:T(8,128)(2,1)} %get-tuple-element.94.refs_8_), channel_id=1, source_target_pairs={{0,8},{8,0},{16,24},{24,16},{1,9},{9,1},{17,25},{25,17},{2,10},{10... | collective-permute-start | bytes 393224 | tf_op jit(solution)/shard_map/ppermute | solution.py:26
  160.4 44.3 %collective-permute-start.15 = (bf16[16,4096]{1,0:T(8,128)(2,1)}, bf16[16,4096]{1,0:T(8,128)(2,1)S(1)}, u32[]{:S(2)}, u32[]{:S(2)}) collective-permute-start(bf16[16,4096]{1,0:T(8,128)(2,1)} %get-tuple-element.94.refs_8_), channel_id=1, source_target_pairs={{0,16},{8,24},{16,0},{24,8},{1,17},{9,25},{17,1},{25,9},{2,18},{10... | collective-permute-start | bytes 393224 | tf_op jit(solution)/shard_map/ppermute | solution.py:26
  163.4 47.9 %collective-permute-start.16 = (bf16[16,4096]{1,0:T(8,128)(2,1)}, bf16[16,4096]{1,0:T(8,128)(2,1)S(1)}, u32[]{:S(2)}, u32[]{:S(2)}) collective-permute-start(bf16[16,4096]{1,0:T(8,128)(2,1)} %get-tuple-element.94.refs_8_), channel_id=1, source_target_pairs={{0,24},{8,16},{16,8},{24,0},{1,25},{9,17},{17,9},{25,1},{2,26},{10... | collective-permute-start | bytes 393224 | tf_op jit(solution)/shard_map/ppermute | solution.py:26
  211.3 27.8 %collective-permute-start.22 = (bf16[112,4096]{1,0:T(8,128)(2,1)S(1)}, bf16[112,4096]{1,0:T(8,128)(2,1)}, u32[]{:S(2)}, u32[]{:S(2)}) collective-permute-start(bf16[112,4096]{1,0:T(8,128)(2,1)S(1)} %get-tuple-element.82), channel_id=1, source_target_pairs={{0,8},{24,16},{1,9},{25,17},{2,10},{26,18},{3,11},{27,19},{4,12},{... | collective-permute-start | bytes 2752520 | tf_op jit(solution)/shard_map/ppermute | solution.py:510
  213.5 25.6 %collective-permute-start.21 = (bf16[112,4096]{1,0:T(8,128)(2,1)}, bf16[112,4096]{1,0:T(8,128)(2,1)}, u32[]{:S(2)}, u32[]{:S(2)}) collective-permute-start(bf16[112,4096]{1,0:T(8,128)(2,1)} %add_convert_fusion.3), channel_id=1, source_target_pairs={{8,16},{16,8},{9,17},{17,9},{10,18},{18,10},{11,19},{19,11},{12,20... | collective-permute-start | bytes 2752520 | tf_op jit(solution)/shard_map/ppermute | solution.py:510
  215.1 1.3 collective-permute-start.17
  216.5 5.9 %collective-permute-start.18 = (f32[16,2048]{1,0:T(8,128)S(1)}, f32[16,2048]{1,0:T(8,128)S(1)}, u32[]{:S(2)}, u32[]{:S(2)}) collective-permute-start(f32[16,2048]{1,0:T(8,128)S(1)} %add.140), channel_id=1, source_target_pairs={{0,2},{1,3},{2,0},{3,1},{4,6},{5,7},{6,4},{7,5},{8,10},{9,11},{10,... | collective-permute-start | bytes 393224 | tf_op jit(solution)/shard_map/ppermute | solution.py:26
  218.2 8.1 %collective-permute-start.19 = (f32[16,2048]{1,0:T(8,128)S(1)}, f32[16,2048]{1,0:T(8,128)S(1)}, u32[]{:S(2)}, u32[]{:S(2)}) collective-permute-start(f32[16,2048]{1,0:T(8,128)S(1)} %add.140), channel_id=1, source_target_pairs={{0,4},{1,5},{2,6},{3,7},{4,0},{5,1},{6,2},{7,3},{8,12},{9,13},{10,... | collective-permute-start | bytes 393224 | tf_op jit(solution)/shard_map/ppermute | solution.py:26
  218.2 8.0 %collective-permute-start.20 = (f32[16,2048]{1,0:T(8,128)S(1)}, f32[16,2048]{1,0:T(8,128)S(1)}, u32[]{:S(2)}, u32[]{:S(2)}) collective-permute-start(f32[16,2048]{1,0:T(8,128)S(1)} %add.140), channel_id=1, source_target_pairs={{0,6},{1,7},{2,4},{3,5},{4,2},{5,3},{6,0},{7,1},{8,14},{9,15},{10,... | collective-permute-start | bytes 393224 | tf_op jit(solution)/shard_map/ppermute | solution.py:26
  240.9 47.1 %collective-permute-start.26 = (bf16[112,4096]{1,0:T(8,128)(2,1)S(1)}, bf16[112,4096]{1,0:T(8,128)(2,1)S(1)}, u32[]{:S(2)}, u32[]{:S(2)}) collective-permute-start(bf16[112,4096]{1,0:T(8,128)(2,1)S(1)} %add_convert_fusion.2.refs_5_), channel_id=1, source_target_pairs={{8,0},{16,24},{9,1},{17,25},{10,2},{18,26},{11,3},{19,27},{12,4},{... | collective-permute-start | bytes 2752520 | tf_op jit(solution)/shard_map/ppermute | solution.py:520
  243.7 44.3 %copy-start.19 = (f32[16,2048]{1,0:T(8,128)S(1)}, f32[16,2048]{1,0:T(8,128)}, u32[]{:S(2)}) copy-start(f32[16,2048]{1,0:T(8,128)} %copy-done.18) | copy-start | bytes 393220
  243.7 51.5 %collective-permute-start.30 = (bf16[112,4096]{1,0:T(8,128)(2,1)S(1)}, bf16[112,4096]{1,0:T(8,128)(2,1)S(1)}, u32[]{:S(2)}, u32[]{:S(2)}) collective-permute-start(bf16[112,4096]{1,0:T(8,128)(2,1)S(1)} %add_convert_fusion.1), channel_id=1, source_target_pairs={{8,16},{16,8},{9,17},{17,9},{10,18},{18,10},{11,19},{19,11},{12,20... | collective-permute-start | bytes 2752520 | tf_op jit(solution)/shard_map/ppermute | solution.py:510
  257.0 13.6 %collective-permute-start.23 = (f32[16,4096]{1,0:T(8,128)S(1)}, f32[16,4096]{1,0:T(8,128)S(1)}, u32[]{:S(2)}, u32[]{:S(2)}) collective-permute-start(f32[16,4096]{1,0:T(8,128)S(1)} %get-tuple-element.86), channel_id=1, source_target_pairs={{0,8},{8,0},{16,24},{24,16},{1,9},{9,1},{17,25},{25,17},{2,10},{10... | collective-permute-start | bytes 786440 | tf_op jit(solution)/shard_map/ppermute | solution.py:26
  261.8 26.2 %collective-permute-start.24 = (f32[16,4096]{1,0:T(8,128)S(1)}, f32[16,4096]{1,0:T(8,128)S(1)}, u32[]{:S(2)}, u32[]{:S(2)}) collective-permute-start(f32[16,4096]{1,0:T(8,128)S(1)} %get-tuple-element.77), channel_id=1, source_target_pairs={{0,16},{8,24},{16,0},{24,8},{1,17},{9,25},{17,1},{25,9},{2,18},{10... | collective-permute-start | bytes 786440 | tf_op jit(solution)/shard_map/ppermute | solution.py:26
  262.5 25.6 %collective-permute-start.25 = (f32[16,4096]{1,0:T(8,128)S(1)}, f32[16,4096]{1,0:T(8,128)S(1)}, u32[]{:S(2)}, u32[]{:S(2)}) collective-permute-start(f32[16,4096]{1,0:T(8,128)S(1)} %get-tuple-element.78), channel_id=1, source_target_pairs={{0,24},{8,16},{16,8},{24,0},{1,25},{9,17},{17,9},{25,1},{2,26},{10... | collective-permute-start | bytes 786440 | tf_op jit(solution)/shard_map/ppermute | solution.py:26
  288.9 7.6 %collective-permute-start.27 = (bf16[16,4096]{1,0:T(8,128)(2,1)S(1)}, bf16[16,4096]{1,0:T(8,128)(2,1)S(1)}, u32[]{:S(2)}, u32[]{:S(2)}) collective-permute-start(bf16[16,4096]{1,0:T(8,128)(2,1)S(1)} %get-tuple-element.110.refs_0_.refs_4_), channel_id=1, source_target_pairs={{0,8},{8,0},{16,24},{24,16},{1,9},{9,1},{17,25},{25,17},{2,10},{10... | collective-permute-start | bytes 393224 | tf_op jit(solution)/shard_map/ppermute | solution.py:26
  292.9 10.7 %collective-permute-start.28 = (bf16[16,4096]{1,0:T(8,128)(2,1)S(1)}, bf16[16,4096]{1,0:T(8,128)(2,1)S(1)}, u32[]{:S(2)}, u32[]{:S(2)}) collective-permute-start(bf16[16,4096]{1,0:T(8,128)(2,1)S(1)} %get-tuple-element.110.refs_0_.refs_4_), channel_id=1, source_target_pairs={{0,16},{8,24},{16,0},{24,8},{1,17},{9,25},{17,1},{25,9},{2,18},{10... | collective-permute-start | bytes 393224 | tf_op jit(solution)/shard_map/ppermute | solution.py:26
  293.2 10.4 %collective-permute-start.29 = (bf16[16,4096]{1,0:T(8,128)(2,1)S(1)}, bf16[16,4096]{1,0:T(8,128)(2,1)S(1)}, u32[]{:S(2)}, u32[]{:S(2)}) collective-permute-start(bf16[16,4096]{1,0:T(8,128)(2,1)S(1)} %get-tuple-element.110.refs_0_.refs_4_), channel_id=1, source_target_pairs={{0,24},{8,16},{16,8},{24,0},{1,25},{9,17},{17,9},{25,1},{2,26},{10... | collective-permute-start | bytes 393224 | tf_op jit(solution)/shard_map/ppermute | solution.py:26
  303.8 23.0 %collective-permute-start.31 = (bf16[112,4096]{1,0:T(8,128)(2,1)S(1)}, bf16[112,4096]{1,0:T(8,128)(2,1)}, u32[]{:S(2)}, u32[]{:S(2)}) collective-permute-start(bf16[112,4096]{1,0:T(8,128)(2,1)S(1)} %add_convert_fusion.refs_4_), channel_id=1, source_target_pairs={{8,0},{16,24},{9,1},{17,25},{10,2},{18,26},{11,3},{19,27},{12,4},{... | collective-permute-start | bytes 2752520 | tf_op jit(solution)/shard_map/ppermute | solution.py:520
  336.8 13.3 %all-to-all-start.1 = ((bf16[8,128,256]{2,1,0:T(8,128)(2,1)}), bf16[8,128,256]{2,1,0:T(8,128)(2,1)S(1)}, u32[]{:S(2)}, u32[]{:S(2)}) async-start(bf16[8,128,256]{2,1,0:T(8,128)(2,1)} %third_forward_1.1), calls=%async_computation.2 | async-start | bytes 1048576 | tf_op jit(solution)/shard_map/all_to_all | solution.py:564
  350.6 1.2 collective-permute-start.32
  351.8 3.6 collective-permute-start.33
  352.4 3.6 collective-permute-start.34
  353.0 4.5 %collective-permute-start.35 = (f32[8,128]{1,0:T(8,128)S(1)}, f32[8,128]{1,0:T(8,128)S(1)}, u32[]{:S(2)}, u32[]{:S(2)}) collective-permute-start(f32[8,128]{1,0:T(8,128)S(1)} %add.155), channel_id=1, source_target_pairs={{0,6},{1,7},{2,4},{3,5},{4,2},{5,3},{6,0},{7,1},{8,14},{9,15},{10,... | collective-permute-start | bytes 12296 | tf_op jit(solution)/shard_map/ppermute | solution.py:26
  357.5 5.9 %collective-permute-start.36 = (f32[8,128]{1,0:T(8,128)S(1)}, f32[8,128]{1,0:T(8,128)S(1)}, u32[]{:S(2)}, u32[]{:S(2)}) collective-permute-start(f32[8,128]{1,0:T(8,128)S(1)} %add_add_fusion.5), channel_id=1, source_target_pairs={{0,8},{8,0},{16,24},{24,16},{1,9},{9,1},{17,25},{25,17},{2,10},{10... | collective-permute-start | bytes 12296 | tf_op jit(solution)/shard_map/ppermute | solution.py:26
  360.7 4.5 %collective-permute-start.37 = (f32[8,128]{1,0:T(8,128)S(1)}, f32[8,128]{1,0:T(8,128)S(1)}, u32[]{:S(2)}, u32[]{:S(2)}) collective-permute-start(f32[8,128]{1,0:T(8,128)S(1)} %add_add_fusion.5), channel_id=1, source_target_pairs={{0,16},{8,24},{16,0},{24,8},{1,17},{9,25},{17,1},{25,9},{2,18},{10... | collective-permute-start | bytes 12296 | tf_op jit(solution)/shard_map/ppermute | solution.py:26
  361.2 5.4 %collective-permute-start.38 = (f32[8,128]{1,0:T(8,128)S(1)}, f32[8,128]{1,0:T(8,128)S(1)}, u32[]{:S(2)}, u32[]{:S(2)}) collective-permute-start(f32[8,128]{1,0:T(8,128)S(1)} %add_add_fusion.5), channel_id=1, source_target_pairs={{0,24},{8,16},{16,8},{24,0},{1,25},{9,17},{17,9},{25,1},{2,26},{10... | collective-permute-start | bytes 12296 | tf_op jit(solution)/shard_map/ppermute | solution.py:26
  (25 other events, 332.7 us)
Sparse Core Ops, SparseCore 0:
  84.8 57.9 reduce-scatter.1
  152.3 64.6 all-gather.1

commit v8 on v5

--- a/solution.py
+++ b/solution.py
@@ -367,17 +367,17 @@
             copies.append(pltpu.make_async_copy(part, lower.at[:, pl.ds(0, unit)], sent.at[j]))
     span = outs[0].shape[1]
     for j, out in enumerate(outs):
-        out[...] = total[:t, j * span : (j + 1) * span]
+        out[...] = total[:t, j * span : (j + 1) * span].astype(out.dtype)
     for copy in copies:
         copy.wait()
 
 
-def backward(rows, places, genotypes, unit, t, base, cut, arrays, name):
+def backward(rows, places, genotypes, unit, t, base, cut, types, name):
     people = genotypes.shape[0]
     r, n = rows.shape[0], places.shape[0]
     pk, mb = block_of(people, 1024), block_of(unit, 2048)
-    out_specs = [VMEM] * arrays
-    out_shape = [jax.ShapeDtypeStruct((t, n * unit // arrays), F32)] * arrays
+    out_specs = [VMEM] * len(types)
+    out_shape = [jax.ShapeDtypeStruct((t, n * unit // len(types)), kind) for kind in types]
     scratch = [pltpu.VMEM((r, n * unit), F32)]
     if t != r:
         out_specs += [ANY] * 2
@@ -403,6 +403,7 @@
     start_hi, back_hi, low = refs[:n], refs[n : 2 * n], refs[2 * n : 3 * n]
     estimate, lmmse = refs[3 * n :]
     t, unit = start_hi[0].shape[0], start_hi[0].shape[1] // 2
+    sums = sums[...].T
     norm_start, du, uu, xx, xw, ww = [sums[:, j : j + 1] for j in range(6)]
     tau, gamma = wide_cols[:, 0:1], wide_cols[:, 1:2]
     second_precision, slab_var, odds = [cols[:, j : j + 1] for j in range(3)]
@@ -440,7 +441,7 @@
 def finish(places, sums, wide_cols, cols, centre, start_hi, back_hi, low):
     n = len(low)
     shape = jax.ShapeDtypeStruct(centre.shape, F32)
-    copies = sums.shape[0] // centre.shape[0]
+    copies = sums.shape[1] // centre.shape[0]
     operands = [sums, wide_cols, cols, centre, *start_hi, *back_hi, *low]
     return pl.pallas_call(
         functools.partial(finish_body, n, copies),
@@ -483,7 +484,7 @@
     for half, cut in enumerate((samples - 1, some)):
         base = half * samples
         *parts, lower, upper = backward(
-            rows, order + base, genotypes, unit, traits, base, cut, samples, f"first_back_{half}"
+            rows, order + base, genotypes, unit, traits, base, cut, [F32] * samples, f"first_back_{half}"
         )
         starts.append([swap(part, "sample", k) if k else part for k, part in enumerate(parts)])
         chunks += [lower, upper]
@@ -519,21 +520,22 @@
 
     start_pieces = [swap(start_high, "sample", k) if k else start_high for k in range(samples)]
     *start_pieces, pair[0], chunks[1] = tie((*start_pieces, pair[0], chunks[1]))
-    full[0], pair[1] = across(pair[0]), inward(1)
     both = jnp.concatenate([near, far])
     value = narrow_forward(start_pieces, both, None, genotypes, "second_forward")
-    value, chunks[2] = tie((value, chunks[2]), full[0], pair[1])
-    ends[0], full[1], pair[2] = outward(full[0]), across(pair[1]), inward(2)
+    full[0], pair[1] = across(pair[0], value), inward(1, value)
+    value, pair[1], chunks[2] = tie((value, pair[1], chunks[2]), full[0])
+    ends[0] = outward(full[0])
     value = sum_marker(value)
     kept_s = lax.dynamic_slice_in_dim(value, column * share, share, 1)
     rows = value.astype(BF16)
-    parts = backward(rows, far, genotypes, unit, traits, 0, 0, some, "second_back_far")
+    parts = backward(rows, far, genotypes, unit, traits, 0, 0, [BF16] * some, "second_back_far")
     sent = [swap(part, "sample", k + some) for k, part in enumerate(parts)]
+    full[1], pair[2] = across(pair[1], *parts), inward(2, *parts)
     (rows,) = tie((rows,), full[1], pair[2], ends[0], *parts)
     ends[1] = outward(full[1])
-    parts = backward(rows, near, genotypes, unit, traits, 0, 0, some, "second_back_near")
+    parts = backward(rows, near, genotypes, unit, traits, 0, 0, [F32] + [BF16] * (some - 1), "second_back_near")
     sent = [swap(part, "sample", k) if k else part for k, part in enumerate(parts)] + sent
-    back_high = tree(list(tie(sent, ends[1]))).astype(BF16)
+    back_high = tree([part.astype(F32) for part in tie(sent, ends[1])]).astype(BF16)
     back = back_high.astype(F32)
     back_pieces = [swap(back_high, "sample", k) if k else back_high for k in range(samples)]
     full[2] = across(pair[2], *back_pieces)
@@ -562,15 +564,14 @@
     kept_p, last_p = kept_x[traits:], last[traits:]
     norms = jnp.concatenate(
         [
-            jnp.stack([dot(start, start), dot(start, back), dot(back, back)], axis=1),
-            jnp.stack(
-                [sum(dot(p, p) for p in probes_here), dot(kept_p, pred_x), dot(last_p, pred_x)], axis=1
-            ),
+            jnp.stack([dot(start, start), dot(start, back), dot(back, back)]),
+            jnp.stack([sum(dot(p, p) for p in probes_here), dot(kept_p, pred_x), dot(last_p, pred_x)]),
         ],
-        axis=0,
-    )
-    squares = jnp.stack([dot(before, before), dot(before, last), dot(last, last)], axis=1)
-    sums = sum_direct(sum_marker(jnp.concatenate([norms, squares], axis=1)), "sample")
+        axis=1,
+    )
+    squares = jnp.stack([dot(before, before), dot(before, last), dot(last, last)])
+    sums = jnp.concatenate([norms, squares, jnp.zeros((2, norms.shape[1]), F32)], axis=0)
+    sums = sum_direct(sum_marker(sums), "sample")
 
     first_slope = slopes[:, 0] / markers
     second_precision = input_precision * (1.0 - first_slope) / first_slope

time: 367 us -> 362 us (0.986)
  waiting for transfers between devices: 119 us -> 113 us
    ppermute x6, waiting for transfers between devices: 17.3 us -> 4.3 us  [hop(): y = lax.ppermute(x, 'sample', pairs)]
    ppermute x3, waiting for transfers between devices: 0.01 us -> 10.7 us  [outward(): return lax.ppermute(x, 'sample', [(1, 0), (2, 3)])]
  transfers between devices with their start and end apart: 44 -> 44, of which waited for: 25 -> 25; matrix products, arithmetic and copies ran while one was open for 4% -> 3% of each run, Pallas kernels for 21% -> 22%
where the time goes in v8:
time: 362 us; the launch traced here: 361 us
  Pallas kernels  129 us (36%)
  waiting for transfers between devices  113 us (31%)
  starting transfers between devices  82.3 us (23%)
  other arithmetic  18.1 us (5%)
  blocking collectives  9.94 us (3%)
  local copies, waits for them, and re-layouts  6.33 us (2%)
    ppermute x33, waiting for transfers between devices, swap(): return lax.ppermute(x, axis, [(i, i ^ bits) for i in range(n)])  87.9 us
    ppermute x33, starting transfers between devices, swap(): return lax.ppermute(x, axis, [(i, i ^ bits) for i in range(n)])  50.6 us
    pallas_call x4, Pallas kernels, backward(): pl.pallas_call(functools.partial(back_body, n, unit, t, base, cut), grid_...  49.9 us
    pallas_call x2, Pallas kernels, wide_forward(): pl.pallas_call(functools.partial(wide_body, n, begin, len(inner), acc is...  28.8 us
    pallas_call x1, Pallas kernels, first_forward(): pl.pallas_call(functools.partial(first_body, markers * columns), grid_spe...  24.5 us
    pallas_call x1, Pallas kernels, narrow_forward(): pl.pallas_call(functools.partial(narrow_body, n, unit, acc is not None),...  22.3 us
    ppermute x6, starting transfers between devices, hop(): y = lax.ppermute(x, 'sample', pairs)  20.4 us
    ppermute x3, waiting for transfers between devices, outward(): return lax.ppermute(x, 'sample', [(1, 0), (2, 3)])  10.7 us
  transfers between devices with their start and end apart: 44, of which 25 were waited for; matrix products, arithmetic and copies ran while one was open for 3% of the time, Pallas kernels for 22%

profile of v8, /device:TPU:0, one launch (start us, length us, event | category | flops | bytes accessed | tf_op | source)
XLA Modules:
  0.0 360.9 jit_solution(13997241984112743509)
XLA Ops:
  4.7 2.8 collective-permute-start.1
  9.1 3.5 convert_element_type.92.probes
  14.3 24.5 %first_forward.1 = (bf16[8,144,256]{2,1,0:T(8,128)(2,1)}, f32[16,16384]{1,0:T(8,128)S(1)}) custom-call(s32[1]{0:T(128)} %constant.7.clone.1.off, f32[16,16384]{1,0:T(8,128)S(1)} %copy-done, f32[16,3]{1,0:T(8,128)S(1)} %copy.31.cols, f32[16,1]{1,0:T(8,128)S(1)} %get-tuple-element.109.slopes, bf16[112,16384]{1,0:T(8,128)(2,1)S(1)} %convert_element_type.92.probes, ...), custom_call_target="tpu_custom_call" | custom-call | flops 8589934592 | bytes 67108864 | tf_op jit(solution)/shard_map/first_forward/pallas_call | solution.py:174
  39.7 3.5 all-to-all-start
  43.3 10.3 %all-to-all-done = bf16[8,144,256]{2,1,0:T(8,128)(2,1)S(1)} async-done(((bf16[8,144,256]{2,1,0:T(8,128)(2,1)}), bf16[8,144,256]{2,1,0:T(8,128)(2,1)S(1)}, u32[]{:S(2)}, u32[]{:S(2)}) %all-to-all-start) | async-done | bytes 589856 | tf_op jit(solution)/shard_map/all_to_all | solution.py:477
  54.5 9.9 %all_gather.3.rows = bf16[128,2048]{1,0:T(8,128)(2,1)S(1)} all-gather(bf16[128,256]{1,0:T(8,128)(2,1)S(1)} %pad_maximum_fusion.2), channel_id=1, replica_groups=mesh['sample'=4,'marker'=8] {'marker'}, dimensions={1}, use_global_device_ids=true | all-gather | bytes 589824 | tf_op jit(solution)/shard_map/all_gather | solution.py:482
  64.5 12.7 %first_back_0.1 = (f32[16,2048]{1,0:T(8,128)S(1)}, f32[16,2048]{1,0:T(8,128)S(1)}, f32[16,2048]{1,0:T(8,128)S(1)}, f32[16,2048]{1,0:T(8,128)S(1)}, bf16[112,6144...) custom-call(s32[4]{0:T(128)S(1)} %iota_xor_fusion.off, bf16[128,2048]{1,0:T(8,128)(2,1)S(1)} %all_gather.3.rows, ...), custom_call_target="tpu_custom_call" | custom-call | flops 4294967296 | bytes 33554432 | tf_op jit(solution)/shard_map/first_back_0/pallas_call | solution.py:386
  77.2 3.6 collective-permute-start.13
  80.9 3.0 collective-permute-start.5
  85.3 12.7 %first_back_1.1 = (f32[16,2048]{1,0:T(8,128)S(1)}, f32[16,2048]{1,0:T(8,128)S(1)}, f32[16,2048]{1,0:T(8,128)S(1)}, f32[16,2048]{1,0:T(8,128)S(1)}, bf16[112,4096...) custom-call(s32[4]{0:T(128)S(1)} %broadcast_add_fusion.off, bf16[128,2048]{1,0:T(8,128)(2,1)S(1)} %all_gather.3.rows, ...), custom_call_target="tpu_custom_call" | custom-call | flops 4294967296 | bytes 33554432 | tf_op jit(solution)/shard_map/first_back_1/pallas_call | solution.py:386
  98.2 15.8 %collective-permute-done.4 = f32[16,2048]{1,0:T(8,128)S(1)} collective-permute-done((f32[16,2048]{1,0:T(8,128)S(1)}, f32[16,2048]{1,0:T(8,128)S(1)}, u32[]{:S(2)}, u32[]{:S(2)}) %collective-permute-start.4) | collective-permute-done | bytes 131104 | tf_op jit(solution)/shard_map/ppermute | solution.py:26
  114.0 3.5 collective-permute-start.8
  117.5 1.8 collective-permute-start.9
  119.4 3.3 collective-permute-done.6
  122.7 2.8 collective-permute-done.8
  125.5 5.1 %collective-permute-done.9 = f32[16,2048]{1,0:T(8,128)S(1)} collective-permute-done((f32[16,2048]{1,0:T(8,128)S(1)}, f32[16,2048]{1,0:T(8,128)S(1)}, u32[]{:S(2)}, u32[]{:S(2)}) %collective-permute-start.9) | collective-permute-done | bytes 131104 | tf_op jit(solution)/shard_map/ppermute | solution.py:26
  131.4 3.2 collective-permute-start.10
  134.6 2.4 collective-permute-start.12
  139.3 7.9 %collective-permute-done.11.refs_2_ = bf16[16,4096]{1,0:T(8,128)(2,1)S(1)} collective-permute-done((bf16[16,4096]{1,0:T(8,128)(2,1)S(1)}, bf16[16,4096]{1,0:T(8,128)(2,1)S(1)}, u32[]{:S(2)}, u32[]{:S(2)}) %collective-permute-start.11) | collective-permute-done | bytes 131104 | tf_op jit(solution)/shard_map/ppermute | solution.py:26
  149.0 6.1 %collective-permute-start.14 = (bf16[112,6144]{1,0:T(8,128)(2,1)S(1)}, bf16[112,6144]{1,0:T(8,128)(2,1)}, u32[]{:S(2)}, u32[]{:S(2)}) collective-permute-start(bf16[112,6144]{1,0:T(8,128)(2,1)S(1)} %pad_maximum_fusion), channel_id=1, source_target_pairs={{0,8},{24,16},{1,9},{25,17},{2,10},{26,18},{3,11},{27,19},{4,12},{... | collective-permute-start | bytes 4128776 | tf_op jit(solution)/shard_map/ppermute | solution.py:501
  155.6 22.3 %second_forward.1 = f32[16,2048]{1,0:T(8,128)S(1)} custom-call(s32[8]{0:T(128)S(1)} %pad_add_fusion.2.off, bf16[16,4096]{1,0:T(8,128)(2,1)S(1)} %get-tuple-element.66.refs_0_, bf16[16,4096]{1,0:T(8,128)(2,1)S(1)} %collective-permute-done.10.refs_1_, bf16[16,4096]{1,0:T(8,128)(2,1)S(1)} %collective-permute-done.11.refs_2_, ...), custom_call_target="tpu_custom_call" | custom-call | flops 1073741824 | bytes 67108864 | tf_op jit(solution)/shard_map/second_forward/pallas_call | solution.py:222
  178.0 4.3 %collective-permute-done.14 = bf16[112,6144]{1,0:T(8,128)(2,1)} collective-permute-done((bf16[112,6144]{1,0:T(8,128)(2,1)S(1)}, bf16[112,6144]{1,0:T(8,128)(2,1)}, u32[]{:S(2)}, u32[]{:S(2)}) %collective-permute-start.14) | collective-permute-done | bytes 1376288 | tf_op jit(solution)/shard_map/ppermute | solution.py:501
  182.3 2.1 add_convert_fusion.1.refs_4_
  186.8 7.4 %collective-permute-start.21 = (bf16[112,4096]{1,0:T(8,128)(2,1)S(1)}, bf16[112,4096]{1,0:T(8,128)(2,1)S(1)}, u32[]{:S(2)}, u32[]{:S(2)}) collective-permute-start(bf16[112,4096]{1,0:T(8,128)(2,1)S(1)} %get-tuple-element.84), channel_id=1, source_target_pairs={{0,8},{24,16},{1,9},{25,17},{2,10},{26,18},{3,11},{27,19},{4,12},{... | collective-permute-start | bytes 2752520 | tf_op jit(solution)/shard_map/ppermute | solution.py:501
  199.2 2.4 collective-permute-done.17
  203.1 2.2 collective-permute-done.18
  206.0 12.2 %second_back_far.1 = (bf16[16,4096]{1,0:T(8,128)(2,1)S(1)}, bf16[16,4096]{1,0:T(8,128)(2,1)S(1)}) custom-call(s32[4]{0:T(128)S(1)} %reshape.28.off, bf16[16,2048]{1,0:T(8,128)(2,1)S(1)} %get-tuple-element.86.rows, bf16[2048,16384]{1,0:T(8,128)(2,1)} %refs_7_.1), custom_call_target="tpu_custom_call" | custom-call | flops 536870912 | bytes 33554432 | tf_op jit(solution)/shard_map/second_back_far/pallas_call | solution.py:386
  221.0 5.4 %collective-permute-start.24 = (bf16[16,4096]{1,0:T(8,128)(2,1)S(1)}, bf16[16,4096]{1,0:T(8,128)(2,1)S(1)}, u32[]{:S(2)}, u32[]{:S(2)}) collective-permute-start(bf16[16,4096]{1,0:T(8,128)(2,1)S(1)} %get-tuple-element.79), channel_id=1, source_target_pairs={{0,16},{8,24},{16,0},{24,8},{1,17},{9,25},{17,1},{25,9},{2,18},{10... | collective-permute-start | bytes 393224 | tf_op jit(solution)/shard_map/ppermute | solution.py:26
  226.4 2.3 collective-permute-start.25
  228.7 10.7 %collective-permute-done.22.refs_6_ = bf16[112,6144]{1,0:T(8,128)(2,1)S(1)} collective-permute-done((bf16[112,6144]{1,0:T(8,128)(2,1)S(1)}, bf16[112,6144]{1,0:T(8,128)(2,1)S(1)}, u32[]{:S(2)}, u32[]{:S(2)}) %collective-permute-start.22) | collective-permute-done | bytes 1376288 | tf_op jit(solution)/shard_map/ppermute | solution.py:511
  240.6 12.2 %second_back_near.1 = (f32[16,4096]{1,0:T(8,128)S(1)}, bf16[16,4096]{1,0:T(8,128)(2,1)S(1)}) custom-call(s32[4]{0:T(128)S(1)} %reshape.27.off, bf16[16,2048]{1,0:T(8,128)(2,1)S(1)} %get-tuple-element.86.rows, bf16[2048,16384]{1,0:T(8,128)(2,1)} %refs_7_.1), custom_call_target="tpu_custom_call" | custom-call | flops 536870912 | bytes 33554432 | tf_op jit(solution)/shard_map/second_back_near/pallas_call | solution.py:386
  252.9 2.1 collective-permute-done.24
  254.9 17.6 %collective-permute-done.23 = bf16[16,4096]{1,0:T(8,128)(2,1)S(1)} collective-permute-done((bf16[16,4096]{1,0:T(8,128)(2,1)S(1)}, bf16[16,4096]{1,0:T(8,128)(2,1)S(1)}, u32[]{:S(2)}, u32[]{:S(2)}) %collective-permute-start.23) | collective-permute-done | bytes 131104 | tf_op jit(solution)/shard_map/ppermute | solution.py:26
  275.2 2.6 collective-permute-start.29
  278.5 6.3 %collective-permute-done.28.refs_2_.refs_6_ = bf16[16,4096]{1,0:T(8,128)(2,1)S(1)} collective-permute-done((bf16[16,4096]{1,0:T(8,128)(2,1)S(1)}, bf16[16,4096]{1,0:T(8,128)(2,1)S(1)}, u32[]{:S(2)}, u32[]{:S(2)}) %collective-permute-start.28) | collective-permute-done | bytes 131104 | tf_op jit(solution)/shard_map/ppermute | solution.py:26
  287.3 2.3 multiply_reduce_fusion
  291.1 18.6 %third_forward_0.1.refs_6_ = f32[2048,128]{1,0:T(8,128)S(1)} custom-call(s32[5]{0:T(128)S(1)} %pad_add_fusion.3.off, bf16[16,4096]{1,0:T(8,128)(2,1)S(1)} %get-tuple-element.110.refs_0_.refs_4_, bf16[16,4096]{1,0:T(8,128)(2,1)S(1)} %collective-permute-done.27.refs_1_.refs_5_, bf16[16,4096]{1,0:T(8,128)(2,1)S(1)} %collective-permute-done.28.refs_2_.refs_6_, ...), custom_call_target="tpu_custom_call" | custom-call | flops 6442450944 | bytes 50331648 | tf_op jit(solution)/shard_map/third_forward_0/pallas_call | solution.py:297
  309.7 10.3 %third_forward_1.1 = bf16[8,128,256]{2,1,0:T(8,128)(2,1)} custom-call(s32[5]{0:T(128)S(1)} %pad_add_fusion.3.off, bf16[16,4096]{1,0:T(8,128)(2,1)S(1)} %get-tuple-element.110.refs_0_.refs_4_, bf16[16,4096]{1,0:T(8,128)(2,1)S(1)} %collective-permute-done.27.refs_1_.refs_5_, bf16[16,4096]{1,0:T(8,128)(2,1)S(1)} %collective-permute-done.28.refs_2_.refs_6_, ...), custom_call_target="tpu_custom_call" | custom-call | flops 2147483648 | bytes 16777216 | tf_op jit(solution)/shard_map/third_forward_1/pallas_call | solution.py:297
  320.1 3.6 %all-to-all-start.1 = ((bf16[8,128,256]{2,1,0:T(8,128)(2,1)}), bf16[8,128,256]{2,1,0:T(8,128)(2,1)S(1)}, u32[]{:S(2)}, u32[]{:S(2)}) async-start(bf16[8,128,256]{2,1,0:T(8,128)(2,1)} %third_forward_1.1), calls=%async_computation.1 | async-start | bytes 1048576 | tf_op jit(solution)/shard_map/all_to_all | solution.py:554
  323.8 3.6 %collective-permute-start.32 = (bf16[16,4096]{1,0:T(8,128)(2,1)S(1)}, bf16[16,4096]{1,0:T(8,128)(2,1)S(1)}, u32[]{:S(2)}, u32[]{:S(2)}) collective-permute-start(bf16[16,4096]{1,0:T(8,128)(2,1)S(1)} %copy-done.13), channel_id=1, source_target_pairs={{0,8},{8,0},{16,24},{24,16},{1,9},{9,1},{17,25},{25,17},{2,10},{10... | collective-permute-start | bytes 393224 | tf_op jit(solution)/shard_map/ppermute | solution.py:26
  327.5 2.4 collective-permute-start.34
  330.7 2.2 collective-permute-done.32.refs_9_
  332.8 7.5 %collective-permute-done.33.refs_10_ = bf16[16,4096]{1,0:T(8,128)(2,1)S(1)} collective-permute-done((bf16[16,4096]{1,0:T(8,128)(2,1)S(1)}, bf16[16,4096]{1,0:T(8,128)(2,1)S(1)}, u32[]{:S(2)}, u32[]{:S(2)}) %collective-permute-start.33) | collective-permute-done | bytes 131104 | tf_op jit(solution)/shard_map/ppermute | solution.py:26
  347.4 2.4 collective-permute-done.38
  349.8 2.4 collective-permute-start.39
  352.3 2.3 collective-permute-start.41
  354.8 1.9 collective-permute-done.40
  357.7 3.2 finish.1
  (166 shorter events, 46.0 us)
Async XLA Ops:
  3.4 1.3 collective-permute-start
  4.7 7.9 %collective-permute-start.1 = (f32[16,1]{1,0:T(8,128)S(1)}, f32[16,1]{1,0:T(8,128)S(1)}, u32[]{:S(2)}, u32[]{:S(2)}) collective-permute-start(f32[16,1]{1,0:T(8,128)S(1)} %add.129), channel_id=1, source_target_pairs={{0,2},{1,3},{2,0},{3,1},{4,6},{5,7},{6,4},{7,5},{8,10},{9,11},{10,... | collective-permute-start | bytes 200 | tf_op jit(solution)/shard_map/ppermute | solution.py:26
  7.5 5.0 %collective-permute-start.2 = (f32[16,1]{1,0:T(8,128)S(1)}, f32[16,1]{1,0:T(8,128)S(1)}, u32[]{:S(2)}, u32[]{:S(2)}) collective-permute-start(f32[16,1]{1,0:T(8,128)S(1)} %add.129), channel_id=1, source_target_pairs={{0,4},{1,5},{2,6},{3,7},{4,0},{5,1},{6,2},{7,3},{8,12},{9,13},{10,... | collective-permute-start | bytes 200 | tf_op jit(solution)/shard_map/ppermute | solution.py:26
  9.0 4.5 %collective-permute-start.3 = (f32[16,1]{1,0:T(8,128)S(1)}, f32[16,1]{1,0:T(8,128)S(1)}, u32[]{:S(2)}, u32[]{:S(2)}) collective-permute-start(f32[16,1]{1,0:T(8,128)S(1)} %add.129), channel_id=1, source_target_pairs={{0,6},{1,7},{2,4},{3,5},{4,2},{5,3},{6,0},{7,1},{8,14},{9,15},{10,... | collective-permute-start | bytes 200 | tf_op jit(solution)/shard_map/ppermute | solution.py:26
  39.7 13.9 %all-to-all-start = ((bf16[8,144,256]{2,1,0:T(8,128)(2,1)}), bf16[8,144,256]{2,1,0:T(8,128)(2,1)S(1)}, u32[]{:S(2)}, u32[]{:S(2)}) async-start(bf16[8,144,256]{2,1,0:T(8,128)(2,1)} %get-tuple-element.51), calls=%async_computation | async-start | bytes 1179648 | tf_op jit(solution)/shard_map/all_to_all | solution.py:477
  77.2 59.8 %collective-permute-start.13 = (bf16[112,6144]{1,0:T(8,128)(2,1)S(1)}, bf16[112,6144]{1,0:T(8,128)(2,1)S(1)}, u32[]{:S(2)}, u32[]{:S(2)}) collective-permute-start(bf16[112,6144]{1,0:T(8,128)(2,1)S(1)} %get-tuple-element.62), channel_id=1, source_target_pairs={{0,8},{24,16},{1,9},{25,17},{2,10},{26,18},{3,11},{27,19},{4,12},{... | collective-permute-start | bytes 4128776 | tf_op jit(solution)/shard_map/ppermute | solution.py:501
  80.8 33.2 %collective-permute-start.4 = (f32[16,2048]{1,0:T(8,128)S(1)}, f32[16,2048]{1,0:T(8,128)S(1)}, u32[]{:S(2)}, u32[]{:S(2)}) collective-permute-start(f32[16,2048]{1,0:T(8,128)S(1)} %get-tuple-element.53), channel_id=1, source_target_pairs={{0,8},{8,0},{16,24},{24,16},{1,9},{9,1},{17,25},{25,17},{2,10},{10... | collective-permute-start | bytes 393224 | tf_op jit(solution)/shard_map/ppermute | solution.py:26
  80.9 36.6 %collective-permute-start.5 = (f32[16,2048]{1,0:T(8,128)S(1)}, f32[16,2048]{1,0:T(8,128)S(1)}, u32[]{:S(2)}, u32[]{:S(2)}) collective-permute-start(f32[16,2048]{1,0:T(8,128)S(1)} %get-tuple-element.54), channel_id=1, source_target_pairs={{0,16},{8,24},{16,0},{24,8},{1,17},{9,25},{17,1},{25,9},{2,18},{10... | collective-permute-start | bytes 393224 | tf_op jit(solution)/shard_map/ppermute | solution.py:26
  83.9 38.7 %collective-permute-start.6 = (f32[16,2048]{1,0:T(8,128)S(1)}, f32[16,2048]{1,0:T(8,128)S(1)}, u32[]{:S(2)}, u32[]{:S(2)}) collective-permute-start(f32[16,2048]{1,0:T(8,128)S(1)} %get-tuple-element.55), channel_id=1, source_target_pairs={{0,24},{8,16},{16,8},{24,0},{1,25},{9,17},{17,9},{25,1},{2,26},{10... | collective-permute-start | bytes 393224 | tf_op jit(solution)/shard_map/ppermute | solution.py:26
  98.0 88.8 %copy-start.7 = (bf16[112,4096]{1,0:T(8,128)(2,1)}, bf16[112,4096]{1,0:T(8,128)(2,1)S(1)}, u32[]{:S(2)}) copy-start(bf16[112,4096]{1,0:T(8,128)(2,1)S(1)} %get-tuple-element.84) | copy-start | bytes 2752516
  98.0 24.6 %collective-permute-start.7 = (f32[16,2048]{1,0:T(8,128)S(1)}, f32[16,2048]{1,0:T(8,128)S(1)}, u32[]{:S(2)}, u32[]{:S(2)}) collective-permute-start(f32[16,2048]{1,0:T(8,128)S(1)} %get-tuple-element.59), channel_id=1, source_target_pairs={{0,8},{8,0},{16,24},{24,16},{1,9},{9,1},{17,25},{25,17},{2,10},{10... | collective-permute-start | bytes 393224 | tf_op jit(solution)/shard_map/ppermute | solution.py:26
  98.2 50.8 %copy-start.14 = (bf16[112,6144]{1,0:T(8,128)(2,1)}, bf16[112,6144]{1,0:T(8,128)(2,1)S(1)}, u32[]{:S(2)}) copy-start(bf16[112,6144]{1,0:T(8,128)(2,1)S(1)} %pad_maximum_fusion) | copy-start | bytes 4128772
  114.0 11.5 %collective-permute-start.8 = (f32[16,2048]{1,0:T(8,128)S(1)}, f32[16,2048]{1,0:T(8,128)S(1)}, u32[]{:S(2)}, u32[]{:S(2)}) collective-permute-start(f32[16,2048]{1,0:T(8,128)S(1)} %get-tuple-element.60), channel_id=1, source_target_pairs={{0,16},{8,24},{16,0},{24,8},{1,17},{9,25},{17,1},{25,9},{2,18},{10... | collective-permute-start | bytes 393224 | tf_op jit(solution)/shard_map/ppermute | solution.py:26
  117.5 13.1 %collective-permute-start.9 = (f32[16,2048]{1,0:T(8,128)S(1)}, f32[16,2048]{1,0:T(8,128)S(1)}, u32[]{:S(2)}, u32[]{:S(2)}) collective-permute-start(f32[16,2048]{1,0:T(8,128)S(1)} %get-tuple-element.61), channel_id=1, source_target_pairs={{0,24},{8,16},{16,8},{24,0},{1,25},{9,17},{17,9},{25,1},{2,26},{10... | collective-permute-start | bytes 393224 | tf_op jit(solution)/shard_map/ppermute | solution.py:26
  131.4 7.9 %collective-permute-start.10 = (bf16[16,4096]{1,0:T(8,128)(2,1)S(1)}, bf16[16,4096]{1,0:T(8,128)(2,1)S(1)}, u32[]{:S(2)}, u32[]{:S(2)}) collective-permute-start(bf16[16,4096]{1,0:T(8,128)(2,1)S(1)} %get-tuple-element.66.refs_0_), channel_id=1, source_target_pairs={{0,8},{8,0},{16,24},{24,16},{1,9},{9,1},{17,25},{25,17},{2,10},{10... | collective-permute-start | bytes 393224 | tf_op jit(solution)/shard_map/ppermute | solution.py:26
  134.6 12.6 %collective-permute-start.11 = (bf16[16,4096]{1,0:T(8,128)(2,1)S(1)}, bf16[16,4096]{1,0:T(8,128)(2,1)S(1)}, u32[]{:S(2)}, u32[]{:S(2)}) collective-permute-start(bf16[16,4096]{1,0:T(8,128)(2,1)S(1)} %get-tuple-element.66.refs_0_), channel_id=1, source_target_pairs={{0,16},{8,24},{16,0},{24,8},{1,17},{9,25},{17,1},{25,9},{2,18},{10... | collective-permute-start | bytes 393224 | tf_op jit(solution)/shard_map/ppermute | solution.py:26
  134.6 12.6 %collective-permute-start.12 = (bf16[16,4096]{1,0:T(8,128)(2,1)S(1)}, bf16[16,4096]{1,0:T(8,128)(2,1)S(1)}, u32[]{:S(2)}, u32[]{:S(2)}) collective-permute-start(bf16[16,4096]{1,0:T(8,128)(2,1)S(1)} %get-tuple-element.66.refs_0_), channel_id=1, source_target_pairs={{0,24},{8,16},{16,8},{24,0},{1,25},{9,17},{17,9},{25,1},{2,26},{10... | collective-permute-start | bytes 393224 | tf_op jit(solution)/shard_map/ppermute | solution.py:26
  147.2 30.7 %collective-permute-start.15 = (bf16[112,6144]{1,0:T(8,128)(2,1)}, bf16[112,6144]{1,0:T(8,128)(2,1)}, u32[]{:S(2)}, u32[]{:S(2)}) collective-permute-start(bf16[112,6144]{1,0:T(8,128)(2,1)} %add_convert_fusion.3), channel_id=1, source_target_pairs={{8,16},{16,8},{9,17},{17,9},{10,18},{18,10},{11,19},{19,11},{12,20... | collective-permute-start | bytes 4128776 | tf_op jit(solution)/shard_map/ppermute | solution.py:501
  149.0 33.3 %collective-permute-start.14 = (bf16[112,6144]{1,0:T(8,128)(2,1)S(1)}, bf16[112,6144]{1,0:T(8,128)(2,1)}, u32[]{:S(2)}, u32[]{:S(2)}) collective-permute-start(bf16[112,6144]{1,0:T(8,128)(2,1)S(1)} %pad_maximum_fusion), channel_id=1, source_target_pairs={{0,8},{24,16},{1,9},{25,17},{2,10},{26,18},{3,11},{27,19},{4,12},{... | collective-permute-start | bytes 4128776 | tf_op jit(solution)/shard_map/ppermute | solution.py:501
  186.0 32.2 %collective-permute-start.20 = (bf16[112,6144]{1,0:T(8,128)(2,1)S(1)}, bf16[112,6144]{1,0:T(8,128)(2,1)S(1)}, u32[]{:S(2)}, u32[]{:S(2)}) collective-permute-start(bf16[112,6144]{1,0:T(8,128)(2,1)S(1)} %add_convert_fusion.2), channel_id=1, source_target_pairs={{8,16},{16,8},{9,17},{17,9},{10,18},{18,10},{11,19},{19,11},{12,20... | collective-permute-start | bytes 4128776 | tf_op jit(solution)/shard_map/ppermute | solution.py:501
  186.8 31.4 %collective-permute-start.21 = (bf16[112,4096]{1,0:T(8,128)(2,1)S(1)}, bf16[112,4096]{1,0:T(8,128)(2,1)S(1)}, u32[]{:S(2)}, u32[]{:S(2)}) collective-permute-start(bf16[112,4096]{1,0:T(8,128)(2,1)S(1)} %get-tuple-element.84), channel_id=1, source_target_pairs={{0,8},{24,16},{1,9},{25,17},{2,10},{26,18},{3,11},{27,19},{4,12},{... | collective-permute-start | bytes 2752520 | tf_op jit(solution)/shard_map/ppermute | solution.py:501
  194.2 1.4 collective-permute-start.16
  195.7 6.0 %collective-permute-start.17 = (f32[16,2048]{1,0:T(8,128)S(1)}, f32[16,2048]{1,0:T(8,128)S(1)}, u32[]{:S(2)}, u32[]{:S(2)}) collective-permute-start(f32[16,2048]{1,0:T(8,128)S(1)} %add.146), channel_id=1, source_target_pairs={{0,2},{1,3},{2,0},{3,1},{4,6},{5,7},{6,4},{7,5},{8,10},{9,11},{10,... | collective-permute-start | bytes 393224 | tf_op jit(solution)/shard_map/ppermute | solution.py:26
  197.2 8.1 %collective-permute-start.18 = (f32[16,2048]{1,0:T(8,128)S(1)}, f32[16,2048]{1,0:T(8,128)S(1)}, u32[]{:S(2)}, u32[]{:S(2)}) collective-permute-start(f32[16,2048]{1,0:T(8,128)S(1)} %add.146), channel_id=1, source_target_pairs={{0,4},{1,5},{2,6},{3,7},{4,0},{5,1},{6,2},{7,3},{8,12},{9,13},{10,... | collective-permute-start | bytes 393224 | tf_op jit(solution)/shard_map/ppermute | solution.py:26
  197.8 7.5 %collective-permute-start.19 = (f32[16,2048]{1,0:T(8,128)S(1)}, f32[16,2048]{1,0:T(8,128)S(1)}, u32[]{:S(2)}, u32[]{:S(2)}) collective-permute-start(f32[16,2048]{1,0:T(8,128)S(1)} %add.146), channel_id=1, source_target_pairs={{0,6},{1,7},{2,4},{3,5},{4,2},{5,3},{6,0},{7,1},{8,14},{9,15},{10,... | collective-permute-start | bytes 393224 | tf_op jit(solution)/shard_map/ppermute | solution.py:26
  201.7 37.8 %collective-permute-start.22 = (bf16[112,6144]{1,0:T(8,128)(2,1)S(1)}, bf16[112,6144]{1,0:T(8,128)(2,1)S(1)}, u32[]{:S(2)}, u32[]{:S(2)}) collective-permute-start(bf16[112,6144]{1,0:T(8,128)(2,1)S(1)} %add_convert_fusion.1.refs_4_), channel_id=1, source_target_pairs={{8,0},{16,24},{9,1},{17,25},{10,2},{18,26},{11,3},{19,27},{12,4},{... | collective-permute-start | bytes 4128776 | tf_op jit(solution)/shard_map/ppermute | solution.py:511
  218.6 53.9 %collective-permute-start.26 = (bf16[112,6144]{1,0:T(8,128)(2,1)S(1)}, bf16[112,6144]{1,0:T(8,128)(2,1)S(1)}, u32[]{:S(2)}, u32[]{:S(2)}) collective-permute-start(bf16[112,6144]{1,0:T(8,128)(2,1)S(1)} %add_convert_fusion.refs_5_), channel_id=1, source_target_pairs={{8,0},{16,24},{9,1},{17,25},{10,2},{18,26},{11,3},{19,27},{12,4},{... | collective-permute-start | bytes 4128776 | tf_op jit(solution)/shard_map/ppermute | solution.py:511
  220.1 52.4 %copy-start.17 = (f32[16,2048]{1,0:T(8,128)S(1)}, f32[16,2048]{1,0:T(8,128)}, u32[]{:S(2)}) copy-start(f32[16,2048]{1,0:T(8,128)} %copy-done.16) | copy-start | bytes 393220
  220.1 52.4 %copy-start.19 = (f32[16,2048]{1,0:T(8,128)S(1)}, f32[16,2048]{1,0:T(8,128)}, u32[]{:S(2)}) copy-start(f32[16,2048]{1,0:T(8,128)} %copy-done.18) | copy-start | bytes 393220
  220.1 57.7 %collective-permute-start.30 = (bf16[112,4096]{1,0:T(8,128)(2,1)S(1)}, bf16[112,4096]{1,0:T(8,128)(2,1)S(1)}, u32[]{:S(2)}, u32[]{:S(2)}) collective-permute-start(bf16[112,4096]{1,0:T(8,128)(2,1)S(1)} %add_convert_fusion.5), channel_id=1, source_target_pairs={{8,16},{16,8},{9,17},{17,9},{10,18},{18,10},{11,19},{19,11},{12,20... | collective-permute-start | bytes 2752520 | tf_op jit(solution)/shard_map/ppermute | solution.py:501
  221.0 34.0 %collective-permute-start.24 = (bf16[16,4096]{1,0:T(8,128)(2,1)S(1)}, bf16[16,4096]{1,0:T(8,128)(2,1)S(1)}, u32[]{:S(2)}, u32[]{:S(2)}) collective-permute-start(bf16[16,4096]{1,0:T(8,128)(2,1)S(1)} %get-tuple-element.79), channel_id=1, source_target_pairs={{0,16},{8,24},{16,0},{24,8},{1,17},{9,25},{17,1},{25,9},{2,18},{10... | collective-permute-start | bytes 393224 | tf_op jit(solution)/shard_map/ppermute | solution.py:26
  226.4 28.5 %collective-permute-start.25 = (bf16[16,4096]{1,0:T(8,128)(2,1)S(1)}, bf16[16,4096]{1,0:T(8,128)(2,1)S(1)}, u32[]{:S(2)}, u32[]{:S(2)}) collective-permute-start(bf16[16,4096]{1,0:T(8,128)(2,1)S(1)} %get-tuple-element.80), channel_id=1, source_target_pairs={{0,24},{8,16},{16,8},{24,0},{1,25},{9,17},{17,9},{25,1},{2,26},{10... | collective-permute-start | bytes 393224 | tf_op jit(solution)/shard_map/ppermute | solution.py:26
  252.8 19.7 %collective-permute-start.23 = (bf16[16,4096]{1,0:T(8,128)(2,1)S(1)}, bf16[16,4096]{1,0:T(8,128)(2,1)S(1)}, u32[]{:S(2)}, u32[]{:S(2)}) collective-permute-start(bf16[16,4096]{1,0:T(8,128)(2,1)S(1)} %get-tuple-element.88), channel_id=1, source_target_pairs={{0,8},{8,0},{16,24},{24,16},{1,9},{9,1},{17,25},{25,17},{2,10},{10... | collective-permute-start | bytes 393224 | tf_op jit(solution)/shard_map/ppermute | solution.py:26
  273.5 5.1 %collective-permute-start.27 = (bf16[16,4096]{1,0:T(8,128)(2,1)S(1)}, bf16[16,4096]{1,0:T(8,128)(2,1)S(1)}, u32[]{:S(2)}, u32[]{:S(2)}) collective-permute-start(bf16[16,4096]{1,0:T(8,128)(2,1)S(1)} %get-tuple-element.110.refs_0_.refs_4_), channel_id=1, source_target_pairs={{0,8},{8,0},{16,24},{24,16},{1,9},{9,1},{17,25},{25,17},{2,10},{10... | collective-permute-start | bytes 393224 | tf_op jit(solution)/shard_map/ppermute | solution.py:26
  273.5 11.4 %collective-permute-start.28 = (bf16[16,4096]{1,0:T(8,128)(2,1)S(1)}, bf16[16,4096]{1,0:T(8,128)(2,1)S(1)}, u32[]{:S(2)}, u32[]{:S(2)}) collective-permute-start(bf16[16,4096]{1,0:T(8,128)(2,1)S(1)} %get-tuple-element.110.refs_0_.refs_4_), channel_id=1, source_target_pairs={{0,16},{8,24},{16,0},{24,8},{1,17},{9,25},{17,1},{25,9},{2,18},{10... | collective-permute-start | bytes 393224 | tf_op jit(solution)/shard_map/ppermute | solution.py:26
  275.2 9.7 %collective-permute-start.29 = (bf16[16,4096]{1,0:T(8,128)(2,1)S(1)}, bf16[16,4096]{1,0:T(8,128)(2,1)S(1)}, u32[]{:S(2)}, u32[]{:S(2)}) collective-permute-start(bf16[16,4096]{1,0:T(8,128)(2,1)S(1)} %get-tuple-element.110.refs_0_.refs_4_), channel_id=1, source_target_pairs={{0,24},{8,16},{16,8},{24,0},{1,25},{9,17},{17,9},{25,1},{2,26},{10... | collective-permute-start | bytes 393224 | tf_op jit(solution)/shard_map/ppermute | solution.py:26
  286.0 23.7 %collective-permute-start.31 = (bf16[112,4096]{1,0:T(8,128)(2,1)}, bf16[112,4096]{1,0:T(8,128)(2,1)}, u32[]{:S(2)}, u32[]{:S(2)}) collective-permute-start(bf16[112,4096]{1,0:T(8,128)(2,1)} %add_convert_fusion.4.refs_4_), channel_id=1, source_target_pairs={{8,0},{16,24},{9,1},{17,25},{10,2},{18,26},{11,3},{19,27},{12,4},{... | collective-permute-start | bytes 2752520 | tf_op jit(solution)/shard_map/ppermute | solution.py:511
  320.1 20.3 %all-to-all-start.1 = ((bf16[8,128,256]{2,1,0:T(8,128)(2,1)}), bf16[8,128,256]{2,1,0:T(8,128)(2,1)S(1)}, u32[]{:S(2)}, u32[]{:S(2)}) async-start(bf16[8,128,256]{2,1,0:T(8,128)(2,1)} %third_forward_1.1), calls=%async_computation.1 | async-start | bytes 1048576 | tf_op jit(solution)/shard_map/all_to_all | solution.py:554
  323.8 9.1 %collective-permute-start.32 = (bf16[16,4096]{1,0:T(8,128)(2,1)S(1)}, bf16[16,4096]{1,0:T(8,128)(2,1)S(1)}, u32[]{:S(2)}, u32[]{:S(2)}) collective-permute-start(bf16[16,4096]{1,0:T(8,128)(2,1)S(1)} %copy-done.13), channel_id=1, source_target_pairs={{0,8},{8,0},{16,24},{24,16},{1,9},{9,1},{17,25},{25,17},{2,10},{10... | collective-permute-start | bytes 393224 | tf_op jit(solution)/shard_map/ppermute | solution.py:26
  327.4 12.9 %collective-permute-start.33 = (bf16[16,4096]{1,0:T(8,128)(2,1)S(1)}, bf16[16,4096]{1,0:T(8,128)(2,1)S(1)}, u32[]{:S(2)}, u32[]{:S(2)}) collective-permute-start(bf16[16,4096]{1,0:T(8,128)(2,1)S(1)} %copy-done.13), channel_id=1, source_target_pairs={{0,16},{8,24},{16,0},{24,8},{1,17},{9,25},{17,1},{25,9},{2,18},{10... | collective-permute-start | bytes 393224 | tf_op jit(solution)/shard_map/ppermute | solution.py:26
  327.5 12.8 %collective-permute-start.34 = (bf16[16,4096]{1,0:T(8,128)(2,1)S(1)}, bf16[16,4096]{1,0:T(8,128)(2,1)S(1)}, u32[]{:S(2)}, u32[]{:S(2)}) collective-permute-start(bf16[16,4096]{1,0:T(8,128)(2,1)S(1)} %copy-done.13), channel_id=1, source_target_pairs={{0,24},{8,16},{16,8},{24,0},{1,25},{9,17},{17,9},{25,1},{2,26},{10... | collective-permute-start | bytes 393224 | tf_op jit(solution)/shard_map/ppermute | solution.py:26
  340.8 1.2 collective-permute-start.35
  342.0 3.6 collective-permute-start.36
  343.7 3.6 collective-permute-start.37
  345.2 4.5 %collective-permute-start.38 = (f32[8,128]{1,0:T(8,128)S(1)}, f32[8,128]{1,0:T(8,128)S(1)}, u32[]{:S(2)}, u32[]{:S(2)}) collective-permute-start(f32[8,128]{1,0:T(8,128)S(1)} %add.161), channel_id=1, source_target_pairs={{0,6},{1,7},{2,4},{3,5},{4,2},{5,3},{6,0},{7,1},{8,14},{9,15},{10,... | collective-permute-start | bytes 12296 | tf_op jit(solution)/shard_map/ppermute | solution.py:26
  349.8 5.0 %collective-permute-start.39 = (f32[8,128]{1,0:T(8,128)S(1)}, f32[8,128]{1,0:T(8,128)S(1)}, u32[]{:S(2)}, u32[]{:S(2)}) collective-permute-start(f32[8,128]{1,0:T(8,128)S(1)} %add_add_fusion.5), channel_id=1, source_target_pairs={{0,8},{8,0},{16,24},{24,16},{1,9},{9,1},{17,25},{25,17},{2,10},{10... | collective-permute-start | bytes 12296 | tf_op jit(solution)/shard_map/ppermute | solution.py:26
  352.1 4.5 %collective-permute-start.40 = (f32[8,128]{1,0:T(8,128)S(1)}, f32[8,128]{1,0:T(8,128)S(1)}, u32[]{:S(2)}, u32[]{:S(2)}) collective-permute-start(f32[8,128]{1,0:T(8,128)S(1)} %add_add_fusion.5), channel_id=1, source_target_pairs={{0,16},{8,24},{16,0},{24,8},{1,17},{9,25},{17,1},{25,9},{2,18},{10... | collective-permute-start | bytes 12296 | tf_op jit(solution)/shard_map/ppermute | solution.py:26
  352.3 5.4 %collective-permute-start.41 = (f32[8,128]{1,0:T(8,128)S(1)}, f32[8,128]{1,0:T(8,128)S(1)}, u32[]{:S(2)}, u32[]{:S(2)}) collective-permute-start(f32[8,128]{1,0:T(8,128)S(1)} %add_add_fusion.5), channel_id=1, source_target_pairs={{0,24},{8,16},{16,8},{24,0},{1,25},{9,17},{17,9},{25,1},{2,26},{10... | collective-permute-start | bytes 12296 | tf_op jit(solution)/shard_map/ppermute | solution.py:26
  (26 other events, 431.1 us)

commit v9 on v8

--- a/solution.py
+++ b/solution.py
@@ -253,7 +253,7 @@
 
     def prepare():
         for j, half in [(j, half) for j in range(n) for half in range(2)]:
-            place = half * n + off[j] - begin
+            place = 2 * off[j] + half - begin
 
             @pl.when((place >= 0) & (place < count))
             def _():
@@ -310,14 +310,14 @@
     )(places, *operands)
 
 
-def backward_loop(g, rows, total, held, sems, off, span, pieces):
+def backward_loop(g, rows, total, held, sems, unit_at, span, pieces):
     people = g.shape[0]
     slots, pk, mb = held.shape
     steps, blocks = span // mb, people // pk
 
     def place(c):
         k, i = c // blocks, lax.rem(c, blocks)
-        col = off[k // steps] * span + lax.rem(k, steps) * mb
+        col = unit_at(k // steps) * span + lax.rem(k, steps) * mb
         return g.at[pl.ds(pl.multiple_of(i * pk, pk), pk), pl.ds(pl.multiple_of(col, mb), mb)]
 
     def use(c, slot):
@@ -337,65 +337,86 @@
     stream(place, held, sems, pieces * steps * blocks, lambda: None, use)
 
 
-def back_body(n, unit, t, base, cut, off, rows, g, *refs):
+def first_back_body(unit, begin, t, arrays, off, rows, g, *refs):
     refs = list(refs)
-    held, sems = refs[-2:]
-    if t == rows.shape[0]:
-        outs, total = refs[:-3], refs[-3]
+    before = refs.pop(0) if begin else None
+    total, held, sems = refs[-3:]
+    count = total.shape[1] // unit
+    backward_loop(g, rows, total, held, sems, lambda j: begin + j, unit, count)
+    if not begin:
+        refs[0][...] = total[:t, :]
+        chunks = refs[1:-3]
     else:
-        outs, (lower, upper, total, made, sent) = refs[:-7], refs[-7:-2]
-    backward_loop(g, rows, total, held, sems, off, unit, n)
-    copies = []
-    if t != rows.shape[0]:
-        made[...] = total[t:, :].astype(BF16)
-        for j in range(n):
-            place = off[j] - base
-            part = made.at[:, pl.ds(j * unit, unit)]
-
-            def copy(whole, first):
-                cols = pl.ds(pl.multiple_of((place - first) * unit, unit), unit)
-                return pltpu.make_async_copy(part, whole.at[:, cols], sent.at[j])
-
-            @pl.when(place < cut)
-            def _():
-                copy(lower, 0).start()
-
-            @pl.when(place >= cut)
-            def _():
-                copy(upper, cut).start()
-
-            copies.append(pltpu.make_async_copy(part, lower.at[:, pl.ds(0, unit)], sent.at[j]))
-    span = outs[0].shape[1]
-    for j, out in enumerate(outs):
-        out[...] = total[:t, j * span : (j + 1) * span].astype(out.dtype)
-    for copy in copies:
-        copy.wait()
-
-
-def backward(rows, places, genotypes, unit, t, base, cut, types, name):
-    people = genotypes.shape[0]
-    r, n = rows.shape[0], places.shape[0]
+        whole = refs[-4]
+        first = begin * unit
+        whole[:, :first] = before[...]
+        whole[:, first:] = total[:t, :]
+        for k in range(arrays):
+            out = refs[k]
+            span = out.shape[1]
+            out[...] = whole[:, pl.ds(pl.multiple_of(off[k] * span, span), span)]
+        chunks = refs[arrays:-4]
+    at = 0
+    for chunk in chunks:
+        chunk[...] = total[t:, at : at + chunk.shape[1]].astype(BF16)
+        at += chunk.shape[1]
+
+
+def first_back(rows, order, genotypes, unit, t, begin, before, sizes, name):
+    people, markers = genotypes.shape
+    r, n = rows.shape[0], sum(sizes)
     pk, mb = block_of(people, 1024), block_of(unit, 2048)
-    out_specs = [VMEM] * len(types)
-    out_shape = [jax.ShapeDtypeStruct((t, n * unit // len(types)), kind) for kind in types]
+    arrays = order.shape[0]
+    operands = [rows, genotypes]
     scratch = [pltpu.VMEM((r, n * unit), F32)]
-    if t != r:
-        out_specs += [ANY] * 2
-        out_shape += [jax.ShapeDtypeStruct((r - t, c * unit), BF16) for c in (cut, n - cut)]
-        scratch += [pltpu.VMEM((r - t, n * unit), BF16), pltpu.SemaphoreType.DMA((n,))]
+    if begin:
+        operands.append(before)
+        out_shape = [jax.ShapeDtypeStruct((t, markers // arrays), F32)] * arrays
+        scratch.insert(0, pltpu.VMEM((t, markers), F32))
+    else:
+        out_shape = [jax.ShapeDtypeStruct((t, n * unit), F32)]
+    out_shape += [jax.ShapeDtypeStruct((r - t, c * unit), BF16) for c in sizes]
     return pl.pallas_call(
-        functools.partial(back_body, n, unit, t, base, cut),
+        functools.partial(first_back_body, unit, begin, t, arrays),
         grid_spec=pltpu.PrefetchScalarGridSpec(
             num_scalar_prefetch=1,
             grid=(),
-            in_specs=[VMEM, ANY],
-            out_specs=out_specs,
+            in_specs=[VMEM, ANY] + [VMEM] * (len(operands) - 2),
+            out_specs=[VMEM] * len(out_shape),
             scratch_shapes=[*scratch, *ring(pk, mb)],
         ),
         out_shape=out_shape,
         compiler_params=pltpu.CompilerParams(vmem_limit_bytes=LIMIT),
         cost_estimate=cost(r, people, n * unit),
         name=name,
+    )(order, *operands)
+
+
+def second_back_body(n, unit, off, rows, g, *refs):
+    outs, (total, held, sems) = refs[:-3], refs[-3:]
+    backward_loop(g, rows, total, held, sems, lambda j: off[j], unit, n)
+    span = outs[0].shape[1]
+    for j, out in enumerate(outs):
+        out[...] = total[:, j * span : (j + 1) * span].astype(out.dtype)
+
+
+def second_back(rows, places, genotypes, unit, types):
+    people = genotypes.shape[0]
+    r, n = rows.shape[0], places.shape[0]
+    pk, mb = block_of(people, 1024), block_of(unit, 2048)
+    return pl.pallas_call(
+        functools.partial(second_back_body, n, unit),
+        grid_spec=pltpu.PrefetchScalarGridSpec(
+            num_scalar_prefetch=1,
+            grid=(),
+            in_specs=[VMEM, ANY],
+            out_specs=[VMEM] * len(types),
+            scratch_shapes=[pltpu.VMEM((r, n * unit), F32), *ring(pk, mb)],
+        ),
+        out_shape=[jax.ShapeDtypeStruct((r, n * unit // len(types)), kind) for kind in types],
+        compiler_params=pltpu.CompilerParams(vmem_limit_bytes=LIMIT),
+        cost_estimate=cost(r, people, n * unit),
+        name="second_back",
     )(places, rows, genotypes)
 
 
@@ -426,7 +447,7 @@
     next_shrink = slab_var * next_precision / (1.0 + slab_var * next_precision)
     next_base = odds + 0.5 * jnp.log(1.0 - next_shrink)
     for j, half in [(j, half) for j in range(n) for half in range(2)]:
-        here = pl.ds(pl.multiple_of((half * n + off[j]) * unit, unit), unit)
+        here = pl.ds(pl.multiple_of((2 * off[j] + half) * unit, unit), unit)
         part = slice(half * unit, (half + 1) * unit)
         start = start_hi[j][:, part].astype(F32) + low[j][:, part].astype(F32)
         back = back_hi[j][:, part].astype(F32)
@@ -466,7 +487,7 @@
     unit, share = markers_here // (2 * samples), people_here // columns
     order = jnp.arange(samples, dtype=jnp.int32) ^ me
     some = samples // 2
-    near, far = [jnp.stack([o, o + samples], axis=1).reshape(-1) for o in (order[:some], order[some:])]
+    owned = jnp.stack([2 * order, 2 * order + 1], axis=1).reshape(-1)
 
     cols = jnp.stack([inclusion, slab_ratio, input_precision], axis=1)
     slopes = slope_sum(message, cols)
@@ -480,16 +501,15 @@
     rows = jnp.concatenate([own, kept_x[traits:]], axis=0).astype(BF16)
     pred_x = rows[traits:].astype(F32)
     rows = lax.all_gather(rows, "marker", axis=1, tiled=True)
-    starts, chunks = [], []
-    for half, cut in enumerate((samples - 1, some)):
-        base = half * samples
-        *parts, lower, upper = backward(
-            rows, order + base, genotypes, unit, traits, base, cut, [F32] * samples, f"first_back_{half}"
-        )
-        starts.append([swap(part, "sample", k) if k else part for k, part in enumerate(parts)])
-        chunks += [lower, upper]
-        rows, *_ = lax.optimization_barrier((rows, lower))
-    chunks = [chunks[0], jnp.concatenate(chunks[1:3], axis=1), chunks[3]]
+    sizes = (some, samples - 1, samples - 1)
+    before, *chunks = first_back(
+        rows, order, genotypes, unit, traits, 0, None, sizes[:1], "first_back_0"
+    )
+    rows, before, chunks[0] = lax.optimization_barrier((rows, before, chunks[0]))
+    outs = first_back(
+        rows, order, genotypes, unit, traits, sizes[0], before, sizes[1:], "first_back_1"
+    )
+    chunks += outs[samples:]
 
     def add(x, y):
         return (x.astype(F32) + y.astype(F32)).astype(BF16)
@@ -497,48 +517,45 @@
     def tie(values, *others):
         return lax.optimization_barrier((tuple(values), others))[0]
 
-    def hop(x, pairs, *others):
-        y = lax.ppermute(x, "sample", pairs)
-        return add(*tie((x, y), *others))
-
-    def inward(c, *others):
-        return hop(chunks[c], [(0, 1), (3, 2)], *others)
-
-    def across(x, *others):
-        return hop(x, [(1, 2), (2, 1)], *others)
+    def inward(c):
+        return lax.ppermute(chunks[c], "sample", [(0, 1), (3, 2)])
+
+    def across(x):
+        return lax.ppermute(x, "sample", [(1, 2), (2, 1)])
 
     def outward(x):
         return lax.ppermute(x, "sample", [(1, 0), (2, 3)])
 
     pair, full, ends = [None] * 3, [None] * 3, [None] * 3
-    pair[0] = inward(0)
+    *parts, pair[0] = tie((*outs[:samples], inward(0)))
+    sent = [swap(part, "sample", k) if k else part for k, part in enumerate(parts)]
+    pair[0] = add(chunks[0], pair[0])
     scale = (noise_precision / people)[:, None]
-    start = scale * jnp.concatenate([tree(parts) for parts in starts], axis=1)
+    start = scale * tree(sent)
     start_high = lax.reduce_precision(start, 8, 7)
     start_low = (start - start_high).astype(BF16)
     start_high = start_high.astype(BF16)
 
     start_pieces = [swap(start_high, "sample", k) if k else start_high for k in range(samples)]
     *start_pieces, pair[0], chunks[1] = tie((*start_pieces, pair[0], chunks[1]))
-    both = jnp.concatenate([near, far])
-    value = narrow_forward(start_pieces, both, None, genotypes, "second_forward")
-    full[0], pair[1] = across(pair[0], value), inward(1, value)
-    value, pair[1], chunks[2] = tie((value, pair[1], chunks[2]), full[0])
-    ends[0] = outward(full[0])
+    full[0], pair[1] = across(pair[0]), inward(1)
+    value = narrow_forward(start_pieces, owned, None, genotypes, "second_forward")
+    value, full[0], pair[1] = tie((value, full[0], pair[1]))
     value = sum_marker(value)
     kept_s = lax.dynamic_slice_in_dim(value, column * share, share, 1)
-    rows = value.astype(BF16)
-    parts = backward(rows, far, genotypes, unit, traits, 0, 0, [BF16] * some, "second_back_far")
-    sent = [swap(part, "sample", k + some) for k, part in enumerate(parts)]
-    full[1], pair[2] = across(pair[1], *parts), inward(2, *parts)
-    (rows,) = tie((rows,), full[1], pair[2], ends[0], *parts)
+    full[0], pair[1] = tie((add(pair[0], full[0]), add(chunks[1], pair[1])))
+    rows, full[0], pair[1], chunks[2] = tie((value.astype(BF16), full[0], pair[1], chunks[2]))
+    ends[0], full[1], pair[2] = outward(full[0]), across(pair[1]), inward(2)
+    parts = second_back(rows, owned, genotypes, unit, [F32] + [BF16] * (samples - 1))
+    *parts, ends[0] = tie((*parts, ends[0]))
+    sent = [swap(part, "sample", k) if k else part for k, part in enumerate(parts)]
+    full[1], pair[2] = tie((full[1], pair[2]), *parts)
+    full[1], pair[2] = add(pair[1], full[1]), add(chunks[2], pair[2])
     ends[1] = outward(full[1])
-    parts = backward(rows, near, genotypes, unit, traits, 0, 0, [F32] + [BF16] * (some - 1), "second_back_near")
-    sent = [swap(part, "sample", k) if k else part for k, part in enumerate(parts)] + sent
-    back_high = tree([part.astype(F32) for part in tie(sent, ends[1])]).astype(BF16)
+    back_high = tree([part.astype(F32) for part in sent]).astype(BF16)
     back = back_high.astype(F32)
     back_pieces = [swap(back_high, "sample", k) if k else back_high for k in range(samples)]
-    full[2] = across(pair[2], *back_pieces)
+    full[2] = add(*tie((pair[2], across(pair[2])), *back_pieces))
     ends[2] = outward(full[2])
 
     inner = ((me == 1) | (me == 2)).astype(jnp.int32)
@@ -549,7 +566,7 @@
     (start_low,) = tie((start_low,), total)
     low_pieces = [swap(start_low, "sample", k) if k else start_low for k in range(samples)]
     value = wide_forward(
-        back_pieces, full[2:], ends[2:], places, 3 * some, total, genotypes, columns, "third_forward_1"
+        back_pieces, full[2:], ends[2:], places, sum(sizes[:2]), total, genotypes, columns, "third_forward_1"
     )
     (last,) = tie((lax.all_to_all(value, "marker", 0, 0),), *low_pieces)
     last = jnp.sum(last.astype(F32), axis=0)
@@ -558,14 +575,12 @@
     def dot(x, y):
         return jnp.sum(x * y, axis=1)
 
-    probes_here = [
-        lax.dynamic_slice_in_dim(probes, (half * samples + me) * unit, unit, 1) for half in range(2)
-    ]
+    probes_here = lax.dynamic_slice_in_dim(probes, 2 * me * unit, 2 * unit, 1)
     kept_p, last_p = kept_x[traits:], last[traits:]
     norms = jnp.concatenate(
         [
             jnp.stack([dot(start, start), dot(start, back), dot(back, back)]),
-            jnp.stack([sum(dot(p, p) for p in probes_here), dot(kept_p, pred_x), dot(last_p, pred_x)]),
+            jnp.stack([dot(probes_here, probes_here), dot(kept_p, pred_x), dot(last_p, pred_x)]),
         ],
         axis=1,
     )

time: 362 us -> 351 us (0.970)
  starting transfers between devices: 82.3 us -> 68.1 us
  waiting for transfers between devices: 113 us -> 121 us
    ppermute x3, waiting for transfers between devices: 10.7 us -> 38.3 us  [outward(): return lax.ppermute(x, 'sample', [(1, 0), (2, 3)])]
    ppermute x33 -> x30, waiting for transfers between devices: 87.9 us -> 65.8 us  [swap(): return lax.ppermute(x, axis, [(i, i ^ bits) for i in range(n)])]
    ppermute x33 -> x30, starting transfers between devices: 50.6 us -> 42.4 us  [swap(): return lax.ppermute(x, axis, [(i, i ^ bits) for i in range(n)])]
    ppermute x6, starting transfers between devices: 20.4 us -> 14 us  [the longest x3 10.9 us: inward(): return lax.ppermute(chunks[c], 'sample', [(0, 1), (3, 2)])]
    pallas_call x4 -> x3, Pallas kernels: 49.9 us -> 46.8 us  [the longest x2 25 us: first_back(): pl.pallas_call(functools.partial(first_back_body, unit, begin, t, arrays)...]
  transfers between devices with their start and end apart: 44 -> 41, of which waited for: 25 -> 25; matrix products, arithmetic and copies ran while one was open for 3% -> 4% of each run, Pallas kernels for 22% -> 23%
where the time goes in v9:
time: 351 us; the launch traced here: 350 us
  Pallas kernels  128 us (36%)
  waiting for transfers between devices  121 us (34%)
  starting transfers between devices  68.1 us (19%)
  other arithmetic  16.4 us (5%)
  blocking collectives  9.96 us (3%)
  local copies, waits for them, and re-layouts  5.91 us (2%)
    ppermute x30, waiting for transfers between devices, swap(): return lax.ppermute(x, axis, [(i, i ^ bits) for i in range(n)])  65.8 us
    ppermute x30, starting transfers between devices, swap(): return lax.ppermute(x, axis, [(i, i ^ bits) for i in range(n)])  42.4 us
    ppermute x3, waiting for transfers between devices, outward(): return lax.ppermute(x, 'sample', [(1, 0), (2, 3)])  38.3 us
    pallas_call x2, Pallas kernels, wide_forward(): pl.pallas_call(functools.partial(wide_body, n, begin, len(inner), acc is...  30 us
    pallas_call x2, Pallas kernels, first_back(): pl.pallas_call(functools.partial(first_back_body, unit, begin, t, arrays)...  25 us
    pallas_call x1, Pallas kernels, first_forward(): pl.pallas_call(functools.partial(first_body, markers * columns), grid_spe...  24.5 us
    pallas_call x1, Pallas kernels, narrow_forward(): pl.pallas_call(functools.partial(narrow_body, n, unit, acc is not None),...  22.3 us
    pallas_call x1, Pallas kernels, second_back(): pl.pallas_call(functools.partial(second_back_body, n, unit), grid_spec=pl...  21.8 us
  transfers between devices with their start and end apart: 41, of which 25 were waited for; matrix products, arithmetic and copies ran while one was open for 4% of the time, Pallas kernels for 23%

profile of v9, /device:TPU:0, one launch (start us, length us, event | category | flops | bytes accessed | tf_op | source)
XLA Modules:
  0.0 349.9 jit_solution(162238260582828955)
XLA Ops:
  4.7 3.8 %collective-permute-start.3 = (f32[16,1]{1,0:T(8,128)S(1)}, f32[16,1]{1,0:T(8,128)S(1)}, u32[]{:S(2)}, u32[]{:S(2)}) collective-permute-start(f32[16,1]{1,0:T(8,128)S(1)} %add.102), channel_id=1, source_target_pairs={{0,6},{1,7},{2,4},{3,5},{4,2},{5,3},{6,0},{7,1},{8,14},{9,15},{10,... | collective-permute-start | bytes 200 | tf_op jit(solution)/shard_map/ppermute | solution.py:26
  9.1 3.5 convert_element_type.92.probes
  13.3 24.5 %first_forward.1 = (bf16[8,144,256]{2,1,0:T(8,128)(2,1)}, f32[16,16384]{1,0:T(8,128)S(1)}) custom-call(s32[1]{0:T(128)} %constant.9.clone.1.off, f32[16,16384]{1,0:T(8,128)S(1)} %copy-done, f32[16,3]{1,0:T(8,128)S(1)} %copy.27.cols, f32[16,1]{1,0:T(8,128)S(1)} %get-tuple-element.109.slopes, bf16[112,16384]{1,0:T(8,128)(2,1)S(1)} %convert_element_type.92.probes, ...), custom_call_target="tpu_custom_call" | custom-call | flops 8589934592 | bytes 67108864 | tf_op jit(solution)/shard_map/first_forward/pallas_call | solution.py:174
  38.8 4.1 %all-to-all-start = ((bf16[8,144,256]{2,1,0:T(8,128)(2,1)}), bf16[8,144,256]{2,1,0:T(8,128)(2,1)S(1)}, u32[]{:S(2)}, u32[]{:S(2)}) async-start(bf16[8,144,256]{2,1,0:T(8,128)(2,1)} %get-tuple-element.52), calls=%async_computation | async-start | bytes 1179648 | tf_op jit(solution)/shard_map/all_to_all | solution.py:498
  42.9 10.4 %all-to-all-done = bf16[8,144,256]{2,1,0:T(8,128)(2,1)S(1)} async-done(((bf16[8,144,256]{2,1,0:T(8,128)(2,1)}), bf16[8,144,256]{2,1,0:T(8,128)(2,1)S(1)}, u32[]{:S(2)}, u32[]{:S(2)}) %all-to-all-start) | async-done | bytes 589856 | tf_op jit(solution)/shard_map/all_to_all | solution.py:498
  54.2 10.0 %all_gather.3.rows = bf16[128,2048]{1,0:T(8,128)(2,1)S(1)} all-gather(bf16[128,256]{1,0:T(8,128)(2,1)S(1)} %pad_maximum_fusion.1), channel_id=1, replica_groups=mesh['sample'=4,'marker'=8] {'marker'}, dimensions={1}, use_global_device_ids=true | all-gather | bytes 589824 | tf_op jit(solution)/shard_map/all_gather | solution.py:503
  64.2 7.4 %first_back_0.1 = (f32[16,4096]{1,0:T(8,128)S(1)}, bf16[112,4096]{1,0:T(8,128)(2,1)S(1)}) custom-call(s32[4]{0:T(128)S(1)} %iota_xor_fusion.off, bf16[128,2048]{1,0:T(8,128)(2,1)S(1)} %all_gather.3.rows, bf16[2048,16384]{1,0:T(8,128)(2,1)} %refs_7_.1), custom_call_target="tpu_custom_call" | custom-call | flops 2147483648 | bytes 16777216 | tf_op jit(solution)/shard_map/first_back_0/pallas_call | solution.py:379
  71.6 3.5 %collective-permute-start.4 = (bf16[112,4096]{1,0:T(8,128)(2,1)S(1)}, bf16[112,4096]{1,0:T(8,128)(2,1)S(1)}, u32[]{:S(2)}, u32[]{:S(2)}) collective-permute-start(bf16[112,4096]{1,0:T(8,128)(2,1)S(1)} %get-tuple-element.61), channel_id=1, source_target_pairs={{0,8},{24,16},{1,9},{25,17},{2,10},{26,18},{3,11},{27,19},{4,12},{... | collective-permute-start | bytes 2752520 | tf_op jit(solution)/shard_map/ppermute | solution.py:521
  75.2 17.6 %first_back_1.1 = (f32[16,4096]{1,0:T(8,128)S(1)}, f32[16,4096]{1,0:T(8,128)S(1)}, f32[16,4096]{1,0:T(8,128)S(1)}, f32[16,4096]{1,0:T(8,128)S(1)}, bf16[112,6144...) custom-call(s32[4]{0:T(128)S(1)} %iota_xor_fusion.off, bf16[128,2048]{1,0:T(8,128)(2,1)S(1)} %all_gather.3.rows, ...), custom_call_target="tpu_custom_call" | custom-call | flops 6442450944 | bytes 50331648 | tf_op jit(solution)/shard_map/first_back_1/pallas_call | solution.py:379
  92.8 2.5 collective-permute-done.4
  95.2 2.5 collective-permute-start.5
  100.2 8.2 %collective-permute-done.5 = f32[16,4096]{1,0:T(8,128)S(1)} collective-permute-done((f32[16,4096]{1,0:T(8,128)S(1)}, f32[16,4096]{1,0:T(8,128)S(1)}, u32[]{:S(2)}, u32[]{:S(2)}) %collective-permute-start.5) | collective-permute-done | bytes 262176 | tf_op jit(solution)/shard_map/ppermute | solution.py:26
  108.4 10.7 %collective-permute-done.6 = f32[16,4096]{1,0:T(8,128)S(1)} collective-permute-done((f32[16,4096]{1,0:T(8,128)S(1)}, f32[16,4096]{1,0:T(8,128)S(1)}, u32[]{:S(2)}, u32[]{:S(2)}) %collective-permute-start.6) | collective-permute-done | bytes 262176 | tf_op jit(solution)/shard_map/ppermute | solution.py:26
  119.9 2.5 collective-permute-start.10
  122.4 4.8 %collective-permute-start.9 = (bf16[16,4096]{1,0:T(8,128)(2,1)S(1)}, bf16[16,4096]{1,0:T(8,128)(2,1)S(1)}, u32[]{:S(2)}, u32[]{:S(2)}) collective-permute-start(bf16[16,4096]{1,0:T(8,128)(2,1)S(1)} %reduce-precision_convert_fusion.refs_0_), channel_id=1, source_target_pairs={{0,16},{8,24},{16,0},{24,8},{1,17},{9,25},{17,1},{25,9},{2,18},{10... | collective-permute-start | bytes 393224 | tf_op jit(solution)/shard_map/ppermute | solution.py:26
  128.5 6.6 %collective-permute-done.9.refs_2_ = bf16[16,4096]{1,0:T(8,128)(2,1)S(1)} collective-permute-done((bf16[16,4096]{1,0:T(8,128)(2,1)S(1)}, bf16[16,4096]{1,0:T(8,128)(2,1)S(1)}, u32[]{:S(2)}, u32[]{:S(2)}) %collective-permute-start.9) | collective-permute-done | bytes 131104 | tf_op jit(solution)/shard_map/ppermute | solution.py:26
  135.1 2.7 collective-permute-start.12
  137.8 1.6 collective-permute-start.11
  139.6 22.3 %second_forward.1 = f32[16,2048]{1,0:T(8,128)S(1)} custom-call(s32[8]{0:T(128)S(1)} %reshape.26.off, bf16[16,4096]{1,0:T(8,128)(2,1)S(1)} %reduce-precision_convert_fusion.refs_0_, bf16[16,4096]{1,0:T(8,128)(2,1)S(1)} %collective-permute-done.8.refs_1_, bf16[16,4096]{1,0:T(8,128)(2,1)S(1)} %collective-permute-done.9.refs_2_, ...), custom_call_target="tpu_custom_call" | custom-call | flops 1073741824 | bytes 67108864 | tf_op jit(solution)/shard_map/second_forward/pallas_call | solution.py:222
  162.0 3.7 %collective-permute-done.12 = bf16[112,6144]{1,0:T(8,128)(2,1)} collective-permute-done((bf16[112,6144]{1,0:T(8,128)(2,1)S(1)}, bf16[112,6144]{1,0:T(8,128)(2,1)}, u32[]{:S(2)}, u32[]{:S(2)}) %collective-permute-start.12) | collective-permute-done | bytes 1376288 | tf_op jit(solution)/shard_map/ppermute | solution.py:521
  165.7 1.8 add_convert_fusion.3
  167.5 1.5 collective-permute-start.16
  171.0 1.7 add_convert_fusion.4.refs_4_
  172.7 2.1 collective-permute-done.16
  174.8 2.4 collective-permute-done.15
  177.9 4.7 %collective-permute-start.25 = (bf16[112,6144]{1,0:T(8,128)(2,1)S(1)}, bf16[112,6144]{1,0:T(8,128)(2,1)S(1)}, u32[]{:S(2)}, u32[]{:S(2)}) collective-permute-start(bf16[112,6144]{1,0:T(8,128)(2,1)S(1)} %get-tuple-element.90), channel_id=1, source_target_pairs={{0,8},{24,16},{1,9},{25,17},{2,10},{26,18},{3,11},{27,19},{4,12},{... | collective-permute-start | bytes 4128776 | tf_op jit(solution)/shard_map/ppermute | solution.py:521
  183.4 1.5 collective-permute-start.17
  184.8 21.8 %second_back.1 = (f32[16,4096]{1,0:T(8,128)S(1)}, bf16[16,4096]{1,0:T(8,128)(2,1)S(1)}, bf16[16,4096]{1,0:T(8,128)(2,1)S(1)}, bf16[16,4096]{1,0:T(8,128)(2,1)S(1)}) custom-call(s32[8]{0:T(128)S(1)} %reshape.26.off, bf16[16,2048]{1,0:T(8,128)(2,1)S(1)} %get-tuple-element.80.rows, bf16[2048,16384]{1,0:T(8,128)(2,1)} %refs_7_.1), custom_call_target="tpu_custom_call" | custom-call | flops 1073741824 | bytes 67108864 | tf_op jit(solution)/shard_map/second_back/pallas_call | solution.py:407
  207.2 2.2 collective-permute-start.18
  212.0 3.9 %collective-permute-done.18 = bf16[16,4096]{1,0:T(8,128)(2,1)S(1)} collective-permute-done((bf16[16,4096]{1,0:T(8,128)(2,1)S(1)}, bf16[16,4096]{1,0:T(8,128)(2,1)S(1)}, u32[]{:S(2)}, u32[]{:S(2)}) %collective-permute-start.18) | collective-permute-done | bytes 131104 | tf_op jit(solution)/shard_map/ppermute | solution.py:26
  215.9 8.8 %collective-permute-done.19 = bf16[16,4096]{1,0:T(8,128)(2,1)S(1)} collective-permute-done((bf16[16,4096]{1,0:T(8,128)(2,1)S(1)}, bf16[16,4096]{1,0:T(8,128)(2,1)S(1)}, u32[]{:S(2)}, u32[]{:S(2)}) %collective-permute-start.19) | collective-permute-done | bytes 131104 | tf_op jit(solution)/shard_map/ppermute | solution.py:26
  225.4 2.5 collective-permute-start.23
  233.3 7.4 %collective-permute-done.22.refs_2_.refs_6_ = bf16[16,4096]{1,0:T(8,128)(2,1)S(1)} collective-permute-done((bf16[16,4096]{1,0:T(8,128)(2,1)S(1)}, bf16[16,4096]{1,0:T(8,128)(2,1)S(1)}, u32[]{:S(2)}, u32[]{:S(2)}) %collective-permute-start.22) | collective-permute-done | bytes 131104 | tf_op jit(solution)/shard_map/ppermute | solution.py:26
  242.4 24.9 %collective-permute-done.28.refs_7_ = bf16[112,6144]{1,0:T(8,128)(2,1)} collective-permute-done((bf16[112,6144]{1,0:T(8,128)(2,1)S(1)}, bf16[112,6144]{1,0:T(8,128)(2,1)}, u32[]{:S(2)}, u32[]{:S(2)}) %collective-permute-start.28) | collective-permute-done | bytes 1376288 | tf_op jit(solution)/shard_map/ppermute | solution.py:527
  269.7 17.3 %third_forward_0.1.refs_6_ = f32[2048,128]{1,0:T(8,128)S(1)} custom-call(s32[5]{0:T(128)S(1)} %pad_add_fusion.1.off, bf16[16,4096]{1,0:T(8,128)(2,1)S(1)} %get-tuple-element.110.refs_0_.refs_4_, bf16[16,4096]{1,0:T(8,128)(2,1)S(1)} %collective-permute-done.21.refs_1_.refs_5_, bf16[16,4096]{1,0:T(8,128)(2,1)S(1)} %collective-permute-done.22.refs_2_.refs_6_, ...), custom_call_target="tpu_custom_call" | custom-call | flops 5368709120 | bytes 41943040 | tf_op jit(solution)/shard_map/third_forward_0/pallas_call | solution.py:297
  287.0 12.8 %collective-permute-done.27.refs_5_ = bf16[112,6144]{1,0:T(8,128)(2,1)} collective-permute-done((bf16[112,6144]{1,0:T(8,128)(2,1)S(1)}, bf16[112,6144]{1,0:T(8,128)(2,1)}, u32[]{:S(2)}, u32[]{:S(2)}) %collective-permute-start.27) | collective-permute-done | bytes 1376288 | tf_op jit(solution)/shard_map/ppermute | solution.py:527
  299.8 12.7 %third_forward_1.1 = bf16[8,128,256]{2,1,0:T(8,128)(2,1)} custom-call(s32[5]{0:T(128)S(1)} %pad_add_fusion.1.off, bf16[16,4096]{1,0:T(8,128)(2,1)S(1)} %get-tuple-element.110.refs_0_.refs_4_, bf16[16,4096]{1,0:T(8,128)(2,1)S(1)} %collective-permute-done.21.refs_1_.refs_5_, bf16[16,4096]{1,0:T(8,128)(2,1)S(1)} %collective-permute-done.22.refs_2_.refs_6_, ...), custom_call_target="tpu_custom_call" | custom-call | flops 3221225472 | bytes 25165824 | tf_op jit(solution)/shard_map/third_forward_1/pallas_call | solution.py:297
  312.5 3.5 %all-to-all-start.1 = ((bf16[8,128,256]{2,1,0:T(8,128)(2,1)}), bf16[8,128,256]{2,1,0:T(8,128)(2,1)S(1)}, u32[]{:S(2)}, u32[]{:S(2)}) async-start(bf16[8,128,256]{2,1,0:T(8,128)(2,1)} %third_forward_1.1), calls=%async_computation.1 | async-start | bytes 1048576 | tf_op jit(solution)/shard_map/all_to_all | solution.py:571
  316.9 3.5 collective-permute-start.31
  321.4 1.7 multiply_reduce_fusion
  323.8 1.6 collective-permute-done.31.refs_11_
  325.4 5.6 %collective-permute-done.30.refs_10_ = bf16[16,4096]{1,0:T(8,128)(2,1)S(1)} collective-permute-done((bf16[16,4096]{1,0:T(8,128)(2,1)}, bf16[16,4096]{1,0:T(8,128)(2,1)S(1)}, u32[]{:S(2)}, u32[]{:S(2)}) %collective-permute-start.30) | collective-permute-done | bytes 131104 | tf_op jit(solution)/shard_map/ppermute | solution.py:26
  332.7 2.6 collective-permute-start.35
  337.2 1.7 collective-permute-done.34
  339.4 2.7 collective-permute-start.38
  342.1 1.7 collective-permute-start.36
  344.8 1.8 collective-permute-done.37
  346.7 3.2 finish.1
  (133 shorter events, 36.2 us)
Async XLA Ops:
  3.4 1.3 collective-permute-start
  4.7 7.9 %collective-permute-start.3 = (f32[16,1]{1,0:T(8,128)S(1)}, f32[16,1]{1,0:T(8,128)S(1)}, u32[]{:S(2)}, u32[]{:S(2)}) collective-permute-start(f32[16,1]{1,0:T(8,128)S(1)} %add.102), channel_id=1, source_target_pairs={{0,6},{1,7},{2,4},{3,5},{4,2},{5,3},{6,0},{7,1},{8,14},{9,15},{10,... | collective-permute-start | bytes 200 | tf_op jit(solution)/shard_map/ppermute | solution.py:26
  8.5 4.1 %collective-permute-start.2 = (f32[16,1]{1,0:T(8,128)S(1)}, f32[16,1]{1,0:T(8,128)S(1)}, u32[]{:S(2)}, u32[]{:S(2)}) collective-permute-start(f32[16,1]{1,0:T(8,128)S(1)} %add.102), channel_id=1, source_target_pairs={{0,4},{1,5},{2,6},{3,7},{4,0},{5,1},{6,2},{7,3},{8,12},{9,13},{10,... | collective-permute-start | bytes 200 | tf_op jit(solution)/shard_map/ppermute | solution.py:26
  9.0 3.7 %collective-permute-start.1 = (f32[16,1]{1,0:T(8,128)S(1)}, f32[16,1]{1,0:T(8,128)S(1)}, u32[]{:S(2)}, u32[]{:S(2)}) collective-permute-start(f32[16,1]{1,0:T(8,128)S(1)} %add.102), channel_id=1, source_target_pairs={{0,2},{1,3},{2,0},{3,1},{4,6},{5,7},{6,4},{7,5},{8,10},{9,11},{10,... | collective-permute-start | bytes 200 | tf_op jit(solution)/shard_map/ppermute | solution.py:26
  38.8 14.6 %all-to-all-start = ((bf16[8,144,256]{2,1,0:T(8,128)(2,1)}), bf16[8,144,256]{2,1,0:T(8,128)(2,1)S(1)}, u32[]{:S(2)}, u32[]{:S(2)}) async-start(bf16[8,144,256]{2,1,0:T(8,128)(2,1)} %get-tuple-element.52), calls=%async_computation | async-start | bytes 1179648 | tf_op jit(solution)/shard_map/all_to_all | solution.py:498
  71.6 28.6 %copy-start.20 = (f32[16]{0:T(128)S(1)}, f32[16]{0:T(128)}, u32[]{:S(2)}) copy-start(f32[16]{0:T(128)} %param.15) | copy-start | bytes 196
  71.6 23.6 %collective-permute-start.4 = (bf16[112,4096]{1,0:T(8,128)(2,1)S(1)}, bf16[112,4096]{1,0:T(8,128)(2,1)S(1)}, u32[]{:S(2)}, u32[]{:S(2)}) collective-permute-start(bf16[112,4096]{1,0:T(8,128)(2,1)S(1)} %get-tuple-element.61), channel_id=1, source_target_pairs={{0,8},{24,16},{1,9},{25,17},{2,10},{26,18},{3,11},{27,19},{4,12},{... | collective-permute-start | bytes 2752520 | tf_op jit(solution)/shard_map/ppermute | solution.py:521
  95.2 13.2 %collective-permute-start.5 = (f32[16,4096]{1,0:T(8,128)S(1)}, f32[16,4096]{1,0:T(8,128)S(1)}, u32[]{:S(2)}, u32[]{:S(2)}) collective-permute-start(f32[16,4096]{1,0:T(8,128)S(1)} %get-tuple-element.63), channel_id=1, source_target_pairs={{0,8},{8,0},{16,24},{24,16},{1,9},{9,1},{17,25},{25,17},{2,10},{10... | collective-permute-start | bytes 786440 | tf_op jit(solution)/shard_map/ppermute | solution.py:26
  97.7 21.4 %collective-permute-start.6 = (f32[16,4096]{1,0:T(8,128)S(1)}, f32[16,4096]{1,0:T(8,128)S(1)}, u32[]{:S(2)}, u32[]{:S(2)}) collective-permute-start(f32[16,4096]{1,0:T(8,128)S(1)} %get-tuple-element.64), channel_id=1, source_target_pairs={{0,16},{8,24},{16,0},{24,8},{1,17},{9,25},{17,1},{25,9},{2,18},{10... | collective-permute-start | bytes 786440 | tf_op jit(solution)/shard_map/ppermute | solution.py:26
  98.7 20.4 %collective-permute-start.7 = (f32[16,4096]{1,0:T(8,128)S(1)}, f32[16,4096]{1,0:T(8,128)S(1)}, u32[]{:S(2)}, u32[]{:S(2)}) collective-permute-start(f32[16,4096]{1,0:T(8,128)S(1)} %get-tuple-element.65), channel_id=1, source_target_pairs={{0,24},{8,16},{16,8},{24,0},{1,25},{9,17},{17,9},{25,1},{2,26},{10... | collective-permute-start | bytes 786440 | tf_op jit(solution)/shard_map/ppermute | solution.py:26
  119.9 8.7 %collective-permute-start.10 = (bf16[16,4096]{1,0:T(8,128)(2,1)S(1)}, bf16[16,4096]{1,0:T(8,128)(2,1)S(1)}, u32[]{:S(2)}, u32[]{:S(2)}) collective-permute-start(bf16[16,4096]{1,0:T(8,128)(2,1)S(1)} %reduce-precision_convert_fusion.refs_0_), channel_id=1, source_target_pairs={{0,24},{8,16},{16,8},{24,0},{1,25},{9,17},{17,9},{25,1},{2,26},{10... | collective-permute-start | bytes 393224 | tf_op jit(solution)/shard_map/ppermute | solution.py:26
  122.4 12.7 %collective-permute-start.9 = (bf16[16,4096]{1,0:T(8,128)(2,1)S(1)}, bf16[16,4096]{1,0:T(8,128)(2,1)S(1)}, u32[]{:S(2)}, u32[]{:S(2)}) collective-permute-start(bf16[16,4096]{1,0:T(8,128)(2,1)S(1)} %reduce-precision_convert_fusion.refs_0_), channel_id=1, source_target_pairs={{0,16},{8,24},{16,0},{24,8},{1,17},{9,25},{17,1},{25,9},{2,18},{10... | collective-permute-start | bytes 393224 | tf_op jit(solution)/shard_map/ppermute | solution.py:26
  127.3 7.9 %collective-permute-start.8 = (bf16[16,4096]{1,0:T(8,128)(2,1)S(1)}, bf16[16,4096]{1,0:T(8,128)(2,1)S(1)}, u32[]{:S(2)}, u32[]{:S(2)}) collective-permute-start(bf16[16,4096]{1,0:T(8,128)(2,1)S(1)} %reduce-precision_convert_fusion.refs_0_), channel_id=1, source_target_pairs={{0,8},{8,0},{16,24},{24,16},{1,9},{9,1},{17,25},{25,17},{2,10},{10... | collective-permute-start | bytes 393224 | tf_op jit(solution)/shard_map/ppermute | solution.py:26
  135.1 30.5 %collective-permute-start.12 = (bf16[112,6144]{1,0:T(8,128)(2,1)S(1)}, bf16[112,6144]{1,0:T(8,128)(2,1)}, u32[]{:S(2)}, u32[]{:S(2)}) collective-permute-start(bf16[112,6144]{1,0:T(8,128)(2,1)S(1)} %get-tuple-element.73), channel_id=1, source_target_pairs={{0,8},{24,16},{1,9},{25,17},{2,10},{26,18},{3,11},{27,19},{4,12},{... | collective-permute-start | bytes 4128776 | tf_op jit(solution)/shard_map/ppermute | solution.py:521
  137.8 24.1 %collective-permute-start.11 = (bf16[112,4096]{1,0:T(8,128)(2,1)}, bf16[112,4096]{1,0:T(8,128)(2,1)}, u32[]{:S(2)}, u32[]{:S(2)}) collective-permute-start(bf16[112,4096]{1,0:T(8,128)(2,1)} %add_convert_fusion.5), channel_id=1, source_target_pairs={{8,16},{16,8},{9,17},{17,9},{10,18},{18,10},{11,19},{19,11},{12,20... | collective-permute-start | bytes 2752520 | tf_op jit(solution)/shard_map/ppermute | solution.py:524
  165.7 1.8 collective-permute-start.13
  167.5 7.3 %collective-permute-start.16 = (f32[16,2048]{1,0:T(8,128)S(1)}, f32[16,2048]{1,0:T(8,128)S(1)}, u32[]{:S(2)}, u32[]{:S(2)}) collective-permute-start(f32[16,2048]{1,0:T(8,128)S(1)} %add.112), channel_id=1, source_target_pairs={{0,6},{1,7},{2,4},{3,5},{4,2},{5,3},{6,0},{7,1},{8,14},{9,15},{10,... | collective-permute-start | bytes 393224 | tf_op jit(solution)/shard_map/ppermute | solution.py:26
  169.0 8.2 %collective-permute-start.15 = (f32[16,2048]{1,0:T(8,128)S(1)}, f32[16,2048]{1,0:T(8,128)S(1)}, u32[]{:S(2)}, u32[]{:S(2)}) collective-permute-start(f32[16,2048]{1,0:T(8,128)S(1)} %add.112), channel_id=1, source_target_pairs={{0,4},{1,5},{2,6},{3,7},{4,0},{5,1},{6,2},{7,3},{8,12},{9,13},{10,... | collective-permute-start | bytes 393224 | tf_op jit(solution)/shard_map/ppermute | solution.py:26
  170.5 6.7 %collective-permute-start.14 = (f32[16,2048]{1,0:T(8,128)S(1)}, f32[16,2048]{1,0:T(8,128)S(1)}, u32[]{:S(2)}, u32[]{:S(2)}) collective-permute-start(f32[16,2048]{1,0:T(8,128)S(1)} %add.112), channel_id=1, source_target_pairs={{0,2},{1,3},{2,0},{3,1},{4,6},{5,7},{6,4},{7,5},{8,10},{9,11},{10,... | collective-permute-start | bytes 393224 | tf_op jit(solution)/shard_map/ppermute | solution.py:26
  172.7 34.0 %copy-start.1 = (bf16[112,4096]{1,0:T(8,128)(2,1)}, bf16[112,4096]{1,0:T(8,128)(2,1)S(1)}, u32[]{:S(2)}) copy-start(bf16[112,4096]{1,0:T(8,128)(2,1)S(1)} %add_convert_fusion.4.refs_4_) | copy-start | bytes 2752516
  177.9 46.8 %copy-start.13 = (f32[16,4096]{1,0:T(8,128)S(1)}, f32[16,4096]{1,0:T(8,128)}, u32[]{:S(2)}) copy-start(f32[16,4096]{1,0:T(8,128)} %copy-done.12) | copy-start | bytes 786436
  177.9 51.9 %collective-permute-start.25 = (bf16[112,6144]{1,0:T(8,128)(2,1)S(1)}, bf16[112,6144]{1,0:T(8,128)(2,1)S(1)}, u32[]{:S(2)}, u32[]{:S(2)}) collective-permute-start(bf16[112,6144]{1,0:T(8,128)(2,1)S(1)} %get-tuple-element.90), channel_id=1, source_target_pairs={{0,8},{24,16},{1,9},{25,17},{2,10},{26,18},{3,11},{27,19},{4,12},{... | collective-permute-start | bytes 4128776 | tf_op jit(solution)/shard_map/ppermute | solution.py:521
  182.6 47.2 %collective-permute-start.24 = (bf16[112,6144]{1,0:T(8,128)(2,1)S(1)}, bf16[112,6144]{1,0:T(8,128)(2,1)S(1)}, u32[]{:S(2)}, u32[]{:S(2)}) collective-permute-start(bf16[112,6144]{1,0:T(8,128)(2,1)S(1)} %add_convert_fusion.3), channel_id=1, source_target_pairs={{8,16},{16,8},{9,17},{17,9},{10,18},{18,10},{11,19},{19,11},{12,20... | collective-permute-start | bytes 4128776 | tf_op jit(solution)/shard_map/ppermute | solution.py:524
  183.4 23.9 %collective-permute-start.17 = (bf16[112,4096]{1,0:T(8,128)(2,1)S(1)}, bf16[112,4096]{1,0:T(8,128)(2,1)S(1)}, u32[]{:S(2)}, u32[]{:S(2)}) collective-permute-start(bf16[112,4096]{1,0:T(8,128)(2,1)S(1)} %add_convert_fusion.4.refs_4_), channel_id=1, source_target_pairs={{8,0},{16,24},{9,1},{17,25},{10,2},{18,26},{11,3},{19,27},{12,4},{... | collective-permute-start | bytes 2752520 | tf_op jit(solution)/shard_map/ppermute | solution.py:527
  207.2 8.6 %collective-permute-start.18 = (bf16[16,4096]{1,0:T(8,128)(2,1)S(1)}, bf16[16,4096]{1,0:T(8,128)(2,1)S(1)}, u32[]{:S(2)}, u32[]{:S(2)}) collective-permute-start(bf16[16,4096]{1,0:T(8,128)(2,1)S(1)} %get-tuple-element.87), channel_id=1, source_target_pairs={{0,8},{8,0},{16,24},{24,16},{1,9},{9,1},{17,25},{25,17},{2,10},{10... | collective-permute-start | bytes 393224 | tf_op jit(solution)/shard_map/ppermute | solution.py:26
  209.5 15.2 %collective-permute-start.19 = (bf16[16,4096]{1,0:T(8,128)(2,1)S(1)}, bf16[16,4096]{1,0:T(8,128)(2,1)S(1)}, u32[]{:S(2)}, u32[]{:S(2)}) collective-permute-start(bf16[16,4096]{1,0:T(8,128)(2,1)S(1)} %get-tuple-element.88), channel_id=1, source_target_pairs={{0,16},{8,24},{16,0},{24,8},{1,17},{9,25},{17,1},{25,9},{2,18},{10... | collective-permute-start | bytes 393224 | tf_op jit(solution)/shard_map/ppermute | solution.py:26
  210.6 14.1 %collective-permute-start.20 = (bf16[16,4096]{1,0:T(8,128)(2,1)S(1)}, bf16[16,4096]{1,0:T(8,128)(2,1)S(1)}, u32[]{:S(2)}, u32[]{:S(2)}) collective-permute-start(bf16[16,4096]{1,0:T(8,128)(2,1)S(1)} %get-tuple-element.89), channel_id=1, source_target_pairs={{0,24},{8,16},{16,8},{24,0},{1,25},{9,17},{17,9},{25,1},{2,26},{10... | collective-permute-start | bytes 393224 | tf_op jit(solution)/shard_map/ppermute | solution.py:26
  225.4 7.9 %collective-permute-start.23 = (bf16[16,4096]{1,0:T(8,128)(2,1)S(1)}, bf16[16,4096]{1,0:T(8,128)(2,1)S(1)}, u32[]{:S(2)}, u32[]{:S(2)}) collective-permute-start(bf16[16,4096]{1,0:T(8,128)(2,1)S(1)} %get-tuple-element.110.refs_0_.refs_4_), channel_id=1, source_target_pairs={{0,24},{8,16},{16,8},{24,0},{1,25},{9,17},{17,9},{25,1},{2,26},{10... | collective-permute-start | bytes 393224 | tf_op jit(solution)/shard_map/ppermute | solution.py:26
  227.9 12.8 %collective-permute-start.22 = (bf16[16,4096]{1,0:T(8,128)(2,1)S(1)}, bf16[16,4096]{1,0:T(8,128)(2,1)S(1)}, u32[]{:S(2)}, u32[]{:S(2)}) collective-permute-start(bf16[16,4096]{1,0:T(8,128)(2,1)S(1)} %get-tuple-element.110.refs_0_.refs_4_), channel_id=1, source_target_pairs={{0,16},{8,24},{16,0},{24,8},{1,17},{9,25},{17,1},{25,9},{2,18},{10... | collective-permute-start | bytes 393224 | tf_op jit(solution)/shard_map/ppermute | solution.py:26
  229.3 11.4 %collective-permute-start.21 = (bf16[16,4096]{1,0:T(8,128)(2,1)S(1)}, bf16[16,4096]{1,0:T(8,128)(2,1)S(1)}, u32[]{:S(2)}, u32[]{:S(2)}) collective-permute-start(bf16[16,4096]{1,0:T(8,128)(2,1)S(1)} %get-tuple-element.110.refs_0_.refs_4_), channel_id=1, source_target_pairs={{0,8},{8,0},{16,24},{24,16},{1,9},{9,1},{17,25},{25,17},{2,10},{10... | collective-permute-start | bytes 393224 | tf_op jit(solution)/shard_map/ppermute | solution.py:26
  230.1 10.6 %collective-permute-start.26 = (bf16[112,6144]{1,0:T(8,128)(2,1)S(1)}, bf16[112,6144]{1,0:T(8,128)(2,1)S(1)}, u32[]{:S(2)}, u32[]{:S(2)}) collective-permute-start(bf16[112,6144]{1,0:T(8,128)(2,1)S(1)} %add_convert_fusion.2), channel_id=1, source_target_pairs={{8,16},{16,8},{9,17},{17,9},{10,18},{18,10},{11,19},{19,11},{12,20... | collective-permute-start | bytes 4128776 | tf_op jit(solution)/shard_map/ppermute | solution.py:524
  231.2 36.1 %collective-permute-start.28 = (bf16[112,6144]{1,0:T(8,128)(2,1)S(1)}, bf16[112,6144]{1,0:T(8,128)(2,1)}, u32[]{:S(2)}, u32[]{:S(2)}) collective-permute-start(bf16[112,6144]{1,0:T(8,128)(2,1)S(1)} %add_convert_fusion.refs_5_), channel_id=1, source_target_pairs={{8,0},{16,24},{9,1},{17,25},{10,2},{18,26},{11,3},{19,27},{12,4},{... | collective-permute-start | bytes 4128776 | tf_op jit(solution)/shard_map/ppermute | solution.py:527
  241.0 58.7 %collective-permute-start.27 = (bf16[112,6144]{1,0:T(8,128)(2,1)S(1)}, bf16[112,6144]{1,0:T(8,128)(2,1)}, u32[]{:S(2)}, u32[]{:S(2)}) collective-permute-start(bf16[112,6144]{1,0:T(8,128)(2,1)S(1)} %add_convert_fusion.1.refs_4_), channel_id=1, source_target_pairs={{8,0},{16,24},{9,1},{17,25},{10,2},{18,26},{11,3},{19,27},{12,4},{... | collective-permute-start | bytes 4128776 | tf_op jit(solution)/shard_map/ppermute | solution.py:527
  312.5 18.5 %all-to-all-start.1 = ((bf16[8,128,256]{2,1,0:T(8,128)(2,1)}), bf16[8,128,256]{2,1,0:T(8,128)(2,1)S(1)}, u32[]{:S(2)}, u32[]{:S(2)}) async-start(bf16[8,128,256]{2,1,0:T(8,128)(2,1)} %third_forward_1.1), calls=%async_computation.1 | async-start | bytes 1048576 | tf_op jit(solution)/shard_map/all_to_all | solution.py:571
  316.8 29.8 %copy-start.4 = (f32[16,16384]{1,0:T(8,128)S(1)}, f32[16,16384]{1,0:T(8,128)}, u32[]{:S(2)}) copy-start(f32[16,16384]{1,0:T(8,128)} %copy-done.3) | copy-start | bytes 3145732
  316.8 29.8 %copy-start.8 = (bf16[16,4096]{1,0:T(8,128)(2,1)S(1)}, bf16[16,4096]{1,0:T(8,128)(2,1)}, u32[]{:S(2)}) copy-start(bf16[16,4096]{1,0:T(8,128)(2,1)} %copy-done.7) | copy-start | bytes 393220
  316.9 29.8 %copy-start.10 = (bf16[16,4096]{1,0:T(8,128)(2,1)S(1)}, bf16[16,4096]{1,0:T(8,128)(2,1)}, u32[]{:S(2)}) copy-start(bf16[16,4096]{1,0:T(8,128)(2,1)} %copy-done.9) | copy-start | bytes 393220
  316.9 29.8 %copy-start.11 = (bf16[16,4096]{1,0:T(8,128)(2,1)S(1)}, bf16[16,4096]{1,0:T(8,128)(2,1)}, u32[]{:S(2)}) copy-start(bf16[16,4096]{1,0:T(8,128)(2,1)} %get-tuple-element.97.refs_8_) | copy-start | bytes 393220
  316.9 8.5 %collective-permute-start.31 = (bf16[16,4096]{1,0:T(8,128)(2,1)}, bf16[16,4096]{1,0:T(8,128)(2,1)S(1)}, u32[]{:S(2)}, u32[]{:S(2)}) collective-permute-start(bf16[16,4096]{1,0:T(8,128)(2,1)} %get-tuple-element.97.refs_8_), channel_id=1, source_target_pairs={{0,24},{8,16},{16,8},{24,0},{1,25},{9,17},{17,9},{25,1},{2,26},{10... | collective-permute-start | bytes 393224 | tf_op jit(solution)/shard_map/ppermute | solution.py:26
  320.3 10.6 %collective-permute-start.30 = (bf16[16,4096]{1,0:T(8,128)(2,1)}, bf16[16,4096]{1,0:T(8,128)(2,1)S(1)}, u32[]{:S(2)}, u32[]{:S(2)}) collective-permute-start(bf16[16,4096]{1,0:T(8,128)(2,1)} %get-tuple-element.97.refs_8_), channel_id=1, source_target_pairs={{0,16},{8,24},{16,0},{24,8},{1,17},{9,25},{17,1},{25,9},{2,18},{10... | collective-permute-start | bytes 393224 | tf_op jit(solution)/shard_map/ppermute | solution.py:26
  320.4 10.6 %collective-permute-start.29 = (bf16[16,4096]{1,0:T(8,128)(2,1)}, bf16[16,4096]{1,0:T(8,128)(2,1)S(1)}, u32[]{:S(2)}, u32[]{:S(2)}) collective-permute-start(bf16[16,4096]{1,0:T(8,128)(2,1)} %get-tuple-element.97.refs_8_), channel_id=1, source_target_pairs={{0,8},{8,0},{16,24},{24,16},{1,9},{9,1},{17,25},{25,17},{2,10},{10... | collective-permute-start | bytes 393224 | tf_op jit(solution)/shard_map/ppermute | solution.py:26
  331.5 1.2 collective-permute-start.32
  332.7 4.5 %collective-permute-start.35 = (f32[8,128]{1,0:T(8,128)S(1)}, f32[8,128]{1,0:T(8,128)S(1)}, u32[]{:S(2)}, u32[]{:S(2)}) collective-permute-start(f32[8,128]{1,0:T(8,128)S(1)} %add.125), channel_id=1, source_target_pairs={{0,6},{1,7},{2,4},{3,5},{4,2},{5,3},{6,0},{7,1},{8,14},{9,15},{10,... | collective-permute-start | bytes 12296 | tf_op jit(solution)/shard_map/ppermute | solution.py:26
  335.3 3.6 %collective-permute-start.34 = (f32[8,128]{1,0:T(8,128)S(1)}, f32[8,128]{1,0:T(8,128)S(1)}, u32[]{:S(2)}, u32[]{:S(2)}) collective-permute-start(f32[8,128]{1,0:T(8,128)S(1)} %add.125), channel_id=1, source_target_pairs={{0,4},{1,5},{2,6},{3,7},{4,0},{5,1},{6,2},{7,3},{8,12},{9,13},{10,... | collective-permute-start | bytes 12296 | tf_op jit(solution)/shard_map/ppermute | solution.py:26
  335.8 3.6 %collective-permute-start.33 = (f32[8,128]{1,0:T(8,128)S(1)}, f32[8,128]{1,0:T(8,128)S(1)}, u32[]{:S(2)}, u32[]{:S(2)}) collective-permute-start(f32[8,128]{1,0:T(8,128)S(1)} %add.125), channel_id=1, source_target_pairs={{0,2},{1,3},{2,0},{3,1},{4,6},{5,7},{6,4},{7,5},{8,10},{9,11},{10,... | collective-permute-start | bytes 12296 | tf_op jit(solution)/shard_map/ppermute | solution.py:26
  339.4 5.4 %collective-permute-start.38 = (f32[8,128]{1,0:T(8,128)S(1)}, f32[8,128]{1,0:T(8,128)S(1)}, u32[]{:S(2)}, u32[]{:S(2)}) collective-permute-start(f32[8,128]{1,0:T(8,128)S(1)} %add_add_fusion.3), channel_id=1, source_target_pairs={{0,24},{8,16},{16,8},{24,0},{1,25},{9,17},{17,9},{25,1},{2,26},{10... | collective-permute-start | bytes 12296 | tf_op jit(solution)/shard_map/ppermute | solution.py:26
  342.1 4.5 %collective-permute-start.37 = (f32[8,128]{1,0:T(8,128)S(1)}, f32[8,128]{1,0:T(8,128)S(1)}, u32[]{:S(2)}, u32[]{:S(2)}) collective-permute-start(f32[8,128]{1,0:T(8,128)S(1)} %add_add_fusion.3), channel_id=1, source_target_pairs={{0,16},{8,24},{16,0},{24,8},{1,17},{9,25},{17,1},{25,9},{2,18},{10... | collective-permute-start | bytes 12296 | tf_op jit(solution)/shard_map/ppermute | solution.py:26
  342.1 4.5 %collective-permute-start.36 = (f32[8,128]{1,0:T(8,128)S(1)}, f32[8,128]{1,0:T(8,128)S(1)}, u32[]{:S(2)}, u32[]{:S(2)}) collective-permute-start(f32[8,128]{1,0:T(8,128)S(1)} %add_add_fusion.3), channel_id=1, source_target_pairs={{0,8},{8,0},{16,24},{24,16},{1,9},{9,1},{17,25},{25,17},{2,10},{10... | collective-permute-start | bytes 12296 | tf_op jit(solution)/shard_map/ppermute | solution.py:26
  (14 other events, 181.7 us)

commit v10 on v9

--- a/solution.py
+++ b/solution.py
@@ -501,7 +501,7 @@
     rows = jnp.concatenate([own, kept_x[traits:]], axis=0).astype(BF16)
     pred_x = rows[traits:].astype(F32)
     rows = lax.all_gather(rows, "marker", axis=1, tiled=True)
-    sizes = (some, samples - 1, samples - 1)
+    sizes = (samples - 1, samples - 1, some)
     before, *chunks = first_back(
         rows, order, genotypes, unit, traits, 0, None, sizes[:1], "first_back_0"
     )

time: 351 us -> 353 us (level)
  starting transfers between devices: 68.1 us -> 73.2 us
    ppermute x3, waiting for transfers between devices: 38.3 us -> 13.6 us  [outward(): return lax.ppermute(x, 'sample', [(1, 0), (2, 3)])]
    ppermute x3, waiting for transfers between devices: 6.17 us -> 19.6 us  [inward(): return lax.ppermute(chunks[c], 'sample', [(0, 1), (3, 2)])]
    ppermute x30, waiting for transfers between devices: 65.8 us -> 75.2 us  [swap(): return lax.ppermute(x, axis, [(i, i ^ bits) for i in range(n)])]
  transfers between devices with their start and end apart: 41 -> 41, of which waited for: 25 -> 24; matrix products, arithmetic and copies ran while one was open for 4% -> 4% of each run, Pallas kernels for 23% -> 22%
where the time goes in v10:
time: 353 us; the launch traced here: 352 us
  Pallas kernels  128 us (36%)
  waiting for transfers between devices  119 us (34%)
  starting transfers between devices  73.2 us (21%)
  other arithmetic  16.2 us (5%)
  blocking collectives  9.96 us (3%)
  local copies, waits for them, and re-layouts  4.92 us (1%)
    ppermute x30, waiting for transfers between devices, swap(): return lax.ppermute(x, axis, [(i, i ^ bits) for i in range(n)])  75.2 us
    ppermute x30, starting transfers between devices, swap(): return lax.ppermute(x, axis, [(i, i ^ bits) for i in range(n)])  43.9 us
    pallas_call x2, Pallas kernels, wide_forward(): pl.pallas_call(functools.partial(wide_body, n, begin, len(inner), acc is...  30.2 us
    pallas_call x2, Pallas kernels, first_back(): pl.pallas_call(functools.partial(first_back_body, unit, begin, t, arrays)...  25.2 us
    pallas_call x1, Pallas kernels, first_forward(): pl.pallas_call(functools.partial(first_body, markers * columns), grid_spe...  24.5 us
    pallas_call x1, Pallas kernels, narrow_forward(): pl.pallas_call(functools.partial(narrow_body, n, unit, acc is not None),...  22.3 us
    pallas_call x1, Pallas kernels, second_back(): pl.pallas_call(functools.partial(second_back_body, n, unit), grid_spec=pl...  21.8 us
    ppermute x3, waiting for transfers between devices, inward(): return lax.ppermute(chunks[c], 'sample', [(0, 1), (3, 2)])  19.6 us
  transfers between devices with their start and end apart: 41, of which 24 were waited for; matrix products, arithmetic and copies ran while one was open for 4% of the time, Pallas kernels for 22%

profile of v10, /device:TPU:0, one launch (start us, length us, event | category | flops | bytes accessed | tf_op | source)
XLA Modules:
  0.0 352.3 jit_solution(4998897305703941492)
XLA Ops:
  4.7 3.8 %collective-permute-start.3 = (f32[16,1]{1,0:T(8,128)S(1)}, f32[16,1]{1,0:T(8,128)S(1)}, u32[]{:S(2)}, u32[]{:S(2)}) collective-permute-start(f32[16,1]{1,0:T(8,128)S(1)} %add.102), channel_id=1, source_target_pairs={{0,6},{1,7},{2,4},{3,5},{4,2},{5,3},{6,0},{7,1},{8,14},{9,15},{10,... | collective-permute-start | bytes 200 | tf_op jit(solution)/shard_map/ppermute | solution.py:26
  9.1 3.5 convert_element_type.92.probes
  13.3 24.5 %first_forward.1 = (bf16[8,144,256]{2,1,0:T(8,128)(2,1)}, f32[16,16384]{1,0:T(8,128)S(1)}) custom-call(s32[1]{0:T(128)} %constant.9.clone.1.off, f32[16,16384]{1,0:T(8,128)S(1)} %copy-done, f32[16,3]{1,0:T(8,128)S(1)} %copy.27.cols, f32[16,1]{1,0:T(8,128)S(1)} %get-tuple-element.109.slopes, bf16[112,16384]{1,0:T(8,128)(2,1)S(1)} %convert_element_type.92.probes, ...), custom_call_target="tpu_custom_call" | custom-call | flops 8589934592 | bytes 67108864 | tf_op jit(solution)/shard_map/first_forward/pallas_call | solution.py:174
  38.9 4.1 %all-to-all-start = ((bf16[8,144,256]{2,1,0:T(8,128)(2,1)}), bf16[8,144,256]{2,1,0:T(8,128)(2,1)S(1)}, u32[]{:S(2)}, u32[]{:S(2)}) async-start(bf16[8,144,256]{2,1,0:T(8,128)(2,1)} %get-tuple-element.52), calls=%async_computation | async-start | bytes 1179648 | tf_op jit(solution)/shard_map/all_to_all | solution.py:498
  43.0 10.4 %all-to-all-done = bf16[8,144,256]{2,1,0:T(8,128)(2,1)S(1)} async-done(((bf16[8,144,256]{2,1,0:T(8,128)(2,1)}), bf16[8,144,256]{2,1,0:T(8,128)(2,1)S(1)}, u32[]{:S(2)}, u32[]{:S(2)}) %all-to-all-start) | async-done | bytes 589856 | tf_op jit(solution)/shard_map/all_to_all | solution.py:498
  54.3 10.0 %all_gather.3.rows = bf16[128,2048]{1,0:T(8,128)(2,1)S(1)} all-gather(bf16[128,256]{1,0:T(8,128)(2,1)S(1)} %pad_maximum_fusion.1), channel_id=1, replica_groups=mesh['sample'=4,'marker'=8] {'marker'}, dimensions={1}, use_global_device_ids=true | all-gather | bytes 589824 | tf_op jit(solution)/shard_map/all_gather | solution.py:503
  64.3 10.1 %first_back_0.1 = (f32[16,6144]{1,0:T(8,128)S(1)}, bf16[112,6144]{1,0:T(8,128)(2,1)S(1)}) custom-call(s32[4]{0:T(128)S(1)} %iota_xor_fusion.off, bf16[128,2048]{1,0:T(8,128)(2,1)S(1)} %all_gather.3.rows, bf16[2048,16384]{1,0:T(8,128)(2,1)} %refs_7_.1), custom_call_target="tpu_custom_call" | custom-call | flops 3221225472 | bytes 25165824 | tf_op jit(solution)/shard_map/first_back_0/pallas_call | solution.py:379
  74.4 3.6 %collective-permute-start.4 = (bf16[112,6144]{1,0:T(8,128)(2,1)S(1)}, bf16[112,6144]{1,0:T(8,128)(2,1)S(1)}, u32[]{:S(2)}, u32[]{:S(2)}) collective-permute-start(bf16[112,6144]{1,0:T(8,128)(2,1)S(1)} %get-tuple-element.61), channel_id=1, source_target_pairs={{0,8},{24,16},{1,9},{25,17},{2,10},{26,18},{3,11},{27,19},{4,12},{... | collective-permute-start | bytes 4128776 | tf_op jit(solution)/shard_map/ppermute | solution.py:521
  78.0 15.1 %first_back_1.1 = (f32[16,4096]{1,0:T(8,128)S(1)}, f32[16,4096]{1,0:T(8,128)S(1)}, f32[16,4096]{1,0:T(8,128)S(1)}, f32[16,4096]{1,0:T(8,128)S(1)}, bf16[112,6144...) custom-call(s32[4]{0:T(128)S(1)} %iota_xor_fusion.off, bf16[128,2048]{1,0:T(8,128)(2,1)S(1)} %all_gather.3.rows, ...), custom_call_target="tpu_custom_call" | custom-call | flops 5368709120 | bytes 41943040 | tf_op jit(solution)/shard_map/first_back_1/pallas_call | solution.py:379
  93.1 14.7 %collective-permute-done.4 = bf16[112,6144]{1,0:T(8,128)(2,1)S(1)} collective-permute-done((bf16[112,6144]{1,0:T(8,128)(2,1)S(1)}, bf16[112,6144]{1,0:T(8,128)(2,1)S(1)}, u32[]{:S(2)}, u32[]{:S(2)}) %collective-permute-start.4) | collective-permute-done | bytes 1376288 | tf_op jit(solution)/shard_map/ppermute | solution.py:521
  107.8 2.5 collective-permute-start.5
  111.3 1.5 collective-permute-start.7
  112.8 8.2 %collective-permute-done.5 = f32[16,4096]{1,0:T(8,128)S(1)} collective-permute-done((f32[16,4096]{1,0:T(8,128)S(1)}, f32[16,4096]{1,0:T(8,128)S(1)}, u32[]{:S(2)}, u32[]{:S(2)}) %collective-permute-start.5) | collective-permute-done | bytes 262176 | tf_op jit(solution)/shard_map/ppermute | solution.py:26
  121.0 10.7 %collective-permute-done.6 = f32[16,4096]{1,0:T(8,128)S(1)} collective-permute-done((f32[16,4096]{1,0:T(8,128)S(1)}, f32[16,4096]{1,0:T(8,128)S(1)}, u32[]{:S(2)}, u32[]{:S(2)}) %collective-permute-start.6) | collective-permute-done | bytes 262176 | tf_op jit(solution)/shard_map/ppermute | solution.py:26
  132.5 2.5 collective-permute-start.10
  135.0 4.8 %collective-permute-start.9 = (bf16[16,4096]{1,0:T(8,128)(2,1)S(1)}, bf16[16,4096]{1,0:T(8,128)(2,1)S(1)}, u32[]{:S(2)}, u32[]{:S(2)}) collective-permute-start(bf16[16,4096]{1,0:T(8,128)(2,1)S(1)} %reduce-precision_convert_fusion.refs_0_), channel_id=1, source_target_pairs={{0,16},{8,24},{16,0},{24,8},{1,17},{9,25},{17,1},{25,9},{2,18},{10... | collective-permute-start | bytes 393224 | tf_op jit(solution)/shard_map/ppermute | solution.py:26
  140.4 7.4 %collective-permute-done.9.refs_2_ = bf16[16,4096]{1,0:T(8,128)(2,1)S(1)} collective-permute-done((bf16[16,4096]{1,0:T(8,128)(2,1)S(1)}, bf16[16,4096]{1,0:T(8,128)(2,1)S(1)}, u32[]{:S(2)}, u32[]{:S(2)}) %collective-permute-start.9) | collective-permute-done | bytes 131104 | tf_op jit(solution)/shard_map/ppermute | solution.py:26
  147.8 1.7 collective-permute-start.11
  149.5 3.3 collective-permute-start.12
  153.0 22.3 %second_forward.1 = f32[16,2048]{1,0:T(8,128)S(1)} custom-call(s32[8]{0:T(128)S(1)} %reshape.26.off, bf16[16,4096]{1,0:T(8,128)(2,1)S(1)} %reduce-precision_convert_fusion.refs_0_, bf16[16,4096]{1,0:T(8,128)(2,1)S(1)} %collective-permute-done.8.refs_1_, bf16[16,4096]{1,0:T(8,128)(2,1)S(1)} %collective-permute-done.9.refs_2_, ...), custom_call_target="tpu_custom_call" | custom-call | flops 1073741824 | bytes 67108864 | tf_op jit(solution)/shard_map/second_forward/pallas_call | solution.py:222
  175.4 4.8 %collective-permute-done.12 = bf16[112,6144]{1,0:T(8,128)(2,1)} collective-permute-done((bf16[112,6144]{1,0:T(8,128)(2,1)S(1)}, bf16[112,6144]{1,0:T(8,128)(2,1)}, u32[]{:S(2)}, u32[]{:S(2)}) %collective-permute-start.12) | collective-permute-done | bytes 1376288 | tf_op jit(solution)/shard_map/ppermute | solution.py:521
  180.2 2.1 add_convert_fusion.2.refs_4_
  182.3 1.5 collective-permute-start.16
  183.8 1.5 collective-permute-start.15
  185.9 1.8 add_convert_fusion.1
  187.7 2.0 collective-permute-done.16
  189.6 2.4 collective-permute-done.15
  194.8 7.6 %collective-permute-start.25 = (bf16[112,4096]{1,0:T(8,128)(2,1)S(1)}, bf16[112,4096]{1,0:T(8,128)(2,1)S(1)}, u32[]{:S(2)}, u32[]{:S(2)}) collective-permute-start(bf16[112,4096]{1,0:T(8,128)(2,1)S(1)} %copy-done.6), channel_id=1, source_target_pairs={{0,8},{24,16},{1,9},{25,17},{2,10},{26,18},{3,11},{27,19},{4,12},{... | collective-permute-start | bytes 2752520 | tf_op jit(solution)/shard_map/ppermute | solution.py:521
  202.4 21.8 %second_back.1 = (f32[16,4096]{1,0:T(8,128)S(1)}, bf16[16,4096]{1,0:T(8,128)(2,1)S(1)}, bf16[16,4096]{1,0:T(8,128)(2,1)S(1)}, bf16[16,4096]{1,0:T(8,128)(2,1)S(1)}) custom-call(s32[8]{0:T(128)S(1)} %reshape.26.off, bf16[16,2048]{1,0:T(8,128)(2,1)S(1)} %get-tuple-element.80.rows, bf16[2048,16384]{1,0:T(8,128)(2,1)} %refs_7_.1), custom_call_target="tpu_custom_call" | custom-call | flops 1073741824 | bytes 67108864 | tf_op jit(solution)/shard_map/second_back/pallas_call | solution.py:407
  224.2 2.7 collective-permute-done.17.refs_6_
  226.9 3.2 collective-permute-start.19
  233.6 6.4 %collective-permute-done.19 = bf16[16,4096]{1,0:T(8,128)(2,1)S(1)} collective-permute-done((bf16[16,4096]{1,0:T(8,128)(2,1)S(1)}, bf16[16,4096]{1,0:T(8,128)(2,1)S(1)}, u32[]{:S(2)}, u32[]{:S(2)}) %collective-permute-start.19) | collective-permute-done | bytes 131104 | tf_op jit(solution)/shard_map/ppermute | solution.py:26
  240.7 2.4 collective-permute-start.23
  243.1 3.8 %collective-permute-start.22 = (bf16[16,4096]{1,0:T(8,128)(2,1)S(1)}, bf16[16,4096]{1,0:T(8,128)(2,1)S(1)}, u32[]{:S(2)}, u32[]{:S(2)}) collective-permute-start(bf16[16,4096]{1,0:T(8,128)(2,1)S(1)} %get-tuple-element.110.refs_0_.refs_4_), channel_id=1, source_target_pairs={{0,16},{8,24},{16,0},{24,8},{1,17},{9,25},{17,1},{25,9},{2,18},{10... | collective-permute-start | bytes 393224 | tf_op jit(solution)/shard_map/ppermute | solution.py:26
  248.9 23.5 %collective-permute-done.22.refs_2_.refs_6_ = bf16[16,4096]{1,0:T(8,128)(2,1)S(1)} collective-permute-done((bf16[16,4096]{1,0:T(8,128)(2,1)S(1)}, bf16[16,4096]{1,0:T(8,128)(2,1)S(1)}, u32[]{:S(2)}, u32[]{:S(2)}) %collective-permute-start.22) | collective-permute-done | bytes 131104 | tf_op jit(solution)/shard_map/ppermute | solution.py:26
  274.9 10.9 %collective-permute-done.28.refs_7_ = bf16[112,6144]{1,0:T(8,128)(2,1)} collective-permute-done((bf16[112,6144]{1,0:T(8,128)(2,1)S(1)}, bf16[112,6144]{1,0:T(8,128)(2,1)}, u32[]{:S(2)}, u32[]{:S(2)}) %collective-permute-start.28) | collective-permute-done | bytes 1376288 | tf_op jit(solution)/shard_map/ppermute | solution.py:527
  287.1 19.9 %third_forward_0.1.refs_6_ = f32[2048,128]{1,0:T(8,128)S(1)} custom-call(s32[5]{0:T(128)S(1)} %pad_add_fusion.1.off, bf16[16,4096]{1,0:T(8,128)(2,1)S(1)} %get-tuple-element.110.refs_0_.refs_4_, bf16[16,4096]{1,0:T(8,128)(2,1)S(1)} %collective-permute-done.21.refs_1_.refs_5_, bf16[16,4096]{1,0:T(8,128)(2,1)S(1)} %collective-permute-done.22.refs_2_.refs_6_, ...), custom_call_target="tpu_custom_call" | custom-call | flops 6442450944 | bytes 50331648 | tf_op jit(solution)/shard_map/third_forward_0/pallas_call | solution.py:297
  307.1 10.3 %third_forward_1.1 = bf16[8,128,256]{2,1,0:T(8,128)(2,1)} custom-call(s32[5]{0:T(128)S(1)} %pad_add_fusion.1.off, bf16[16,4096]{1,0:T(8,128)(2,1)S(1)} %get-tuple-element.110.refs_0_.refs_4_, bf16[16,4096]{1,0:T(8,128)(2,1)S(1)} %collective-permute-done.21.refs_1_.refs_5_, bf16[16,4096]{1,0:T(8,128)(2,1)S(1)} %collective-permute-done.22.refs_2_.refs_6_, ...), custom_call_target="tpu_custom_call" | custom-call | flops 2147483648 | bytes 16777216 | tf_op jit(solution)/shard_map/third_forward_1/pallas_call | solution.py:297
  317.3 3.5 all-to-all-start.1
  321.1 1.8 collective-permute-start.31
  322.8 2.7 collective-permute-start.29
  325.5 1.7 multiply_reduce_fusion
  329.4 5.0 %collective-permute-done.30.refs_10_ = bf16[16,4096]{1,0:T(8,128)(2,1)S(1)} collective-permute-done((bf16[16,4096]{1,0:T(8,128)(2,1)S(1)}, bf16[16,4096]{1,0:T(8,128)(2,1)S(1)}, u32[]{:S(2)}, u32[]{:S(2)}) %collective-permute-start.30) | collective-permute-done | bytes 131104 | tf_op jit(solution)/shard_map/ppermute | solution.py:26
  336.1 2.6 collective-permute-start.35
  340.6 1.7 collective-permute-done.34
  342.8 1.8 collective-permute-start.38
  344.6 2.6 collective-permute-start.36
  349.1 3.2 finish.1
  (137 shorter events, 31.3 us)
Async XLA Ops:
  3.4 1.3 collective-permute-start
  4.7 7.9 %collective-permute-start.3 = (f32[16,1]{1,0:T(8,128)S(1)}, f32[16,1]{1,0:T(8,128)S(1)}, u32[]{:S(2)}, u32[]{:S(2)}) collective-permute-start(f32[16,1]{1,0:T(8,128)S(1)} %add.102), channel_id=1, source_target_pairs={{0,6},{1,7},{2,4},{3,5},{4,2},{5,3},{6,0},{7,1},{8,14},{9,15},{10,... | collective-permute-start | bytes 200 | tf_op jit(solution)/shard_map/ppermute | solution.py:26
  8.5 4.1 %collective-permute-start.2 = (f32[16,1]{1,0:T(8,128)S(1)}, f32[16,1]{1,0:T(8,128)S(1)}, u32[]{:S(2)}, u32[]{:S(2)}) collective-permute-start(f32[16,1]{1,0:T(8,128)S(1)} %add.102), channel_id=1, source_target_pairs={{0,4},{1,5},{2,6},{3,7},{4,0},{5,1},{6,2},{7,3},{8,12},{9,13},{10,... | collective-permute-start | bytes 200 | tf_op jit(solution)/shard_map/ppermute | solution.py:26
  9.0 3.7 %collective-permute-start.1 = (f32[16,1]{1,0:T(8,128)S(1)}, f32[16,1]{1,0:T(8,128)S(1)}, u32[]{:S(2)}, u32[]{:S(2)}) collective-permute-start(f32[16,1]{1,0:T(8,128)S(1)} %add.102), channel_id=1, source_target_pairs={{0,2},{1,3},{2,0},{3,1},{4,6},{5,7},{6,4},{7,5},{8,10},{9,11},{10,... | collective-permute-start | bytes 200 | tf_op jit(solution)/shard_map/ppermute | solution.py:26
  38.9 14.6 %all-to-all-start = ((bf16[8,144,256]{2,1,0:T(8,128)(2,1)}), bf16[8,144,256]{2,1,0:T(8,128)(2,1)S(1)}, u32[]{:S(2)}, u32[]{:S(2)}) async-start(bf16[8,144,256]{2,1,0:T(8,128)(2,1)} %get-tuple-element.52), calls=%async_computation | async-start | bytes 1179648 | tf_op jit(solution)/shard_map/all_to_all | solution.py:498
  74.4 38.4 %copy-start.22 = (f32[16]{0:T(128)S(1)}, f32[16]{0:T(128)}, u32[]{:S(2)}) copy-start(f32[16]{0:T(128)} %param.15) | copy-start | bytes 196
  74.4 33.4 %collective-permute-start.4 = (bf16[112,6144]{1,0:T(8,128)(2,1)S(1)}, bf16[112,6144]{1,0:T(8,128)(2,1)S(1)}, u32[]{:S(2)}, u32[]{:S(2)}) collective-permute-start(bf16[112,6144]{1,0:T(8,128)(2,1)S(1)} %get-tuple-element.61), channel_id=1, source_target_pairs={{0,8},{24,16},{1,9},{25,17},{2,10},{26,18},{3,11},{27,19},{4,12},{... | collective-permute-start | bytes 4128776 | tf_op jit(solution)/shard_map/ppermute | solution.py:521
  93.1 47.2 %copy-start.5 = (bf16[112,4096]{1,0:T(8,128)(2,1)}, bf16[112,4096]{1,0:T(8,128)(2,1)S(1)}, u32[]{:S(2)}) copy-start(bf16[112,4096]{1,0:T(8,128)(2,1)S(1)} %get-tuple-element.90) | copy-start | bytes 2752516
  107.8 13.2 %collective-permute-start.5 = (f32[16,4096]{1,0:T(8,128)S(1)}, f32[16,4096]{1,0:T(8,128)S(1)}, u32[]{:S(2)}, u32[]{:S(2)}) collective-permute-start(f32[16,4096]{1,0:T(8,128)S(1)} %get-tuple-element.63), channel_id=1, source_target_pairs={{0,8},{8,0},{16,24},{24,16},{1,9},{9,1},{17,25},{25,17},{2,10},{10... | collective-permute-start | bytes 786440 | tf_op jit(solution)/shard_map/ppermute | solution.py:26
  110.3 21.4 %collective-permute-start.6 = (f32[16,4096]{1,0:T(8,128)S(1)}, f32[16,4096]{1,0:T(8,128)S(1)}, u32[]{:S(2)}, u32[]{:S(2)}) collective-permute-start(f32[16,4096]{1,0:T(8,128)S(1)} %get-tuple-element.64), channel_id=1, source_target_pairs={{0,16},{8,24},{16,0},{24,8},{1,17},{9,25},{17,1},{25,9},{2,18},{10... | collective-permute-start | bytes 786440 | tf_op jit(solution)/shard_map/ppermute | solution.py:26
  111.3 20.4 %collective-permute-start.7 = (f32[16,4096]{1,0:T(8,128)S(1)}, f32[16,4096]{1,0:T(8,128)S(1)}, u32[]{:S(2)}, u32[]{:S(2)}) collective-permute-start(f32[16,4096]{1,0:T(8,128)S(1)} %get-tuple-element.65), channel_id=1, source_target_pairs={{0,24},{8,16},{16,8},{24,0},{1,25},{9,17},{17,9},{25,1},{2,26},{10... | collective-permute-start | bytes 786440 | tf_op jit(solution)/shard_map/ppermute | solution.py:26
  132.5 7.9 %collective-permute-start.10 = (bf16[16,4096]{1,0:T(8,128)(2,1)S(1)}, bf16[16,4096]{1,0:T(8,128)(2,1)S(1)}, u32[]{:S(2)}, u32[]{:S(2)}) collective-permute-start(bf16[16,4096]{1,0:T(8,128)(2,1)S(1)} %reduce-precision_convert_fusion.refs_0_), channel_id=1, source_target_pairs={{0,24},{8,16},{16,8},{24,0},{1,25},{9,17},{17,9},{25,1},{2,26},{10... | collective-permute-start | bytes 393224 | tf_op jit(solution)/shard_map/ppermute | solution.py:26
  135.0 12.7 %collective-permute-start.9 = (bf16[16,4096]{1,0:T(8,128)(2,1)S(1)}, bf16[16,4096]{1,0:T(8,128)(2,1)S(1)}, u32[]{:S(2)}, u32[]{:S(2)}) collective-permute-start(bf16[16,4096]{1,0:T(8,128)(2,1)S(1)} %reduce-precision_convert_fusion.refs_0_), channel_id=1, source_target_pairs={{0,16},{8,24},{16,0},{24,8},{1,17},{9,25},{17,1},{25,9},{2,18},{10... | collective-permute-start | bytes 393224 | tf_op jit(solution)/shard_map/ppermute | solution.py:26
  139.9 7.9 %collective-permute-start.8 = (bf16[16,4096]{1,0:T(8,128)(2,1)S(1)}, bf16[16,4096]{1,0:T(8,128)(2,1)S(1)}, u32[]{:S(2)}, u32[]{:S(2)}) collective-permute-start(bf16[16,4096]{1,0:T(8,128)(2,1)S(1)} %reduce-precision_convert_fusion.refs_0_), channel_id=1, source_target_pairs={{0,8},{8,0},{16,24},{24,16},{1,9},{9,1},{17,25},{25,17},{2,10},{10... | collective-permute-start | bytes 393224 | tf_op jit(solution)/shard_map/ppermute | solution.py:26
  140.3 35.0 %copy-start.12 = (bf16[112,6144]{1,0:T(8,128)(2,1)}, bf16[112,6144]{1,0:T(8,128)(2,1)S(1)}, u32[]{:S(2)}) copy-start(bf16[112,6144]{1,0:T(8,128)(2,1)S(1)} %add_convert_fusion.3) | copy-start | bytes 4128772
  147.8 27.6 %copy-start.9 = (bf16[16,4096]{1,0:T(8,128)(2,1)}, bf16[16,4096]{1,0:T(8,128)(2,1)S(1)}, u32[]{:S(2)}) copy-start(bf16[16,4096]{1,0:T(8,128)(2,1)S(1)} %collective-permute-done.8.refs_1_) | copy-start | bytes 393220
  147.8 27.6 %collective-permute-start.11 = (bf16[112,6144]{1,0:T(8,128)(2,1)S(1)}, bf16[112,6144]{1,0:T(8,128)(2,1)}, u32[]{:S(2)}, u32[]{:S(2)}) collective-permute-start(bf16[112,6144]{1,0:T(8,128)(2,1)S(1)} %add_convert_fusion.3), channel_id=1, source_target_pairs={{8,16},{16,8},{9,17},{17,9},{10,18},{18,10},{11,19},{19,11},{12,20... | collective-permute-start | bytes 4128776 | tf_op jit(solution)/shard_map/ppermute | solution.py:524
  149.5 30.7 %collective-permute-start.12 = (bf16[112,6144]{1,0:T(8,128)(2,1)S(1)}, bf16[112,6144]{1,0:T(8,128)(2,1)}, u32[]{:S(2)}, u32[]{:S(2)}) collective-permute-start(bf16[112,6144]{1,0:T(8,128)(2,1)S(1)} %get-tuple-element.73), channel_id=1, source_target_pairs={{0,8},{24,16},{1,9},{25,17},{2,10},{26,18},{3,11},{27,19},{4,12},{... | collective-permute-start | bytes 4128776 | tf_op jit(solution)/shard_map/ppermute | solution.py:521
  180.2 2.1 collective-permute-start.13
  182.3 7.3 %collective-permute-start.16 = (f32[16,2048]{1,0:T(8,128)S(1)}, f32[16,2048]{1,0:T(8,128)S(1)}, u32[]{:S(2)}, u32[]{:S(2)}) collective-permute-start(f32[16,2048]{1,0:T(8,128)S(1)} %add.112), channel_id=1, source_target_pairs={{0,6},{1,7},{2,4},{3,5},{4,2},{5,3},{6,0},{7,1},{8,14},{9,15},{10,... | collective-permute-start | bytes 393224 | tf_op jit(solution)/shard_map/ppermute | solution.py:26
  183.8 8.2 %collective-permute-start.15 = (f32[16,2048]{1,0:T(8,128)S(1)}, f32[16,2048]{1,0:T(8,128)S(1)}, u32[]{:S(2)}, u32[]{:S(2)}) collective-permute-start(f32[16,2048]{1,0:T(8,128)S(1)} %add.112), channel_id=1, source_target_pairs={{0,4},{1,5},{2,6},{3,7},{4,0},{5,1},{6,2},{7,3},{8,12},{9,13},{10,... | collective-permute-start | bytes 393224 | tf_op jit(solution)/shard_map/ppermute | solution.py:26
  185.3 6.7 %collective-permute-start.14 = (f32[16,2048]{1,0:T(8,128)S(1)}, f32[16,2048]{1,0:T(8,128)S(1)}, u32[]{:S(2)}, u32[]{:S(2)}) collective-permute-start(f32[16,2048]{1,0:T(8,128)S(1)} %add.112), channel_id=1, source_target_pairs={{0,2},{1,3},{2,0},{3,1},{4,6},{5,7},{6,4},{7,5},{8,10},{9,11},{10,... | collective-permute-start | bytes 393224 | tf_op jit(solution)/shard_map/ppermute | solution.py:26
  192.7 34.2 %collective-permute-start.17 = (bf16[112,6144]{1,0:T(8,128)(2,1)S(1)}, bf16[112,6144]{1,0:T(8,128)(2,1)S(1)}, u32[]{:S(2)}, u32[]{:S(2)}) collective-permute-start(bf16[112,6144]{1,0:T(8,128)(2,1)S(1)} %add_convert_fusion.2.refs_4_), channel_id=1, source_target_pairs={{8,0},{16,24},{9,1},{17,25},{10,2},{18,26},{11,3},{19,27},{12,4},{... | collective-permute-start | bytes 4128776 | tf_op jit(solution)/shard_map/ppermute | solution.py:527
  194.0 37.3 %collective-permute-start.24 = (bf16[112,6144]{1,0:T(8,128)(2,1)S(1)}, bf16[112,6144]{1,0:T(8,128)(2,1)S(1)}, u32[]{:S(2)}, u32[]{:S(2)}) collective-permute-start(bf16[112,6144]{1,0:T(8,128)(2,1)S(1)} %add_convert_fusion.1), channel_id=1, source_target_pairs={{8,16},{16,8},{9,17},{17,9},{10,18},{18,10},{11,19},{19,11},{12,20... | collective-permute-start | bytes 4128776 | tf_op jit(solution)/shard_map/ppermute | solution.py:524
  194.8 36.5 %collective-permute-start.25 = (bf16[112,4096]{1,0:T(8,128)(2,1)S(1)}, bf16[112,4096]{1,0:T(8,128)(2,1)S(1)}, u32[]{:S(2)}, u32[]{:S(2)}) collective-permute-start(bf16[112,4096]{1,0:T(8,128)(2,1)S(1)} %copy-done.6), channel_id=1, source_target_pairs={{0,8},{24,16},{1,9},{25,17},{2,10},{26,18},{3,11},{27,19},{4,12},{... | collective-permute-start | bytes 2752520 | tf_op jit(solution)/shard_map/ppermute | solution.py:521
  226.9 6.7 %collective-permute-start.18 = (bf16[16,4096]{1,0:T(8,128)(2,1)S(1)}, bf16[16,4096]{1,0:T(8,128)(2,1)S(1)}, u32[]{:S(2)}, u32[]{:S(2)}) collective-permute-start(bf16[16,4096]{1,0:T(8,128)(2,1)S(1)} %get-tuple-element.87), channel_id=1, source_target_pairs={{0,8},{8,0},{16,24},{24,16},{1,9},{9,1},{17,25},{25,17},{2,10},{10... | collective-permute-start | bytes 393224 | tf_op jit(solution)/shard_map/ppermute | solution.py:26
  226.9 13.1 %collective-permute-start.19 = (bf16[16,4096]{1,0:T(8,128)(2,1)S(1)}, bf16[16,4096]{1,0:T(8,128)(2,1)S(1)}, u32[]{:S(2)}, u32[]{:S(2)}) collective-permute-start(bf16[16,4096]{1,0:T(8,128)(2,1)S(1)} %get-tuple-element.88), channel_id=1, source_target_pairs={{0,16},{8,24},{16,0},{24,8},{1,17},{9,25},{17,1},{25,9},{2,18},{10... | collective-permute-start | bytes 393224 | tf_op jit(solution)/shard_map/ppermute | solution.py:26
  230.1 9.9 %collective-permute-start.20 = (bf16[16,4096]{1,0:T(8,128)(2,1)S(1)}, bf16[16,4096]{1,0:T(8,128)(2,1)S(1)}, u32[]{:S(2)}, u32[]{:S(2)}) collective-permute-start(bf16[16,4096]{1,0:T(8,128)(2,1)S(1)} %get-tuple-element.89), channel_id=1, source_target_pairs={{0,24},{8,16},{16,8},{24,0},{1,25},{9,17},{17,9},{25,1},{2,26},{10... | collective-permute-start | bytes 393224 | tf_op jit(solution)/shard_map/ppermute | solution.py:26
  231.6 40.8 %collective-permute-start.26 = (bf16[112,4096]{1,0:T(8,128)(2,1)S(1)}, bf16[112,4096]{1,0:T(8,128)(2,1)S(1)}, u32[]{:S(2)}, u32[]{:S(2)}) collective-permute-start(bf16[112,4096]{1,0:T(8,128)(2,1)S(1)} %add_convert_fusion.5), channel_id=1, source_target_pairs={{8,16},{16,8},{9,17},{17,9},{10,18},{18,10},{11,19},{19,11},{12,20... | collective-permute-start | bytes 2752520 | tf_op jit(solution)/shard_map/ppermute | solution.py:524
  240.7 8.2 %collective-permute-start.23 = (bf16[16,4096]{1,0:T(8,128)(2,1)S(1)}, bf16[16,4096]{1,0:T(8,128)(2,1)S(1)}, u32[]{:S(2)}, u32[]{:S(2)}) collective-permute-start(bf16[16,4096]{1,0:T(8,128)(2,1)S(1)} %get-tuple-element.110.refs_0_.refs_4_), channel_id=1, source_target_pairs={{0,24},{8,16},{16,8},{24,0},{1,25},{9,17},{17,9},{25,1},{2,26},{10... | collective-permute-start | bytes 393224 | tf_op jit(solution)/shard_map/ppermute | solution.py:26
  243.1 29.3 %collective-permute-start.22 = (bf16[16,4096]{1,0:T(8,128)(2,1)S(1)}, bf16[16,4096]{1,0:T(8,128)(2,1)S(1)}, u32[]{:S(2)}, u32[]{:S(2)}) collective-permute-start(bf16[16,4096]{1,0:T(8,128)(2,1)S(1)} %get-tuple-element.110.refs_0_.refs_4_), channel_id=1, source_target_pairs={{0,16},{8,24},{16,0},{24,8},{1,17},{9,25},{17,1},{25,9},{2,18},{10... | collective-permute-start | bytes 393224 | tf_op jit(solution)/shard_map/ppermute | solution.py:26
  246.9 25.5 %collective-permute-start.21 = (bf16[16,4096]{1,0:T(8,128)(2,1)S(1)}, bf16[16,4096]{1,0:T(8,128)(2,1)S(1)}, u32[]{:S(2)}, u32[]{:S(2)}) collective-permute-start(bf16[16,4096]{1,0:T(8,128)(2,1)S(1)} %get-tuple-element.110.refs_0_.refs_4_), channel_id=1, source_target_pairs={{0,8},{8,0},{16,24},{24,16},{1,9},{9,1},{17,25},{25,17},{2,10},{10... | collective-permute-start | bytes 393224 | tf_op jit(solution)/shard_map/ppermute | solution.py:26
  247.3 38.5 %collective-permute-start.28 = (bf16[112,6144]{1,0:T(8,128)(2,1)S(1)}, bf16[112,6144]{1,0:T(8,128)(2,1)}, u32[]{:S(2)}, u32[]{:S(2)}) collective-permute-start(bf16[112,6144]{1,0:T(8,128)(2,1)S(1)} %add_convert_fusion.refs_5_), channel_id=1, source_target_pairs={{8,0},{16,24},{9,1},{17,25},{10,2},{18,26},{11,3},{19,27},{12,4},{... | collective-permute-start | bytes 4128776 | tf_op jit(solution)/shard_map/ppermute | solution.py:527
  273.5 33.5 %collective-permute-start.27 = (bf16[112,4096]{1,0:T(8,128)(2,1)}, bf16[112,4096]{1,0:T(8,128)(2,1)}, u32[]{:S(2)}, u32[]{:S(2)}) collective-permute-start(bf16[112,4096]{1,0:T(8,128)(2,1)} %add_convert_fusion.4.refs_4_), channel_id=1, source_target_pairs={{8,0},{16,24},{9,1},{17,25},{10,2},{18,26},{11,3},{19,27},{12,4},{... | collective-permute-start | bytes 2752520 | tf_op jit(solution)/shard_map/ppermute | solution.py:527
  317.3 17.0 %all-to-all-start.1 = ((bf16[8,128,256]{2,1,0:T(8,128)(2,1)}), bf16[8,128,256]{2,1,0:T(8,128)(2,1)S(1)}, u32[]{:S(2)}, u32[]{:S(2)}) async-start(bf16[8,128,256]{2,1,0:T(8,128)(2,1)} %third_forward_1.1), calls=%async_computation.1 | async-start | bytes 1048576 | tf_op jit(solution)/shard_map/all_to_all | solution.py:571
  321.0 28.1 %copy-start.4 = (f32[16,16384]{1,0:T(8,128)S(1)}, f32[16,16384]{1,0:T(8,128)}, u32[]{:S(2)}) copy-start(f32[16,16384]{1,0:T(8,128)} %copy-done.3) | copy-start | bytes 3145732
  321.0 28.1 %copy-start.8 = (bf16[16,4096]{1,0:T(8,128)(2,1)S(1)}, bf16[16,4096]{1,0:T(8,128)(2,1)}, u32[]{:S(2)}) copy-start(bf16[16,4096]{1,0:T(8,128)(2,1)} %copy-done.7) | copy-start | bytes 393220
  321.0 28.1 %copy-start.10 = (bf16[16,4096]{1,0:T(8,128)(2,1)S(1)}, bf16[16,4096]{1,0:T(8,128)(2,1)}, u32[]{:S(2)}) copy-start(bf16[16,4096]{1,0:T(8,128)(2,1)} %copy-done.9) | copy-start | bytes 393220
  321.1 8.3 %collective-permute-start.31 = (bf16[16,4096]{1,0:T(8,128)(2,1)S(1)}, bf16[16,4096]{1,0:T(8,128)(2,1)S(1)}, u32[]{:S(2)}, u32[]{:S(2)}) collective-permute-start(bf16[16,4096]{1,0:T(8,128)(2,1)S(1)} %copy-done.11), channel_id=1, source_target_pairs={{0,24},{8,16},{16,8},{24,0},{1,25},{9,17},{17,9},{25,1},{2,26},{10... | collective-permute-start | bytes 393224 | tf_op jit(solution)/shard_map/ppermute | solution.py:26
  322.8 11.6 %collective-permute-start.30 = (bf16[16,4096]{1,0:T(8,128)(2,1)S(1)}, bf16[16,4096]{1,0:T(8,128)(2,1)S(1)}, u32[]{:S(2)}, u32[]{:S(2)}) collective-permute-start(bf16[16,4096]{1,0:T(8,128)(2,1)S(1)} %copy-done.11), channel_id=1, source_target_pairs={{0,16},{8,24},{16,0},{24,8},{1,17},{9,25},{17,1},{25,9},{2,18},{10... | collective-permute-start | bytes 393224 | tf_op jit(solution)/shard_map/ppermute | solution.py:26
  322.8 11.6 %collective-permute-start.29 = (bf16[16,4096]{1,0:T(8,128)(2,1)S(1)}, bf16[16,4096]{1,0:T(8,128)(2,1)S(1)}, u32[]{:S(2)}, u32[]{:S(2)}) collective-permute-start(bf16[16,4096]{1,0:T(8,128)(2,1)S(1)} %copy-done.11), channel_id=1, source_target_pairs={{0,8},{8,0},{16,24},{24,16},{1,9},{9,1},{17,25},{25,17},{2,10},{10... | collective-permute-start | bytes 393224 | tf_op jit(solution)/shard_map/ppermute | solution.py:26
  334.9 1.2 collective-permute-start.32
  336.1 4.5 %collective-permute-start.35 = (f32[8,128]{1,0:T(8,128)S(1)}, f32[8,128]{1,0:T(8,128)S(1)}, u32[]{:S(2)}, u32[]{:S(2)}) collective-permute-start(f32[8,128]{1,0:T(8,128)S(1)} %add.125), channel_id=1, source_target_pairs={{0,6},{1,7},{2,4},{3,5},{4,2},{5,3},{6,0},{7,1},{8,14},{9,15},{10,... | collective-permute-start | bytes 12296 | tf_op jit(solution)/shard_map/ppermute | solution.py:26
  338.7 3.6 %collective-permute-start.34 = (f32[8,128]{1,0:T(8,128)S(1)}, f32[8,128]{1,0:T(8,128)S(1)}, u32[]{:S(2)}, u32[]{:S(2)}) collective-permute-start(f32[8,128]{1,0:T(8,128)S(1)} %add.125), channel_id=1, source_target_pairs={{0,4},{1,5},{2,6},{3,7},{4,0},{5,1},{6,2},{7,3},{8,12},{9,13},{10,... | collective-permute-start | bytes 12296 | tf_op jit(solution)/shard_map/ppermute | solution.py:26
  339.2 3.6 %collective-permute-start.33 = (f32[8,128]{1,0:T(8,128)S(1)}, f32[8,128]{1,0:T(8,128)S(1)}, u32[]{:S(2)}, u32[]{:S(2)}) collective-permute-start(f32[8,128]{1,0:T(8,128)S(1)} %add.125), channel_id=1, source_target_pairs={{0,2},{1,3},{2,0},{3,1},{4,6},{5,7},{6,4},{7,5},{8,10},{9,11},{10,... | collective-permute-start | bytes 12296 | tf_op jit(solution)/shard_map/ppermute | solution.py:26
  342.8 5.4 %collective-permute-start.38 = (f32[8,128]{1,0:T(8,128)S(1)}, f32[8,128]{1,0:T(8,128)S(1)}, u32[]{:S(2)}, u32[]{:S(2)}) collective-permute-start(f32[8,128]{1,0:T(8,128)S(1)} %add_add_fusion.3), channel_id=1, source_target_pairs={{0,24},{8,16},{16,8},{24,0},{1,25},{9,17},{17,9},{25,1},{2,26},{10... | collective-permute-start | bytes 12296 | tf_op jit(solution)/shard_map/ppermute | solution.py:26
  344.6 4.5 %collective-permute-start.37 = (f32[8,128]{1,0:T(8,128)S(1)}, f32[8,128]{1,0:T(8,128)S(1)}, u32[]{:S(2)}, u32[]{:S(2)}) collective-permute-start(f32[8,128]{1,0:T(8,128)S(1)} %add_add_fusion.3), channel_id=1, source_target_pairs={{0,16},{8,24},{16,0},{24,8},{1,17},{9,25},{17,1},{25,9},{2,18},{10... | collective-permute-start | bytes 12296 | tf_op jit(solution)/shard_map/ppermute | solution.py:26
  344.6 4.5 %collective-permute-start.36 = (f32[8,128]{1,0:T(8,128)S(1)}, f32[8,128]{1,0:T(8,128)S(1)}, u32[]{:S(2)}, u32[]{:S(2)}) collective-permute-start(f32[8,128]{1,0:T(8,128)S(1)} %add_add_fusion.3), channel_id=1, source_target_pairs={{0,8},{8,0},{16,24},{24,16},{1,9},{9,1},{17,25},{25,17},{2,10},{10... | collective-permute-start | bytes 12296 | tf_op jit(solution)/shard_map/ppermute | solution.py:26
  (16 other events, 187.1 us)

commit v11 on v9

--- a/solution.py
+++ b/solution.py
@@ -568,7 +568,8 @@
     value = wide_forward(
         back_pieces, full[2:], ends[2:], places, sum(sizes[:2]), total, genotypes, columns, "third_forward_1"
     )
-    (last,) = tie((lax.all_to_all(value, "marker", 0, 0),), *low_pieces)
+    (value,) = tie((value,), *low_pieces)
+    last = lax.all_to_all(value, "marker", 0, 0)
     last = jnp.sum(last.astype(F32), axis=0)
     before = jnp.concatenate([kept_s, kept_x[traits:]], axis=0)
 

time: 351 us -> 354 us (level)
    ppermute x30, waiting for transfers between devices: 65.8 us -> 58.2 us  [swap(): return lax.ppermute(x, axis, [(i, i ^ bits) for i in range(n)])]
    all_to_all x1, waiting for transfers between devices: 0.01 us -> 6.87 us  [per_device(): last = lax.all_to_all(value, 'marker', 0, 0)]
  transfers between devices with their start and end apart: 41 -> 41, of which waited for: 25 -> 23; matrix products, arithmetic and copies ran while one was open for 4% -> 4% of each run, Pallas kernels for 23% -> 26%
where the time goes in v11:
time: 354 us; the launch traced here: 353 us
  Pallas kernels  128 us (36%)
  waiting for transfers between devices  121 us (34%)
  starting transfers between devices  70.1 us (20%)
  other arithmetic  16 us (5%)
  blocking collectives  9.96 us (3%)
  local copies, waits for them, and re-layouts  7.9 us (2%)
    ppermute x30, waiting for transfers between devices, swap(): return lax.ppermute(x, axis, [(i, i ^ bits) for i in range(n)])  58.2 us
    ppermute x30, starting transfers between devices, swap(): return lax.ppermute(x, axis, [(i, i ^ bits) for i in range(n)])  44.4 us
    ppermute x3, waiting for transfers between devices, outward(): return lax.ppermute(x, 'sample', [(1, 0), (2, 3)])  38.8 us
    pallas_call x2, Pallas kernels, wide_forward(): pl.pallas_call(functools.partial(wide_body, n, begin, len(inner), acc is...  30 us
    pallas_call x2, Pallas kernels, first_back(): pl.pallas_call(functools.partial(first_back_body, unit, begin, t, arrays)...  25 us
    pallas_call x1, Pallas kernels, first_forward(): pl.pallas_call(functools.partial(first_body, markers * columns), grid_spe...  24.5 us
    pallas_call x1, Pallas kernels, narrow_forward(): pl.pallas_call(functools.partial(narrow_body, n, unit, acc is not None),...  22.3 us
    pallas_call x1, Pallas kernels, second_back(): pl.pallas_call(functools.partial(second_back_body, n, unit), grid_spec=pl...  21.8 us
  transfers between devices with their start and end apart: 41, of which 23 were waited for; matrix products, arithmetic and copies ran while one was open for 4% of the time, Pallas kernels for 26%

profile of v11, /device:TPU:0, one launch (start us, length us, event | category | flops | bytes accessed | tf_op | source)
XLA Modules:
  0.0 353.3 jit_solution(14788324984391911432)
XLA Ops:
  4.7 3.8 %collective-permute-start.3 = (f32[16,1]{1,0:T(8,128)S(1)}, f32[16,1]{1,0:T(8,128)S(1)}, u32[]{:S(2)}, u32[]{:S(2)}) collective-permute-start(f32[16,1]{1,0:T(8,128)S(1)} %add.102), channel_id=1, source_target_pairs={{0,6},{1,7},{2,4},{3,5},{4,2},{5,3},{6,0},{7,1},{8,14},{9,15},{10,... | collective-permute-start | bytes 200 | tf_op jit(solution)/shard_map/ppermute | solution.py:26
  9.1 3.5 convert_element_type.92.probes
  13.3 24.5 %first_forward.1 = (bf16[8,144,256]{2,1,0:T(8,128)(2,1)}, f32[16,16384]{1,0:T(8,128)S(1)}) custom-call(s32[1]{0:T(128)} %constant.9.clone.1.off, f32[16,16384]{1,0:T(8,128)S(1)} %copy-done, f32[16,3]{1,0:T(8,128)S(1)} %copy.27.cols, f32[16,1]{1,0:T(8,128)S(1)} %get-tuple-element.109.slopes, bf16[112,16384]{1,0:T(8,128)(2,1)S(1)} %convert_element_type.92.probes, ...), custom_call_target="tpu_custom_call" | custom-call | flops 8589934592 | bytes 67108864 | tf_op jit(solution)/shard_map/first_forward/pallas_call | solution.py:174
  38.8 4.1 %all-to-all-start = ((bf16[8,144,256]{2,1,0:T(8,128)(2,1)}), bf16[8,144,256]{2,1,0:T(8,128)(2,1)S(1)}, u32[]{:S(2)}, u32[]{:S(2)}) async-start(bf16[8,144,256]{2,1,0:T(8,128)(2,1)} %get-tuple-element.52), calls=%async_computation | async-start | bytes 1179648 | tf_op jit(solution)/shard_map/all_to_all | solution.py:498
  43.0 10.4 %all-to-all-done = bf16[8,144,256]{2,1,0:T(8,128)(2,1)S(1)} async-done(((bf16[8,144,256]{2,1,0:T(8,128)(2,1)}), bf16[8,144,256]{2,1,0:T(8,128)(2,1)S(1)}, u32[]{:S(2)}, u32[]{:S(2)}) %all-to-all-start) | async-done | bytes 589856 | tf_op jit(solution)/shard_map/all_to_all | solution.py:498
  54.3 10.0 %all_gather.3.rows = bf16[128,2048]{1,0:T(8,128)(2,1)S(1)} all-gather(bf16[128,256]{1,0:T(8,128)(2,1)S(1)} %pad_maximum_fusion.1), channel_id=1, replica_groups=mesh['sample'=4,'marker'=8] {'marker'}, dimensions={1}, use_global_device_ids=true | all-gather | bytes 589824 | tf_op jit(solution)/shard_map/all_gather | solution.py:503
  64.3 7.4 %first_back_0.1 = (f32[16,4096]{1,0:T(8,128)S(1)}, bf16[112,4096]{1,0:T(8,128)(2,1)S(1)}) custom-call(s32[4]{0:T(128)S(1)} %iota_xor_fusion.off, bf16[128,2048]{1,0:T(8,128)(2,1)S(1)} %all_gather.3.rows, bf16[2048,16384]{1,0:T(8,128)(2,1)} %refs_7_.1), custom_call_target="tpu_custom_call" | custom-call | flops 2147483648 | bytes 16777216 | tf_op jit(solution)/shard_map/first_back_0/pallas_call | solution.py:379
  71.7 3.5 %collective-permute-start.4 = (bf16[112,4096]{1,0:T(8,128)(2,1)S(1)}, bf16[112,4096]{1,0:T(8,128)(2,1)S(1)}, u32[]{:S(2)}, u32[]{:S(2)}) collective-permute-start(bf16[112,4096]{1,0:T(8,128)(2,1)S(1)} %get-tuple-element.61), channel_id=1, source_target_pairs={{0,8},{24,16},{1,9},{25,17},{2,10},{26,18},{3,11},{27,19},{4,12},{... | collective-permute-start | bytes 2752520 | tf_op jit(solution)/shard_map/ppermute | solution.py:521
  75.3 17.6 %first_back_1.1 = (f32[16,4096]{1,0:T(8,128)S(1)}, f32[16,4096]{1,0:T(8,128)S(1)}, f32[16,4096]{1,0:T(8,128)S(1)}, f32[16,4096]{1,0:T(8,128)S(1)}, bf16[112,6144...) custom-call(s32[4]{0:T(128)S(1)} %iota_xor_fusion.off, bf16[128,2048]{1,0:T(8,128)(2,1)S(1)} %all_gather.3.rows, ...), custom_call_target="tpu_custom_call" | custom-call | flops 6442450944 | bytes 50331648 | tf_op jit(solution)/shard_map/first_back_1/pallas_call | solution.py:379
  92.8 2.5 collective-permute-done.4
  95.3 2.5 collective-permute-start.5
  98.8 1.5 collective-permute-start.7
  100.3 8.2 %collective-permute-done.5 = f32[16,4096]{1,0:T(8,128)S(1)} collective-permute-done((f32[16,4096]{1,0:T(8,128)S(1)}, f32[16,4096]{1,0:T(8,128)S(1)}, u32[]{:S(2)}, u32[]{:S(2)}) %collective-permute-start.5) | collective-permute-done | bytes 262176 | tf_op jit(solution)/shard_map/ppermute | solution.py:26
  108.5 10.7 %collective-permute-done.6 = f32[16,4096]{1,0:T(8,128)S(1)} collective-permute-done((f32[16,4096]{1,0:T(8,128)S(1)}, f32[16,4096]{1,0:T(8,128)S(1)}, u32[]{:S(2)}, u32[]{:S(2)}) %collective-permute-start.6) | collective-permute-done | bytes 262176 | tf_op jit(solution)/shard_map/ppermute | solution.py:26
  120.0 2.5 collective-permute-start.10
  122.5 4.8 %collective-permute-start.9 = (bf16[16,4096]{1,0:T(8,128)(2,1)S(1)}, bf16[16,4096]{1,0:T(8,128)(2,1)S(1)}, u32[]{:S(2)}, u32[]{:S(2)}) collective-permute-start(bf16[16,4096]{1,0:T(8,128)(2,1)S(1)} %reduce-precision_convert_fusion.refs_0_), channel_id=1, source_target_pairs={{0,16},{8,24},{16,0},{24,8},{1,17},{9,25},{17,1},{25,9},{2,18},{10... | collective-permute-start | bytes 393224 | tf_op jit(solution)/shard_map/ppermute | solution.py:26
  128.6 6.6 %collective-permute-done.9.refs_2_ = bf16[16,4096]{1,0:T(8,128)(2,1)S(1)} collective-permute-done((bf16[16,4096]{1,0:T(8,128)(2,1)S(1)}, bf16[16,4096]{1,0:T(8,128)(2,1)S(1)}, u32[]{:S(2)}, u32[]{:S(2)}) %collective-permute-start.9) | collective-permute-done | bytes 131104 | tf_op jit(solution)/shard_map/ppermute | solution.py:26
  135.2 2.7 collective-permute-start.12
  137.9 1.6 collective-permute-start.11
  139.6 22.3 %second_forward.1 = f32[16,2048]{1,0:T(8,128)S(1)} custom-call(s32[8]{0:T(128)S(1)} %reshape.26.off, bf16[16,4096]{1,0:T(8,128)(2,1)S(1)} %reduce-precision_convert_fusion.refs_0_, bf16[16,4096]{1,0:T(8,128)(2,1)S(1)} %collective-permute-done.8.refs_1_, bf16[16,4096]{1,0:T(8,128)(2,1)S(1)} %collective-permute-done.9.refs_2_, ...), custom_call_target="tpu_custom_call" | custom-call | flops 1073741824 | bytes 67108864 | tf_op jit(solution)/shard_map/second_forward/pallas_call | solution.py:222
  162.0 3.7 %collective-permute-done.12 = bf16[112,6144]{1,0:T(8,128)(2,1)} collective-permute-done((bf16[112,6144]{1,0:T(8,128)(2,1)S(1)}, bf16[112,6144]{1,0:T(8,128)(2,1)}, u32[]{:S(2)}, u32[]{:S(2)}) %collective-permute-start.12) | collective-permute-done | bytes 1376288 | tf_op jit(solution)/shard_map/ppermute | solution.py:521
  165.7 1.8 add_convert_fusion.3
  167.6 1.5 collective-permute-start.16
  171.1 1.7 add_convert_fusion.4.refs_4_
  172.8 2.1 collective-permute-done.16
  174.9 2.4 collective-permute-done.15
  178.0 4.7 %collective-permute-start.25 = (bf16[112,6144]{1,0:T(8,128)(2,1)S(1)}, bf16[112,6144]{1,0:T(8,128)(2,1)S(1)}, u32[]{:S(2)}, u32[]{:S(2)}) collective-permute-start(bf16[112,6144]{1,0:T(8,128)(2,1)S(1)} %get-tuple-element.90), channel_id=1, source_target_pairs={{0,8},{24,16},{1,9},{25,17},{2,10},{26,18},{3,11},{27,19},{4,12},{... | collective-permute-start | bytes 4128776 | tf_op jit(solution)/shard_map/ppermute | solution.py:521
  183.4 1.5 collective-permute-start.17
  184.9 21.8 %second_back.1 = (f32[16,4096]{1,0:T(8,128)S(1)}, bf16[16,4096]{1,0:T(8,128)(2,1)S(1)}, bf16[16,4096]{1,0:T(8,128)(2,1)S(1)}, bf16[16,4096]{1,0:T(8,128)(2,1)S(1)}) custom-call(s32[8]{0:T(128)S(1)} %reshape.26.off, bf16[16,2048]{1,0:T(8,128)(2,1)S(1)} %get-tuple-element.80.rows, bf16[2048,16384]{1,0:T(8,128)(2,1)} %refs_7_.1), custom_call_target="tpu_custom_call" | custom-call | flops 1073741824 | bytes 67108864 | tf_op jit(solution)/shard_map/second_back/pallas_call | solution.py:407
  207.3 2.2 collective-permute-start.18
  212.0 3.9 %collective-permute-done.18 = bf16[16,4096]{1,0:T(8,128)(2,1)S(1)} collective-permute-done((bf16[16,4096]{1,0:T(8,128)(2,1)S(1)}, bf16[16,4096]{1,0:T(8,128)(2,1)S(1)}, u32[]{:S(2)}, u32[]{:S(2)}) %collective-permute-start.18) | collective-permute-done | bytes 131104 | tf_op jit(solution)/shard_map/ppermute | solution.py:26
  215.9 8.8 %collective-permute-done.19 = bf16[16,4096]{1,0:T(8,128)(2,1)S(1)} collective-permute-done((bf16[16,4096]{1,0:T(8,128)(2,1)S(1)}, bf16[16,4096]{1,0:T(8,128)(2,1)S(1)}, u32[]{:S(2)}, u32[]{:S(2)}) %collective-permute-start.19) | collective-permute-done | bytes 131104 | tf_op jit(solution)/shard_map/ppermute | solution.py:26
  225.5 2.5 collective-permute-start.23
  233.4 7.4 %collective-permute-done.22.refs_2_.refs_6_ = bf16[16,4096]{1,0:T(8,128)(2,1)S(1)} collective-permute-done((bf16[16,4096]{1,0:T(8,128)(2,1)S(1)}, bf16[16,4096]{1,0:T(8,128)(2,1)S(1)}, u32[]{:S(2)}, u32[]{:S(2)}) %collective-permute-start.22) | collective-permute-done | bytes 131104 | tf_op jit(solution)/shard_map/ppermute | solution.py:26
  242.5 24.9 %collective-permute-done.28.refs_7_ = bf16[112,6144]{1,0:T(8,128)(2,1)} collective-permute-done((bf16[112,6144]{1,0:T(8,128)(2,1)S(1)}, bf16[112,6144]{1,0:T(8,128)(2,1)}, u32[]{:S(2)}, u32[]{:S(2)}) %collective-permute-start.28) | collective-permute-done | bytes 1376288 | tf_op jit(solution)/shard_map/ppermute | solution.py:527
  269.8 17.3 %third_forward_0.1.refs_6_ = f32[2048,128]{1,0:T(8,128)S(1)} custom-call(s32[5]{0:T(128)S(1)} %pad_add_fusion.1.off, bf16[16,4096]{1,0:T(8,128)(2,1)S(1)} %get-tuple-element.110.refs_0_.refs_4_, bf16[16,4096]{1,0:T(8,128)(2,1)S(1)} %collective-permute-done.21.refs_1_.refs_5_, bf16[16,4096]{1,0:T(8,128)(2,1)S(1)} %collective-permute-done.22.refs_2_.refs_6_, ...), custom_call_target="tpu_custom_call" | custom-call | flops 5368709120 | bytes 41943040 | tf_op jit(solution)/shard_map/third_forward_0/pallas_call | solution.py:297
  287.1 2.3 collective-permute-start.31
  289.4 3.8 %collective-permute-start.30 = (bf16[16,4096]{1,0:T(8,128)(2,1)S(1)}, bf16[16,4096]{1,0:T(8,128)(2,1)S(1)}, u32[]{:S(2)}, u32[]{:S(2)}) collective-permute-start(bf16[16,4096]{1,0:T(8,128)(2,1)S(1)} %copy-done.11), channel_id=1, source_target_pairs={{0,16},{8,24},{16,0},{24,8},{1,17},{9,25},{17,1},{25,9},{2,18},{10... | collective-permute-start | bytes 393224 | tf_op jit(solution)/shard_map/ppermute | solution.py:26
  293.6 13.4 %collective-permute-done.27.refs_5_ = bf16[112,6144]{1,0:T(8,128)(2,1)} collective-permute-done((bf16[112,6144]{1,0:T(8,128)(2,1)S(1)}, bf16[112,6144]{1,0:T(8,128)(2,1)}, u32[]{:S(2)}, u32[]{:S(2)}) %collective-permute-start.27) | collective-permute-done | bytes 1376288 | tf_op jit(solution)/shard_map/ppermute | solution.py:527
  306.9 12.7 %third_forward_1.1 = bf16[8,128,256]{2,1,0:T(8,128)(2,1)} custom-call(s32[5]{0:T(128)S(1)} %pad_add_fusion.1.off, bf16[16,4096]{1,0:T(8,128)(2,1)S(1)} %get-tuple-element.110.refs_0_.refs_4_, bf16[16,4096]{1,0:T(8,128)(2,1)S(1)} %collective-permute-done.21.refs_1_.refs_5_, bf16[16,4096]{1,0:T(8,128)(2,1)S(1)} %collective-permute-done.22.refs_2_.refs_6_, ...), custom_call_target="tpu_custom_call" | custom-call | flops 3221225472 | bytes 25165824 | tf_op jit(solution)/shard_map/third_forward_1/pallas_call | solution.py:297
  321.7 3.5 all-to-all-start.1
  325.4 1.8 multiply_reduce_fusion
  328.0 6.9 %all-to-all-done.1 = bf16[8,128,256]{2,1,0:T(8,128)(2,1)S(1)} async-done(((bf16[8,128,256]{2,1,0:T(8,128)(2,1)}), bf16[8,128,256]{2,1,0:T(8,128)(2,1)S(1)}, u32[]{:S(2)}, u32[]{:S(2)}) %all-to-all-start.1) | async-done | bytes 524320 | tf_op jit(solution)/shard_map/all_to_all | solution.py:572
  337.1 1.5 collective-permute-start.34
  338.6 1.5 collective-permute-start.33
  342.2 3.4 collective-permute-start.38
  347.6 2.5 collective-permute-done.37
  350.1 3.2 finish.1
  (149 shorter events, 36.8 us)
Async XLA Ops:
  3.4 1.3 collective-permute-start
  4.7 7.9 %collective-permute-start.3 = (f32[16,1]{1,0:T(8,128)S(1)}, f32[16,1]{1,0:T(8,128)S(1)}, u32[]{:S(2)}, u32[]{:S(2)}) collective-permute-start(f32[16,1]{1,0:T(8,128)S(1)} %add.102), channel_id=1, source_target_pairs={{0,6},{1,7},{2,4},{3,5},{4,2},{5,3},{6,0},{7,1},{8,14},{9,15},{10,... | collective-permute-start | bytes 200 | tf_op jit(solution)/shard_map/ppermute | solution.py:26
  8.5 4.1 %collective-permute-start.2 = (f32[16,1]{1,0:T(8,128)S(1)}, f32[16,1]{1,0:T(8,128)S(1)}, u32[]{:S(2)}, u32[]{:S(2)}) collective-permute-start(f32[16,1]{1,0:T(8,128)S(1)} %add.102), channel_id=1, source_target_pairs={{0,4},{1,5},{2,6},{3,7},{4,0},{5,1},{6,2},{7,3},{8,12},{9,13},{10,... | collective-permute-start | bytes 200 | tf_op jit(solution)/shard_map/ppermute | solution.py:26
  9.0 3.7 %collective-permute-start.1 = (f32[16,1]{1,0:T(8,128)S(1)}, f32[16,1]{1,0:T(8,128)S(1)}, u32[]{:S(2)}, u32[]{:S(2)}) collective-permute-start(f32[16,1]{1,0:T(8,128)S(1)} %add.102), channel_id=1, source_target_pairs={{0,2},{1,3},{2,0},{3,1},{4,6},{5,7},{6,4},{7,5},{8,10},{9,11},{10,... | collective-permute-start | bytes 200 | tf_op jit(solution)/shard_map/ppermute | solution.py:26
  38.8 14.6 %all-to-all-start = ((bf16[8,144,256]{2,1,0:T(8,128)(2,1)}), bf16[8,144,256]{2,1,0:T(8,128)(2,1)S(1)}, u32[]{:S(2)}, u32[]{:S(2)}) async-start(bf16[8,144,256]{2,1,0:T(8,128)(2,1)} %get-tuple-element.52), calls=%async_computation | async-start | bytes 1179648 | tf_op jit(solution)/shard_map/all_to_all | solution.py:498
  71.7 28.6 %copy-start.28 = (f32[16]{0:T(128)S(1)}, f32[16]{0:T(128)}, u32[]{:S(2)}) copy-start(f32[16]{0:T(128)} %param.15) | copy-start | bytes 196
  71.7 23.6 %collective-permute-start.4 = (bf16[112,4096]{1,0:T(8,128)(2,1)S(1)}, bf16[112,4096]{1,0:T(8,128)(2,1)S(1)}, u32[]{:S(2)}, u32[]{:S(2)}) collective-permute-start(bf16[112,4096]{1,0:T(8,128)(2,1)S(1)} %get-tuple-element.61), channel_id=1, source_target_pairs={{0,8},{24,16},{1,9},{25,17},{2,10},{26,18},{3,11},{27,19},{4,12},{... | collective-permute-start | bytes 2752520 | tf_op jit(solution)/shard_map/ppermute | solution.py:521
  95.3 13.2 %collective-permute-start.5 = (f32[16,4096]{1,0:T(8,128)S(1)}, f32[16,4096]{1,0:T(8,128)S(1)}, u32[]{:S(2)}, u32[]{:S(2)}) collective-permute-start(f32[16,4096]{1,0:T(8,128)S(1)} %get-tuple-element.63), channel_id=1, source_target_pairs={{0,8},{8,0},{16,24},{24,16},{1,9},{9,1},{17,25},{25,17},{2,10},{10... | collective-permute-start | bytes 786440 | tf_op jit(solution)/shard_map/ppermute | solution.py:26
  97.8 21.4 %collective-permute-start.6 = (f32[16,4096]{1,0:T(8,128)S(1)}, f32[16,4096]{1,0:T(8,128)S(1)}, u32[]{:S(2)}, u32[]{:S(2)}) collective-permute-start(f32[16,4096]{1,0:T(8,128)S(1)} %get-tuple-element.64), channel_id=1, source_target_pairs={{0,16},{8,24},{16,0},{24,8},{1,17},{9,25},{17,1},{25,9},{2,18},{10... | collective-permute-start | bytes 786440 | tf_op jit(solution)/shard_map/ppermute | solution.py:26
  98.8 20.4 %collective-permute-start.7 = (f32[16,4096]{1,0:T(8,128)S(1)}, f32[16,4096]{1,0:T(8,128)S(1)}, u32[]{:S(2)}, u32[]{:S(2)}) collective-permute-start(f32[16,4096]{1,0:T(8,128)S(1)} %get-tuple-element.65), channel_id=1, source_target_pairs={{0,24},{8,16},{16,8},{24,0},{1,25},{9,17},{17,9},{25,1},{2,26},{10... | collective-permute-start | bytes 786440 | tf_op jit(solution)/shard_map/ppermute | solution.py:26
  120.0 8.7 %collective-permute-start.10 = (bf16[16,4096]{1,0:T(8,128)(2,1)S(1)}, bf16[16,4096]{1,0:T(8,128)(2,1)S(1)}, u32[]{:S(2)}, u32[]{:S(2)}) collective-permute-start(bf16[16,4096]{1,0:T(8,128)(2,1)S(1)} %reduce-precision_convert_fusion.refs_0_), channel_id=1, source_target_pairs={{0,24},{8,16},{16,8},{24,0},{1,25},{9,17},{17,9},{25,1},{2,26},{10... | collective-permute-start | bytes 393224 | tf_op jit(solution)/shard_map/ppermute | solution.py:26
  122.5 12.7 %collective-permute-start.9 = (bf16[16,4096]{1,0:T(8,128)(2,1)S(1)}, bf16[16,4096]{1,0:T(8,128)(2,1)S(1)}, u32[]{:S(2)}, u32[]{:S(2)}) collective-permute-start(bf16[16,4096]{1,0:T(8,128)(2,1)S(1)} %reduce-precision_convert_fusion.refs_0_), channel_id=1, source_target_pairs={{0,16},{8,24},{16,0},{24,8},{1,17},{9,25},{17,1},{25,9},{2,18},{10... | collective-permute-start | bytes 393224 | tf_op jit(solution)/shard_map/ppermute | solution.py:26
  127.3 7.9 %collective-permute-start.8 = (bf16[16,4096]{1,0:T(8,128)(2,1)S(1)}, bf16[16,4096]{1,0:T(8,128)(2,1)S(1)}, u32[]{:S(2)}, u32[]{:S(2)}) collective-permute-start(bf16[16,4096]{1,0:T(8,128)(2,1)S(1)} %reduce-precision_convert_fusion.refs_0_), channel_id=1, source_target_pairs={{0,8},{8,0},{16,24},{24,16},{1,9},{9,1},{17,25},{25,17},{2,10},{10... | collective-permute-start | bytes 393224 | tf_op jit(solution)/shard_map/ppermute | solution.py:26
  135.2 26.8 %copy-start.7 = (bf16[16,4096]{1,0:T(8,128)(2,1)}, bf16[16,4096]{1,0:T(8,128)(2,1)S(1)}, u32[]{:S(2)}) copy-start(bf16[16,4096]{1,0:T(8,128)(2,1)S(1)} %collective-permute-done.9.refs_2_) | copy-start | bytes 393220
  135.2 26.8 %copy-start.9 = (bf16[16,4096]{1,0:T(8,128)(2,1)}, bf16[16,4096]{1,0:T(8,128)(2,1)S(1)}, u32[]{:S(2)}) copy-start(bf16[16,4096]{1,0:T(8,128)(2,1)S(1)} %collective-permute-done.8.refs_1_) | copy-start | bytes 393220
  135.2 30.5 %collective-permute-start.12 = (bf16[112,6144]{1,0:T(8,128)(2,1)S(1)}, bf16[112,6144]{1,0:T(8,128)(2,1)}, u32[]{:S(2)}, u32[]{:S(2)}) collective-permute-start(bf16[112,6144]{1,0:T(8,128)(2,1)S(1)} %get-tuple-element.73), channel_id=1, source_target_pairs={{0,8},{24,16},{1,9},{25,17},{2,10},{26,18},{3,11},{27,19},{4,12},{... | collective-permute-start | bytes 4128776 | tf_op jit(solution)/shard_map/ppermute | solution.py:521
  137.9 24.1 %collective-permute-start.11 = (bf16[112,4096]{1,0:T(8,128)(2,1)}, bf16[112,4096]{1,0:T(8,128)(2,1)}, u32[]{:S(2)}, u32[]{:S(2)}) collective-permute-start(bf16[112,4096]{1,0:T(8,128)(2,1)} %add_convert_fusion.5), channel_id=1, source_target_pairs={{8,16},{16,8},{9,17},{17,9},{10,18},{18,10},{11,19},{19,11},{12,20... | collective-permute-start | bytes 2752520 | tf_op jit(solution)/shard_map/ppermute | solution.py:524
  165.7 1.8 collective-permute-start.13
  167.6 7.3 %collective-permute-start.16 = (f32[16,2048]{1,0:T(8,128)S(1)}, f32[16,2048]{1,0:T(8,128)S(1)}, u32[]{:S(2)}, u32[]{:S(2)}) collective-permute-start(f32[16,2048]{1,0:T(8,128)S(1)} %add.112), channel_id=1, source_target_pairs={{0,6},{1,7},{2,4},{3,5},{4,2},{5,3},{6,0},{7,1},{8,14},{9,15},{10,... | collective-permute-start | bytes 393224 | tf_op jit(solution)/shard_map/ppermute | solution.py:26
  169.1 8.2 %collective-permute-start.15 = (f32[16,2048]{1,0:T(8,128)S(1)}, f32[16,2048]{1,0:T(8,128)S(1)}, u32[]{:S(2)}, u32[]{:S(2)}) collective-permute-start(f32[16,2048]{1,0:T(8,128)S(1)} %add.112), channel_id=1, source_target_pairs={{0,4},{1,5},{2,6},{3,7},{4,0},{5,1},{6,2},{7,3},{8,12},{9,13},{10,... | collective-permute-start | bytes 393224 | tf_op jit(solution)/shard_map/ppermute | solution.py:26
  170.5 6.7 %collective-permute-start.14 = (f32[16,2048]{1,0:T(8,128)S(1)}, f32[16,2048]{1,0:T(8,128)S(1)}, u32[]{:S(2)}, u32[]{:S(2)}) collective-permute-start(f32[16,2048]{1,0:T(8,128)S(1)} %add.112), channel_id=1, source_target_pairs={{0,2},{1,3},{2,0},{3,1},{4,6},{5,7},{6,4},{7,5},{8,10},{9,11},{10,... | collective-permute-start | bytes 393224 | tf_op jit(solution)/shard_map/ppermute | solution.py:26
  172.8 34.0 %copy-start.1 = (bf16[112,4096]{1,0:T(8,128)(2,1)}, bf16[112,4096]{1,0:T(8,128)(2,1)S(1)}, u32[]{:S(2)}) copy-start(bf16[112,4096]{1,0:T(8,128)(2,1)S(1)} %add_convert_fusion.4.refs_4_) | copy-start | bytes 2752516
  178.0 46.8 %copy-start.20 = (f32[16,4096]{1,0:T(8,128)S(1)}, f32[16,4096]{1,0:T(8,128)}, u32[]{:S(2)}) copy-start(f32[16,4096]{1,0:T(8,128)} %copy-done.19) | copy-start | bytes 786436
  178.0 51.9 %collective-permute-start.25 = (bf16[112,6144]{1,0:T(8,128)(2,1)S(1)}, bf16[112,6144]{1,0:T(8,128)(2,1)S(1)}, u32[]{:S(2)}, u32[]{:S(2)}) collective-permute-start(bf16[112,6144]{1,0:T(8,128)(2,1)S(1)} %get-tuple-element.90), channel_id=1, source_target_pairs={{0,8},{24,16},{1,9},{25,17},{2,10},{26,18},{3,11},{27,19},{4,12},{... | collective-permute-start | bytes 4128776 | tf_op jit(solution)/shard_map/ppermute | solution.py:521
  182.7 47.2 %collective-permute-start.24 = (bf16[112,6144]{1,0:T(8,128)(2,1)S(1)}, bf16[112,6144]{1,0:T(8,128)(2,1)S(1)}, u32[]{:S(2)}, u32[]{:S(2)}) collective-permute-start(bf16[112,6144]{1,0:T(8,128)(2,1)S(1)} %add_convert_fusion.3), channel_id=1, source_target_pairs={{8,16},{16,8},{9,17},{17,9},{10,18},{18,10},{11,19},{19,11},{12,20... | collective-permute-start | bytes 4128776 | tf_op jit(solution)/shard_map/ppermute | solution.py:524
  183.4 23.9 %collective-permute-start.17 = (bf16[112,4096]{1,0:T(8,128)(2,1)S(1)}, bf16[112,4096]{1,0:T(8,128)(2,1)S(1)}, u32[]{:S(2)}, u32[]{:S(2)}) collective-permute-start(bf16[112,4096]{1,0:T(8,128)(2,1)S(1)} %add_convert_fusion.4.refs_4_), channel_id=1, source_target_pairs={{8,0},{16,24},{9,1},{17,25},{10,2},{18,26},{11,3},{19,27},{12,4},{... | collective-permute-start | bytes 2752520 | tf_op jit(solution)/shard_map/ppermute | solution.py:527
  207.3 8.6 %collective-permute-start.18 = (bf16[16,4096]{1,0:T(8,128)(2,1)S(1)}, bf16[16,4096]{1,0:T(8,128)(2,1)S(1)}, u32[]{:S(2)}, u32[]{:S(2)}) collective-permute-start(bf16[16,4096]{1,0:T(8,128)(2,1)S(1)} %get-tuple-element.87), channel_id=1, source_target_pairs={{0,8},{8,0},{16,24},{24,16},{1,9},{9,1},{17,25},{25,17},{2,10},{10... | collective-permute-start | bytes 393224 | tf_op jit(solution)/shard_map/ppermute | solution.py:26
  209.5 15.2 %collective-permute-start.19 = (bf16[16,4096]{1,0:T(8,128)(2,1)S(1)}, bf16[16,4096]{1,0:T(8,128)(2,1)S(1)}, u32[]{:S(2)}, u32[]{:S(2)}) collective-permute-start(bf16[16,4096]{1,0:T(8,128)(2,1)S(1)} %get-tuple-element.88), channel_id=1, source_target_pairs={{0,16},{8,24},{16,0},{24,8},{1,17},{9,25},{17,1},{25,9},{2,18},{10... | collective-permute-start | bytes 393224 | tf_op jit(solution)/shard_map/ppermute | solution.py:26
  210.7 14.1 %collective-permute-start.20 = (bf16[16,4096]{1,0:T(8,128)(2,1)S(1)}, bf16[16,4096]{1,0:T(8,128)(2,1)S(1)}, u32[]{:S(2)}, u32[]{:S(2)}) collective-permute-start(bf16[16,4096]{1,0:T(8,128)(2,1)S(1)} %get-tuple-element.89), channel_id=1, source_target_pairs={{0,24},{8,16},{16,8},{24,0},{1,25},{9,17},{17,9},{25,1},{2,26},{10... | collective-permute-start | bytes 393224 | tf_op jit(solution)/shard_map/ppermute | solution.py:26
  225.5 7.9 %collective-permute-start.23 = (bf16[16,4096]{1,0:T(8,128)(2,1)S(1)}, bf16[16,4096]{1,0:T(8,128)(2,1)S(1)}, u32[]{:S(2)}, u32[]{:S(2)}) collective-permute-start(bf16[16,4096]{1,0:T(8,128)(2,1)S(1)} %get-tuple-element.110.refs_0_.refs_4_), channel_id=1, source_target_pairs={{0,24},{8,16},{16,8},{24,0},{1,25},{9,17},{17,9},{25,1},{2,26},{10... | collective-permute-start | bytes 393224 | tf_op jit(solution)/shard_map/ppermute | solution.py:26
  228.0 12.8 %collective-permute-start.22 = (bf16[16,4096]{1,0:T(8,128)(2,1)S(1)}, bf16[16,4096]{1,0:T(8,128)(2,1)S(1)}, u32[]{:S(2)}, u32[]{:S(2)}) collective-permute-start(bf16[16,4096]{1,0:T(8,128)(2,1)S(1)} %get-tuple-element.110.refs_0_.refs_4_), channel_id=1, source_target_pairs={{0,16},{8,24},{16,0},{24,8},{1,17},{9,25},{17,1},{25,9},{2,18},{10... | collective-permute-start | bytes 393224 | tf_op jit(solution)/shard_map/ppermute | solution.py:26
  229.4 11.4 %collective-permute-start.21 = (bf16[16,4096]{1,0:T(8,128)(2,1)S(1)}, bf16[16,4096]{1,0:T(8,128)(2,1)S(1)}, u32[]{:S(2)}, u32[]{:S(2)}) collective-permute-start(bf16[16,4096]{1,0:T(8,128)(2,1)S(1)} %get-tuple-element.110.refs_0_.refs_4_), channel_id=1, source_target_pairs={{0,8},{8,0},{16,24},{24,16},{1,9},{9,1},{17,25},{25,17},{2,10},{10... | collective-permute-start | bytes 393224 | tf_op jit(solution)/shard_map/ppermute | solution.py:26
  230.3 10.6 %collective-permute-start.26 = (bf16[112,6144]{1,0:T(8,128)(2,1)S(1)}, bf16[112,6144]{1,0:T(8,128)(2,1)S(1)}, u32[]{:S(2)}, u32[]{:S(2)}) collective-permute-start(bf16[112,6144]{1,0:T(8,128)(2,1)S(1)} %add_convert_fusion.2), channel_id=1, source_target_pairs={{8,16},{16,8},{9,17},{17,9},{10,18},{18,10},{11,19},{19,11},{12,20... | collective-permute-start | bytes 4128776 | tf_op jit(solution)/shard_map/ppermute | solution.py:524
  231.3 36.1 %collective-permute-start.28 = (bf16[112,6144]{1,0:T(8,128)(2,1)S(1)}, bf16[112,6144]{1,0:T(8,128)(2,1)}, u32[]{:S(2)}, u32[]{:S(2)}) collective-permute-start(bf16[112,6144]{1,0:T(8,128)(2,1)S(1)} %add_convert_fusion.refs_5_), channel_id=1, source_target_pairs={{8,0},{16,24},{9,1},{17,25},{10,2},{18,26},{11,3},{19,27},{12,4},{... | collective-permute-start | bytes 4128776 | tf_op jit(solution)/shard_map/ppermute | solution.py:527
  241.1 65.8 %collective-permute-start.27 = (bf16[112,6144]{1,0:T(8,128)(2,1)S(1)}, bf16[112,6144]{1,0:T(8,128)(2,1)}, u32[]{:S(2)}, u32[]{:S(2)}) collective-permute-start(bf16[112,6144]{1,0:T(8,128)(2,1)S(1)} %add_convert_fusion.1.refs_4_), channel_id=1, source_target_pairs={{8,0},{16,24},{9,1},{17,25},{10,2},{18,26},{11,3},{19,27},{12,4},{... | collective-permute-start | bytes 4128776 | tf_op jit(solution)/shard_map/ppermute | solution.py:527
  287.1 32.6 %collective-permute-start.31 = (bf16[16,4096]{1,0:T(8,128)(2,1)S(1)}, bf16[16,4096]{1,0:T(8,128)(2,1)S(1)}, u32[]{:S(2)}, u32[]{:S(2)}) collective-permute-start(bf16[16,4096]{1,0:T(8,128)(2,1)S(1)} %copy-done.11), channel_id=1, source_target_pairs={{0,24},{8,16},{16,8},{24,0},{1,25},{9,17},{17,9},{25,1},{2,26},{10... | collective-permute-start | bytes 393224 | tf_op jit(solution)/shard_map/ppermute | solution.py:26
  289.4 31.0 %collective-permute-start.30 = (bf16[16,4096]{1,0:T(8,128)(2,1)S(1)}, bf16[16,4096]{1,0:T(8,128)(2,1)S(1)}, u32[]{:S(2)}, u32[]{:S(2)}) collective-permute-start(bf16[16,4096]{1,0:T(8,128)(2,1)S(1)} %copy-done.11), channel_id=1, source_target_pairs={{0,16},{8,24},{16,0},{24,8},{1,17},{9,25},{17,1},{25,9},{2,18},{10... | collective-permute-start | bytes 393224 | tf_op jit(solution)/shard_map/ppermute | solution.py:26
  293.1 27.9 %collective-permute-start.29 = (bf16[16,4096]{1,0:T(8,128)(2,1)S(1)}, bf16[16,4096]{1,0:T(8,128)(2,1)S(1)}, u32[]{:S(2)}, u32[]{:S(2)}) collective-permute-start(bf16[16,4096]{1,0:T(8,128)(2,1)S(1)} %copy-done.11), channel_id=1, source_target_pairs={{0,8},{8,0},{16,24},{24,16},{1,9},{9,1},{17,25},{25,17},{2,10},{10... | collective-permute-start | bytes 393224 | tf_op jit(solution)/shard_map/ppermute | solution.py:26
  321.7 13.2 %all-to-all-start.1 = ((bf16[8,128,256]{2,1,0:T(8,128)(2,1)}), bf16[8,128,256]{2,1,0:T(8,128)(2,1)S(1)}, u32[]{:S(2)}, u32[]{:S(2)}) async-start(bf16[8,128,256]{2,1,0:T(8,128)(2,1)} %third_forward_1.1), calls=%async_computation.1 | async-start | bytes 1048576 | tf_op jit(solution)/shard_map/all_to_all | solution.py:572
  325.3 24.8 %copy-start.4 = (f32[16,16384]{1,0:T(8,128)S(1)}, f32[16,16384]{1,0:T(8,128)}, u32[]{:S(2)}) copy-start(f32[16,16384]{1,0:T(8,128)} %copy-done.3) | copy-start | bytes 3145732
  325.3 24.8 %copy-start.8 = (bf16[16,4096]{1,0:T(8,128)(2,1)S(1)}, bf16[16,4096]{1,0:T(8,128)(2,1)}, u32[]{:S(2)}) copy-start(bf16[16,4096]{1,0:T(8,128)(2,1)} %copy-done.7) | copy-start | bytes 393220
  335.3 1.2 collective-permute-start.32
  336.5 4.5 %collective-permute-start.35 = (f32[8,128]{1,0:T(8,128)S(1)}, f32[8,128]{1,0:T(8,128)S(1)}, u32[]{:S(2)}, u32[]{:S(2)}) collective-permute-start(f32[8,128]{1,0:T(8,128)S(1)} %add.125), channel_id=1, source_target_pairs={{0,6},{1,7},{2,4},{3,5},{4,2},{5,3},{6,0},{7,1},{8,14},{9,15},{10,... | collective-permute-start | bytes 12296 | tf_op jit(solution)/shard_map/ppermute | solution.py:26
  337.1 4.0 %collective-permute-start.34 = (f32[8,128]{1,0:T(8,128)S(1)}, f32[8,128]{1,0:T(8,128)S(1)}, u32[]{:S(2)}, u32[]{:S(2)}) collective-permute-start(f32[8,128]{1,0:T(8,128)S(1)} %add.125), channel_id=1, source_target_pairs={{0,4},{1,5},{2,6},{3,7},{4,0},{5,1},{6,2},{7,3},{8,12},{9,13},{10,... | collective-permute-start | bytes 12296 | tf_op jit(solution)/shard_map/ppermute | solution.py:26
  338.6 3.6 %collective-permute-start.33 = (f32[8,128]{1,0:T(8,128)S(1)}, f32[8,128]{1,0:T(8,128)S(1)}, u32[]{:S(2)}, u32[]{:S(2)}) collective-permute-start(f32[8,128]{1,0:T(8,128)S(1)} %add.125), channel_id=1, source_target_pairs={{0,2},{1,3},{2,0},{3,1},{4,6},{5,7},{6,4},{7,5},{8,10},{9,11},{10,... | collective-permute-start | bytes 12296 | tf_op jit(solution)/shard_map/ppermute | solution.py:26
  342.2 5.4 %collective-permute-start.38 = (f32[8,128]{1,0:T(8,128)S(1)}, f32[8,128]{1,0:T(8,128)S(1)}, u32[]{:S(2)}, u32[]{:S(2)}) collective-permute-start(f32[8,128]{1,0:T(8,128)S(1)} %add_add_fusion.3), channel_id=1, source_target_pairs={{0,24},{8,16},{16,8},{24,0},{1,25},{9,17},{17,9},{25,1},{2,26},{10... | collective-permute-start | bytes 12296 | tf_op jit(solution)/shard_map/ppermute | solution.py:26
  345.6 4.5 %collective-permute-start.37 = (f32[8,128]{1,0:T(8,128)S(1)}, f32[8,128]{1,0:T(8,128)S(1)}, u32[]{:S(2)}, u32[]{:S(2)}) collective-permute-start(f32[8,128]{1,0:T(8,128)S(1)} %add_add_fusion.3), channel_id=1, source_target_pairs={{0,16},{8,24},{16,0},{24,8},{1,17},{9,25},{17,1},{25,9},{2,18},{10... | collective-permute-start | bytes 12296 | tf_op jit(solution)/shard_map/ppermute | solution.py:26
  345.6 4.5 %collective-permute-start.36 = (f32[8,128]{1,0:T(8,128)S(1)}, f32[8,128]{1,0:T(8,128)S(1)}, u32[]{:S(2)}, u32[]{:S(2)}) collective-permute-start(f32[8,128]{1,0:T(8,128)S(1)} %add_add_fusion.3), channel_id=1, source_target_pairs={{0,8},{8,0},{16,24},{24,16},{1,9},{9,1},{17,25},{25,17},{2,10},{10... | collective-permute-start | bytes 12296 | tf_op jit(solution)/shard_map/ppermute | solution.py:26
  (22 other events, 255.1 us)
